TPU v7x, 32 devices: a whole 2x2x4 slice. The times are simulated.
32 devices in a mesh: lat: 8 (over z, x), lon: 4 (over y, core).
Axes of the slice: x: 2, y: 2, z: 4, core: 2. Of those that a mesh axis runs over, the one named last changes fastest.
Arguments:
- displacement: float32 [32, 192, 512], P(None, 'lat', 'lon'), may hold values from -6 to 6
- materials: int32 [32, 192, 512], P(None, 'lat', 'lon'), may hold values from 0 to 3
- ice_mask: int32 [192, 512], P('lat', 'lon'), may hold values 0 or 1
- ice_height: float32 [192, 512], P('lat', 'lon'), may hold values from 0.5 to 3
- shear: float32 [4], replicated, may hold values from 0.5 to 4
- restoring: float32 [4], replicated, may hold values from 0.5 to 2
- contrast: float32 [4], replicated, may hold values from 0.3 to 3
- green: float32 [256, 32, 32], P('lat'), may hold values from -1 to 1
Outputs:
- final_displacement: float32 [32, 192, 512], P(None, 'lat', 'lon')
- potential: float32 [32, 192, 512], P(None, 'lat', 'lon')
All inputs are finite; a program needn't handle non-finite values. No bound on the sum of `ice_mask` on one device may be relied on, other than what follows from the above.
Results may differ from a plain program's by a relative error of at most 0.0003.
Values sent between devices are 32-bit elements; how exact they have to be, the bound alone decides.
No kernel may reach another device: no remote copies, remote signals or barrier semaphores. Data moves between devices by JAX's collectives and lax.ppermute only.
A program may use at most 128 MiB of HBM per device.

v0:
```python
import jax
import jax.numpy as jnp
from jax import lax
from jax.sharding import PartitionSpec as P

LMAX = 256
NMAT = 4
ITERS = 2
SWEEPS = 4


def extended(cells, sides, width, closed):
    for axis, dim in sides:
        count = lax.axis_size(axis)
        ends = count if closed else count - 1
        head = lax.slice_in_dim(cells, 0, width, axis=dim)
        tail = lax.slice_in_dim(cells, cells.shape[dim] - width, cells.shape[dim], axis=dim)
        cells = jnp.concatenate(
            [
                lax.ppermute(tail, axis, [(i, (i + 1) % count) for i in range(ends)]),
                cells,
                lax.ppermute(head, axis, [((i + 1) % count, i) for i in range(ends)]),
            ],
            axis=dim,
        )
    return cells


def legendre(theta):
    orders = jnp.arange(LMAX)
    order_f = orders.astype(jnp.float32)
    cosine = jnp.cos(theta)[:, None]
    sine = jnp.sin(theta)[:, None]
    safe = jnp.maximum(order_f, 1.0)
    growth = jnp.where(orders >= 2, 0.5 * jnp.log((2.0 * safe + 1.0) / (2.0 * safe)), 0.0)
    log_diag = jnp.where(orders >= 1, 0.5 * jnp.log(3.0) + jnp.cumsum(growth), 0.0)
    diagonal = jnp.exp(log_diag[None, :] + order_f[None, :] * jnp.log(sine))

    def advance(carry, degree):
        prev_one, prev_two = carry
        deg_f = degree.astype(jnp.float32)
        first = jnp.sqrt(
            (4.0 * deg_f * deg_f - 1.0) / jnp.maximum(deg_f * deg_f - order_f * order_f, 1.0)
        )
        second = jnp.sqrt(
            jnp.maximum((deg_f - 1.0) ** 2 - order_f * order_f, 0.0)
            / jnp.maximum(4.0 * (deg_f - 1.0) ** 2 - 1.0, 1.0)
        )
        general = first * (cosine * prev_one - second * prev_two)
        start_next = jnp.sqrt(2.0 * order_f + 3.0) * cosine * diagonal
        value = jnp.where(
            orders == degree,
            diagonal,
            jnp.where(
                orders == degree - 1, start_next, jnp.where(orders < degree - 1, general, 0.0)
            ),
        )
        return ((value, prev_one), value)

    zeros = jnp.zeros((theta.shape[0], LMAX), jnp.float32)
    _, table = lax.scan(advance, (zeros, zeros), jnp.arange(LMAX), unroll=8)
    return table


def fourier_tables(columns, total):
    orders = jnp.arange(LMAX)
    phase = columns[:, None] * orders[None, :] % total
    angle = 2.0 * jnp.pi / total * phase.astype(jnp.float32)
    forward = jnp.concatenate([jnp.cos(angle), jnp.sin(angle)], axis=1) * (2.0 * jnp.pi / total)
    inverse = jnp.concatenate([jnp.cos(angle), jnp.sin(angle)], axis=1).T
    return (forward, inverse)


def lookup(materials, table):
    result = jnp.zeros(materials.shape, jnp.float32)
    for material in range(NMAT):
        result = result + jnp.where(materials == material, table[material], 0.0)
    return result


def crop_block(block, margin):
    return block[:, margin : block.shape[1] - margin, margin : block.shape[2] - margin]


def margin_sweeps(field, force, stiff, restore, depth, lat_first, total_lat):
    stacked = jnp.stack([field, force, stiff, restore], axis=0)
    lat_wide = extended(stacked, (("lat", 2),), depth, False)
    wide = extended(lat_wide, (("lon", 3),), depth, True)
    current = wide[0]
    rows_wide = wide.shape[2]
    global_rows = lat_first - depth + jnp.arange(rows_wide)
    inside = ((global_rows >= 0) & (global_rows < total_lat))[None, :, None]
    for step in range(depth):
        margin = step + 1
        inner = current[:, 1:-1, 1:-1]
        beside_all = (
            current[:, 2:, 1:-1]
            + current[:, :-2, 1:-1]
            + current[:, 1:-1, 2:]
            + current[:, 1:-1, :-2]
        )
        layer_pad = jnp.pad(inner, ((1, 1), (0, 0), (0, 0)))
        beside_all = beside_all + layer_pad[2:] + layer_pad[:-2]
        force_part = crop_block(wide[1], margin)
        stiff_part = crop_block(wide[2], margin)
        restore_part = crop_block(wide[3], margin)
        valid = inside[:, margin : rows_wide - margin, :]
        denominator = jnp.where(valid, 6.0 * stiff_part + restore_part, 1.0)
        current = jnp.where(valid, (force_part + stiff_part * beside_all) / denominator, 0.0)
    return current


def on_device(displacement, materials, ice_mask, ice_height, shear, restoring, contrast, green):
    highest = lax.Precision.HIGHEST
    layers, lat_rows, lon_cols = displacement.shape
    lon_count = lax.axis_size("lon")
    lat_count = lax.axis_size("lat")
    total_lat = lat_rows * lat_count
    total_lon = lon_cols * lon_count
    layer_share = layers // lon_count
    stiff = lookup(materials, shear)
    restore = lookup(materials, restoring)
    rho_scale = lookup(materials, contrast)
    surface = (ice_mask.astype(jnp.float32) * ice_height)[None]
    load = jnp.concatenate(
        [surface, jnp.zeros((layers - 1, lat_rows, lon_cols), jnp.float32)], axis=0
    )
    lat_first = lax.axis_index("lat") * lat_rows
    theta = ((lat_first + jnp.arange(lat_rows)).astype(jnp.float32) + 0.5) * (jnp.pi / total_lat)
    table = legendre(theta)
    weights = jnp.sin(theta) / (4.0 * total_lat)
    own_columns = lax.axis_index("lon") * lon_cols + jnp.arange(lon_cols)
    layer_first = lax.axis_index("lon") * layer_share
    depth = 1
    for candidate in range(1, SWEEPS + 1):
        if SWEEPS % candidate == 0 and candidate <= min(lat_rows, lon_cols):
            depth = candidate
    forward, inverse = fourier_tables(own_columns, total_lon)
    field = displacement
    potential = jnp.zeros((layers, lat_rows, lon_cols), jnp.float32)
    for iteration in range(ITERS):
        force = load + potential
        field = margin_sweeps(field, force, stiff, restore, depth, lat_first, total_lat)
        density = rho_scale * field
        product = jnp.dot(
            density.reshape(layer_share * lax.axis_size("lon") * lat_rows, lon_cols),
            forward,
            precision=highest,
            preferred_element_type=jnp.float32,
        )
        spectrum = lax.psum_scatter(
            product.reshape(layer_share * lax.axis_size("lon"), lat_rows, 2 * LMAX),
            "lon",
            scatter_dimension=0,
            tiled=True,
        )
        weighted = spectrum.reshape(layer_share, lat_rows, 2, LMAX) * weights[None, :, None, None]
        coeffs = lax.psum_scatter(
            jnp.einsum("lam,kacm->lkcm", table, weighted, precision=highest),
            "lat",
            scatter_dimension=0,
            tiled=True,
        )
        green_part = lax.dynamic_slice_in_dim(green, layer_first, layer_share, 2)
        partial_pot = jnp.einsum("lkj,ljcm->lkcm", green_part, coeffs, precision=highest)
        pot_coeffs = lax.psum_scatter(partial_pot, "lon", scatter_dimension=1, tiled=True)
        synth = jnp.einsum(
            "lam,lkcm->kacm",
            table,
            lax.all_gather(pot_coeffs, "lat", axis=0, tiled=True),
            precision=highest,
        )
        synth = synth.reshape(layer_share, lat_rows, 2 * LMAX)
        piece = lax.all_gather(synth, "lon", axis=0, tiled=True)
        synth_product = jnp.dot(
            piece.reshape(piece.shape[0] * lat_rows, 2 * LMAX),
            inverse,
            precision=highest,
            preferred_element_type=jnp.float32,
        )
        potential = synth_product.reshape(piece.shape[0], lat_rows, lon_cols)
    return (field, potential)


def solution(mesh):
    in_specs = (
        P(None, "lat", "lon"),
        P(None, "lat", "lon"),
        P("lat", "lon"),
        P("lat", "lon"),
        P(),
        P(),
        P(),
        P("lat", None, None),
    )
    out_specs = (P(None, "lat", "lon"), P(None, "lat", "lon"))
    return jax.shard_map(
        on_device, mesh=mesh, in_specs=in_specs, out_specs=out_specs, check_vma=False
    )
```

profile of v0, /device:TPU:1, one launch (start us, length us, event | category | flops | bytes accessed | tf_op | source)
XLA Modules:
  0.0 1261.9 jit_solution(13655230548487754552)
XLA Ops:
  10.9 3.9 add_bitcast_fusion.1
  17.8 4.0 collective-permute-start
  26.6 3.9 collective-permute-done.1
  38.6 4.1 collective-permute-start.3
  44.0 5.3 collective-permute-done.2
  54.2 5.6 fusion.92
  67.7 5.0 fusion.170
  73.2 576.0 %while.19 = (s32[]{:T(128)}, f32[24,256]{1,0:T(8,128)S(1)}, f32[24,256]{1,0:T(8,128)S(1)}, f32[32,8,24,256]{3,2,1,0:T(8,128)}, s32[32,8]{0,1:T(8,128)S(1)}, /*in...) while((s32[]{:T(128)}, f32[24,256]{1,0:T(8,128)S(1)}, ...), condition=%wide.region_4.5_spmd.clone.clone, body=%wide.region_3.4_spmd.clone.clone.sunk | while | flops 1102778 | bytes 1254927 | solution.py:61
  649.2 6.6 copy.37
  659.1 9.8 convolution_bitcast_fusion.1
  668.9 5.6 copy.23
  674.6 91.5 %reduce-scatter.9.cloned.1.call-done = f32[32,8,2,256]{3,1,2,0:T(8,128)} async-done(((f32[256,8,2,256]{3,1,2,0:T(8,128)}), f32[32,8,2,256]{3,1,2,0:T(8,128)}) %reduce-scatter.9.cloned.1.call-update) | async-done | bytes 524304 | tf_op jit(solution)/shard_map/reduce_scatter | solution.py:158
  766.0 4.3 fusion.150
  770.4 31.2 %reduce-scatter.11.cloned.1.call-done = f32[32,8,2,256]{3,1,2,0:T(8,128)} async-done(((f32[32,32,2,256]{3,1,2,0:T(8,128)}), f32[32,8,2,256]{3,1,2,0:T(8,128)}) %reduce-scatter.11.cloned.1.call-update) | async-done | bytes 524304 | tf_op jit(solution)/shard_map/reduce_scatter | solution.py:166
  801.8 74.2 %all-gather.5.cloned.1.call-done = f32[256,8,2,256]{3,1,2,0:T(8,128)} async-done(((f32[32,8,2,256]{3,1,2,0:T(8,128)}), f32[256,8,2,256]{3,1,2,0:T(8,128)}) %all-gather.5.cloned.1.call-update) | async-done | bytes 4194320 | tf_op jit(solution)/shard_map/all_gather | solution.py:170
  876.1 5.6 copy.24
  881.7 10.8 convolution_bitcast_fusion.3
  895.7 19.6 %all-gather.7.cloned.1.call-done = f32[32,24,512]{2,1,0:T(8,128)} async-done(((f32[8,24,512]{2,1,0:T(8,128)}), f32[32,24,512]{2,1,0:T(8,128)}) %all-gather.7.cloned.1.call-update) | async-done | bytes 1572880 | tf_op jit(solution)/shard_map/all_gather | solution.py:174
  922.8 9.7 collective-permute-done.4
  952.6 6.0 fusion.96
  966.9 5.1 fusion.168
  972.1 29.6 %reduce-scatter.13.cloned.1.call-done = f32[8,24,512]{2,1,0:T(8,128)} async-done(((f32[32,24,512]{2,1,0:T(8,128)}), f32[8,24,512]{2,1,0:T(8,128)}) %reduce-scatter.13.cloned.1.call-update) | async-done | bytes 393232 | tf_op jit(solution)/shard_map/reduce_scatter | solution.py:151
  1004.4 7.4 convolution_bitcast_fusion
  1011.8 5.6 copy.33
  1017.5 88.2 %reduce-scatter.15.cloned.1.call-done = f32[32,8,2,256]{3,1,2,0:T(8,128)} async-done(((f32[256,8,2,256]{3,1,2,0:T(8,128)}), f32[32,8,2,256]{3,1,2,0:T(8,128)}) %reduce-scatter.15.cloned.1.call-update) | async-done | bytes 524304 | tf_op jit(solution)/shard_map/reduce_scatter | solution.py:158
  1105.7 4.3 fusion.148
  1110.0 31.3 %reduce-scatter.17.cloned.1.call-done = f32[32,8,2,256]{3,1,2,0:T(8,128)} async-done(((f32[32,32,2,256]{3,1,2,0:T(8,128)}), f32[32,8,2,256]{3,1,2,0:T(8,128)}) %reduce-scatter.17.cloned.1.call-update) | async-done | bytes 524304 | tf_op jit(solution)/shard_map/reduce_scatter | solution.py:166
  1141.4 74.3 %all-gather.9.cloned.1.call-done = f32[256,8,2,256]{3,1,2,0:T(8,128)} async-done(((f32[32,8,2,256]{3,1,2,0:T(8,128)}), f32[256,8,2,256]{3,1,2,0:T(8,128)}) %all-gather.9.cloned.1.call-update) | async-done | bytes 4194320 | tf_op jit(solution)/shard_map/all_gather | solution.py:170
  1215.7 5.6 copy.34
  1221.3 8.0 convolution_bitcast_fusion.2
  1231.4 19.7 %all-gather.11.cloned.1.call-done = f32[32,24,512]{2,1,0:T(8,128)} async-done(((f32[8,24,512]{2,1,0:T(8,128)}), f32[32,24,512]{2,1,0:T(8,128)}) %all-gather.11.cloned.1.call-update) | async-done | bytes 1572880 | tf_op jit(solution)/shard_map/all_gather | solution.py:174
  1251.1 3.5 fusion.172
  (1498 shorter events, 327.2 us)
Async XLA Ops:
  7.2 758.9 %copy-start = (f32[32,32,32]{2,1,0:T(8,128)S(1)}, f32[32,32,32]{2,1,0:T(8,128)}, u32[]{:S(2)}) copy-start(f32[32,32,32]{2,1,0:T(8,128)} %param.17) | copy-start | bytes 393220
  7.2 10.4 copy-start.2
  7.2 648.7 %reduce-scatter.7.cloned.1.call-start = ((), (), s32[]{:S(2)}) async-start(), calls=%async_computation.6 | async-start | bytes 1966080 | tf_op jit(solution)/shard_map/reduce_scatter | solution.py:151
  10.9 6.6 copy-start.17
  14.7 2.8 copy-start.6
  14.7 2.8 copy-start.8
  17.5 13.0 %copy-start.1 = (f32[1,32,24,128]{3,2,1,0:T(8,128)}, f32[1,32,24,128]{3,2,1,0:T(8,128)S(1)}, u32[]{:S(2)}) copy-start(f32[1,32,24,128]{3,2,1,0:T(8,128)S(1)} %get-tuple-element.511) | copy-start | bytes 1179652
  17.5 7.0 copy-start.19
  17.8 8.8 collective-permute-start
  21.7 8.8 collective-permute-start.1
  23.1 37.4 %copy-start.24 = (pred[30]{0:T(512)(128)(4,1)}, pred[30]{0:T(512)(128)(4,1)S(1)}, u32[]{:S(2)}) copy-start(pred[30]{0:T(512)(128)(4,1)S(1)} %slice_bitcast_fusion.8) | copy-start | bytes 94
  23.2 39.4 %copy-start.22 = (pred[28]{0:T(512)(128)(4,1)}, pred[28]{0:T(512)(128)(4,1)S(1)}, u32[]{:S(2)}) copy-start(pred[28]{0:T(512)(128)(4,1)S(1)} %slice_bitcast_fusion.9) | copy-start | bytes 88
  23.3 41.5 %copy-start.20 = (pred[26]{0:T(512)(128)(4,1)}, pred[26]{0:T(512)(128)(4,1)S(1)}, u32[]{:S(2)}) copy-start(pred[26]{0:T(512)(128)(4,1)S(1)} %slice_bitcast_fusion.10) | copy-start | bytes 82
  26.5 3.9 copy-start.15
  38.6 12.5 collective-permute-start.3
  42.6 6.6 collective-permute-start.2
  72.8 693.3 %reduce-scatter.9.cloned.1.call-start = ((), (), s32[]{:S(2)}) async-start(), calls=%async_computation.7 | async-start | bytes 4718592 | tf_op jit(solution)/shard_map/reduce_scatter | solution.py:158
  674.5 127.1 %reduce-scatter.11.cloned.1.call-start = ((), (), s32[]{:S(2)}) async-start(), calls=%async_computation.8 | async-start | bytes 2621440 | tf_op jit(solution)/shard_map/reduce_scatter | solution.py:166
  770.3 105.7 %all-gather.5.cloned.1.call-start = ((), (), s32[]{:S(2)}) async-start(), calls=%async_computation.9 | async-start | bytes 4718592 | tf_op jit(solution)/shard_map/all_gather | solution.py:170
  801.6 113.7 %all-gather.7.cloned.1.call-start = ((), (), s32[]{:S(2)}) async-start(), calls=%async_computation.10 | async-start | bytes 1966080 | tf_op jit(solution)/shard_map/all_gather | solution.py:174
  892.5 22.9 %copy-start.18 = (f32[1,24,128]{2,1,0:T(8,128)S(1)}, f32[1,24,128]{2,1,0:T(8,128)}, u32[]{:S(2)}) copy-start(f32[1,24,128]{2,1,0:T(8,128)} %copy-done.17) | copy-start | bytes 36868
  895.7 106.0 %reduce-scatter.13.cloned.1.call-start = ((), (), s32[]{:S(2)}) async-start(), calls=%async_computation.11 | async-start | bytes 1966080 | tf_op jit(solution)/shard_map/reduce_scatter | solution.py:151
  918.4 14.1 %collective-permute-start.4 = (f32[4,32,4,128]{3,2,1,0:T(4,128)S(1)}, f32[4,32,4,128]{3,2,1,0:T(4,128)S(1)}, u32[]{:S(2)}, u32[]{:S(2)}) collective-permute-start(f32[4,32,4,128]{3,2,1,0:T(4,128)S(1)} %get-tuple-element.493), channel_id=1, source_target_pairs={{0,4},{4,8},{8,12},{12,16},{16,20},{20,24},{24,28},{1,5},{5,9},{9,... | collective-permute-start | bytes 786440 | tf_op jit(solution)/shard_map/ppermute | solution.py:20
  921.5 11.0 collective-permute-start.5
  938.9 4.9 collective-permute-start.6
  943.4 6.1 collective-permute-start.7
  966.9 5.1 copy-start.14
  972.1 133.7 %reduce-scatter.15.cloned.1.call-start = ((), (), s32[]{:S(2)}) async-start(), calls=%async_computation.12 | async-start | bytes 4718592 | tf_op jit(solution)/shard_map/reduce_scatter | solution.py:158
  1017.4 123.9 %reduce-scatter.17.cloned.1.call-start = ((), (), s32[]{:S(2)}) async-start(), calls=%async_computation.13 | async-start | bytes 2621440 | tf_op jit(solution)/shard_map/reduce_scatter | solution.py:166
  1110.0 105.7 %all-gather.9.cloned.1.call-start = ((), (), s32[]{:S(2)}) async-start(), calls=%async_computation.14 | async-start | bytes 4718592 | tf_op jit(solution)/shard_map/all_gather | solution.py:170
  1141.3 109.8 %all-gather.11.cloned.1.call-start = ((), (), s32[]{:S(2)}) async-start(), calls=%async_computation.15 | async-start | bytes 1966080 | tf_op jit(solution)/shard_map/all_gather | solution.py:174
  1229.3 21.8 %copy-start.5 = (f32[128,256]{1,0:T(8,128)S(1)}, f32[128,256]{1,0:T(8,128)}, u32[]{:S(2)}) copy-start(f32[128,256]{1,0:T(8,128)} %get-tuple-element.498) | copy-start | bytes 393220
  (13 other events, 16.2 us)
Sparse Core Ops, SparseCore 0:
  72.9 31.4 reduce-scatter.6
  674.6 91.3 reduce-scatter.8
  770.5 31.1 reduce-scatter.10
  803.8 72.2 all-gather.4
  895.8 19.5 all-gather.6
  972.2 29.5 reduce-scatter.12
  1017.5 88.1 reduce-scatter.14
  1110.1 31.1 reduce-scatter.16
  1143.4 72.1 all-gather.8
  1231.5 19.5 all-gather.10
where the time goes:
time: 1270 us; the launch traced here: 1260 us
  waiting for transfers between devices  482 us (38%)
  loops' own time  330 us (26%)
  other arithmetic  235 us (19%)
  local copies, waits for them, and re-layouts  121 us (10%)
  matrix products  60.9 us (5%)
  starting transfers between devices  17.3 us (1%)
  between operations  15.2 us (1%)
    another operation x1, loops' own time, legendre(): _, table = lax.scan(advance, (zeros, zeros), jnp.arange(LMAX), unroll=8)  330 us
    reduce_scatter x2, waiting for transfers between devices, on_device(): lax.psum_scatter(jnp.einsum('lam,kacm->lkcm', table, weighted, precision=...  180 us
    eq x160, other arithmetic, advance(): orders == degree  161 us
    all_gather x2, waiting for transfers between devices, on_device(): lax.all_gather(pot_coeffs, 'lat', axis=0, tiled=True)  149 us
    reduce_scatter x2, waiting for transfers between devices, on_device(): lax.psum_scatter(partial_pot, 'lon', scatter_dimension=1, tiled=True)  62.5 us
    all_gather x2, waiting for transfers between devices, on_device(): piece = lax.all_gather(synth, 'lon', axis=0, tiled=True)  39.3 us
    reduce_scatter x2, waiting for transfers between devices, on_device(): lax.psum_scatter(product.reshape(layer_share * lax.axis_size('lon'), lat_...  29.7 us
  transfers between devices with their start and end apart: 18, of which 16 were waited for; matrix products, arithmetic and copies ran while one was open for 21% of the time, Pallas kernels for 0%

commit v1 on v0

--- a/solution.py
+++ b/solution.py
@@ -1,12 +1,23 @@
+import functools
+import math
+
 import jax
 import jax.numpy as jnp
 from jax import lax
+from jax.experimental import pallas as pl
+from jax.experimental.pallas import tpu as pltpu
 from jax.sharding import PartitionSpec as P
 
 LMAX = 256
 NMAT = 4
 ITERS = 2
 SWEEPS = 4
+LANES = 128
+DEEP = 8
+SHALLOW = 4
+HALF = jnp.bfloat16
+VMEM_LIMIT = 48 * 1024 * 1024
+BOTH = ("lat", "lon")
 
 
 def extended(cells, sides, width, closed):
@@ -110,7 +121,7 @@
     return current
 
 
-def on_device(displacement, materials, ice_mask, ice_height, shear, restoring, contrast, green):
+def general_device(displacement, materials, ice_mask, ice_height, shear, restoring, contrast, green):
     highest = lax.Precision.HIGHEST
     layers, lat_rows, lon_cols = displacement.shape
     lon_count = lax.axis_size("lon")
@@ -182,6 +193,601 @@
     return (field, potential)
 
 
+def call(kernel, outs, scratch=(), cost=0, smem=()):
+    def run(*args):
+        specs = [
+            pl.BlockSpec(memory_space=pltpu.SMEM if i in smem else pltpu.VMEM)
+            for i in range(len(args))
+        ]
+        out_specs = jax.tree.map(lambda _: pl.BlockSpec(memory_space=pltpu.VMEM), outs)
+        return pl.pallas_call(
+            kernel,
+            out_shape=outs,
+            in_specs=specs,
+            out_specs=out_specs,
+            scratch_shapes=list(scratch),
+            compiler_params=pltpu.CompilerParams(vmem_limit_bytes=VMEM_LIMIT),
+            cost_estimate=pl.CostEstimate(flops=cost, bytes_accessed=1 << 20, transcendentals=0),
+        )(*args)
+
+    return run
+
+
+def f32(*shape):
+    return jax.ShapeDtypeStruct(shape, jnp.float32)
+
+
+def halves(x):
+    high = x.astype(HALF)
+    return high, (x - high.astype(jnp.float32)).astype(HALF)
+
+
+def dot(a, b, dims):
+    return lax.dot_general(a, b, (dims, ((), ())), preferred_element_type=jnp.float32)
+
+
+def dot3(a, b, dims):
+    return dot(a[0], b[0], dims) + (dot(a[0], b[1], dims) + dot(a[1], b[0], dims))
+
+
+def every(ref, start, stride, count):
+    at = pl.ds(start, count, stride=stride)
+    return jnp.concatenate([ref[c, at, :] for c in range(ref.shape[0])], axis=1)
+
+
+def put_every(ref, start, stride, value):
+    at = pl.ds(start, value.shape[0], stride=stride)
+    for c in range(ref.shape[0]):
+        ref[c, at, :] = value[:, c * LANES : (c + 1) * LANES]
+
+
+NN = ((1,), (0,))
+NT = ((1,), (1,))
+
+
+def iota(shape, dim):
+    return lax.broadcasted_iota(jnp.int32, shape, dim)
+
+
+def fourier_kernel(total, share, high_ref, low_ref):
+    rows = 32
+
+    def block(i, carry):
+        column = iota((rows, 2 * LMAX), 1)
+        owner = column // (2 * share)
+        part = (column // share) % 2
+        order = owner * share + column % share
+        j = iota((rows, 2 * LMAX), 0) + i * rows
+        phase = lax.rem(j * order + part * (total - total // 4), total)
+        value = jnp.cos((2.0 * math.pi / total) * phase.astype(jnp.float32))
+        at = pl.ds(pl.multiple_of(i * rows, rows), rows)
+        high, low = halves(value)
+        high_ref[at, :] = high
+        low_ref[at, :] = low
+        return carry
+
+    lax.fori_loop(0, total // rows, block, 0)
+
+
+def legendre_kernel(total_lat, share, index_ref, high_ref, low_ref, table):
+    width = table.shape[0] * LANES
+    base = index_ref[0] * share
+    shape = (share, width)
+    order = iota(shape, 0) + base
+    order_f = order.astype(jnp.float32)
+    row = iota(shape, 1)
+    theta = (row.astype(jnp.float32) + 0.5) * (math.pi / total_lat)
+    cosine = jnp.cos(theta)
+    sine = jnp.where(row < total_lat, jnp.sin(theta), 1.0)
+    terms = (share, LMAX)
+    term = iota(terms, 1)
+    term_f = jnp.maximum(term.astype(jnp.float32), 1.0)
+    growth = 0.5 * jnp.log((2.0 * term_f + 1.0) / (2.0 * term_f))
+    used = (term >= 2) & (term <= iota(terms, 0) + base)
+    total = jnp.sum(jnp.where(used, growth, 0.0), axis=1, keepdims=True)
+    log_diag = jnp.where(order >= 1, 0.5 * math.log(3.0) + total, 0.0)
+    diagonal = jnp.exp(log_diag + order_f * jnp.log(sine))
+    diagonal = jnp.where(row < total_lat, diagonal, 0.0)
+    start_next = jnp.sqrt(2.0 * order_f + 3.0) * cosine * diagonal
+    narrow = (share, LANES)
+    square = ((iota(narrow, 0) + base).astype(jnp.float32)) ** 2
+
+    def wide(x):
+        return jnp.concatenate([x] * (width // LANES), axis=1)
+
+    def advance(degree, carry):
+        prev_one, prev_two = carry
+        deg = jnp.full(narrow, degree, jnp.int32).astype(jnp.float32)
+        first = jnp.sqrt((4.0 * deg * deg - 1.0) / jnp.maximum(deg * deg - square, 1.0))
+        below = (deg - 1.0) * (deg - 1.0)
+        second = jnp.sqrt(jnp.maximum(below - square, 0.0) / jnp.maximum(4.0 * below - 1.0, 1.0))
+        general = wide(first) * (cosine * prev_one - wide(second) * prev_two)
+        value = jnp.where(
+            order == degree,
+            diagonal,
+            jnp.where(
+                order == degree - 1, start_next, jnp.where(order < degree - 1, general, 0.0)
+            ),
+        )
+        for c in range(width // LANES):
+            at = pl.ds(pl.multiple_of(degree * share, share), share)
+            table[c, at, :] = value[:, c * LANES : (c + 1) * LANES]
+        return (value, prev_one)
+
+    table[:, 0:share, :] = jnp.zeros((width // LANES, share, LANES), jnp.float32)
+    zeros = jnp.concatenate([table[c, 0:share, :] for c in range(width // LANES)], axis=1)
+    lax.fori_loop(0, LMAX, advance, (zeros, zeros), unroll=8)
+    for m in range(share):
+        high, low = halves(every(table, m, share, LMAX))
+        high_ref[m] = high
+        low_ref[m] = low
+
+
+def turn_kernel(x_ref, o_ref):
+    o_ref[...] = x_ref[...].T
+
+
+def pack_kernel(u_ref, mat_ref, mask_ref, height_ref, above_ref, below_ref, first_ref, last_ref):
+    layers, rows, cols = u_ref.shape
+    group = LANES // DEEP
+    lane = iota((rows + 2 * DEEP, cols), 1)
+
+    def pack(cells, count):
+        for block in range(-(-count // group)):
+            first = jnp.zeros(lane.shape, jnp.float32)
+            last = first
+            for t in range(min(group, count - block * group)):
+                x = cells(block * group + t)
+                chosen = lane // DEEP == t
+                first = jnp.where(chosen, roll(x, t * DEEP, 1), first)
+                last = jnp.where(chosen, roll(x, (t + 1) * DEEP, 1), last)
+            yield first, last
+
+    def tall(own, at):
+        return jnp.concatenate([above_ref[at], own, below_ref[at]], axis=0)
+
+    surface = mask_ref[...].astype(jnp.float32) * height_ref[...]
+    blocks = [
+        *pack(lambda k: tall(u_ref[k], k), layers),
+        *pack(lambda k: tall(mat_ref[k].astype(jnp.float32), layers + k), layers),
+        *pack(lambda k: tall(surface, 2 * layers), 1),
+    ]
+    for i, (first, last) in enumerate(blocks):
+        first_ref[i] = first
+        last_ref[i] = last
+
+
+def roll(x, shift, axis):
+    shift = shift % x.shape[axis]
+    return x if shift == 0 else pltpu.roll(x, shift, axis)
+
+
+def pick(material, table):
+    value = jnp.full(material.shape, table[NMAT - 1], jnp.float32)
+    for i in range(NMAT - 1):
+        value = jnp.where(material == i, table[i], value)
+    return value
+
+
+def run_sweeps(a_ref, f_ref, now, other):
+    layers, rows, width = a_ref.shape
+    for sweep in range(SWEEPS):
+        src, dst = (now, other) if sweep % 2 == 0 else (other, now)
+
+        def layer(k, carry, src=src, dst=dst):
+            x = src[k + 1]
+            total = roll(x, 1, 1) + roll(x, width - 1, 1) + roll(x, 1, 0) + roll(x, rows - 1, 0)
+            total = total + src[k] + src[k + 2]
+            dst[k + 1] = a_ref[k] * total + f_ref[k]
+            return carry
+
+        lax.fori_loop(0, layers, layer, 0, unroll=2)
+
+
+def clear_ends(ref):
+    zero = jnp.zeros(ref.shape[1:], jnp.float32)
+    ref[0] = zero
+    ref[ref.shape[0] - 1] = zero
+
+
+def put_density(material, field, contrast, index_ref, lon_count, layers, scratch, pieces):
+    share = layers // lon_count
+    for k in range(layers):
+        scratch[k // share, k % share] = pick(material(k), contrast) * field(k)
+    for s in range(lon_count):
+        pieces[s][...] = scratch[lax.rem(index_ref[1] + s, lon_count)]
+
+
+def first_sweeps_kernel(
+    lon_count, total_lat, index_ref, shear_ref, restoring_ref, contrast_ref, u_ref, mat_ref, mask_ref,
+    height_ref, above_ref, below_ref, left_ref, right_ref, *rest,
+):
+    pieces, rest = rest[:lon_count], rest[lon_count:]
+    u_out, a_out, b_out, load_out, now, other, a_scr, b_scr, f_scr, d_scr = rest
+    layers, rows, cols = u_ref.shape
+    tall_rows = rows + 2 * DEEP
+    group = LANES // DEEP
+    cell = (8, LANES)
+    a_of, b_of = [], []
+    for i in range(NMAT):
+        stiff = jnp.full(cell, shear_ref[i], jnp.float32)
+        restore = jnp.full(cell, restoring_ref[i], jnp.float32)
+        b_of.append(1.0 / (6.0 * stiff + restore))
+        a_of.append(stiff * b_of[i])
+    wide_shape = (tall_rows, cols + LANES)
+    spread = lambda x: jnp.concatenate(
+        [jnp.concatenate([x] * (wide_shape[1] // LANES), axis=1)] * (tall_rows // 8), axis=0
+    )
+    a_of = [spread(x) for x in a_of]
+    b_of = [spread(x) for x in b_of]
+    lane = iota((tall_rows, LANES), 1)
+    global_row = iota(wide_shape, 0) + (index_ref[0] * rows - DEEP)
+    inside = (global_row >= 0) & (global_row < total_lat)
+
+    def widened(own, at, block, t):
+        main = jnp.concatenate([above_ref[at], own, below_ref[at]], axis=0)
+        right = roll(right_ref[block], LANES - t * DEEP, 1)
+        left = roll(left_ref[block], LANES - (t + 1) * DEEP, 1)
+        side = jnp.where(lane < DEEP, right, jnp.where(lane >= LANES - DEEP, left, 0.0))
+        return jnp.concatenate([main, side], axis=1)
+
+    blocks = layers // group
+    clear_ends(now)
+    clear_ends(other)
+    load = widened(
+        mask_ref[...].astype(jnp.float32) * height_ref[...], 2 * layers, 2 * blocks, 0
+    )
+    zero = jnp.zeros(wide_shape, jnp.float32)
+    for k in range(layers):
+        now[k + 1] = widened(u_ref[k], k, k // group, k % group)
+        material = widened(
+            mat_ref[k].astype(jnp.float32), layers + k, blocks + k // group, k % group
+        )
+        a_scr[k] = jnp.where(inside, pick(material, a_of), 0.0)
+        b = jnp.where(inside, pick(material, b_of), 0.0)
+        b_scr[k] = b
+        f_scr[k] = b * load if k == 0 else zero
+    run_sweeps(a_scr, f_scr, now, other)
+    keep = pl.ds(DEEP - SHALLOW, rows + 2 * SHALLOW)
+    for k in range(layers):
+        u_out[k] = now[k + 1, keep, :]
+        a_out[k] = a_scr[k, keep, :]
+        b_out[k] = b_scr[k, keep, :]
+    load_out[...] = load[DEEP - SHALLOW : rows + DEEP + SHALLOW]
+    put_density(
+        lambda k: mat_ref[k],
+        lambda k: now[k + 1, pl.ds(DEEP, rows), pl.ds(0, cols)],
+        contrast_ref,
+        index_ref,
+        lon_count,
+        layers,
+        d_scr,
+        pieces,
+    )
+
+
+def second_sweeps_kernel(
+    lon_count, index_ref, contrast_ref, mat_ref, u_ref, a_ref, b_ref, load_ref, *rest
+):
+    parts, rest = rest[:lon_count], rest[lon_count:]
+    pieces, rest = rest[:lon_count], rest[lon_count:]
+    field_out, now, other, f_scr, d_scr = rest
+    layers, rows, cols = mat_ref.shape
+    tall_rows = rows + 2 * SHALLOW
+    share = layers // lon_count
+    chunk = LANES // share
+    lane = iota((tall_rows, LANES), 1)
+    clear_ends(now)
+    clear_ends(other)
+    for s in range(lon_count):
+        source = lax.rem(index_ref[1] + (lon_count - s), lon_count)
+        packed = parts[s][share * tall_rows :]
+        for t in range(share):
+            k = source * share + t
+            main = parts[s][t * tall_rows : (t + 1) * tall_rows]
+            right = roll(packed, LANES - t * chunk, 1)
+            left = roll(packed, LANES - (t + 1) * chunk, 1)
+            side = jnp.where(lane < DEEP, right, left)
+            f_scr[k] = b_ref[k] * jnp.concatenate([main, side], axis=1)
+    f_scr[0] = f_scr[0] + b_ref[0] * load_ref[...]
+    for k in range(layers):
+        now[k + 1] = u_ref[k]
+    run_sweeps(a_ref, f_scr, now, other)
+
+    def field(k):
+        return now[k + 1, pl.ds(SHALLOW, rows), pl.ds(0, cols)]
+
+    for k in range(layers):
+        field_out[k] = field(k)
+    put_density(
+        lambda k: mat_ref[k], field, contrast_ref, index_ref, lon_count, layers, d_scr, pieces
+    )
+
+
+def swap_chunks(blocks, chunk):
+    blocks = list(blocks)
+    lane = iota(blocks[0].shape, 1)
+    step = 1
+    while step < len(blocks):
+        upper = (lane // (chunk * step)) % 2 == 1
+        for i in range(len(blocks)):
+            if i & step:
+                continue
+            a, b = blocks[i], blocks[i + step]
+            blocks[i] = jnp.where(upper, roll(b, chunk * step, 1), a)
+            blocks[i + step] = jnp.where(upper, b, roll(a, LANES - chunk * step, 1))
+        step *= 2
+    return blocks
+
+
+def forward_kernel(lon_count, scale, index_ref, weight_ref, high_ref, low_ref, *rest):
+    parts, (o_ref,) = rest[:lon_count], rest[lon_count:]
+    share, rows, cols = parts[0].shape
+    chunk = LANES // share
+    product = None
+    for s in range(lon_count):
+        source = lax.rem(index_ref[1] + (lon_count - s), lon_count)
+        at = pl.ds(pl.multiple_of(source * cols, cols), cols)
+        term = dot3(
+            halves(parts[s][...].reshape(share * rows, cols)), (high_ref[at, :], low_ref[at, :]), NN
+        )
+        product = term if product is None else product + term
+    weight = weight_ref[...] * scale
+    for g in range(product.shape[1] // LANES):
+        blocks = swap_chunks(
+            [
+                product[k * rows : (k + 1) * rows, g * LANES : (g + 1) * LANES] * weight
+                for k in range(share)
+            ],
+            chunk,
+        )
+        for i in range(share):
+            o_ref[g * share + i] = blocks[i]
+
+
+def spectral_kernel(margin, high_ref, low_ref, green_ref, x_ref, o_ref, turned, coeffs, pots):
+    share, degrees, width = high_ref.shape
+    lat_count, lon_count, rows, _ = x_ref.shape
+    total_lat = lat_count * rows
+    size = 2 * share
+    layers = turned.shape[1] // size
+    pad = jnp.zeros((width - total_lat, LANES), jnp.float32)
+    for q in range(lon_count):
+        x = x_ref[:, q].reshape(total_lat, LANES)
+        x = jnp.concatenate([x, pad], axis=0)
+        for c in range(width // LANES):
+            turned[c, q * LANES : (q + 1) * LANES, :] = x[c * LANES : (c + 1) * LANES].T
+    for m in range(share):
+        x = halves(every(turned, m, share, 2 * layers))
+        put_every(coeffs, m, share, dot3(x, (high_ref[m], low_ref[m]), NT))
+    block = 4
+
+    def targets(i, carry):
+        for c in range(degrees // LANES):
+            sums = [jnp.zeros((size, LANES), jnp.float32) for _ in range(block)]
+            for k in range(0, layers, 8):
+                part = [
+                    green_ref[
+                        pl.ds(pl.multiple_of((i * block + t) * layers + k, 8), 8),
+                        c * LANES : (c + 1) * LANES,
+                    ]
+                    for t in range(block)
+                ]
+                for e in range(8):
+                    x = coeffs[c, (k + e) * size : (k + e + 1) * size, :]
+                    for t in range(block):
+                        sums[t] = sums[t] + part[t][e : e + 1] * x
+            for t in range(block):
+                pots[c, pl.ds(pl.multiple_of((i * block + t) * size, size), size), :] = sums[t]
+        return carry
+
+    lax.fori_loop(0, layers // block, targets, 0)
+    for m in range(share):
+        x = halves(every(pots, m, share, 2 * layers))
+        put_every(turned, m, share, dot3(x, (high_ref[m], low_ref[m]), NN))
+    for q in range(lon_count):
+        x = [turned[c, q * LANES : (q + 1) * LANES, :].T for c in range(width // LANES)]
+        x = jnp.concatenate(x, axis=0)[:total_lat]
+        if margin > 0:
+            edge = jnp.zeros((margin, LANES), jnp.float32)
+            x = jnp.concatenate([edge, x, edge], axis=0)
+        for i in range(lat_count):
+            o_ref[i, q] = x[i * rows : (i + 1) * rows + 2 * margin]
+
+
+def inverse_kernel(lon_count, margin, index_ref, high_ref, low_ref, x_ref, *rest):
+    pieces, (columns,) = rest[:lon_count], rest[lon_count:]
+    owners, rows, _ = x_ref.shape
+    cols = high_ref.shape[0] // lon_count
+    share = columns.shape[1] // rows
+    chunk = LANES // share
+    groups = [
+        swap_chunks([x_ref[g * share + i] for i in range(share)], chunk)
+        for g in range(owners // share)
+    ]
+    terms = jnp.concatenate(
+        [jnp.concatenate([group[k] for group in groups], axis=1) for k in range(share)], axis=0
+    )
+    terms = halves(terms)
+    for q in range(lon_count):
+        at = slice(q * cols, (q + 1) * cols)
+        columns[q] = dot3(terms, (high_ref[at, :], low_ref[at, :]), NT)
+    lane = iota((rows, LANES), 1)
+    for s in range(lon_count):
+        dest = lax.rem(index_ref[1] + s, lon_count)
+        pieces[s][0 : share * rows] = columns[dest]
+        if margin == 0:
+            continue
+        after = lax.rem(dest + 1, lon_count)
+        before = lax.rem(dest + lon_count - 1, lon_count)
+        packed = jnp.zeros((rows, LANES), jnp.float32)
+        for k in range(share):
+            right = roll(columns[after, k * rows : (k + 1) * rows, :], k * chunk, 1)
+            left = roll(columns[before, k * rows : (k + 1) * rows, :], (k + 1) * chunk, 1)
+            packed = jnp.where(
+                lane // DEEP == 2 * k, right, jnp.where(lane // DEEP == 2 * k + 1, left, packed)
+            )
+        pieces[s][share * rows :] = packed
+
+
+def assemble_kernel(lon_count, index_ref, *rest):
+    parts, (o_ref,) = rest[:lon_count], rest[lon_count:]
+    share = o_ref.shape[1]
+    for s in range(lon_count):
+        source = lax.rem(index_ref[1] + (lon_count - s), lon_count)
+        o_ref[source] = parts[s][...].reshape(o_ref.shape[1:])
+
+
+def exchange(pieces):
+    count = len(pieces)
+    return [pieces[0]] + [
+        lax.ppermute(pieces[s], "lon", [(i, (i + s) % count) for i in range(count)])
+        for s in range(1, count)
+    ]
+
+
+def on_device(displacement, materials, ice_mask, ice_height, shear, restoring, contrast, green):
+    layers, rows, cols = displacement.shape
+    lat_count, lon_count = lax.axis_size("lat"), lax.axis_size("lon")
+    total_lat, total_lon = rows * lat_count, cols * lon_count
+    owners = lat_count * lon_count
+    share, orders = layers // lon_count, LMAX // owners
+    width = -(-total_lat // LANES) * LANES
+    tall = rows + 2 * SHALLOW
+    lat_index = lax.axis_index("lat")
+    index = jnp.stack([lat_index, lax.axis_index("lon")]).astype(jnp.int32)
+    owner = (index[0] * lon_count + index[1])[None]
+
+    down = [(i, i + 1) for i in range(lat_count - 1)]
+    up = [(i + 1, i) for i in range(lat_count - 1)]
+
+    def slab(at):
+        return jnp.concatenate(
+            [
+                displacement[:, at],
+                materials[:, at].astype(jnp.float32),
+                (ice_mask[at].astype(jnp.float32) * ice_height[at])[None],
+            ],
+            axis=0,
+        )
+
+    above = lax.ppermute(slab(slice(rows - DEEP, rows)), "lat", down)
+    below = lax.ppermute(slab(slice(0, DEEP)), "lat", up)
+    all_green = lax.all_gather(
+        green.reshape(green.shape[0], layers * layers), "lat", axis=0, tiled=True
+    )
+    table = call(
+        functools.partial(fourier_kernel, total_lon, orders),
+        (jax.ShapeDtypeStruct((total_lon, 2 * LMAX), HALF),) * 2,
+        cost=100_000_000,
+    )()
+    blocks = 2 * (layers * DEEP // LANES) + 1
+    first, last = call(
+        pack_kernel, (f32(blocks, rows + 2 * DEEP, cols),) * 2, cost=10_000_000
+    )(displacement, materials, ice_mask, ice_height, above, below)
+    left = lax.ppermute(last, "lon", [(i, (i + 1) % lon_count) for i in range(lon_count)])
+    right = lax.ppermute(first, "lon", [((i + 1) % lon_count, i) for i in range(lon_count)])
+    legendre_table = call(
+        functools.partial(legendre_kernel, total_lat, orders),
+        (jax.ShapeDtypeStruct((orders, LMAX, width), HALF),) * 2,
+        scratch=[pltpu.VMEM((width // LANES, LMAX * orders, LANES), jnp.float32)],
+        cost=100_000_000,
+        smem=(0,),
+    )(owner)
+    theta = ((lat_index * rows + jnp.arange(rows)).astype(jnp.float32) + 0.5) * (
+        jnp.pi / total_lat
+    )
+    weight = jnp.broadcast_to((jnp.sin(theta) / (4.0 * total_lat))[:, None], (rows, LANES))
+
+    deep = pltpu.VMEM((layers + 2, rows + 2 * DEEP, cols + LANES), jnp.float32)
+    deep_in = pltpu.VMEM((layers, rows + 2 * DEEP, cols + LANES), jnp.float32)
+    flat = pltpu.VMEM((lon_count, share, rows, cols), jnp.float32)
+    kept = f32(layers, tall, cols + LANES)
+    out = call(
+        functools.partial(first_sweeps_kernel, lon_count, total_lat),
+        (f32(share, rows, cols),) * lon_count + (kept,) * 3 + (f32(tall, cols + LANES),),
+        scratch=[deep, deep, deep_in, deep_in, deep_in, flat],
+        cost=100_000_000,
+        smem=(0, 1, 2, 3),
+    )(
+        index, shear, restoring, contrast, displacement, materials, ice_mask, ice_height, above,
+        below, left, right,
+    )
+    pieces, state = out[:lon_count], out[lon_count:]
+    turned_green = call(turn_kernel, f32(layers * layers, LMAX), cost=1_000_000)(all_green)
+
+    for iteration in range(ITERS):
+        margin = SHALLOW if iteration < ITERS - 1 else 0
+        spectrum = call(
+            functools.partial(forward_kernel, lon_count, 2.0 * math.pi / total_lon),
+            f32(owners, rows, LANES),
+            cost=300_000_000,
+            smem=(0,),
+        )(index, weight, *table, *exchange(pieces))
+        spectrum = lax.all_to_all(spectrum, BOTH, 0, 0, tiled=True)
+        square = pltpu.VMEM((width // LANES, lon_count * LANES, LANES), jnp.float32)
+        coeff_shape = pltpu.VMEM((LMAX // LANES, lon_count * LANES, LANES), jnp.float32)
+        synth = call(
+            functools.partial(spectral_kernel, margin),
+            f32(lat_count, lon_count, rows + 2 * margin, LANES),
+            scratch=[square, coeff_shape, coeff_shape],
+            cost=300_000_000,
+        )(
+            *legendre_table,
+            turned_green,
+            spectrum.reshape(lat_count, lon_count, rows, LANES),
+        )
+        synth = lax.all_to_all(
+            synth.reshape(owners, rows + 2 * margin, LANES), BOTH, 0, 0, tiled=True
+        )
+        high = rows + 2 * margin
+        sent = share * high + (high if margin > 0 else 0)
+        parts = call(
+            functools.partial(inverse_kernel, lon_count, margin),
+            (f32(sent, cols),) * lon_count,
+            scratch=[pltpu.VMEM((lon_count, share * high, cols), jnp.float32)],
+            cost=300_000_000,
+            smem=(0,),
+        )(index, *table, synth)
+        parts = exchange(parts)
+        if iteration < ITERS - 1:
+            wide = pltpu.VMEM((layers + 2, tall, cols + LANES), jnp.float32)
+            wide_in = pltpu.VMEM((layers, tall, cols + LANES), jnp.float32)
+            out = call(
+                functools.partial(second_sweeps_kernel, lon_count),
+                (f32(share, rows, cols),) * lon_count + (f32(layers, rows, cols),),
+                scratch=[wide, wide, wide_in, flat],
+                cost=100_000_000,
+                smem=(0, 1),
+            )(index, contrast, materials, *state, *parts)
+            pieces, field = out[:lon_count], out[lon_count]
+    potential = call(
+        functools.partial(assemble_kernel, lon_count),
+        f32(lon_count, share, rows, cols),
+        cost=1_000_000,
+        smem=(0,),
+    )(index, *parts)
+    return (field, potential.reshape(layers, rows, cols))
+
+
+def aligned(mesh, displacement):
+    lat_count, lon_count = mesh.shape["lat"], mesh.shape["lon"]
+    layers, total_lat, total_lon = displacement.shape
+    rows, cols = total_lat // lat_count, total_lon // lon_count
+    owners = lat_count * lon_count
+    return (
+        ITERS == 2
+        and cols == LANES
+        and rows % 8 == 0
+        and layers % (LANES // DEEP) == 0
+        and layers % lon_count == 0
+        and LMAX % owners == 0
+        and 2 * (LMAX // owners) * (layers // lon_count) == LANES
+        and 2 * (LMAX // owners) == 2 * DEEP
+        and LMAX % LANES == 0
+    )
+
+
 def solution(mesh):
     in_specs = (
         P(None, "lat", "lon"),
@@ -194,6 +800,11 @@
         P("lat", None, None),
     )
     out_specs = (P(None, "lat", "lon"), P(None, "lat", "lon"))
-    return jax.shard_map(
-        on_device, mesh=mesh, in_specs=in_specs, out_specs=out_specs, check_vma=False
-    )
+
+    def step(displacement, *others):
+        device = on_device if aligned(mesh, displacement) else general_device
+        return jax.shard_map(
+            device, mesh=mesh, in_specs=in_specs, out_specs=out_specs, check_vma=False
+        )(displacement, *others)
+
+    return step

time: 1270 us -> 179 us (0.14)
  waiting for transfers between devices: 482 us -> 36.2 us
  loops' own time: 330 us -> 0 us
  other arithmetic: 235 us -> 0.19 us
  local copies, waits for them, and re-layouts: 121 us -> 10.6 us
  matrix products: 60.9 us -> 0 us
  blocking collectives: 0 us -> 48.9 us
  Pallas kernels: 0 us -> 43.6 us
    another operation x1 -> x0, loops' own time: 330 us -> none  [legendre(): _, table = lax.scan(advance, (zeros, zeros), jnp.arange(LMAX), unroll=8)]
    reduce_scatter x6 -> x0, waiting for transfers between devices: 272 us -> none  [the longest x2 180 us: on_device(): lax.psum_scatter(jnp.einsum('lam,kacm->lkcm', table, weighted, precision=...]
    all_gather x4 -> x1, waiting for transfers between devices: 188 us -> 0.01 us  [on_device(): lax.all_gather(green.reshape(green.shape[0], layers * layers), 'lat', axi...]
    eq x160 -> x0, other arithmetic: 161 us -> none  [advance(): orders == degree]
    dot_general x10 -> x0, matrix products: 60.9 us -> none  [the longest x2 18.8 us: on_device(): jnp.einsum('lam,lkcm->kacm', table, lax.all_gather(pot_coeffs, 'lat', axi...]
    all_to_all x0 -> x3, blocking collectives: none -> 48.9 us  [the longest x2 34.1 us: on_device(): lax.all_to_all(synth.reshape(owners, rows + 2 * margin, LANES), BOTH, 0,...]
    pallas_call x0 -> x13, Pallas kernels: none -> 43.6 us  [run(): pl.pallas_call(kernel, out_shape=outs, in_specs=specs, out_specs=out_spec...]
    slice x52 -> x1, local copies, waits for them, and re-layouts: 41.7 us -> 0.02 us  [slab(): displacement[:, at]]
  transfers between devices with their start and end apart: 18 -> 18, of which waited for: 16 -> 16; matrix products, arithmetic and copies ran while one was open for 21% -> 0% of each run, Pallas kernels for 0% -> 11%
where the time goes in v1:
time: 179 us; the launch traced here: 178 us
  blocking collectives  48.9 us (27%)
  Pallas kernels  43.6 us (24%)
  waiting for transfers between devices  36.2 us (20%)
  starting transfers between devices  24.5 us (14%)
  between operations  14.3 us (8%)
  local copies, waits for them, and re-layouts  10.6 us (6%)
    pallas_call x13, Pallas kernels, run(): pl.pallas_call(kernel, out_shape=outs, in_specs=specs, out_specs=out_spec...  43.6 us
    all_to_all x2, blocking collectives, on_device(): lax.all_to_all(synth.reshape(owners, rows + 2 * margin, LANES), BOTH, 0,...  34.1 us
    ppermute x12, waiting for transfers between devices, exchange(): lax.ppermute(pieces[s], 'lon', [(i, (i + s) % count) for i in range(count)])  21.5 us
    all_to_all x1, blocking collectives, on_device(): spectrum = lax.all_to_all(spectrum, BOTH, 0, 0, tiled=True)  14.8 us
    unnamed x40, local copies, waits for them, and re-layouts  8.59 us
    ppermute x12, starting transfers between devices, exchange(): lax.ppermute(pieces[s], 'lon', [(i, (i + s) % count) for i in range(count)])  7.3 us
    all_to_all x1, waiting for transfers between devices, on_device(): spectrum = lax.all_to_all(spectrum, BOTH, 0, 0, tiled=True)  7.01 us
    ppermute x1, starting transfers between devices, on_device(): lax.ppermute(last, 'lon', [(i, (i + 1) % lon_count) for i in range(lon_co...  6 us
  transfers between devices with their start and end apart: 18, of which 16 were waited for; matrix products, arithmetic and copies ran while one was open for 0% of the time, Pallas kernels for 11%

profile of v1, /device:TPU:1, one launch (start us, length us, event | category | flops | bytes accessed | tf_op | source)
XLA Modules:
  0.0 178.4 jit_solution(1296189902495311236)
XLA Ops:
  7.2 2.0 %reshape.31 = f32[32,1024]{1,0:T(8,128)} reshape(f32[32,32,32]{2,1,0:T(8,128)} %param.15) | data formatting | bytes 262144 | tf_op jit(solution)/shard_map/reshape | solution.py:677
  10.3 4.0 %collective-permute-start = (f32[65,8,128]{2,1,0:T(8,128)S(1)}, f32[65,8,128]{2,1,0:T(8,128)S(1)}, u32[]{:S(2)}, u32[]{:S(2)}) collective-permute-start(f32[65,8,128]{2,1,0:T(8,128)S(1)} %pad_maximum_fusion), channel_id=1, source_target_pairs={{0,4},{4,8},{8,12},{12,16},{16,20},{20,24},{24,28},{1,5},{5,9},{9,... | collective-permute-start | bytes 798728 | tf_op jit(solution)/shard_map/ppermute | solution.py:674
  14.3 1.3 collective-permute-start.1
  15.6 4.2 %shard_map.97 = (bf16[512,512]{1,0:T(8,128)(2,1)S(1)}, bf16[512,512]{1,0:T(8,128)(2,1)S(1)}) custom-call(), custom_call_target="tpu_custom_call" | custom-call | flops 100000000 | bytes 1048576 | tf_op jit(solution)/shard_map/pallas_call | solution.py:203
  19.8 3.3 %collective-permute-done.1.below_ref = f32[65,8,128]{2,1,0:T(8,128)S(1)} collective-permute-done((f32[65,8,128]{2,1,0:T(8,128)S(1)}, f32[65,8,128]{2,1,0:T(8,128)S(1)}, u32[]{:S(2)}, u32[]{:S(2)}) %collective-permute-start.1) | collective-permute-done | bytes 266272 | tf_op jit(solution)/shard_map/ppermute | solution.py:675
  23.8 6.0 %collective-permute-start.2 = (f32[5,40,128]{2,1,0:T(8,128)S(1)}, f32[5,40,128]{2,1,0:T(8,128)S(1)}, u32[]{:S(2)}, u32[]{:S(2)}) collective-permute-start(f32[5,40,128]{2,1,0:T(8,128)S(1)} %get-tuple-element.29), channel_id=1, source_target_pairs={{0,1},{1,2},{2,3},{3,0},{4,5},{5,6},{6,7},{7,4},{8,9},{9,10},{10,1... | collective-permute-start | bytes 307208 | tf_op jit(solution)/shard_map/ppermute | solution.py:688
  29.9 1.8 %collective-permute-done.2.left_ref = f32[5,40,128]{2,1,0:T(8,128)S(1)} collective-permute-done((f32[5,40,128]{2,1,0:T(8,128)S(1)}, f32[5,40,128]{2,1,0:T(8,128)S(1)}, u32[]{:S(2)}, u32[]{:S(2)}) %collective-permute-start.2) | collective-permute-done | bytes 102432 | tf_op jit(solution)/shard_map/ppermute | solution.py:688
  31.7 2.6 %collective-permute-done.3.right_ref = f32[5,40,128]{2,1,0:T(8,128)S(1)} collective-permute-done((f32[5,40,128]{2,1,0:T(8,128)S(1)}, f32[5,40,128]{2,1,0:T(8,128)S(1)}, u32[]{:S(2)}, u32[]{:S(2)}) %collective-permute-start.3) | collective-permute-done | bytes 102432 | tf_op jit(solution)/shard_map/ppermute | solution.py:689
  34.3 9.8 %shard_map.96 = (f32[8,24,128]{2,1,0:T(8,128)S(1)}, f32[8,24,128]{2,1,0:T(8,128)S(1)}, f32[8,24,128]{2,1,0:T(8,128)S(1)}, f32[8,24,128]{2,1,0:T(8,128)S(1)}, f32...) custom-call(s32[2]{0:T(128)S(1)} %pad_add_fusion.index_ref, ...), custom_call_target="tpu_custom_call" | custom-call | flops 100000000 | bytes 1048576 | tf_op jit(solution)/shard_map/pallas_call | solution.py:203
  49.3 2.5 %collective-permute-done.5.rest_2_ = f32[8,24,128]{2,1,0:T(8,128)S(1)} collective-permute-done((f32[8,24,128]{2,1,0:T(8,128)S(1)}, f32[8,24,128]{2,1,0:T(8,128)S(1)}, u32[]{:S(2)}, u32[]{:S(2)}) %collective-permute-start.5) | collective-permute-done | bytes 98336 | tf_op jit(solution)/shard_map/ppermute | solution.py:644
  51.7 2.0 %collective-permute-done.6.rest_3_ = f32[8,24,128]{2,1,0:T(8,128)S(1)} collective-permute-done((f32[8,24,128]{2,1,0:T(8,128)S(1)}, f32[8,24,128]{2,1,0:T(8,128)S(1)}, u32[]{:S(2)}, u32[]{:S(2)}) %collective-permute-start.6) | collective-permute-done | bytes 98336 | tf_op jit(solution)/shard_map/ppermute | solution.py:644
  53.8 2.4 %shard_map.100 = f32[32,24,128]{2,1,0:T(8,128)} custom-call(s32[2]{0:T(128)S(1)} %pad_add_fusion.index_ref, f32[24,128]{1,0:T(8,128)S(1)} %broadcast_in_dim.18.weight_ref, bf16[512,512]{1,0:T(8,128)(2,1)S(1)} %get-tuple-element.35.high_ref, bf16[512,512]{1,0:T(8,128)(2,1)S(1)} %get-tuple-element.36.low_ref, f32[8,24,128]{2,1,0:T(8,128)S(1)} %get-tuple-element.39.rest_0_, ...), custom_call_target="tpu_custom_call" | custom-call | flops 300000000 | bytes 1048576 | tf_op jit(solution)/shard_map/pallas_call | solution.py:203
  56.2 5.9 %all-to-all-start = ((f32[32,24,128]{2,1,0:T(8,128)}), f32[32,24,128]{2,1,0:T(8,128)}, u32[]{:S(2)}, u32[]{:S(2)}) async-start(f32[32,24,128]{2,1,0:T(8,128)} %shard_map.100), calls=%async_computation | async-start | bytes 786432 | tf_op jit(solution)/shard_map/all_to_all | solution.py:727
  62.1 2.8 %shard_map.98 = (bf16[8,256,256]{2,1,0:T(8,128)(2,1)S(1)}, bf16[8,256,256]{2,1,0:T(8,128)(2,1)S(1)}) custom-call(s32[1]{0:T(128)} %bitcast.4.index_ref), custom_call_target="tpu_custom_call" | custom-call | flops 100000000 | bytes 1048576 | tf_op jit(solution)/shard_map/pallas_call | solution.py:203
  67.5 7.0 %all-to-all-done = f32[32,24,128]{2,1,0:T(8,128)} async-done(((f32[32,24,128]{2,1,0:T(8,128)}), f32[32,24,128]{2,1,0:T(8,128)}, u32[]{:S(2)}, u32[]{:S(2)}) %all-to-all-start) | async-done | bytes 393248 | tf_op jit(solution)/shard_map/all_to_all | solution.py:727
  75.7 4.5 %shard_map.101 = f32[8,4,32,128]{3,2,1,0:T(8,128)S(1)} custom-call(bf16[8,256,256]{2,1,0:T(8,128)(2,1)S(1)} %get-tuple-element.37.high_ref, bf16[8,256,256]{2,1,0:T(8,128)(2,1)S(1)} %copy-done.2, f32[1024,256]{1,0:T(8,128)S(1)} %shard_map.99.green_ref, f32[8,4,24,128]{3,2,1,0:T(8,128)} %bitcast.5.x_ref), custom_call_target="tpu_custom_call" | custom-call | flops 300000000 | bytes 1048576 | tf_op jit(solution)/shard_map/pallas_call | solution.py:203
  80.2 18.5 %all_to_all.20.x_ref = f32[32,32,128]{2,1,0:T(8,128)S(1)} all-to-all(f32[32,32,128]{2,1,0:T(8,128)S(1)} %bitcast.12), channel_id=1, replica_groups=mesh['lat'=8,'lon'=4] {'lat','lon'}, dimensions={0} | all-to-all | bytes 1048576 | tf_op jit(solution)/shard_map/all_to_all | solution.py:740
  98.7 2.2 %shard_map.102 = (f32[288,128]{1,0:T(8,128)S(1)}, f32[288,128]{1,0:T(8,128)S(1)}, f32[288,128]{1,0:T(8,128)S(1)}, f32[288,128]{1,0:T(8,128)S(1)}) custom-call(s32[2]{0:T(128)S(1)} %pad_add_fusion.index_ref, bf16[512,512]{1,0:T(8,128)(2,1)S(1)} %get-tuple-element.35.high_ref, bf16[512,512]{1,0:T(8,128)(2,1)S(1)} %get-tuple-element.36.low_ref, ...), custom_call_target="tpu_custom_call" | custom-call | flops 300000000 | bytes 1048576 | tf_op jit(solution)/shard_map/pallas_call | solution.py:203
  103.0 1.9 %collective-permute-done.7.rest_1_ = f32[288,128]{1,0:T(8,128)S(1)} collective-permute-done((f32[288,128]{1,0:T(8,128)S(1)}, f32[288,128]{1,0:T(8,128)S(1)}, u32[]{:S(2)}, u32[]{:S(2)}) %collective-permute-start.7) | collective-permute-done | bytes 147488 | tf_op jit(solution)/shard_map/ppermute | solution.py:644
  104.8 4.8 %collective-permute-done.8.rest_2_ = f32[288,128]{1,0:T(8,128)S(1)} collective-permute-done((f32[288,128]{1,0:T(8,128)S(1)}, f32[288,128]{1,0:T(8,128)S(1)}, u32[]{:S(2)}, u32[]{:S(2)}) %collective-permute-start.8) | collective-permute-done | bytes 147488 | tf_op jit(solution)/shard_map/ppermute | solution.py:644
  110.9 8.7 %shard_map.103 = (f32[8,24,128]{2,1,0:T(8,128)S(1)}, f32[8,24,128]{2,1,0:T(8,128)S(1)}, f32[8,24,128]{2,1,0:T(8,128)S(1)}, f32[8,24,128]{2,1,0:T(8,128)S(1)}, f32[32,24,128]{2,1,0:T(8,128)}) custom-call(s32[2]{0:T(128)S(1)} %pad_add_fusion.index_ref, f32[4]{0:T(128)S(1)} %copy-done.17, s32[32,24,128]{2,1,0:T(8,128)S(1)} %copy-done, ...), custom_call_target="tpu_custom_call" | custom-call | flops 100000000 | bytes 1048576 | tf_op jit(solution)/shard_map/pallas_call | solution.py:203
  121.2 2.6 %collective-permute-done.11.rest_2_ = f32[8,24,128]{2,1,0:T(8,128)S(1)} collective-permute-done((f32[8,24,128]{2,1,0:T(8,128)S(1)}, f32[8,24,128]{2,1,0:T(8,128)S(1)}, u32[]{:S(2)}, u32[]{:S(2)}) %collective-permute-start.11) | collective-permute-done | bytes 98336 | tf_op jit(solution)/shard_map/ppermute | solution.py:644
  123.8 1.6 collective-permute-done.12.rest_3_
  125.4 1.6 shard_map.104
  127.0 14.8 %all_to_all.21 = f32[32,24,128]{2,1,0:T(8,128)S(1)} all-to-all(f32[32,24,128]{2,1,0:T(8,128)S(1)} %shard_map.104), channel_id=1, replica_groups=mesh['lat'=8,'lon'=4] {'lat','lon'}, dimensions={0} | all-to-all | bytes 786432 | tf_op jit(solution)/shard_map/all_to_all | solution.py:727
  141.8 3.4 %shard_map.105 = f32[8,4,24,128]{3,2,1,0:T(8,128)S(1)} custom-call(bf16[8,256,256]{2,1,0:T(8,128)(2,1)S(1)} %get-tuple-element.37.high_ref, bf16[8,256,256]{2,1,0:T(8,128)(2,1)S(1)} %copy-done.3, f32[1024,256]{1,0:T(8,128)S(1)} %shard_map.99.green_ref, f32[8,4,24,128]{3,2,1,0:T(8,128)S(1)} %bitcast.13), custom_call_target="tpu_custom_call" | custom-call | flops 300000000 | bytes 1048576 | tf_op jit(solution)/shard_map/pallas_call | solution.py:203
  145.3 15.6 %all_to_all.22.x_ref = f32[32,24,128]{2,1,0:T(8,128)S(1)} all-to-all(f32[32,24,128]{2,1,0:T(8,128)S(1)} %bitcast.14), channel_id=1, replica_groups=mesh['lat'=8,'lon'=4] {'lat','lon'}, dimensions={0} | all-to-all | bytes 786432 | tf_op jit(solution)/shard_map/all_to_all | solution.py:740
  160.9 1.7 shard_map.106
  162.5 1.3 collective-permute-start.13
  163.8 1.3 collective-permute-start.14
  165.4 4.2 %collective-permute-done.14.rest_2_ = f32[192,128]{1,0:T(8,128)S(1)} collective-permute-done((f32[192,128]{1,0:T(8,128)S(1)}, f32[192,128]{1,0:T(8,128)S(1)}, u32[]{:S(2)}, u32[]{:S(2)}) %collective-permute-start.14) | collective-permute-done | bytes 98336 | tf_op jit(solution)/shard_map/ppermute | solution.py:644
  170.2 1.3 shard_map.107
  (70 shorter events, 16.8 us)
Async XLA Ops:
  7.2 2.1 %copy-start.4 = (f32[32,24,128]{2,1,0:T(8,128)S(1)}, f32[32,24,128]{2,1,0:T(8,128)}, u32[]{:S(2)}) copy-start(f32[32,24,128]{2,1,0:T(8,128)} %u_ref.3) | copy-start | bytes 1179652
  7.2 58.7 %all-gather.2.cloned.1.call-start = ((), (), s32[]{:S(2)}) async-start(), calls=%async_computation.4 | async-start | bytes 1179648 | tf_op jit(solution)/shard_map/all_gather | solution.py:676
  9.2 1.0 copy-start
  10.3 9.6 %collective-permute-start = (f32[65,8,128]{2,1,0:T(8,128)S(1)}, f32[65,8,128]{2,1,0:T(8,128)S(1)}, u32[]{:S(2)}, u32[]{:S(2)}) collective-permute-start(f32[65,8,128]{2,1,0:T(8,128)S(1)} %pad_maximum_fusion), channel_id=1, source_target_pairs={{0,4},{4,8},{8,12},{12,16},{16,20},{20,24},{24,28},{1,5},{5,9},{9,... | collective-permute-start | bytes 798728 | tf_op jit(solution)/shard_map/ppermute | solution.py:674
  14.3 8.8 %collective-permute-start.1 = (f32[65,8,128]{2,1,0:T(8,128)S(1)}, f32[65,8,128]{2,1,0:T(8,128)S(1)}, u32[]{:S(2)}, u32[]{:S(2)}) collective-permute-start(f32[65,8,128]{2,1,0:T(8,128)S(1)} %pad_maximum_fusion.1), channel_id=1, source_target_pairs={{4,0},{8,4},{12,8},{16,12},{20,16},{24,20},{28,24},{5,1},{9,5},{13... | collective-permute-start | bytes 798728 | tf_op jit(solution)/shard_map/ppermute | solution.py:675
  23.8 7.9 %collective-permute-start.2 = (f32[5,40,128]{2,1,0:T(8,128)S(1)}, f32[5,40,128]{2,1,0:T(8,128)S(1)}, u32[]{:S(2)}, u32[]{:S(2)}) collective-permute-start(f32[5,40,128]{2,1,0:T(8,128)S(1)} %get-tuple-element.29), channel_id=1, source_target_pairs={{0,1},{1,2},{2,3},{3,0},{4,5},{5,6},{6,7},{7,4},{8,9},{9,10},{10,1... | collective-permute-start | bytes 307208 | tf_op jit(solution)/shard_map/ppermute | solution.py:688
  29.8 4.5 %collective-permute-start.3 = (f32[5,40,128]{2,1,0:T(8,128)S(1)}, f32[5,40,128]{2,1,0:T(8,128)S(1)}, u32[]{:S(2)}, u32[]{:S(2)}) collective-permute-start(f32[5,40,128]{2,1,0:T(8,128)S(1)} %get-tuple-element.30), channel_id=1, source_target_pairs={{1,0},{2,1},{3,2},{0,3},{5,4},{6,5},{7,6},{4,7},{9,8},{10,9},{11,1... | collective-permute-start | bytes 307208 | tf_op jit(solution)/shard_map/ppermute | solution.py:689
  29.8 4.5 %copy-start.16 = (f32[4]{0:T(128)S(1)}, f32[4]{0:T(128)}, u32[]{:S(2)}) copy-start(f32[4]{0:T(128)} %contrast_ref.3) | copy-start | bytes 52
  29.8 4.5 %copy-start.18 = (f32[4]{0:T(128)S(1)}, f32[4]{0:T(128)}, u32[]{:S(2)}) copy-start(f32[4]{0:T(128)} %shear_ref.1) | copy-start | bytes 52
  29.8 4.5 %copy-start.19 = (f32[4]{0:T(128)S(1)}, f32[4]{0:T(128)}, u32[]{:S(2)}) copy-start(f32[4]{0:T(128)} %restoring_ref.1) | copy-start | bytes 52
  44.1 1.0 copy-start.5
  47.6 1.6 collective-permute-start.4
  47.6 4.1 %collective-permute-start.5 = (f32[8,24,128]{2,1,0:T(8,128)S(1)}, f32[8,24,128]{2,1,0:T(8,128)S(1)}, u32[]{:S(2)}, u32[]{:S(2)}) collective-permute-start(f32[8,24,128]{2,1,0:T(8,128)S(1)} %get-tuple-element.41), channel_id=1, source_target_pairs={{0,2},{1,3},{2,0},{3,1},{4,6},{5,7},{6,4},{7,5},{8,10},{9,11},{10,... | collective-permute-start | bytes 294920 | tf_op jit(solution)/shard_map/ppermute | solution.py:644
  48.2 5.6 %collective-permute-start.6 = (f32[8,24,128]{2,1,0:T(8,128)S(1)}, f32[8,24,128]{2,1,0:T(8,128)S(1)}, u32[]{:S(2)}, u32[]{:S(2)}) collective-permute-start(f32[8,24,128]{2,1,0:T(8,128)S(1)} %get-tuple-element.42), channel_id=1, source_target_pairs={{0,3},{1,0},{2,1},{3,2},{4,7},{5,4},{6,5},{7,6},{8,11},{9,8},{10,9... | collective-permute-start | bytes 294920 | tf_op jit(solution)/shard_map/ppermute | solution.py:644
  56.2 18.3 %all-to-all-start = ((f32[32,24,128]{2,1,0:T(8,128)}), f32[32,24,128]{2,1,0:T(8,128)}, u32[]{:S(2)}, u32[]{:S(2)}) async-start(f32[32,24,128]{2,1,0:T(8,128)} %shard_map.100), calls=%async_computation | async-start | bytes 786432 | tf_op jit(solution)/shard_map/all_to_all | solution.py:727
  64.9 1.0 copy-start.1
  65.9 1.2 copy-start.11
  74.5 1.2 copy-start.2
  75.7 34.5 %copy-start.10 = (f32[32,32,256]{2,1,0:T(8,128)S(1)}, f32[32,32,256]{2,1,0:T(8,128)}, u32[]{:S(2)}) copy-start(f32[32,32,256]{2,1,0:T(8,128)} %copy-done.9) | copy-start | bytes 3145732
  80.2 30.0 %copy-start.8 = (f32[32,32,256]{2,1,0:T(8,128)S(1)}, f32[32,32,256]{2,1,0:T(8,128)}, u32[]{:S(2)}) copy-start(f32[32,32,256]{2,1,0:T(8,128)} %copy-done.7) | copy-start | bytes 3145732
  98.7 11.5 %copy-start.6 = (f32[32,32,256]{2,1,0:T(8,128)S(1)}, f32[32,32,256]{2,1,0:T(8,128)}, u32[]{:S(2)}) copy-start(f32[32,32,256]{2,1,0:T(8,128)} %copy-done.5) | copy-start | bytes 3145732
  98.7 11.5 %copy-start.15 = (f32[32,256]{1,0:T(8,128)S(1)}, f32[32,256]{1,0:T(8,128)}, u32[]{:S(2)}) copy-start(f32[32,256]{1,0:T(8,128)} %copy-done.14) | copy-start | bytes 98308
  100.9 3.9 %collective-permute-start.7 = (f32[288,128]{1,0:T(8,128)S(1)}, f32[288,128]{1,0:T(8,128)S(1)}, u32[]{:S(2)}, u32[]{:S(2)}) collective-permute-start(f32[288,128]{1,0:T(8,128)S(1)} %get-tuple-element.44), channel_id=1, source_target_pairs={{0,1},{1,2},{2,3},{3,0},{4,5},{5,6},{6,7},{7,4},{8,9},{9,10},{10,1... | collective-permute-start | bytes 442376 | tf_op jit(solution)/shard_map/ppermute | solution.py:644
  102.1 7.5 %collective-permute-start.8 = (f32[288,128]{1,0:T(8,128)S(1)}, f32[288,128]{1,0:T(8,128)S(1)}, u32[]{:S(2)}, u32[]{:S(2)}) collective-permute-start(f32[288,128]{1,0:T(8,128)S(1)} %get-tuple-element.45), channel_id=1, source_target_pairs={{0,2},{1,3},{2,0},{3,1},{4,6},{5,7},{6,4},{7,5},{8,10},{9,11},{10,... | collective-permute-start | bytes 442376 | tf_op jit(solution)/shard_map/ppermute | solution.py:644
  103.0 7.3 %collective-permute-start.9 = (f32[288,128]{1,0:T(8,128)S(1)}, f32[288,128]{1,0:T(8,128)S(1)}, u32[]{:S(2)}, u32[]{:S(2)}) collective-permute-start(f32[288,128]{1,0:T(8,128)S(1)} %get-tuple-element.46), channel_id=1, source_target_pairs={{0,3},{1,0},{2,1},{3,2},{4,7},{5,4},{6,5},{7,6},{8,11},{9,8},{10,9... | collective-permute-start | bytes 442376 | tf_op jit(solution)/shard_map/ppermute | solution.py:644
  119.6 1.6 collective-permute-start.10
  119.6 4.3 %collective-permute-start.11 = (f32[8,24,128]{2,1,0:T(8,128)S(1)}, f32[8,24,128]{2,1,0:T(8,128)S(1)}, u32[]{:S(2)}, u32[]{:S(2)}) collective-permute-start(f32[8,24,128]{2,1,0:T(8,128)S(1)} %get-tuple-element.50), channel_id=1, source_target_pairs={{0,2},{1,3},{2,0},{3,1},{4,6},{5,7},{6,4},{7,5},{8,10},{9,11},{10,... | collective-permute-start | bytes 294920 | tf_op jit(solution)/shard_map/ppermute | solution.py:644
  120.2 5.2 %collective-permute-start.12 = (f32[8,24,128]{2,1,0:T(8,128)S(1)}, f32[8,24,128]{2,1,0:T(8,128)S(1)}, u32[]{:S(2)}, u32[]{:S(2)}) collective-permute-start(f32[8,24,128]{2,1,0:T(8,128)S(1)} %get-tuple-element.51), channel_id=1, source_target_pairs={{0,3},{1,0},{2,1},{3,2},{4,7},{5,4},{6,5},{7,6},{8,11},{9,8},{10,9... | collective-permute-start | bytes 294920 | tf_op jit(solution)/shard_map/ppermute | solution.py:644
  125.4 16.5 %copy-start.3 = (bf16[8,256,256]{2,1,0:T(8,128)(2,1)S(1)}, bf16[8,256,256]{2,1,0:T(8,128)(2,1)}, u32[]{:S(2)}) copy-start(bf16[8,256,256]{2,1,0:T(8,128)(2,1)} %copy-done.1) | copy-start | bytes 3145732
  162.5 2.9 %collective-permute-start.13 = (f32[192,128]{1,0:T(8,128)S(1)}, f32[192,128]{1,0:T(8,128)S(1)}, u32[]{:S(2)}, u32[]{:S(2)}) collective-permute-start(f32[192,128]{1,0:T(8,128)S(1)} %get-tuple-element.53), channel_id=1, source_target_pairs={{0,1},{1,2},{2,3},{3,0},{4,5},{5,6},{6,7},{7,4},{8,9},{9,10},{10,1... | collective-permute-start | bytes 294920 | tf_op jit(solution)/shard_map/ppermute | solution.py:644
  163.8 5.8 %collective-permute-start.14 = (f32[192,128]{1,0:T(8,128)S(1)}, f32[192,128]{1,0:T(8,128)S(1)}, u32[]{:S(2)}, u32[]{:S(2)}) collective-permute-start(f32[192,128]{1,0:T(8,128)S(1)} %get-tuple-element.54), channel_id=1, source_target_pairs={{0,2},{1,3},{2,0},{3,1},{4,6},{5,7},{6,4},{7,5},{8,10},{9,11},{10,... | collective-permute-start | bytes 294920 | tf_op jit(solution)/shard_map/ppermute | solution.py:644
  165.1 5.2 %collective-permute-start.15 = (f32[192,128]{1,0:T(8,128)S(1)}, f32[192,128]{1,0:T(8,128)S(1)}, u32[]{:S(2)}, u32[]{:S(2)}) collective-permute-start(f32[192,128]{1,0:T(8,128)S(1)} %get-tuple-element.55), channel_id=1, source_target_pairs={{0,3},{1,0},{2,1},{3,2},{4,7},{5,4},{6,5},{7,6},{8,11},{9,8},{10,9... | collective-permute-start | bytes 294920 | tf_op jit(solution)/shard_map/ppermute | solution.py:644
  (6 other events, 4.7 us)
Sparse Core Ops, SparseCore 0:
  10.7 43.7 all-gather.1

commit v2 on v1

--- a/solution.py
+++ b/solution.py
@@ -16,7 +16,7 @@
 DEEP = 8
 SHALLOW = 4
 HALF = jnp.bfloat16
-VMEM_LIMIT = 48 * 1024 * 1024
+VMEM_LIMIT = 16 * 1024 * 1024
 BOTH = ("lat", "lon")
 
 
@@ -193,21 +193,22 @@
     return (field, potential)
 
 
-def call(kernel, outs, scratch=(), cost=0, smem=()):
+def call(kernel, outs, scratch=(), smem=(), hbm=()):
+    def space(i):
+        return pl.BlockSpec(memory_space=pl.ANY if i in hbm else pltpu.VMEM)
+
     def run(*args):
-        specs = [
-            pl.BlockSpec(memory_space=pltpu.SMEM if i in smem else pltpu.VMEM)
-            for i in range(len(args))
-        ]
-        out_specs = jax.tree.map(lambda _: pl.BlockSpec(memory_space=pltpu.VMEM), outs)
         return pl.pallas_call(
             kernel,
             out_shape=outs,
-            in_specs=specs,
-            out_specs=out_specs,
+            in_specs=[
+                pl.BlockSpec(memory_space=pltpu.SMEM if i in smem else pltpu.VMEM)
+                for i in range(len(args))
+            ],
+            out_specs=tuple(space(i) for i in range(len(outs))) if type(outs) is tuple else space(0),
             scratch_shapes=list(scratch),
             compiler_params=pltpu.CompilerParams(vmem_limit_bytes=VMEM_LIMIT),
-            cost_estimate=pl.CostEstimate(flops=cost, bytes_accessed=1 << 20, transcendentals=0),
+            cost_estimate=pl.CostEstimate(flops=1, bytes_accessed=1, transcendentals=0),
         )(*args)
 
     return run
@@ -250,26 +251,33 @@
 
 
 def fourier_kernel(total, share, high_ref, low_ref):
-    rows = 32
+    shape = (16, 2 * LMAX)
+    column = iota(shape, 1)
+    order = column // (2 * share) * share + column % share
+    shift = (column // share) % 2 * (total - total // 4)
+    first = iota(shape, 0) * order + shift
+    quarter, half = total // 4, total // 2
 
     def block(i, carry):
-        column = iota((rows, 2 * LMAX), 1)
-        owner = column // (2 * share)
-        part = (column // share) % 2
-        order = owner * share + column % share
-        j = iota((rows, 2 * LMAX), 0) + i * rows
-        phase = lax.rem(j * order + part * (total - total // 4), total)
-        value = jnp.cos((2.0 * math.pi / total) * phase.astype(jnp.float32))
-        at = pl.ds(pl.multiple_of(i * rows, rows), rows)
-        high, low = halves(value)
+        phase = first + order * (i * shape[0])
+        phase = phase & (total - 1) if total & (total - 1) == 0 else lax.rem(phase, total)
+        near = jnp.minimum(phase, total - phase)
+        beyond = near > quarter
+        angle = jnp.where(beyond, half - near, near).astype(jnp.float32) * (2.0 * math.pi / total)
+        square = angle * angle
+        value = jnp.full(shape, 1.0 / math.factorial(14), jnp.float32)
+        for n in range(12, -1, -2):
+            value = 1.0 / math.factorial(n) - square * value
+        high, low = halves(jnp.where(beyond, -value, value))
+        at = pl.ds(pl.multiple_of(i * shape[0], shape[0]), shape[0])
         high_ref[at, :] = high
         low_ref[at, :] = low
         return carry
 
-    lax.fori_loop(0, total // rows, block, 0)
-
-
-def legendre_kernel(total_lat, share, index_ref, high_ref, low_ref, table):
+    lax.fori_loop(0, total // shape[0], block, 0, unroll=2)
+
+
+def legendre_kernel(total_lat, share, index_ref, high_out, low_out, table, high_ref, low_ref, sem):
     width = table.shape[0] * LANES
     base = index_ref[0] * share
     shape = (share, width)
@@ -321,40 +329,47 @@
         high, low = halves(every(table, m, share, LMAX))
         high_ref[m] = high
         low_ref[m] = low
-
-
-def turn_kernel(x_ref, o_ref):
-    o_ref[...] = x_ref[...].T
-
-
-def pack_kernel(u_ref, mat_ref, mask_ref, height_ref, above_ref, below_ref, first_ref, last_ref):
-    layers, rows, cols = u_ref.shape
-    group = LANES // DEEP
-    lane = iota((rows + 2 * DEEP, cols), 1)
-
-    def pack(cells, count):
-        for block in range(-(-count // group)):
-            first = jnp.zeros(lane.shape, jnp.float32)
-            last = first
-            for t in range(min(group, count - block * group)):
-                x = cells(block * group + t)
-                chosen = lane // DEEP == t
-                first = jnp.where(chosen, roll(x, t * DEEP, 1), first)
-                last = jnp.where(chosen, roll(x, (t + 1) * DEEP, 1), last)
-            yield first, last
-
-    def tall(own, at):
-        return jnp.concatenate([above_ref[at], own, below_ref[at]], axis=0)
-
+    copies = [
+        pltpu.make_async_copy(high_ref, high_out, sem.at[0]),
+        pltpu.make_async_copy(low_ref, low_out, sem.at[1]),
+    ]
+    for copy in copies:
+        copy.start()
+    for copy in copies:
+        copy.wait()
+
+
+def turn_kernel(size, index_ref, *rest):
+    blocks, (o_ref, ordered) = rest[:-2], rest[-2:]
+    near = blocks[0].shape[0] // size
+    width = blocks[0].shape[1]
+    order, step = [0], near
+    while step > 0:
+        order, step = order + [i ^ step for i in order], step // 2
+    for half in range(2):
+        for i in range(2 * near):
+            at = pl.ds(pl.multiple_of((index_ref[0] ^ order[i]) * size, size), size)
+            block = blocks[2 * half + i // near]
+            ordered[at, :] = block[(i % near) * size : (i % near + 1) * size, :]
+        first = (index_ref[1] ^ half) % 2 * width
+        o_ref[pl.ds(pl.multiple_of(first, width), width), :] = ordered[...].T
+
+
+def slab_kernel(u_ref, mat_ref, mask_ref, height_ref, first_ref, last_ref):
+    rows = mask_ref.shape[0]
+    layers = u_ref.shape[0] // rows
+    for k in range(layers):
+        for ref, at in ((first_ref, 0), (last_ref, rows - DEEP)):
+            source = slice(k * rows + at, k * rows + at + DEEP)
+            ref[k * DEEP : (k + 1) * DEEP, :] = u_ref[source, :]
+            to = (layers + k) * DEEP
+            ref[to : to + DEEP, :] = mat_ref[source, :].astype(jnp.float32)
     surface = mask_ref[...].astype(jnp.float32) * height_ref[...]
-    blocks = [
-        *pack(lambda k: tall(u_ref[k], k), layers),
-        *pack(lambda k: tall(mat_ref[k].astype(jnp.float32), layers + k), layers),
-        *pack(lambda k: tall(surface, 2 * layers), 1),
-    ]
-    for i, (first, last) in enumerate(blocks):
-        first_ref[i] = first
-        last_ref[i] = last
+    first_ref[2 * layers * DEEP :, :] = surface[:DEEP]
+    last_ref[2 * layers * DEEP :, :] = surface[rows - DEEP :]
+
+
+SUB = 8
 
 
 def roll(x, shift, axis):
@@ -369,33 +384,126 @@
     return value
 
 
-def run_sweeps(a_ref, f_ref, now, other):
-    layers, rows, width = a_ref.shape
+def tile(row):
+    return pl.ds(pl.multiple_of(row * SUB, SUB), SUB)
+
+
+def by_layer(ref, rows, first, t, steps, row):
+    return ref[pl.ds((first + t) * rows + row, SUB, stride=steps * rows), :].astype(jnp.float32)
+
+
+def for_rows(rows, own, above, below, body):
+    u_ref, mat_ref, mask_ref, height_ref = own
+    steps = u_ref.shape[0] // rows // SUB
+    layers = SUB * steps
+
+    def margin(ref, offset):
+        def one(i, carry):
+            body(
+                i + offset,
+                lambda t: by_layer(ref, DEEP, 0, t, steps, i),
+                lambda t: by_layer(ref, DEEP, layers, t, steps, i),
+                ref[pl.ds(2 * layers * DEEP + i, 1), :],
+            )
+            return carry
+
+        lax.fori_loop(0, DEEP, one, 0, unroll=8)
+
+    def inner(i, carry):
+        at = pl.ds(i, 1)
+        body(
+            i + DEEP,
+            lambda t: by_layer(u_ref, rows, 0, t, steps, i),
+            lambda t: by_layer(mat_ref, rows, 0, t, steps, i),
+            mask_ref[at, :].astype(jnp.float32) * height_ref[at, :],
+        )
+        return carry
+
+    margin(above, 0)
+    lax.fori_loop(0, rows, inner, 0, unroll=8)
+    margin(below, rows + DEEP)
+
+
+def pack_kernel(
+    u_ref, mat_ref, mask_ref, height_ref, above_ref, below_ref, first_ref, last_ref
+):
+    rows = mask_ref.shape[0]
+    steps = u_ref.shape[0] // rows // SUB
+    slot = iota((SUB, LANES), 1) // DEEP
+
+    def body(row, u, mat, load):
+        first = jnp.zeros((SUB, LANES), jnp.float32)
+        last = first
+        fields = [u(t) for t in range(steps)] + [mat(t) for t in range(steps)]
+        fields.append(jnp.broadcast_to(load, (SUB, LANES)))
+        for i, x in enumerate(fields):
+            first = jnp.where(slot == i, roll(x, i * DEEP, 1), first)
+            last = jnp.where(slot == i, roll(x, (i + 1) * DEEP, 1), last)
+        first_ref[tile(row), :] = first
+        last_ref[tile(row), :] = last
+
+    for_rows(rows, (u_ref, mat_ref, mask_ref, height_ref), above_ref, below_ref, body)
+
+
+def run_sweeps(src, offset, a_ref, f_ref, two):
+    steps = a_ref.shape[0]
+    rows = a_ref.shape[2] // SUB - 2 * offset
+    lane = iota((SUB, LANES), 1)
+    sub = iota((SUB, LANES), 0)
+    cells = [(t, c) for t in range(steps) for c in range(2)]
     for sweep in range(SWEEPS):
-        src, dst = (now, other) if sweep % 2 == 0 else (other, now)
-
-        def layer(k, carry, src=src, dst=dst):
-            x = src[k + 1]
-            total = roll(x, 1, 1) + roll(x, width - 1, 1) + roll(x, 1, 0) + roll(x, rows - 1, 0)
-            total = total + src[k] + src[k + 2]
-            dst[k + 1] = a_ref[k] * total + f_ref[k]
-            return carry
-
-        lax.fori_loop(0, layers, layer, 0, unroll=2)
-
-
-def clear_ends(ref):
-    zero = jnp.zeros(ref.shape[1:], jnp.float32)
-    ref[0] = zero
-    ref[ref.shape[0] - 1] = zero
-
-
-def put_density(material, field, contrast, index_ref, lon_count, layers, scratch, pieces):
-    share = layers // lon_count
-    for k in range(layers):
-        scratch[k // share, k % share] = pick(material(k), contrast) * field(k)
+        dst = two[sweep % 2]
+        shift = offset if sweep == 0 else 0
+
+        def load(row, src=src, shift=shift):
+            return {cell: src[cell[0], cell[1], tile(row + shift), :] for cell in cells}
+
+        def one(row, carry, load=load, dst=dst):
+            before, x = ({cell: carry[j][i] for i, cell in enumerate(cells)} for j in range(2))
+            after = load(row + 1)
+            for t in range(steps):
+                to_right = [roll(x[t, c], 1, 1) for c in range(2)]
+                to_left = [roll(x[t, c], LANES - 1, 1) for c in range(2)]
+                for c in range(2):
+                    total = jnp.where(lane == 0, to_right[1 - c], to_right[c])
+                    total = total + jnp.where(lane == LANES - 1, to_left[1 - c], to_left[c])
+                    total = total + (before[t, c] + after[t, c])
+                    if t > 0:
+                        under = x[t - 1, c]
+                    else:
+                        under = jnp.where(sub == 0, 0.0, roll(x[steps - 1, c], 1, 0))
+                    if t < steps - 1:
+                        over = x[t + 1, c]
+                    else:
+                        over = jnp.where(sub == SUB - 1, 0.0, roll(x[0, c], SUB - 1, 0))
+                    total = total + (under + over)
+                    value = a_ref[t, c, tile(row + offset), :] * total
+                    if t < f_ref.shape[0]:
+                        value = value + f_ref[t, c, tile(row), :]
+                    dst[t, c, tile(row), :] = value
+            return (
+                tuple(x[cell] for cell in cells),
+                tuple(after[cell] for cell in cells),
+            )
+
+        start = (tuple(load(sweep).values()), tuple(load(sweep + 1).values()))
+        lax.fori_loop(sweep + 1, rows - 1 - sweep, one, start, unroll=8)
+        src = dst
+
+
+def put_density(mat_ref, contrast, field, index_ref, scratch, pieces):
+    lon_count = len(pieces)
+    share, rows, _ = pieces[0].shape
+    for k in range(lon_count * share):
+        material = mat_ref[k * rows : (k + 1) * rows, :]
+        scratch[k // share, k % share] = pick(material, contrast) * field(k)
     for s in range(lon_count):
         pieces[s][...] = scratch[lax.rem(index_ref[1] + s, lon_count)]
+
+
+def layer_of(ref, k, margin, rows):
+    steps = ref.shape[0]
+    return ref[k % steps, 0, pl.ds(margin * SUB + k // steps, rows, stride=SUB), :]
 
 
 def first_sweeps_kernel(
@@ -403,67 +511,55 @@
     height_ref, above_ref, below_ref, left_ref, right_ref, *rest,
 ):
     pieces, rest = rest[:lon_count], rest[lon_count:]
-    u_out, a_out, b_out, load_out, now, other, a_scr, b_scr, f_scr, d_scr = rest
-    layers, rows, cols = u_ref.shape
-    tall_rows = rows + 2 * DEEP
-    group = LANES // DEEP
-    cell = (8, LANES)
+    u_hbm, a_hbm, b_hbm, load_hbm, first, middle, u_out, a_out, b_out, load_out, f_scr, d_scr, sem = rest
+    rows = mask_ref.shape[0]
+    steps = u_out.shape[0]
     a_of, b_of = [], []
     for i in range(NMAT):
-        stiff = jnp.full(cell, shear_ref[i], jnp.float32)
-        restore = jnp.full(cell, restoring_ref[i], jnp.float32)
+        stiff = jnp.full((SUB, LANES), shear_ref[i], jnp.float32)
+        restore = jnp.full((SUB, LANES), restoring_ref[i], jnp.float32)
         b_of.append(1.0 / (6.0 * stiff + restore))
         a_of.append(stiff * b_of[i])
-    wide_shape = (tall_rows, cols + LANES)
-    spread = lambda x: jnp.concatenate(
-        [jnp.concatenate([x] * (wide_shape[1] // LANES), axis=1)] * (tall_rows // 8), axis=0
+    lane = iota((SUB, LANES), 1)
+    sub = iota((SUB, LANES), 0)
+
+    def body(row, u, mat, load):
+        at = tile(row)
+        left, right = left_ref[at, :], right_ref[at, :]
+        global_row = index_ref[0] * rows - DEEP + row
+        inside = ((global_row >= 0) & (global_row < total_lat)).astype(jnp.float32)
+
+        def side(i):
+            after = roll(right, LANES - i * DEEP, 1)
+            before = roll(left, LANES - (i + 1) * DEEP, 1)
+            return jnp.where(lane < DEEP, after, jnp.where(lane >= LANES - DEEP, before, 0.0))
+
+        loads = (jnp.broadcast_to(load, (SUB, LANES)), side(2 * steps))
+        for t in range(steps):
+            fields = ((u(t), mat(t)), (side(t), side(steps + t)))
+            for c in range(2):
+                value, material = fields[c]
+                first[t, c, at, :] = value
+                a_out[t, c, at, :] = pick(material, a_of) * inside
+                b = pick(material, b_of) * inside
+                b_out[t, c, at, :] = b
+                if t == 0:
+                    surface = jnp.where(sub == 0, loads[c], 0.0)
+                    load_out[0, c, at, :] = surface
+                    f_scr[0, c, at, :] = b * surface
+
+    for_rows(rows, (u_ref, mat_ref, mask_ref, height_ref), above_ref, below_ref, body)
+    kept = ((a_out, a_hbm), (b_out, b_hbm), (load_out, load_hbm), (u_out, u_hbm))
+    copies = [pltpu.make_async_copy(*pair, sem.at[i]) for i, pair in enumerate(kept)]
+    for copy in copies[:-1]:
+        copy.start()
+    run_sweeps(first, 0, a_out, f_scr, (middle, u_out))
+    copies[-1].start()
+    put_density(
+        mat_ref, contrast_ref, lambda k: layer_of(u_out, k, DEEP, rows), index_ref, d_scr, pieces
     )
-    a_of = [spread(x) for x in a_of]
-    b_of = [spread(x) for x in b_of]
-    lane = iota((tall_rows, LANES), 1)
-    global_row = iota(wide_shape, 0) + (index_ref[0] * rows - DEEP)
-    inside = (global_row >= 0) & (global_row < total_lat)
-
-    def widened(own, at, block, t):
-        main = jnp.concatenate([above_ref[at], own, below_ref[at]], axis=0)
-        right = roll(right_ref[block], LANES - t * DEEP, 1)
-        left = roll(left_ref[block], LANES - (t + 1) * DEEP, 1)
-        side = jnp.where(lane < DEEP, right, jnp.where(lane >= LANES - DEEP, left, 0.0))
-        return jnp.concatenate([main, side], axis=1)
-
-    blocks = layers // group
-    clear_ends(now)
-    clear_ends(other)
-    load = widened(
-        mask_ref[...].astype(jnp.float32) * height_ref[...], 2 * layers, 2 * blocks, 0
-    )
-    zero = jnp.zeros(wide_shape, jnp.float32)
-    for k in range(layers):
-        now[k + 1] = widened(u_ref[k], k, k // group, k % group)
-        material = widened(
-            mat_ref[k].astype(jnp.float32), layers + k, blocks + k // group, k % group
-        )
-        a_scr[k] = jnp.where(inside, pick(material, a_of), 0.0)
-        b = jnp.where(inside, pick(material, b_of), 0.0)
-        b_scr[k] = b
-        f_scr[k] = b * load if k == 0 else zero
-    run_sweeps(a_scr, f_scr, now, other)
-    keep = pl.ds(DEEP - SHALLOW, rows + 2 * SHALLOW)
-    for k in range(layers):
-        u_out[k] = now[k + 1, keep, :]
-        a_out[k] = a_scr[k, keep, :]
-        b_out[k] = b_scr[k, keep, :]
-    load_out[...] = load[DEEP - SHALLOW : rows + DEEP + SHALLOW]
-    put_density(
-        lambda k: mat_ref[k],
-        lambda k: now[k + 1, pl.ds(DEEP, rows), pl.ds(0, cols)],
-        contrast_ref,
-        index_ref,
-        lon_count,
-        layers,
-        d_scr,
-        pieces,
-    )
+    for copy in copies:
+        copy.wait()
 
 
 def second_sweeps_kernel(
@@ -471,37 +567,43 @@
 ):
     parts, rest = rest[:lon_count], rest[lon_count:]
     pieces, rest = rest[:lon_count], rest[lon_count:]
-    field_out, now, other, f_scr, d_scr = rest
-    layers, rows, cols = mat_ref.shape
-    tall_rows = rows + 2 * SHALLOW
+    field_out, middle, last, f_scr, pot, edge, d_scr = rest
+    layers, rows, _ = field_out.shape
+    steps = u_ref.shape[0]
+    tall = rows + 2 * SHALLOW
     share = layers // lon_count
+    spread = share // steps
     chunk = LANES // share
-    lane = iota((tall_rows, LANES), 1)
-    clear_ends(now)
-    clear_ends(other)
+    lane = iota((SUB, LANES), 1)
     for s in range(lon_count):
         source = lax.rem(index_ref[1] + (lon_count - s), lon_count)
-        packed = parts[s][share * tall_rows :]
-        for t in range(share):
-            k = source * share + t
-            main = parts[s][t * tall_rows : (t + 1) * tall_rows]
-            right = roll(packed, LANES - t * chunk, 1)
-            left = roll(packed, LANES - (t + 1) * chunk, 1)
-            side = jnp.where(lane < DEEP, right, left)
-            f_scr[k] = b_ref[k] * jnp.concatenate([main, side], axis=1)
-    f_scr[0] = f_scr[0] + b_ref[0] * load_ref[...]
+        for k in range(share):
+            at = pl.ds(source * spread + k // steps, tall, stride=SUB)
+            pot[k % steps, at, :] = parts[s][k * tall : (k + 1) * tall, :]
+        packed = parts[s][share * tall :, :]
+        for e in range(spread):
+            at = pl.ds(source * spread + e, tall, stride=SUB)
+            edge[at, :] = roll(packed, LANES - e * steps * chunk, 1)
+
+    def force(row, carry):
+        at, deep = tile(row), tile(row + DEEP - SHALLOW)
+        ends = edge[at, :]
+        for t in range(steps):
+            after = roll(ends, LANES - t * chunk, 1)
+            before = roll(ends, LANES - (t + 1) * chunk, 1)
+            potential = (pot[t, at, :], jnp.where(lane < DEEP, after, before))
+            for c in range(2):
+                value = potential[c]
+                if t == 0:
+                    value = value + load_ref[0, c, deep, :]
+                f_scr[t, c, at, :] = b_ref[t, c, deep, :] * value
+        return carry
+
+    lax.fori_loop(0, tall, force, 0, unroll=8)
+    run_sweeps(u_ref, DEEP - SHALLOW, a_ref, f_scr, (middle, last))
     for k in range(layers):
-        now[k + 1] = u_ref[k]
-    run_sweeps(a_ref, f_scr, now, other)
-
-    def field(k):
-        return now[k + 1, pl.ds(SHALLOW, rows), pl.ds(0, cols)]
-
-    for k in range(layers):
-        field_out[k] = field(k)
-    put_density(
-        lambda k: mat_ref[k], field, contrast_ref, index_ref, lon_count, layers, d_scr, pieces
-    )
+        field_out[k] = layer_of(last, k, SHALLOW, rows)
+    put_density(mat_ref, contrast_ref, lambda k: field_out[k], index_ref, d_scr, pieces)
 
 
 def swap_chunks(blocks, chunk):
@@ -658,72 +760,98 @@
     index = jnp.stack([lat_index, lax.axis_index("lon")]).astype(jnp.int32)
     owner = (index[0] * lon_count + index[1])[None]
 
-    down = [(i, i + 1) for i in range(lat_count - 1)]
-    up = [(i + 1, i) for i in range(lat_count - 1)]
-
-    def slab(at):
-        return jnp.concatenate(
-            [
-                displacement[:, at],
-                materials[:, at].astype(jnp.float32),
-                (ice_mask[at].astype(jnp.float32) * ice_height[at])[None],
-            ],
-            axis=0,
-        )
-
-    above = lax.ppermute(slab(slice(rows - DEEP, rows)), "lat", down)
-    below = lax.ppermute(slab(slice(0, DEEP)), "lat", up)
-    all_green = lax.all_gather(
-        green.reshape(green.shape[0], layers * layers), "lat", axis=0, tiled=True
+    own = (
+        displacement.reshape(layers * rows, cols),
+        materials.reshape(layers * rows, cols),
+        ice_mask,
+        ice_height,
     )
+    first, last = call(slab_kernel, (f32((2 * layers + 1) * DEEP, cols),) * 2)(*own)
+    above = lax.ppermute(last, "lat", [(i, i + 1) for i in range(lat_count - 1)])
+    below = lax.ppermute(first, "lat", [(i + 1, i) for i in range(lat_count - 1)])
     table = call(
         functools.partial(fourier_kernel, total_lon, orders),
         (jax.ShapeDtypeStruct((total_lon, 2 * LMAX), HALF),) * 2,
-        cost=100_000_000,
     )()
-    blocks = 2 * (layers * DEEP // LANES) + 1
-    first, last = call(
-        pack_kernel, (f32(blocks, rows + 2 * DEEP, cols),) * 2, cost=10_000_000
-    )(displacement, materials, ice_mask, ice_height, above, below)
+    def partner(x, axis, step):
+        return lax.ppermute(x, axis, [(i, i ^ step) for i in range(lax.axis_size(axis))])
+
+    half = layers * layers // 2
+    near = lax.dynamic_slice_in_dim(
+        green.reshape(green.shape[0], layers * layers), index[1] % 2 * half, half, 1
+    )
+    step = lat_count // 2
+    far = partner(near, "lat", step)
+    above, below, far, table = lax.optimization_barrier((above, below, far, table))
+    first, last = call(pack_kernel, (f32((rows + 2 * DEEP) * SUB, cols),) * 2)(
+        *own, above, below
+    )
     left = lax.ppermute(last, "lon", [(i, (i + 1) % lon_count) for i in range(lon_count)])
     right = lax.ppermute(first, "lon", [((i + 1) % lon_count, i) for i in range(lon_count)])
-    legendre_table = call(
-        functools.partial(legendre_kernel, total_lat, orders),
-        (jax.ShapeDtypeStruct((orders, LMAX, width), HALF),) * 2,
-        scratch=[pltpu.VMEM((width // LANES, LMAX * orders, LANES), jnp.float32)],
-        cost=100_000_000,
-        smem=(0,),
-    )(owner)
+    stage = 0
+    while step > 1:
+        step //= 2
+        near = jnp.concatenate([near, far], axis=0)
+        far = partner(near, "lat", step)
+        if stage == 0:
+            left, right, far = lax.optimization_barrier((left, right, far))
+        stage += 1
     theta = ((lat_index * rows + jnp.arange(rows)).astype(jnp.float32) + 0.5) * (
         jnp.pi / total_lat
     )
     weight = jnp.broadcast_to((jnp.sin(theta) / (4.0 * total_lat))[:, None], (rows, LANES))
 
-    deep = pltpu.VMEM((layers + 2, rows + 2 * DEEP, cols + LANES), jnp.float32)
-    deep_in = pltpu.VMEM((layers, rows + 2 * DEEP, cols + LANES), jnp.float32)
+    steps = layers // SUB
+
+    def worked(t, height):
+        return (t, 2, height * SUB, LANES)
+
+    deep = rows + 2 * DEEP
     flat = pltpu.VMEM((lon_count, share, rows, cols), jnp.float32)
-    kept = f32(layers, tall, cols + LANES)
     out = call(
         functools.partial(first_sweeps_kernel, lon_count, total_lat),
-        (f32(share, rows, cols),) * lon_count + (kept,) * 3 + (f32(tall, cols + LANES),),
-        scratch=[deep, deep, deep_in, deep_in, deep_in, flat],
-        cost=100_000_000,
+        (f32(share, rows, cols),) * lon_count
+        + (f32(*worked(steps, deep)),) * 3
+        + (f32(*worked(1, deep)),),
+        scratch=[pltpu.VMEM(worked(steps, deep), jnp.float32)] * 5
+        + [pltpu.VMEM(worked(1, deep), jnp.float32)] * 2
+        + [flat, pltpu.SemaphoreType.DMA((4,))],
         smem=(0, 1, 2, 3),
-    )(
-        index, shear, restoring, contrast, displacement, materials, ice_mask, ice_height, above,
-        below, left, right,
-    )
+        hbm=range(lon_count, lon_count + 4),
+    )(index, shear, restoring, contrast, *own, above, below, left, right)
     pieces, state = out[:lon_count], out[lon_count:]
-    turned_green = call(turn_kernel, f32(layers * layers, LMAX), cost=1_000_000)(all_green)
-
     for iteration in range(ITERS):
         margin = SHALLOW if iteration < ITERS - 1 else 0
+        parts = exchange(pieces)
+        if iteration == 0:
+            parts, near, far = lax.optimization_barrier((parts, near, far))
         spectrum = call(
             functools.partial(forward_kernel, lon_count, 2.0 * math.pi / total_lon),
             f32(owners, rows, LANES),
-            cost=300_000_000,
             smem=(0,),
-        )(index, weight, *table, *exchange(pieces))
+        )(index, weight, *table, *parts)
+        if iteration == 0:
+            owner, spectrum = lax.optimization_barrier((owner, spectrum))
+            half_table = (orders, LMAX, width)
+            legendre_table = call(
+                functools.partial(legendre_kernel, total_lat, orders),
+                (jax.ShapeDtypeStruct(half_table, HALF),) * 2,
+                scratch=[
+                    pltpu.VMEM((width // LANES, LMAX * orders, LANES), jnp.float32),
+                    pltpu.VMEM(half_table, HALF),
+                    pltpu.VMEM(half_table, HALF),
+                    pltpu.SemaphoreType.DMA((2,)),
+                ],
+                smem=(0,),
+                hbm=(0, 1),
+            )(owner)
+            blocks = (near, far, partner(near, "lon", 1), partner(far, "lon", 1))
+            turned_green = call(
+                functools.partial(turn_kernel, green.shape[0]),
+                f32(layers * layers, LMAX),
+                scratch=[pltpu.VMEM((LMAX, half), jnp.float32)],
+                smem=(0,),
+            )(index, *blocks)
         spectrum = lax.all_to_all(spectrum, BOTH, 0, 0, tiled=True)
         square = pltpu.VMEM((width // LANES, lon_count * LANES, LANES), jnp.float32)
         coeff_shape = pltpu.VMEM((LMAX // LANES, lon_count * LANES, LANES), jnp.float32)
@@ -731,7 +859,6 @@
             functools.partial(spectral_kernel, margin),
             f32(lat_count, lon_count, rows + 2 * margin, LANES),
             scratch=[square, coeff_shape, coeff_shape],
-            cost=300_000_000,
         )(
             *legendre_table,
             turned_green,
@@ -746,25 +873,25 @@
             functools.partial(inverse_kernel, lon_count, margin),
             (f32(sent, cols),) * lon_count,
             scratch=[pltpu.VMEM((lon_count, share * high, cols), jnp.float32)],
-            cost=300_000_000,
             smem=(0,),
         )(index, *table, synth)
         parts = exchange(parts)
         if iteration < ITERS - 1:
-            wide = pltpu.VMEM((layers + 2, tall, cols + LANES), jnp.float32)
-            wide_in = pltpu.VMEM((layers, tall, cols + LANES), jnp.float32)
             out = call(
                 functools.partial(second_sweeps_kernel, lon_count),
                 (f32(share, rows, cols),) * lon_count + (f32(layers, rows, cols),),
-                scratch=[wide, wide, wide_in, flat],
-                cost=100_000_000,
+                scratch=[pltpu.VMEM(worked(steps, tall), jnp.float32)] * 3
+                + [
+                    pltpu.VMEM((steps, tall * SUB, LANES), jnp.float32),
+                    pltpu.VMEM((tall * SUB, LANES), jnp.float32),
+                    flat,
+                ],
                 smem=(0, 1),
-            )(index, contrast, materials, *state, *parts)
+            )(index, contrast, own[1], *state, *parts)
             pieces, field = out[:lon_count], out[lon_count]
     potential = call(
         functools.partial(assemble_kernel, lon_count),
         f32(lon_count, share, rows, cols),
-        cost=1_000_000,
         smem=(0,),
     )(index, *parts)
     return (field, potential.reshape(layers, rows, cols))
@@ -779,7 +906,12 @@
         ITERS == 2
         and cols == LANES
         and rows % 8 == 0
-        and layers % (LANES // DEEP) == 0
+        and layers % SUB == 0
+        and (2 * (layers // SUB) + 1) * DEEP <= LANES
+        and (layers // lon_count) % (layers // SUB) == 0
+        and lat_count > 2
+        and lon_count % 2 == 0
+        and lat_count & (lat_count - 1) == 0
         and layers % lon_count == 0
         and LMAX % owners == 0
         and 2 * (LMAX // owners) * (layers // lon_count) == LANES

time: 179 us -> 163 us (0.911)
  between operations: 14.3 us -> 0.94 us
  Pallas kernels: 43.6 us -> 36.2 us
  starting transfers between devices: 24.5 us -> 27.4 us
    pallas_call x13 -> x14, Pallas kernels: 43.6 us -> 36.2 us  [run(): pl.pallas_call(kernel, out_shape=outs, in_specs=[pl.BlockSpec(memory_spac...]
    ppermute x2 -> x7, waiting for transfers between devices: 3.28 us -> 8.78 us  [the longest x5 8.78 us: partner(): lax.ppermute(x, axis, [(i, i ^ step) for i in range(lax.axis_size(axis))])]
    ppermute x2 -> x7, starting transfers between devices: 5.25 us -> 10.2 us  [the longest x5 4.78 us: partner(): lax.ppermute(x, axis, [(i, i ^ step) for i in range(lax.axis_size(axis))])]
    ppermute x1, waiting for transfers between devices: 2.56 us -> 0.53 us  [on_device(): lax.ppermute(first, 'lon', [((i + 1) % lon_count, i) for i in range(lon_c...]
    ppermute x1, waiting for transfers between devices: 1.83 us -> 0.01 us  [on_device(): lax.ppermute(last, 'lon', [(i, (i + 1) % lon_count) for i in range(lon_co...]
    unnamed x40 -> x46, local copies, waits for them, and re-layouts: 8.59 us -> 9.64 us
  transfers between devices with their start and end apart: 18 -> 22, of which waited for: 16 -> 16; matrix products, arithmetic and copies ran while one was open for 0% -> 1% of each run, Pallas kernels for 11% -> 8%
where the time goes in v2:
time: 163 us
  blocking collectives  48.9 us (30%)
  waiting for transfers between devices  37.6 us (23%)
  Pallas kernels  36.2 us (22%)
  starting transfers between devices  27.4 us (17%)
  local copies, waits for them, and re-layouts  11 us (7%)
    pallas_call x14, Pallas kernels, run(): pl.pallas_call(kernel, out_shape=outs, in_specs=[pl.BlockSpec(memory_spac...  36.2 us
    all_to_all x2, blocking collectives, on_device(): lax.all_to_all(synth.reshape(owners, rows + 2 * margin, LANES), BOTH, 0,...  34.1 us
    ppermute x12, waiting for transfers between devices, exchange(): lax.ppermute(pieces[s], 'lon', [(i, (i + s) % count) for i in range(count)])  21.9 us
    all_to_all x1, blocking collectives, on_device(): spectrum = lax.all_to_all(spectrum, BOTH, 0, 0, tiled=True)  14.8 us
    unnamed x46, local copies, waits for them, and re-layouts  9.64 us
    ppermute x5, waiting for transfers between devices, partner(): lax.ppermute(x, axis, [(i, i ^ step) for i in range(lax.axis_size(axis))])  8.78 us
    ppermute x12, starting transfers between devices, exchange(): lax.ppermute(pieces[s], 'lon', [(i, (i + s) % count) for i in range(count)])  8.31 us
    all_to_all x1, waiting for transfers between devices, on_device(): spectrum = lax.all_to_all(spectrum, BOTH, 0, 0, tiled=True)  6.37 us
  transfers between devices with their start and end apart: 22, of which 16 were waited for; matrix products, arithmetic and copies ran while one was open for 1% of the time, Pallas kernels for 8%

profile of v2, /device:TPU:1, one launch (start us, length us, event | category | flops | bytes accessed | tf_op | source)
XLA Modules:
  0.0 162.9 jit_solution(7602551760030577154)
XLA Ops:
  4.1 4.1 %collective-permute-start = (f32[520,128]{1,0:T(8,128)S(1)}, f32[520,128]{1,0:T(8,128)S(1)}, u32[]{:S(2)}, u32[]{:S(2)}) collective-permute-start(f32[520,128]{1,0:T(8,128)S(1)} %get-tuple-element.47), channel_id=1, source_target_pairs={{0,4},{4,8},{8,12},{12,16},{16,20},{20,24},{24,28},{1,5},{5,9},{9,... | collective-permute-start | bytes 798728 | tf_op jit(solution)/shard_map/ppermute | solution.py:770
  8.2 1.3 collective-permute-start.1
  9.5 1.3 reshape.39
  10.9 4.1 %collective-permute-start.2 = (f32[32,512]{1,0:T(8,128)S(1)}, f32[32,512]{1,0:T(8,128)S(1)}, u32[]{:S(2)}, u32[]{:S(2)}) collective-permute-start(f32[32,512]{1,0:T(8,128)S(1)} %constant_dynamic-slice_fusion), channel_id=1, source_target_pairs={{0,16},{4,20},{8,24},{12,28},{16,0},{20,4},{24,8},{28,12},{1,17},{... | collective-permute-start | bytes 196616 | tf_op jit(solution)/shard_map/ppermute | solution.py:777
  16.2 4.4 %collective-permute-done.2 = f32[32,512]{1,0:T(8,128)S(1)} collective-permute-done((f32[32,512]{1,0:T(8,128)S(1)}, f32[32,512]{1,0:T(8,128)S(1)}, u32[]{:S(2)}, u32[]{:S(2)}) %collective-permute-start.2) | collective-permute-done | bytes 65568 | tf_op jit(solution)/shard_map/ppermute | solution.py:777
  21.8 4.3 %collective-permute-start.3 = (f32[320,128]{1,0:T(8,128)S(1)}, f32[320,128]{1,0:T(8,128)S(1)}, u32[]{:S(2)}, u32[]{:S(2)}) collective-permute-start(f32[320,128]{1,0:T(8,128)S(1)} %get-tuple-element.53), channel_id=1, source_target_pairs={{0,1},{1,2},{2,3},{3,0},{4,5},{5,6},{6,7},{7,4},{8,9},{9,10},{10,1... | collective-permute-start | bytes 491528 | tf_op jit(solution)/shard_map/ppermute | solution.py:789
  26.2 4.4 %collective-permute-done.5 = f32[64,512]{1,0:T(8,128)S(1)} collective-permute-done((f32[64,512]{1,0:T(8,128)S(1)}, f32[64,512]{1,0:T(8,128)S(1)}, u32[]{:S(2)}, u32[]{:S(2)}) %collective-permute-start.5) | collective-permute-done | bytes 131104 | tf_op jit(solution)/shard_map/ppermute | solution.py:777
  31.9 6.8 %shard_map.98 = (f32[8,24,128]{2,1,0:T(8,128)S(1)}, f32[8,24,128]{2,1,0:T(8,128)S(1)}, f32[8,24,128]{2,1,0:T(8,128)S(1)}, f32[8,24,128]{2,1,0:T(8,128)S(1)}, f32...) custom-call(s32[2]{0:T(128)S(1)} %pad_add_fusion.index_ref, ...), custom_call_target="tpu_custom_call" | custom-call | flops 1 | bytes 1 | tf_op jit(solution)/shard_map/pallas_call | solution.py:201
  42.6 1.8 %collective-permute-start.6 = (f32[8,24,128]{2,1,0:T(8,128)S(1)}, f32[8,24,128]{2,1,0:T(8,128)S(1)}, u32[]{:S(2)}, u32[]{:S(2)}) collective-permute-start(f32[8,24,128]{2,1,0:T(8,128)S(1)} %get-tuple-element.65), channel_id=1, source_target_pairs={{0,1},{1,2},{2,3},{3,0},{4,5},{5,6},{6,7},{7,4},{8,9},{9,10},{10,1... | collective-permute-start | bytes 294920 | tf_op jit(solution)/shard_map/ppermute | solution.py:746
  45.0 1.5 collective-permute-done.6.rest_1_
  46.5 3.1 %collective-permute-done.7.rest_2_ = f32[8,24,128]{2,1,0:T(8,128)S(1)} collective-permute-done((f32[8,24,128]{2,1,0:T(8,128)S(1)}, f32[8,24,128]{2,1,0:T(8,128)S(1)}, u32[]{:S(2)}, u32[]{:S(2)}) %collective-permute-start.7) | collective-permute-done | bytes 98336 | tf_op jit(solution)/shard_map/ppermute | solution.py:746
  50.2 2.4 %shard_map.99 = f32[32,24,128]{2,1,0:T(8,128)} custom-call(s32[2]{0:T(128)S(1)} %pad_add_fusion.index_ref, f32[24,128]{1,0:T(8,128)S(1)} %broadcast_in_dim.10.weight_ref, bf16[512,512]{1,0:T(8,128)(2,1)S(1)} %get-tuple-element.62.high_ref, bf16[512,512]{1,0:T(8,128)(2,1)S(1)} %get-tuple-element.63.low_ref, f32[8,24,128]{2,1,0:T(8,128)S(1)} %get-tuple-element.69.rest_0_, ...), custom_call_target="tpu_custom_call" | custom-call | flops 1 | bytes 1 | tf_op jit(solution)/shard_map/pallas_call | solution.py:201
  52.6 4.6 %all-to-all-start = ((f32[32,24,128]{2,1,0:T(8,128)}), f32[32,24,128]{2,1,0:T(8,128)}, u32[]{:S(2)}, u32[]{:S(2)}) async-start(f32[32,24,128]{2,1,0:T(8,128)} %shard_map.99), calls=%async_computation | async-start | bytes 786432 | tf_op jit(solution)/shard_map/all_to_all | solution.py:855
  57.7 3.0 %shard_map.100 = (bf16[8,256,256]{2,1,0:T(8,128)(2,1)S(1)}, bf16[8,256,256]{2,1,0:T(8,128)(2,1)S(1)}) custom-call(s32[1]{0:T(128)} %bitcast.4.index_ref), custom_call_target="tpu_custom_call" | custom-call | flops 1 | bytes 1 | tf_op jit(solution)/shard_map/pallas_call | solution.py:201
  61.7 1.4 shard_map.101.green_ref
  63.1 6.4 %all-to-all-done = f32[32,24,128]{2,1,0:T(8,128)} async-done(((f32[32,24,128]{2,1,0:T(8,128)}), f32[32,24,128]{2,1,0:T(8,128)}, u32[]{:S(2)}, u32[]{:S(2)}) %all-to-all-start) | async-done | bytes 393248 | tf_op jit(solution)/shard_map/all_to_all | solution.py:855
  70.8 4.5 %shard_map.102 = f32[8,4,32,128]{3,2,1,0:T(8,128)S(1)} custom-call(bf16[8,256,256]{2,1,0:T(8,128)(2,1)S(1)} %get-tuple-element.74.high_ref, bf16[8,256,256]{2,1,0:T(8,128)(2,1)S(1)} %copy-done.3, f32[1024,256]{1,0:T(8,128)S(1)} %shard_map.101.green_ref, f32[8,4,24,128]{3,2,1,0:T(8,128)} %bitcast.5.x_ref), custom_call_target="tpu_custom_call" | custom-call | flops 1 | bytes 1 | tf_op jit(solution)/shard_map/pallas_call | solution.py:201
  75.3 18.5 %all_to_all.20.x_ref = f32[32,32,128]{2,1,0:T(8,128)S(1)} all-to-all(f32[32,32,128]{2,1,0:T(8,128)S(1)} %bitcast.17), channel_id=1, replica_groups=mesh['lat'=8,'lon'=4] {'lat','lon'}, dimensions={0} | all-to-all | bytes 1048576 | tf_op jit(solution)/shard_map/all_to_all | solution.py:867
  93.8 2.2 %shard_map.103 = (f32[288,128]{1,0:T(8,128)S(1)}, f32[288,128]{1,0:T(8,128)S(1)}, f32[288,128]{1,0:T(8,128)S(1)}, f32[288,128]{1,0:T(8,128)S(1)}) custom-call(s32[2]{0:T(128)S(1)} %pad_add_fusion.index_ref, bf16[512,512]{1,0:T(8,128)(2,1)S(1)} %get-tuple-element.62.high_ref, bf16[512,512]{1,0:T(8,128)(2,1)S(1)} %get-tuple-element.63.low_ref, ...), custom_call_target="tpu_custom_call" | custom-call | flops 1 | bytes 1 | tf_op jit(solution)/shard_map/pallas_call | solution.py:201
  98.0 1.9 %collective-permute-done.12.rest_1_ = f32[288,128]{1,0:T(8,128)S(1)} collective-permute-done((f32[288,128]{1,0:T(8,128)S(1)}, f32[288,128]{1,0:T(8,128)S(1)}, u32[]{:S(2)}, u32[]{:S(2)}) %collective-permute-start.12) | collective-permute-done | bytes 147488 | tf_op jit(solution)/shard_map/ppermute | solution.py:746
  99.9 4.8 %collective-permute-done.13.rest_2_ = f32[288,128]{1,0:T(8,128)S(1)} collective-permute-done((f32[288,128]{1,0:T(8,128)S(1)}, f32[288,128]{1,0:T(8,128)S(1)}, u32[]{:S(2)}, u32[]{:S(2)}) %collective-permute-start.13) | collective-permute-done | bytes 147488 | tf_op jit(solution)/shard_map/ppermute | solution.py:746
  105.3 5.5 %shard_map.104 = (f32[8,24,128]{2,1,0:T(8,128)S(1)}, f32[8,24,128]{2,1,0:T(8,128)S(1)}, f32[8,24,128]{2,1,0:T(8,128)S(1)}, f32[8,24,128]{2,1,0:T(8,128)S(1)}, f32[32,24,128]{2,1,0:T(8,128)}) custom-call(s32[2]{0:T(128)S(1)} %pad_add_fusion.index_ref, f32[4]{0:T(128)S(1)} %copy-done.20, s32[768,128]{1,0:T(8,128)S(1)} %bitcast.13, ...), custom_call_target="tpu_custom_call" | custom-call | flops 1 | bytes 1 | tf_op jit(solution)/shard_map/pallas_call | solution.py:201
  112.5 2.6 %collective-permute-done.16.rest_2_ = f32[8,24,128]{2,1,0:T(8,128)S(1)} collective-permute-done((f32[8,24,128]{2,1,0:T(8,128)S(1)}, f32[8,24,128]{2,1,0:T(8,128)S(1)}, u32[]{:S(2)}, u32[]{:S(2)}) %collective-permute-start.16) | collective-permute-done | bytes 98336 | tf_op jit(solution)/shard_map/ppermute | solution.py:746
  115.1 1.6 collective-permute-done.17.rest_3_
  116.7 1.6 shard_map.105
  118.3 14.8 %all_to_all.21 = f32[32,24,128]{2,1,0:T(8,128)S(1)} all-to-all(f32[32,24,128]{2,1,0:T(8,128)S(1)} %shard_map.105), channel_id=1, replica_groups=mesh['lat'=8,'lon'=4] {'lat','lon'}, dimensions={0} | all-to-all | bytes 786432 | tf_op jit(solution)/shard_map/all_to_all | solution.py:855
  133.2 3.4 %shard_map.106 = f32[8,4,24,128]{3,2,1,0:T(8,128)S(1)} custom-call(bf16[8,256,256]{2,1,0:T(8,128)(2,1)S(1)} %get-tuple-element.74.high_ref, bf16[8,256,256]{2,1,0:T(8,128)(2,1)S(1)} %copy-done.4, f32[1024,256]{1,0:T(8,128)S(1)} %shard_map.101.green_ref, f32[8,4,24,128]{3,2,1,0:T(8,128)S(1)} %bitcast.18), custom_call_target="tpu_custom_call" | custom-call | flops 1 | bytes 1 | tf_op jit(solution)/shard_map/pallas_call | solution.py:201
  136.6 15.6 %all_to_all.22.x_ref = f32[32,24,128]{2,1,0:T(8,128)S(1)} all-to-all(f32[32,24,128]{2,1,0:T(8,128)S(1)} %bitcast.19), channel_id=1, replica_groups=mesh['lat'=8,'lon'=4] {'lat','lon'}, dimensions={0} | all-to-all | bytes 786432 | tf_op jit(solution)/shard_map/all_to_all | solution.py:867
  152.2 1.7 %shard_map.107 = (f32[192,128]{1,0:T(8,128)S(1)}, f32[192,128]{1,0:T(8,128)S(1)}, f32[192,128]{1,0:T(8,128)S(1)}, f32[192,128]{1,0:T(8,128)S(1)}) custom-call(s32[2]{0:T(128)S(1)} %pad_add_fusion.index_ref, bf16[512,512]{1,0:T(8,128)(2,1)S(1)} %get-tuple-element.62.high_ref, bf16[512,512]{1,0:T(8,128)(2,1)S(1)} %get-tuple-element.63.low_ref, ...), custom_call_target="tpu_custom_call" | custom-call | flops 1 | bytes 1 | tf_op jit(solution)/shard_map/pallas_call | solution.py:201
  153.9 1.3 collective-permute-start.18
  156.8 4.2 %collective-permute-done.19.rest_2_ = f32[192,128]{1,0:T(8,128)S(1)} collective-permute-done((f32[192,128]{1,0:T(8,128)S(1)}, f32[192,128]{1,0:T(8,128)S(1)}, u32[]{:S(2)}, u32[]{:S(2)}) %collective-permute-start.19) | collective-permute-done | bytes 98336 | tf_op jit(solution)/shard_map/ppermute | solution.py:746
  161.6 1.3 shard_map.108
  (82 shorter events, 21.8 us)
Async XLA Ops:
  4.0 16.6 %copy-start.16 = (s32[24,128]{1,0:T(8,128)S(1)}, s32[24,128]{1,0:T(8,128)}, u32[]{:S(2)}) copy-start(s32[24,128]{1,0:T(8,128)} %mask_ref.5) | copy-start | bytes 36868
  4.0 16.6 %copy-start.18 = (f32[24,128]{1,0:T(8,128)S(1)}, f32[24,128]{1,0:T(8,128)}, u32[]{:S(2)}) copy-start(f32[24,128]{1,0:T(8,128)} %height_ref.5) | copy-start | bytes 36868
  4.1 16.5 %collective-permute-start = (f32[520,128]{1,0:T(8,128)S(1)}, f32[520,128]{1,0:T(8,128)S(1)}, u32[]{:S(2)}, u32[]{:S(2)}) collective-permute-start(f32[520,128]{1,0:T(8,128)S(1)} %get-tuple-element.47), channel_id=1, source_target_pairs={{0,4},{4,8},{8,12},{12,16},{16,20},{20,24},{24,28},{1,5},{5,9},{9,... | collective-permute-start | bytes 798728 | tf_op jit(solution)/shard_map/ppermute | solution.py:770
  8.2 12.4 %collective-permute-start.1 = (f32[520,128]{1,0:T(8,128)S(1)}, f32[520,128]{1,0:T(8,128)S(1)}, u32[]{:S(2)}, u32[]{:S(2)}) collective-permute-start(f32[520,128]{1,0:T(8,128)S(1)} %get-tuple-element.48), channel_id=1, source_target_pairs={{4,0},{8,4},{12,8},{16,12},{20,16},{24,20},{28,24},{5,1},{9,5},{13... | collective-permute-start | bytes 798728 | tf_op jit(solution)/shard_map/ppermute | solution.py:771
  9.5 22.4 %copy-start.19 = (f32[4]{0:T(128)S(1)}, f32[4]{0:T(128)}, u32[]{:S(2)}) copy-start(f32[4]{0:T(128)} %contrast_ref.3) | copy-start | bytes 52
  9.5 22.4 %copy-start.21 = (f32[4]{0:T(128)S(1)}, f32[4]{0:T(128)}, u32[]{:S(2)}) copy-start(f32[4]{0:T(128)} %shear_ref.1) | copy-start | bytes 52
  9.5 22.4 %copy-start.22 = (f32[4]{0:T(128)S(1)}, f32[4]{0:T(128)}, u32[]{:S(2)}) copy-start(f32[4]{0:T(128)} %restoring_ref.1) | copy-start | bytes 52
  10.9 9.7 %collective-permute-start.2 = (f32[32,512]{1,0:T(8,128)S(1)}, f32[32,512]{1,0:T(8,128)S(1)}, u32[]{:S(2)}, u32[]{:S(2)}) collective-permute-start(f32[32,512]{1,0:T(8,128)S(1)} %constant_dynamic-slice_fusion), channel_id=1, source_target_pairs={{0,16},{4,20},{8,24},{12,28},{16,0},{20,4},{24,8},{28,12},{1,17},{... | collective-permute-start | bytes 196616 | tf_op jit(solution)/shard_map/ppermute | solution.py:777
  21.8 8.8 %collective-permute-start.3 = (f32[320,128]{1,0:T(8,128)S(1)}, f32[320,128]{1,0:T(8,128)S(1)}, u32[]{:S(2)}, u32[]{:S(2)}) collective-permute-start(f32[320,128]{1,0:T(8,128)S(1)} %get-tuple-element.53), channel_id=1, source_target_pairs={{0,1},{1,2},{2,3},{3,0},{4,5},{5,6},{6,7},{7,4},{8,9},{9,10},{10,1... | collective-permute-start | bytes 491528 | tf_op jit(solution)/shard_map/ppermute | solution.py:789
  26.1 5.0 %collective-permute-start.4 = (f32[320,128]{1,0:T(8,128)S(1)}, f32[320,128]{1,0:T(8,128)S(1)}, u32[]{:S(2)}, u32[]{:S(2)}) collective-permute-start(f32[320,128]{1,0:T(8,128)S(1)} %get-tuple-element.54), channel_id=1, source_target_pairs={{1,0},{2,1},{3,2},{0,3},{5,4},{6,5},{7,6},{4,7},{9,8},{10,9},{11,1... | collective-permute-start | bytes 491528 | tf_op jit(solution)/shard_map/ppermute | solution.py:790
  26.1 4.5 %collective-permute-start.5 = (f32[64,512]{1,0:T(8,128)S(1)}, f32[64,512]{1,0:T(8,128)S(1)}, u32[]{:S(2)}, u32[]{:S(2)}) collective-permute-start(f32[64,512]{1,0:T(8,128)S(1)} %pad_maximum_fusion.1), channel_id=1, source_target_pairs={{0,8},{4,12},{8,0},{12,4},{16,24},{20,28},{24,16},{28,20},{1,9},{5... | collective-permute-start | bytes 393224 | tf_op jit(solution)/shard_map/ppermute | solution.py:777
  31.8 18.3 %collective-permute-start.9 = (f32[128,512]{1,0:T(8,128)}, f32[128,512]{1,0:T(8,128)}, u32[]{:S(2)}, u32[]{:S(2)}) collective-permute-start(f32[128,512]{1,0:T(8,128)} %pad_maximum_fusion.rest_0_), channel_id=1, source_target_pairs={{0,4},{4,0},{8,12},{12,8},{16,20},{20,16},{24,28},{28,24},{1,5},{5... | collective-permute-start | bytes 786440 | tf_op jit(solution)/shard_map/ppermute | solution.py:777
  42.6 3.8 %collective-permute-start.6 = (f32[8,24,128]{2,1,0:T(8,128)S(1)}, f32[8,24,128]{2,1,0:T(8,128)S(1)}, u32[]{:S(2)}, u32[]{:S(2)}) collective-permute-start(f32[8,24,128]{2,1,0:T(8,128)S(1)} %get-tuple-element.65), channel_id=1, source_target_pairs={{0,1},{1,2},{2,3},{3,0},{4,5},{5,6},{6,7},{7,4},{8,9},{9,10},{10,1... | collective-permute-start | bytes 294920 | tf_op jit(solution)/shard_map/ppermute | solution.py:746
  44.4 5.2 %collective-permute-start.7 = (f32[8,24,128]{2,1,0:T(8,128)S(1)}, f32[8,24,128]{2,1,0:T(8,128)S(1)}, u32[]{:S(2)}, u32[]{:S(2)}) collective-permute-start(f32[8,24,128]{2,1,0:T(8,128)S(1)} %get-tuple-element.66), channel_id=1, source_target_pairs={{0,2},{1,3},{2,0},{3,1},{4,6},{5,7},{6,4},{7,5},{8,10},{9,11},{10,... | collective-permute-start | bytes 294920 | tf_op jit(solution)/shard_map/ppermute | solution.py:746
  45.0 5.2 %collective-permute-start.8 = (f32[8,24,128]{2,1,0:T(8,128)S(1)}, f32[8,24,128]{2,1,0:T(8,128)S(1)}, u32[]{:S(2)}, u32[]{:S(2)}) collective-permute-start(f32[8,24,128]{2,1,0:T(8,128)S(1)} %get-tuple-element.67), channel_id=1, source_target_pairs={{0,3},{1,0},{2,1},{3,2},{4,7},{5,4},{6,5},{7,6},{8,11},{9,8},{10,9... | collective-permute-start | bytes 294920 | tf_op jit(solution)/shard_map/ppermute | solution.py:746
  52.6 17.0 %all-to-all-start = ((f32[32,24,128]{2,1,0:T(8,128)}), f32[32,24,128]{2,1,0:T(8,128)}, u32[]{:S(2)}, u32[]{:S(2)}) async-start(f32[32,24,128]{2,1,0:T(8,128)} %shard_map.99), calls=%async_computation | async-start | bytes 786432 | tf_op jit(solution)/shard_map/all_to_all | solution.py:855
  57.1 4.6 %collective-permute-start.10 = (f32[128,512]{1,0:T(8,128)}, f32[128,512]{1,0:T(8,128)S(1)}, u32[]{:S(2)}, u32[]{:S(2)}) collective-permute-start(f32[128,512]{1,0:T(8,128)} %pad_maximum_fusion.rest_0_), channel_id=1, source_target_pairs={{0,1},{1,0},{2,3},{3,2},{4,5},{5,4},{6,7},{7,6},{8,9},{9,8},{10,11... | collective-permute-start | bytes 786440 | tf_op jit(solution)/shard_map/ppermute | solution.py:777
  57.5 4.2 %collective-permute-start.11 = (f32[128,512]{1,0:T(8,128)}, f32[128,512]{1,0:T(8,128)S(1)}, u32[]{:S(2)}, u32[]{:S(2)}) collective-permute-start(f32[128,512]{1,0:T(8,128)} %collective-permute-done.9.rest_1_), channel_id=1, source_target_pairs={{0,1},{1,0},{2,3},{3,2},{4,5},{5,4},{6,7},{7,6},{8,9},{9,8},{10,11... | collective-permute-start | bytes 786440 | tf_op jit(solution)/shard_map/ppermute | solution.py:777
  70.7 34.6 %copy-start.12 = (f32[4,2,320,128]{3,2,1,0:T(8,128)S(1)}, f32[4,2,320,128]{3,2,1,0:T(8,128)}, u32[]{:S(2)}) copy-start(f32[4,2,320,128]{3,2,1,0:T(8,128)} %copy-done.11) | copy-start | bytes 3932164
  70.7 34.6 %copy-start.14 = (f32[1,2,320,128]{3,2,1,0:T(8,128)S(1)}, f32[1,2,320,128]{3,2,1,0:T(8,128)}, u32[]{:S(2)}) copy-start(f32[1,2,320,128]{3,2,1,0:T(8,128)} %copy-done.13) | copy-start | bytes 983044
  75.3 30.0 %copy-start.8 = (f32[4,2,320,128]{3,2,1,0:T(8,128)S(1)}, f32[4,2,320,128]{3,2,1,0:T(8,128)}, u32[]{:S(2)}) copy-start(f32[4,2,320,128]{3,2,1,0:T(8,128)} %copy-done.7) | copy-start | bytes 3932164
  75.3 30.0 %copy-start.10 = (f32[4,2,320,128]{3,2,1,0:T(8,128)S(1)}, f32[4,2,320,128]{3,2,1,0:T(8,128)}, u32[]{:S(2)}) copy-start(f32[4,2,320,128]{3,2,1,0:T(8,128)} %copy-done.9) | copy-start | bytes 3932164
  75.3 30.0 %copy-start.20 = (f32[4]{0:T(128)S(1)}, f32[4]{0:T(128)}, u32[]{:S(2)}) copy-start(f32[4]{0:T(128)} %contrast_ref.3) | copy-start | bytes 52
  96.0 3.9 %collective-permute-start.12 = (f32[288,128]{1,0:T(8,128)S(1)}, f32[288,128]{1,0:T(8,128)S(1)}, u32[]{:S(2)}, u32[]{:S(2)}) collective-permute-start(f32[288,128]{1,0:T(8,128)S(1)} %get-tuple-element.80), channel_id=1, source_target_pairs={{0,1},{1,2},{2,3},{3,0},{4,5},{5,6},{6,7},{7,4},{8,9},{9,10},{10,1... | collective-permute-start | bytes 442376 | tf_op jit(solution)/shard_map/ppermute | solution.py:746
  97.2 7.5 %collective-permute-start.13 = (f32[288,128]{1,0:T(8,128)S(1)}, f32[288,128]{1,0:T(8,128)S(1)}, u32[]{:S(2)}, u32[]{:S(2)}) collective-permute-start(f32[288,128]{1,0:T(8,128)S(1)} %get-tuple-element.81), channel_id=1, source_target_pairs={{0,2},{1,3},{2,0},{3,1},{4,6},{5,7},{6,4},{7,5},{8,10},{9,11},{10,... | collective-permute-start | bytes 442376 | tf_op jit(solution)/shard_map/ppermute | solution.py:746
  98.0 7.3 %collective-permute-start.14 = (f32[288,128]{1,0:T(8,128)S(1)}, f32[288,128]{1,0:T(8,128)S(1)}, u32[]{:S(2)}, u32[]{:S(2)}) collective-permute-start(f32[288,128]{1,0:T(8,128)S(1)} %get-tuple-element.82), channel_id=1, source_target_pairs={{0,3},{1,0},{2,1},{3,2},{4,7},{5,4},{6,5},{7,6},{8,11},{9,8},{10,9... | collective-permute-start | bytes 442376 | tf_op jit(solution)/shard_map/ppermute | solution.py:746
  110.9 1.6 %collective-permute-start.15 = (f32[8,24,128]{2,1,0:T(8,128)S(1)}, f32[8,24,128]{2,1,0:T(8,128)S(1)}, u32[]{:S(2)}, u32[]{:S(2)}) collective-permute-start(f32[8,24,128]{2,1,0:T(8,128)S(1)} %get-tuple-element.85), channel_id=1, source_target_pairs={{0,1},{1,2},{2,3},{3,0},{4,5},{5,6},{6,7},{7,4},{8,9},{9,10},{10,1... | collective-permute-start | bytes 294920 | tf_op jit(solution)/shard_map/ppermute | solution.py:746
  110.9 4.3 %collective-permute-start.16 = (f32[8,24,128]{2,1,0:T(8,128)S(1)}, f32[8,24,128]{2,1,0:T(8,128)S(1)}, u32[]{:S(2)}, u32[]{:S(2)}) collective-permute-start(f32[8,24,128]{2,1,0:T(8,128)S(1)} %get-tuple-element.86), channel_id=1, source_target_pairs={{0,2},{1,3},{2,0},{3,1},{4,6},{5,7},{6,4},{7,5},{8,10},{9,11},{10,... | collective-permute-start | bytes 294920 | tf_op jit(solution)/shard_map/ppermute | solution.py:746
  111.5 5.2 %collective-permute-start.17 = (f32[8,24,128]{2,1,0:T(8,128)S(1)}, f32[8,24,128]{2,1,0:T(8,128)S(1)}, u32[]{:S(2)}, u32[]{:S(2)}) collective-permute-start(f32[8,24,128]{2,1,0:T(8,128)S(1)} %get-tuple-element.87), channel_id=1, source_target_pairs={{0,3},{1,0},{2,1},{3,2},{4,7},{5,4},{6,5},{7,6},{8,11},{9,8},{10,9... | collective-permute-start | bytes 294920 | tf_op jit(solution)/shard_map/ppermute | solution.py:746
  153.9 2.9 %collective-permute-start.18 = (f32[192,128]{1,0:T(8,128)S(1)}, f32[192,128]{1,0:T(8,128)S(1)}, u32[]{:S(2)}, u32[]{:S(2)}) collective-permute-start(f32[192,128]{1,0:T(8,128)S(1)} %get-tuple-element.89), channel_id=1, source_target_pairs={{0,1},{1,2},{2,3},{3,0},{4,5},{5,6},{6,7},{7,4},{8,9},{9,10},{10,1... | collective-permute-start | bytes 294920 | tf_op jit(solution)/shard_map/ppermute | solution.py:746
  155.1 5.8 %collective-permute-start.19 = (f32[192,128]{1,0:T(8,128)S(1)}, f32[192,128]{1,0:T(8,128)S(1)}, u32[]{:S(2)}, u32[]{:S(2)}) collective-permute-start(f32[192,128]{1,0:T(8,128)S(1)} %get-tuple-element.90), channel_id=1, source_target_pairs={{0,2},{1,3},{2,0},{3,1},{4,6},{5,7},{6,4},{7,5},{8,10},{9,11},{10,... | collective-permute-start | bytes 294920 | tf_op jit(solution)/shard_map/ppermute | solution.py:746
  156.4 5.2 %collective-permute-start.20 = (f32[192,128]{1,0:T(8,128)S(1)}, f32[192,128]{1,0:T(8,128)S(1)}, u32[]{:S(2)}, u32[]{:S(2)}) collective-permute-start(f32[192,128]{1,0:T(8,128)S(1)} %get-tuple-element.91), channel_id=1, source_target_pairs={{0,3},{1,0},{2,1},{3,2},{4,7},{5,4},{6,5},{7,6},{8,11},{9,8},{10,9... | collective-permute-start | bytes 294920 | tf_op jit(solution)/shard_map/ppermute | solution.py:746
  (13 other events, 59.2 us)

commit v3 on v2

--- a/solution.py
+++ b/solution.py
@@ -193,25 +193,35 @@
     return (field, potential)
 
 
-def call(kernel, outs, scratch=(), smem=(), hbm=()):
-    def space(i):
-        return pl.BlockSpec(memory_space=pl.ANY if i in hbm else pltpu.VMEM)
+def call(kernel, outs, micros, scratch=(), smem=(), far=(), hbm=()):
+    def place(i, scalars, away):
+        space = pltpu.SMEM if i in scalars else pltpu.HBM if i in away else pltpu.VMEM
+        return pl.BlockSpec(memory_space=space)
 
     def run(*args):
         return pl.pallas_call(
             kernel,
             out_shape=outs,
-            in_specs=[
-                pl.BlockSpec(memory_space=pltpu.SMEM if i in smem else pltpu.VMEM)
-                for i in range(len(args))
-            ],
-            out_specs=tuple(space(i) for i in range(len(outs))) if type(outs) is tuple else space(0),
+            in_specs=[place(i, smem, far) for i in range(len(args))],
+            out_specs=tuple(place(i, (), hbm) for i in range(len(outs)))
+            if type(outs) is tuple
+            else place(0, (), hbm),
             scratch_shapes=list(scratch),
             compiler_params=pltpu.CompilerParams(vmem_limit_bytes=VMEM_LIMIT),
-            cost_estimate=pl.CostEstimate(flops=1, bytes_accessed=1, transcendentals=0),
+            cost_estimate=pl.CostEstimate(
+                flops=int(micros * 1e9), bytes_accessed=1, transcendentals=0
+            ),
         )(*args)
 
     return run
+
+
+def copy_all(sem, *pairs):
+    copies = [pltpu.make_async_copy(*pair, sem.at[i]) for i, pair in enumerate(pairs)]
+    for copy in copies:
+        copy.start()
+    for copy in copies:
+        copy.wait()
 
 
 def f32(*shape):
@@ -329,44 +339,27 @@
         high, low = halves(every(table, m, share, LMAX))
         high_ref[m] = high
         low_ref[m] = low
-    copies = [
-        pltpu.make_async_copy(high_ref, high_out, sem.at[0]),
-        pltpu.make_async_copy(low_ref, low_out, sem.at[1]),
-    ]
-    for copy in copies:
-        copy.start()
-    for copy in copies:
-        copy.wait()
-
-
-def turn_kernel(size, index_ref, *rest):
-    blocks, (o_ref, ordered) = rest[:-2], rest[-2:]
-    near = blocks[0].shape[0] // size
-    width = blocks[0].shape[1]
-    order, step = [0], near
-    while step > 0:
-        order, step = order + [i ^ step for i in order], step // 2
-    for half in range(2):
-        for i in range(2 * near):
-            at = pl.ds(pl.multiple_of((index_ref[0] ^ order[i]) * size, size), size)
-            block = blocks[2 * half + i // near]
-            ordered[at, :] = block[(i % near) * size : (i % near + 1) * size, :]
-        first = (index_ref[1] ^ half) % 2 * width
-        o_ref[pl.ds(pl.multiple_of(first, width), width), :] = ordered[...].T
-
-
-def slab_kernel(u_ref, mat_ref, mask_ref, height_ref, first_ref, last_ref):
-    rows = mask_ref.shape[0]
-    layers = u_ref.shape[0] // rows
-    for k in range(layers):
-        for ref, at in ((first_ref, 0), (last_ref, rows - DEEP)):
-            source = slice(k * rows + at, k * rows + at + DEEP)
-            ref[k * DEEP : (k + 1) * DEEP, :] = u_ref[source, :]
-            to = (layers + k) * DEEP
-            ref[to : to + DEEP, :] = mat_ref[source, :].astype(jnp.float32)
-    surface = mask_ref[...].astype(jnp.float32) * height_ref[...]
-    first_ref[2 * layers * DEEP :, :] = surface[:DEEP]
-    last_ref[2 * layers * DEEP :, :] = surface[rows - DEEP :]
+    copy_all(sem, (high_ref, high_out), (low_ref, low_out))
+
+
+def turn_kernel(size, index_ref, near_ref, far_ref, o_ref, ordered):
+    count = 2 * near_ref.shape[0] // size
+    for i in range(count):
+        partner = 2 * i if 2 * i < count else 2 * i - count + 1
+        block = near_ref if 2 * i < count else far_ref
+        first = i % (count // 2) * size
+        at = pl.ds(pl.multiple_of((index_ref[0] ^ partner) * size, size), size)
+        ordered[at, :] = block[first : first + size, :]
+    o_ref[...] = ordered[...].T
+
+
+def slab_kernel(u_ref, mat_ref, surface_ref, first_ref, last_ref):
+    layers, rows, _ = u_ref.shape
+    for ref, at in ((first_ref, pl.ds(0, DEEP)), (last_ref, pl.ds(rows - DEEP, DEEP))):
+        for k in range(layers):
+            ref[k] = u_ref[k, at, :]
+            ref[layers + k] = mat_ref[k, at, :].astype(jnp.float32)
+        ref[2 * layers] = surface_ref[at, :]
 
 
 SUB = 8
@@ -393,7 +386,7 @@
 
 
 def for_rows(rows, own, above, below, body):
-    u_ref, mat_ref, mask_ref, height_ref = own
+    u_ref, mat_ref, surface_ref = own
     steps = u_ref.shape[0] // rows // SUB
     layers = SUB * steps
 
@@ -410,12 +403,11 @@
         lax.fori_loop(0, DEEP, one, 0, unroll=8)
 
     def inner(i, carry):
-        at = pl.ds(i, 1)
         body(
             i + DEEP,
             lambda t: by_layer(u_ref, rows, 0, t, steps, i),
             lambda t: by_layer(mat_ref, rows, 0, t, steps, i),
-            mask_ref[at, :].astype(jnp.float32) * height_ref[at, :],
+            surface_ref[pl.ds(i, 1), :],
         )
         return carry
 
@@ -425,9 +417,9 @@
 
 
 def pack_kernel(
-    u_ref, mat_ref, mask_ref, height_ref, above_ref, below_ref, first_ref, last_ref
+    u_ref, mat_ref, surface_ref, above_ref, below_ref, first_ref, last_ref
 ):
-    rows = mask_ref.shape[0]
+    rows = surface_ref.shape[0]
     steps = u_ref.shape[0] // rows // SUB
     slot = iota((SUB, LANES), 1) // DEEP
 
@@ -442,7 +434,7 @@
         first_ref[tile(row), :] = first
         last_ref[tile(row), :] = last
 
-    for_rows(rows, (u_ref, mat_ref, mask_ref, height_ref), above_ref, below_ref, body)
+    for_rows(rows, (u_ref, mat_ref, surface_ref), above_ref, below_ref, body)
 
 
 def run_sweeps(src, offset, a_ref, f_ref, two):
@@ -507,12 +499,12 @@
 
 
 def first_sweeps_kernel(
-    lon_count, total_lat, index_ref, shear_ref, restoring_ref, contrast_ref, u_ref, mat_ref, mask_ref,
-    height_ref, above_ref, below_ref, left_ref, right_ref, *rest,
+    lon_count, total_lat, index_ref, shear_ref, restoring_ref, contrast_ref, u_ref, mat_ref,
+    surface_ref, above_ref, below_ref, left_ref, right_ref, *rest,
 ):
     pieces, rest = rest[:lon_count], rest[lon_count:]
     u_hbm, a_hbm, b_hbm, load_hbm, first, middle, u_out, a_out, b_out, load_out, f_scr, d_scr, sem = rest
-    rows = mask_ref.shape[0]
+    rows = surface_ref.shape[0]
     steps = u_out.shape[0]
     a_of, b_of = [], []
     for i in range(NMAT):
@@ -548,7 +540,7 @@
                     load_out[0, c, at, :] = surface
                     f_scr[0, c, at, :] = b * surface
 
-    for_rows(rows, (u_ref, mat_ref, mask_ref, height_ref), above_ref, below_ref, body)
+    for_rows(rows, (u_ref, mat_ref, surface_ref), above_ref, below_ref, body)
     kept = ((a_out, a_hbm), (b_out, b_hbm), (load_out, load_hbm), (u_out, u_hbm))
     copies = [pltpu.make_async_copy(*pair, sem.at[i]) for i, pair in enumerate(kept)]
     for copy in copies[:-1]:
@@ -733,11 +725,9 @@
 
 
 def assemble_kernel(lon_count, index_ref, *rest):
-    parts, (o_ref,) = rest[:lon_count], rest[lon_count:]
-    share = o_ref.shape[1]
-    for s in range(lon_count):
-        source = lax.rem(index_ref[1] + (lon_count - s), lon_count)
-        o_ref[source] = parts[s][...].reshape(o_ref.shape[1:])
+    parts, o_hbm, sem = rest[:lon_count], rest[lon_count], rest[lon_count + 1]
+    sources = [lax.rem(index_ref[1] + (lon_count - s), lon_count) for s in range(lon_count)]
+    copy_all(sem, *((part, o_hbm.at[source]) for part, source in zip(parts, sources)))
 
 
 def exchange(pieces):
@@ -760,42 +750,56 @@
     index = jnp.stack([lat_index, lax.axis_index("lon")]).astype(jnp.int32)
     owner = (index[0] * lon_count + index[1])[None]
 
+    surface = ice_mask.astype(jnp.float32) * ice_height
     own = (
         displacement.reshape(layers * rows, cols),
         materials.reshape(layers * rows, cols),
-        ice_mask,
-        ice_height,
+        surface,
     )
-    first, last = call(slab_kernel, (f32((2 * layers + 1) * DEEP, cols),) * 2)(*own)
+    first, last = call(
+        slab_kernel,
+        (f32(2 * layers + 1, DEEP, cols),) * 2,
+        1.0,
+    )(displacement, materials, surface)
+    green, first, last = lax.optimization_barrier((green, first, last))
+    first, last = (x.reshape(-1, cols) for x in (first, last))
     above = lax.ppermute(last, "lat", [(i, i + 1) for i in range(lat_count - 1)])
     below = lax.ppermute(first, "lat", [(i + 1, i) for i in range(lat_count - 1)])
     table = call(
         functools.partial(fourier_kernel, total_lon, orders),
         (jax.ShapeDtypeStruct((total_lon, 2 * LMAX), HALF),) * 2,
+        1.2,
     )()
-    def partner(x, axis, step):
-        return lax.ppermute(x, axis, [(i, i ^ step) for i in range(lax.axis_size(axis))])
-
-    half = layers * layers // 2
-    near = lax.dynamic_slice_in_dim(
-        green.reshape(green.shape[0], layers * layers), index[1] % 2 * half, half, 1
+    def partner(x, step):
+        return lax.ppermute(x, "lat", [(i, i ^ step) for i in range(lat_count)])
+
+    near = green.reshape(green.shape[0], layers * layers)
+    near, table = lax.optimization_barrier((near, table))
+    others = [partner(near, i) for i in range(2, lat_count, 2)]
+    half_table = (orders, LMAX, width)
+    legendre_table = call(
+        functools.partial(legendre_kernel, total_lat, orders),
+        (jax.ShapeDtypeStruct(half_table, HALF),) * 2,
+        2.9,
+        scratch=[
+            pltpu.VMEM((width // LANES, LMAX * orders, LANES), jnp.float32),
+            pltpu.VMEM(half_table, HALF),
+            pltpu.VMEM(half_table, HALF),
+            pltpu.SemaphoreType.DMA((2,)),
+        ],
+        smem=(0,),
+        hbm=(0, 1),
+    )(owner)
+    above, below, others, table, legendre_table = lax.optimization_barrier(
+        (above, below, others, table, legendre_table)
     )
-    step = lat_count // 2
-    far = partner(near, "lat", step)
-    above, below, far, table = lax.optimization_barrier((above, below, far, table))
-    first, last = call(pack_kernel, (f32((rows + 2 * DEEP) * SUB, cols),) * 2)(
+    near = jnp.concatenate([near, *others], axis=0)
+    far = partner(near, 1)
+    first, last = call(pack_kernel, (f32((rows + 2 * DEEP) * SUB, cols),) * 2, 1.5)(
         *own, above, below
     )
     left = lax.ppermute(last, "lon", [(i, (i + 1) % lon_count) for i in range(lon_count)])
     right = lax.ppermute(first, "lon", [((i + 1) % lon_count, i) for i in range(lon_count)])
-    stage = 0
-    while step > 1:
-        step //= 2
-        near = jnp.concatenate([near, far], axis=0)
-        far = partner(near, "lat", step)
-        if stage == 0:
-            left, right, far = lax.optimization_barrier((left, right, far))
-        stage += 1
     theta = ((lat_index * rows + jnp.arange(rows)).astype(jnp.float32) + 0.5) * (
         jnp.pi / total_lat
     )
@@ -813,6 +817,7 @@
         (f32(share, rows, cols),) * lon_count
         + (f32(*worked(steps, deep)),) * 3
         + (f32(*worked(1, deep)),),
+        6.6,
         scratch=[pltpu.VMEM(worked(steps, deep), jnp.float32)] * 5
         + [pltpu.VMEM(worked(1, deep), jnp.float32)] * 2
         + [flat, pltpu.SemaphoreType.DMA((4,))],
@@ -824,40 +829,27 @@
         margin = SHALLOW if iteration < ITERS - 1 else 0
         parts = exchange(pieces)
         if iteration == 0:
-            parts, near, far = lax.optimization_barrier((parts, near, far))
+            turned_green = call(
+                functools.partial(turn_kernel, green.shape[0]),
+                f32(layers * layers, LMAX),
+                1.4,
+                scratch=[pltpu.VMEM((LMAX, layers * layers), jnp.float32)],
+                smem=(0,),
+            )(index, near, far)
+            parts, turned_green = lax.optimization_barrier((parts, turned_green))
         spectrum = call(
             functools.partial(forward_kernel, lon_count, 2.0 * math.pi / total_lon),
             f32(owners, rows, LANES),
+            2.0,
             smem=(0,),
         )(index, weight, *table, *parts)
-        if iteration == 0:
-            owner, spectrum = lax.optimization_barrier((owner, spectrum))
-            half_table = (orders, LMAX, width)
-            legendre_table = call(
-                functools.partial(legendre_kernel, total_lat, orders),
-                (jax.ShapeDtypeStruct(half_table, HALF),) * 2,
-                scratch=[
-                    pltpu.VMEM((width // LANES, LMAX * orders, LANES), jnp.float32),
-                    pltpu.VMEM(half_table, HALF),
-                    pltpu.VMEM(half_table, HALF),
-                    pltpu.SemaphoreType.DMA((2,)),
-                ],
-                smem=(0,),
-                hbm=(0, 1),
-            )(owner)
-            blocks = (near, far, partner(near, "lon", 1), partner(far, "lon", 1))
-            turned_green = call(
-                functools.partial(turn_kernel, green.shape[0]),
-                f32(layers * layers, LMAX),
-                scratch=[pltpu.VMEM((LMAX, half), jnp.float32)],
-                smem=(0,),
-            )(index, *blocks)
         spectrum = lax.all_to_all(spectrum, BOTH, 0, 0, tiled=True)
         square = pltpu.VMEM((width // LANES, lon_count * LANES, LANES), jnp.float32)
         coeff_shape = pltpu.VMEM((LMAX // LANES, lon_count * LANES, LANES), jnp.float32)
         synth = call(
             functools.partial(spectral_kernel, margin),
             f32(lat_count, lon_count, rows + 2 * margin, LANES),
+            4.0,
             scratch=[square, coeff_shape, coeff_shape],
         )(
             *legendre_table,
@@ -872,6 +864,7 @@
         parts = call(
             functools.partial(inverse_kernel, lon_count, margin),
             (f32(sent, cols),) * lon_count,
+            2.0,
             scratch=[pltpu.VMEM((lon_count, share * high, cols), jnp.float32)],
             smem=(0,),
         )(index, *table, synth)
@@ -880,6 +873,7 @@
             out = call(
                 functools.partial(second_sweeps_kernel, lon_count),
                 (f32(share, rows, cols),) * lon_count + (f32(layers, rows, cols),),
+                5.4,
                 scratch=[pltpu.VMEM(worked(steps, tall), jnp.float32)] * 3
                 + [
                     pltpu.VMEM((steps, tall * SUB, LANES), jnp.float32),
@@ -891,8 +885,11 @@
             pieces, field = out[:lon_count], out[lon_count]
     potential = call(
         functools.partial(assemble_kernel, lon_count),
-        f32(lon_count, share, rows, cols),
+        f32(lon_count, share * rows, cols),
+        1.0,
+        scratch=[pltpu.SemaphoreType.DMA((lon_count,))],
         smem=(0,),
+        hbm=(0,),
     )(index, *parts)
     return (field, potential.reshape(layers, rows, cols))
 
@@ -910,7 +907,6 @@
         and (2 * (layers // SUB) + 1) * DEEP <= LANES
         and (layers // lon_count) % (layers // SUB) == 0
         and lat_count > 2
-        and lon_count % 2 == 0
         and lat_count & (lat_count - 1) == 0
         and layers % lon_count == 0
         and LMAX % owners == 0

time: 163 us -> 156 us (0.957)
  blocking collectives: 48.9 us -> 66.4 us
  local copies, waits for them, and re-layouts: 11 us -> 1.37 us
  waiting for transfers between devices: 37.6 us -> 30.5 us
  starting transfers between devices: 27.4 us -> 22.5 us
  Pallas kernels: 36.2 us -> 34.3 us
    all_to_all x1 -> x2, blocking collectives: 14.8 us -> 32.3 us  [on_device(): spectrum = lax.all_to_all(spectrum, BOTH, 0, 0, tiled=True)]
    unnamed x46 -> x19, local copies, waits for them, and re-layouts: 9.64 us -> 1.05 us
    ppermute x5 -> x4, waiting for transfers between devices: 8.78 us -> 2.01 us  [partner(): return lax.ppermute(x, 'lat', [(i, i ^ step) for i in range(lat_count)])]
    all_to_all x1 -> x0, waiting for transfers between devices: 6.37 us -> none  [on_device(): spectrum = lax.all_to_all(spectrum, BOTH, 0, 0, tiled=True)]
    ppermute x1, waiting for transfers between devices: 0.01 us -> 5.72 us  [on_device(): lax.ppermute(last, 'lat', [(i, i + 1) for i in range(lat_count - 1)])]
    all_to_all x1 -> x0, starting transfers between devices: 4.57 us -> none  [on_device(): spectrum = lax.all_to_all(spectrum, BOTH, 0, 0, tiled=True)]
    ppermute x5 -> x4, starting transfers between devices: 4.78 us -> 6.85 us  [partner(): return lax.ppermute(x, 'lat', [(i, i ^ step) for i in range(lat_count)])]
    ppermute x1, starting transfers between devices: 4.31 us -> 2.35 us  [on_device(): lax.ppermute(last, 'lon', [(i, (i + 1) % lon_count) for i in range(lon_co...]
  transfers between devices with their start and end apart: 22 -> 20, of which waited for: 16 -> 16; matrix products, arithmetic and copies ran while one was open for 1% -> 0% of each run, Pallas kernels for 8% -> 7%
where the time goes in v3:
time: 156 us
  blocking collectives  66.4 us (43%)
  Pallas kernels  34.3 us (22%)
  waiting for transfers between devices  30.5 us (20%)
  starting transfers between devices  22.5 us (14%)
    pallas_call x14, Pallas kernels, run(): pl.pallas_call(kernel, out_shape=outs, in_specs=[place(i, smem, far) for...  34.3 us
    all_to_all x2, blocking collectives, on_device(): lax.all_to_all(synth.reshape(owners, rows + 2 * margin, LANES), BOTH, 0,...  34.1 us
    all_to_all x2, blocking collectives, on_device(): spectrum = lax.all_to_all(spectrum, BOTH, 0, 0, tiled=True)  32.3 us
    ppermute x12, waiting for transfers between devices, exchange(): lax.ppermute(pieces[s], 'lon', [(i, (i + s) % count) for i in range(count)])  20.1 us
    ppermute x12, starting transfers between devices, exchange(): lax.ppermute(pieces[s], 'lon', [(i, (i + s) % count) for i in range(count)])  8.01 us
    ppermute x4, starting transfers between devices, partner(): return lax.ppermute(x, 'lat', [(i, i ^ step) for i in range(lat_count)])  6.85 us
    ppermute x1, waiting for transfers between devices, on_device(): lax.ppermute(last, 'lat', [(i, i + 1) for i in range(lat_count - 1)])  5.72 us
    ppermute x1, starting transfers between devices, on_device(): lax.ppermute(last, 'lat', [(i, i + 1) for i in range(lat_count - 1)])  4 us
  transfers between devices with their start and end apart: 20, of which 16 were waited for; matrix products, arithmetic and copies ran while one was open for 0% of the time, Pallas kernels for 7%

profile of v3, /device:TPU:1, one launch (start us, length us, event | category | flops | bytes accessed | tf_op | source)
XLA Modules:
  0.0 156.2 jit_solution(500550201027484492)
XLA Ops:
  0.7 1.2 shard_map.96
  3.3 4.2 %collective-permute-start.4 = (f32[32,1024]{1,0:T(8,128)S(1)}, f32[32,1024]{1,0:T(8,128)S(1)}, u32[]{:S(2)}, u32[]{:S(2)}) collective-permute-start(f32[32,1024]{1,0:T(8,128)S(1)} %reshape.47), channel_id=1, source_target_pairs={{0,24},{4,28},{8,16},{12,20},{16,8},{20,12},{24,0},{28,4},{1,25},{... | collective-permute-start | bytes 393224 | tf_op jit(solution)/shard_map/ppermute | solution.py:774
  7.8 1.3 collective-permute-start.1
  9.1 4.0 %collective-permute-start = (f32[520,128]{1,0:T(8,128)S(1)}, f32[520,128]{1,0:T(8,128)S(1)}, u32[]{:S(2)}, u32[]{:S(2)}) collective-permute-start(f32[520,128]{1,0:T(8,128)S(1)} %bitcast.21), channel_id=1, source_target_pairs={{0,4},{4,8},{8,12},{12,16},{16,20},{20,24},{24,28},{1,5},{5,9},{9,... | collective-permute-start | bytes 798728 | tf_op jit(solution)/shard_map/ppermute | solution.py:766
  13.1 3.0 %shard_map.97 = (bf16[8,256,256]{2,1,0:T(8,128)(2,1)S(1)}, bf16[8,256,256]{2,1,0:T(8,128)(2,1)S(1)}) custom-call(s32[1]{0:T(128)} %bitcast.6.index_ref), custom_call_target="tpu_custom_call" | custom-call | flops 2900000000 | bytes 1 | tf_op jit(solution)/shard_map/pallas_call | solution.py:202
  16.3 1.9 %collective-permute-done.3 = f32[32,1024]{1,0:T(8,128)S(1)} collective-permute-done((f32[32,1024]{1,0:T(8,128)S(1)}, f32[32,1024]{1,0:T(8,128)S(1)}, u32[]{:S(2)}, u32[]{:S(2)}) %collective-permute-start.3) | collective-permute-done | bytes 131104 | tf_op jit(solution)/shard_map/ppermute | solution.py:774
  18.1 5.7 %collective-permute-done.above_ref = f32[520,128]{1,0:T(8,128)S(1)} collective-permute-done((f32[520,128]{1,0:T(8,128)S(1)}, f32[520,128]{1,0:T(8,128)S(1)}, u32[]{:S(2)}, u32[]{:S(2)}) %collective-permute-start) | collective-permute-done | bytes 266272 | tf_op jit(solution)/shard_map/ppermute | solution.py:766
  25.0 2.4 %collective-permute-start.5 = (f32[320,128]{1,0:T(8,128)S(1)}, f32[320,128]{1,0:T(8,128)S(1)}, u32[]{:S(2)}, u32[]{:S(2)}) collective-permute-start(f32[320,128]{1,0:T(8,128)S(1)} %get-tuple-element.65), channel_id=1, source_target_pairs={{0,1},{1,2},{2,3},{3,0},{4,5},{5,6},{6,7},{7,4},{8,9},{9,10},{10,1... | collective-permute-start | bytes 491528 | tf_op jit(solution)/shard_map/ppermute | solution.py:801
  27.4 2.3 %collective-permute-start.10 = (f32[128,1024]{1,0:T(8,128)S(1)}, f32[128,1024]{1,0:T(8,128)S(1)}, u32[]{:S(2)}, u32[]{:S(2)}) collective-permute-start(f32[128,1024]{1,0:T(8,128)S(1)} %constant_dynamic-update-slice_fusion.near_ref), channel_id=1, source_target_pairs={{0,4},{4,0},{8,12},{12,8},{16,20},{20,16},{24,28},{28,24},{1,5},{5... | collective-permute-start | bytes 1572872 | tf_op jit(solution)/shard_map/ppermute | solution.py:774
  30.5 1.9 %collective-permute-done.6.right_ref = f32[320,128]{1,0:T(8,128)S(1)} collective-permute-done((f32[320,128]{1,0:T(8,128)S(1)}, f32[320,128]{1,0:T(8,128)S(1)}, u32[]{:S(2)}, u32[]{:S(2)}) %collective-permute-start.6) | collective-permute-done | bytes 163872 | tf_op jit(solution)/shard_map/ppermute | solution.py:802
  32.4 6.8 %shard_map.99 = (f32[8,24,128]{2,1,0:T(8,128)S(1)}, f32[8,24,128]{2,1,0:T(8,128)S(1)}, f32[8,24,128]{2,1,0:T(8,128)S(1)}, f32[8,24,128]{2,1,0:T(8,128)S(1)}, f32...) custom-call(s32[2]{0:T(128)S(1)} %pad_add_fusion.index_ref, ...), custom_call_target="tpu_custom_call" | custom-call | flops 6600000000 | bytes 1 | tf_op jit(solution)/shard_map/pallas_call | solution.py:202
  42.3 2.3 %collective-permute-done.8.rest_2_ = f32[8,24,128]{2,1,0:T(8,128)S(1)} collective-permute-done((f32[8,24,128]{2,1,0:T(8,128)S(1)}, f32[8,24,128]{2,1,0:T(8,128)S(1)}, u32[]{:S(2)}, u32[]{:S(2)}) %collective-permute-start.8) | collective-permute-done | bytes 98336 | tf_op jit(solution)/shard_map/ppermute | solution.py:736
  45.6 1.6 %shard_map.101 = f32[32,24,128]{2,1,0:T(8,128)S(1)} custom-call(s32[2]{0:T(128)S(1)} %pad_add_fusion.index_ref, f32[24,128]{1,0:T(8,128)S(1)} %broadcast_in_dim.10.weight_ref, bf16[512,512]{1,0:T(8,128)(2,1)S(1)} %get-tuple-element.71.high_ref, bf16[512,512]{1,0:T(8,128)(2,1)S(1)} %get-tuple-element.72.low_ref, f32[8,24,128]{2,1,0:T(8,128)S(1)} %get-tuple-element.83.rest_0_, ...), custom_call_target="tpu_custom_call" | custom-call | flops 2000000000 | bytes 1 | tf_op jit(solution)/shard_map/pallas_call | solution.py:202
  47.2 17.4 %all_to_all.20 = f32[32,24,128]{2,1,0:T(8,128)S(1)} all-to-all(f32[32,24,128]{2,1,0:T(8,128)S(1)} %shard_map.101), channel_id=1, replica_groups=mesh['lat'=8,'lon'=4] {'lat','lon'}, dimensions={0} | all-to-all | bytes 786432 | tf_op jit(solution)/shard_map/all_to_all | solution.py:846
  64.7 3.6 %shard_map.102 = f32[8,4,32,128]{3,2,1,0:T(8,128)S(1)} custom-call(bf16[8,256,256]{2,1,0:T(8,128)(2,1)S(1)} %get-tuple-element.73.high_ref, bf16[8,256,256]{2,1,0:T(8,128)(2,1)S(1)} %get-tuple-element.74.low_ref, f32[1024,256]{1,0:T(8,128)S(1)} %shard_map.100.green_ref, f32[8,4,24,128]{3,2,1,0:T(8,128)S(1)} %bitcast.15), custom_call_target="tpu_custom_call" | custom-call | flops 4000000000 | bytes 1 | tf_op jit(solution)/shard_map/pallas_call | solution.py:202
  68.3 18.5 %all_to_all.21.x_ref = f32[32,32,128]{2,1,0:T(8,128)S(1)} all-to-all(f32[32,32,128]{2,1,0:T(8,128)S(1)} %bitcast.12), channel_id=1, replica_groups=mesh['lat'=8,'lon'=4] {'lat','lon'}, dimensions={0} | all-to-all | bytes 1048576 | tf_op jit(solution)/shard_map/all_to_all | solution.py:859
  86.8 2.2 %shard_map.103 = (f32[288,128]{1,0:T(8,128)S(1)}, f32[288,128]{1,0:T(8,128)S(1)}, f32[288,128]{1,0:T(8,128)S(1)}, f32[288,128]{1,0:T(8,128)S(1)}) custom-call(s32[2]{0:T(128)S(1)} %pad_add_fusion.index_ref, bf16[512,512]{1,0:T(8,128)(2,1)S(1)} %get-tuple-element.71.high_ref, bf16[512,512]{1,0:T(8,128)(2,1)S(1)} %get-tuple-element.72.low_ref, ...), custom_call_target="tpu_custom_call" | custom-call | flops 2000000000 | bytes 1 | tf_op jit(solution)/shard_map/pallas_call | solution.py:202
  89.0 1.2 collective-permute-start.11
  91.0 1.9 %collective-permute-done.11.rest_1_ = f32[288,128]{1,0:T(8,128)S(1)} collective-permute-done((f32[288,128]{1,0:T(8,128)S(1)}, f32[288,128]{1,0:T(8,128)S(1)}, u32[]{:S(2)}, u32[]{:S(2)}) %collective-permute-start.11) | collective-permute-done | bytes 147488 | tf_op jit(solution)/shard_map/ppermute | solution.py:736
  92.9 4.8 %collective-permute-done.12.rest_2_ = f32[288,128]{1,0:T(8,128)S(1)} collective-permute-done((f32[288,128]{1,0:T(8,128)S(1)}, f32[288,128]{1,0:T(8,128)S(1)}, u32[]{:S(2)}, u32[]{:S(2)}) %collective-permute-start.12) | collective-permute-done | bytes 147488 | tf_op jit(solution)/shard_map/ppermute | solution.py:736
  98.3 5.6 %shard_map.104 = (f32[8,24,128]{2,1,0:T(8,128)S(1)}, f32[8,24,128]{2,1,0:T(8,128)S(1)}, f32[8,24,128]{2,1,0:T(8,128)S(1)}, f32[8,24,128]{2,1,0:T(8,128)S(1)}, f32[32,24,128]{2,1,0:T(8,128)}) custom-call(s32[2]{0:T(128)S(1)} %pad_add_fusion.index_ref, f32[4]{0:T(128)S(1)} %copy-done.4, s32[768,128]{1,0:T(8,128)S(1)} %bitcast.20, ...), custom_call_target="tpu_custom_call" | custom-call | flops 5400000000 | bytes 1 | tf_op jit(solution)/shard_map/pallas_call | solution.py:202
  105.5 2.6 %collective-permute-done.15.rest_2_ = f32[8,24,128]{2,1,0:T(8,128)S(1)} collective-permute-done((f32[8,24,128]{2,1,0:T(8,128)S(1)}, f32[8,24,128]{2,1,0:T(8,128)S(1)}, u32[]{:S(2)}, u32[]{:S(2)}) %collective-permute-start.15) | collective-permute-done | bytes 98336 | tf_op jit(solution)/shard_map/ppermute | solution.py:736
  108.1 1.6 collective-permute-done.16.rest_3_
  109.7 1.6 %shard_map.105 = f32[32,24,128]{2,1,0:T(8,128)S(1)} custom-call(s32[2]{0:T(128)S(1)} %pad_add_fusion.index_ref, f32[24,128]{1,0:T(8,128)S(1)} %broadcast_in_dim.10.weight_ref, bf16[512,512]{1,0:T(8,128)(2,1)S(1)} %get-tuple-element.71.high_ref, bf16[512,512]{1,0:T(8,128)(2,1)S(1)} %get-tuple-element.72.low_ref, f32[8,24,128]{2,1,0:T(8,128)S(1)} %get-tuple-element.92.rest_0_, ...), custom_call_target="tpu_custom_call" | custom-call | flops 2000000000 | bytes 1 | tf_op jit(solution)/shard_map/pallas_call | solution.py:202
  111.3 14.8 %all_to_all.22 = f32[32,24,128]{2,1,0:T(8,128)S(1)} all-to-all(f32[32,24,128]{2,1,0:T(8,128)S(1)} %shard_map.105), channel_id=1, replica_groups=mesh['lat'=8,'lon'=4] {'lat','lon'}, dimensions={0} | all-to-all | bytes 786432 | tf_op jit(solution)/shard_map/all_to_all | solution.py:846
  126.1 3.6 %shard_map.106 = f32[8,4,24,128]{3,2,1,0:T(8,128)S(1)} custom-call(bf16[8,256,256]{2,1,0:T(8,128)(2,1)S(1)} %get-tuple-element.73.high_ref, bf16[8,256,256]{2,1,0:T(8,128)(2,1)S(1)} %get-tuple-element.74.low_ref, f32[1024,256]{1,0:T(8,128)S(1)} %shard_map.100.green_ref, f32[8,4,24,128]{3,2,1,0:T(8,128)S(1)} %bitcast.13), custom_call_target="tpu_custom_call" | custom-call | flops 4000000000 | bytes 1 | tf_op jit(solution)/shard_map/pallas_call | solution.py:202
  129.8 15.6 %all_to_all.23.x_ref = f32[32,24,128]{2,1,0:T(8,128)S(1)} all-to-all(f32[32,24,128]{2,1,0:T(8,128)S(1)} %bitcast.14), channel_id=1, replica_groups=mesh['lat'=8,'lon'=4] {'lat','lon'}, dimensions={0} | all-to-all | bytes 786432 | tf_op jit(solution)/shard_map/all_to_all | solution.py:859
  145.4 1.7 %shard_map.107 = (f32[192,128]{1,0:T(8,128)S(1)}, f32[192,128]{1,0:T(8,128)S(1)}, f32[192,128]{1,0:T(8,128)S(1)}, f32[192,128]{1,0:T(8,128)S(1)}) custom-call(s32[2]{0:T(128)S(1)} %pad_add_fusion.index_ref, bf16[512,512]{1,0:T(8,128)(2,1)S(1)} %get-tuple-element.71.high_ref, bf16[512,512]{1,0:T(8,128)(2,1)S(1)} %get-tuple-element.72.low_ref, ...), custom_call_target="tpu_custom_call" | custom-call | flops 2000000000 | bytes 1 | tf_op jit(solution)/shard_map/pallas_call | solution.py:202
  147.0 1.3 collective-permute-start.17
  148.3 1.3 collective-permute-start.18
  149.9 4.2 %collective-permute-done.18.rest_2_ = f32[192,128]{1,0:T(8,128)S(1)} collective-permute-done((f32[192,128]{1,0:T(8,128)S(1)}, f32[192,128]{1,0:T(8,128)S(1)}, u32[]{:S(2)}, u32[]{:S(2)}) %collective-permute-start.18) | collective-permute-done | bytes 98336 | tf_op jit(solution)/shard_map/ppermute | solution.py:736
  154.7 1.3 shard_map.108
  (51 shorter events, 12.0 us)
Async XLA Ops:
  0.6 1.3 copy-start.6
  0.6 1.3 copy-start.7
  0.7 1.3 copy-start.1
  0.7 1.3 copy-start
  2.0 1.0 copy-start.5
  3.3 13.0 %collective-permute-start.4 = (f32[32,1024]{1,0:T(8,128)S(1)}, f32[32,1024]{1,0:T(8,128)S(1)}, u32[]{:S(2)}, u32[]{:S(2)}) collective-permute-start(f32[32,1024]{1,0:T(8,128)S(1)} %reshape.47), channel_id=1, source_target_pairs={{0,24},{4,28},{8,16},{12,20},{16,8},{20,12},{24,0},{28,4},{1,25},{... | collective-permute-start | bytes 393224 | tf_op jit(solution)/shard_map/ppermute | solution.py:774
  7.5 10.7 %collective-permute-start.3 = (f32[32,1024]{1,0:T(8,128)S(1)}, f32[32,1024]{1,0:T(8,128)S(1)}, u32[]{:S(2)}, u32[]{:S(2)}) collective-permute-start(f32[32,1024]{1,0:T(8,128)S(1)} %reshape.47), channel_id=1, source_target_pairs={{0,16},{4,20},{8,24},{12,28},{16,0},{20,4},{24,8},{28,12},{1,17},{... | collective-permute-start | bytes 393224 | tf_op jit(solution)/shard_map/ppermute | solution.py:774
  7.5 10.7 %collective-permute-start.2 = (f32[32,1024]{1,0:T(8,128)S(1)}, f32[32,1024]{1,0:T(8,128)S(1)}, u32[]{:S(2)}, u32[]{:S(2)}) collective-permute-start(f32[32,1024]{1,0:T(8,128)S(1)} %reshape.47), channel_id=1, source_target_pairs={{0,8},{4,12},{8,0},{12,4},{16,24},{20,28},{24,16},{28,20},{1,9},{5... | collective-permute-start | bytes 393224 | tf_op jit(solution)/shard_map/ppermute | solution.py:774
  7.8 10.3 %collective-permute-start.1 = (f32[520,128]{1,0:T(8,128)S(1)}, f32[520,128]{1,0:T(8,128)S(1)}, u32[]{:S(2)}, u32[]{:S(2)}) collective-permute-start(f32[520,128]{1,0:T(8,128)S(1)} %bitcast.22), channel_id=1, source_target_pairs={{4,0},{8,4},{12,8},{16,12},{20,16},{24,20},{28,24},{5,1},{9,5},{13... | collective-permute-start | bytes 798728 | tf_op jit(solution)/shard_map/ppermute | solution.py:767
  9.1 14.7 %collective-permute-start = (f32[520,128]{1,0:T(8,128)S(1)}, f32[520,128]{1,0:T(8,128)S(1)}, u32[]{:S(2)}, u32[]{:S(2)}) collective-permute-start(f32[520,128]{1,0:T(8,128)S(1)} %bitcast.21), channel_id=1, source_target_pairs={{0,4},{4,8},{8,12},{12,16},{16,20},{20,24},{24,28},{1,5},{5,9},{9,... | collective-permute-start | bytes 798728 | tf_op jit(solution)/shard_map/ppermute | solution.py:766
  23.9 8.5 %copy-start.2 = (f32[4]{0:T(128)S(1)}, f32[4]{0:T(128)}, u32[]{:S(2)}) copy-start(f32[4]{0:T(128)} %shear_ref.1) | copy-start | bytes 52
  23.9 8.5 %copy-start.3 = (f32[4]{0:T(128)S(1)}, f32[4]{0:T(128)}, u32[]{:S(2)}) copy-start(f32[4]{0:T(128)} %restoring_ref.1) | copy-start | bytes 52
  23.9 8.5 %copy-start.4 = (f32[4]{0:T(128)S(1)}, f32[4]{0:T(128)}, u32[]{:S(2)}) copy-start(f32[4]{0:T(128)} %contrast_ref.3) | copy-start | bytes 52
  25.0 5.5 %collective-permute-start.5 = (f32[320,128]{1,0:T(8,128)S(1)}, f32[320,128]{1,0:T(8,128)S(1)}, u32[]{:S(2)}, u32[]{:S(2)}) collective-permute-start(f32[320,128]{1,0:T(8,128)S(1)} %get-tuple-element.65), channel_id=1, source_target_pairs={{0,1},{1,2},{2,3},{3,0},{4,5},{5,6},{6,7},{7,4},{8,9},{9,10},{10,1... | collective-permute-start | bytes 491528 | tf_op jit(solution)/shard_map/ppermute | solution.py:801
  27.3 5.0 %collective-permute-start.6 = (f32[320,128]{1,0:T(8,128)S(1)}, f32[320,128]{1,0:T(8,128)S(1)}, u32[]{:S(2)}, u32[]{:S(2)}) collective-permute-start(f32[320,128]{1,0:T(8,128)S(1)} %get-tuple-element.66), channel_id=1, source_target_pairs={{1,0},{2,1},{3,2},{0,3},{5,4},{6,5},{7,6},{4,7},{9,8},{10,9},{11,1... | collective-permute-start | bytes 491528 | tf_op jit(solution)/shard_map/ppermute | solution.py:802
  27.4 13.9 %collective-permute-start.10 = (f32[128,1024]{1,0:T(8,128)S(1)}, f32[128,1024]{1,0:T(8,128)S(1)}, u32[]{:S(2)}, u32[]{:S(2)}) collective-permute-start(f32[128,1024]{1,0:T(8,128)S(1)} %constant_dynamic-update-slice_fusion.near_ref), channel_id=1, source_target_pairs={{0,4},{4,0},{8,12},{12,8},{16,20},{20,16},{24,28},{28,24},{1,5},{5... | collective-permute-start | bytes 1572872 | tf_op jit(solution)/shard_map/ppermute | solution.py:774
  39.1 3.1 %collective-permute-start.7 = (f32[8,24,128]{2,1,0:T(8,128)S(1)}, f32[8,24,128]{2,1,0:T(8,128)S(1)}, u32[]{:S(2)}, u32[]{:S(2)}) collective-permute-start(f32[8,24,128]{2,1,0:T(8,128)S(1)} %get-tuple-element.76), channel_id=1, source_target_pairs={{0,1},{1,2},{2,3},{3,0},{4,5},{5,6},{6,7},{7,4},{8,9},{9,10},{10,1... | collective-permute-start | bytes 294920 | tf_op jit(solution)/shard_map/ppermute | solution.py:736
  39.8 4.7 %collective-permute-start.8 = (f32[8,24,128]{2,1,0:T(8,128)S(1)}, f32[8,24,128]{2,1,0:T(8,128)S(1)}, u32[]{:S(2)}, u32[]{:S(2)}) collective-permute-start(f32[8,24,128]{2,1,0:T(8,128)S(1)} %get-tuple-element.77), channel_id=1, source_target_pairs={{0,2},{1,3},{2,0},{3,1},{4,6},{5,7},{6,4},{7,5},{8,10},{9,11},{10,... | collective-permute-start | bytes 294920 | tf_op jit(solution)/shard_map/ppermute | solution.py:736
  40.5 5.1 %collective-permute-start.9 = (f32[8,24,128]{2,1,0:T(8,128)S(1)}, f32[8,24,128]{2,1,0:T(8,128)S(1)}, u32[]{:S(2)}, u32[]{:S(2)}) collective-permute-start(f32[8,24,128]{2,1,0:T(8,128)S(1)} %get-tuple-element.78), channel_id=1, source_target_pairs={{0,3},{1,0},{2,1},{3,2},{4,7},{5,4},{6,5},{7,6},{8,11},{9,8},{10,9... | collective-permute-start | bytes 294920 | tf_op jit(solution)/shard_map/ppermute | solution.py:736
  89.0 3.9 %collective-permute-start.11 = (f32[288,128]{1,0:T(8,128)S(1)}, f32[288,128]{1,0:T(8,128)S(1)}, u32[]{:S(2)}, u32[]{:S(2)}) collective-permute-start(f32[288,128]{1,0:T(8,128)S(1)} %get-tuple-element.88), channel_id=1, source_target_pairs={{0,1},{1,2},{2,3},{3,0},{4,5},{5,6},{6,7},{7,4},{8,9},{9,10},{10,1... | collective-permute-start | bytes 442376 | tf_op jit(solution)/shard_map/ppermute | solution.py:736
  90.2 7.5 %collective-permute-start.12 = (f32[288,128]{1,0:T(8,128)S(1)}, f32[288,128]{1,0:T(8,128)S(1)}, u32[]{:S(2)}, u32[]{:S(2)}) collective-permute-start(f32[288,128]{1,0:T(8,128)S(1)} %get-tuple-element.89), channel_id=1, source_target_pairs={{0,2},{1,3},{2,0},{3,1},{4,6},{5,7},{6,4},{7,5},{8,10},{9,11},{10,... | collective-permute-start | bytes 442376 | tf_op jit(solution)/shard_map/ppermute | solution.py:736
  91.0 7.3 %collective-permute-start.13 = (f32[288,128]{1,0:T(8,128)S(1)}, f32[288,128]{1,0:T(8,128)S(1)}, u32[]{:S(2)}, u32[]{:S(2)}) collective-permute-start(f32[288,128]{1,0:T(8,128)S(1)} %get-tuple-element.90), channel_id=1, source_target_pairs={{0,3},{1,0},{2,1},{3,2},{4,7},{5,4},{6,5},{7,6},{8,11},{9,8},{10,9... | collective-permute-start | bytes 442376 | tf_op jit(solution)/shard_map/ppermute | solution.py:736
  103.8 1.6 %collective-permute-start.14 = (f32[8,24,128]{2,1,0:T(8,128)S(1)}, f32[8,24,128]{2,1,0:T(8,128)S(1)}, u32[]{:S(2)}, u32[]{:S(2)}) collective-permute-start(f32[8,24,128]{2,1,0:T(8,128)S(1)} %get-tuple-element.93), channel_id=1, source_target_pairs={{0,1},{1,2},{2,3},{3,0},{4,5},{5,6},{6,7},{7,4},{8,9},{9,10},{10,1... | collective-permute-start | bytes 294920 | tf_op jit(solution)/shard_map/ppermute | solution.py:736
  103.9 4.3 %collective-permute-start.15 = (f32[8,24,128]{2,1,0:T(8,128)S(1)}, f32[8,24,128]{2,1,0:T(8,128)S(1)}, u32[]{:S(2)}, u32[]{:S(2)}) collective-permute-start(f32[8,24,128]{2,1,0:T(8,128)S(1)} %get-tuple-element.94), channel_id=1, source_target_pairs={{0,2},{1,3},{2,0},{3,1},{4,6},{5,7},{6,4},{7,5},{8,10},{9,11},{10,... | collective-permute-start | bytes 294920 | tf_op jit(solution)/shard_map/ppermute | solution.py:736
  104.5 5.2 %collective-permute-start.16 = (f32[8,24,128]{2,1,0:T(8,128)S(1)}, f32[8,24,128]{2,1,0:T(8,128)S(1)}, u32[]{:S(2)}, u32[]{:S(2)}) collective-permute-start(f32[8,24,128]{2,1,0:T(8,128)S(1)} %get-tuple-element.95), channel_id=1, source_target_pairs={{0,3},{1,0},{2,1},{3,2},{4,7},{5,4},{6,5},{7,6},{8,11},{9,8},{10,9... | collective-permute-start | bytes 294920 | tf_op jit(solution)/shard_map/ppermute | solution.py:736
  147.0 2.9 %collective-permute-start.17 = (f32[192,128]{1,0:T(8,128)S(1)}, f32[192,128]{1,0:T(8,128)S(1)}, u32[]{:S(2)}, u32[]{:S(2)}) collective-permute-start(f32[192,128]{1,0:T(8,128)S(1)} %get-tuple-element.97), channel_id=1, source_target_pairs={{0,1},{1,2},{2,3},{3,0},{4,5},{5,6},{6,7},{7,4},{8,9},{9,10},{10,1... | collective-permute-start | bytes 294920 | tf_op jit(solution)/shard_map/ppermute | solution.py:736
  148.3 5.8 %collective-permute-start.18 = (f32[192,128]{1,0:T(8,128)S(1)}, f32[192,128]{1,0:T(8,128)S(1)}, u32[]{:S(2)}, u32[]{:S(2)}) collective-permute-start(f32[192,128]{1,0:T(8,128)S(1)} %get-tuple-element.98), channel_id=1, source_target_pairs={{0,2},{1,3},{2,0},{3,1},{4,6},{5,7},{6,4},{7,5},{8,10},{9,11},{10,... | collective-permute-start | bytes 294920 | tf_op jit(solution)/shard_map/ppermute | solution.py:736
  149.6 5.2 %collective-permute-start.19 = (f32[192,128]{1,0:T(8,128)S(1)}, f32[192,128]{1,0:T(8,128)S(1)}, u32[]{:S(2)}, u32[]{:S(2)}) collective-permute-start(f32[192,128]{1,0:T(8,128)S(1)} %get-tuple-element.99), channel_id=1, source_target_pairs={{0,3},{1,0},{2,1},{3,2},{4,7},{5,4},{6,5},{7,6},{8,11},{9,8},{10,9... | collective-permute-start | bytes 294920 | tf_op jit(solution)/shard_map/ppermute | solution.py:736

commit v4 on v3

--- a/solution.py
+++ b/solution.py
@@ -238,7 +238,9 @@
 
 
 def dot3(a, b, dims):
-    return dot(a[0], b[0], dims) + (dot(a[0], b[1], dims) + dot(a[1], b[0], dims))
+    rows = a[0].shape[0]
+    both = dot(jnp.concatenate(a, axis=0), b[0], dims)
+    return both[:rows] + (both[rows:] + dot(a[0], b[1], dims))
 
 
 def every(ref, start, stride, count):
@@ -363,6 +365,8 @@
 
 
 SUB = 8
+PARTS = 2
+UNROLL = True
 
 
 def roll(x, shift, axis):
@@ -437,49 +441,55 @@
     for_rows(rows, (u_ref, mat_ref, surface_ref), above_ref, below_ref, body)
 
 
-def run_sweeps(src, offset, a_ref, f_ref, two):
+def lon_neighbours(near):
+    width = near.shape[0]
+    apart = iota(near.shape, 0) - iota(near.shape, 1)
+    apart = jnp.where(apart < 0, apart + width, apart)
+    near[...] = ((apart == 1) | (apart == width - 1)).astype(jnp.float32).astype(HALF)
+
+
+def run_sweeps(src, offset, a_ref, f_ref, two, near):
     steps = a_ref.shape[0]
     rows = a_ref.shape[2] // SUB - 2 * offset
-    lane = iota((SUB, LANES), 1)
-    sub = iota((SUB, LANES), 0)
-    cells = [(t, c) for t in range(steps) for c in range(2)]
     for sweep in range(SWEEPS):
         dst = two[sweep % 2]
         shift = offset if sweep == 0 else 0
-
-        def load(row, src=src, shift=shift):
-            return {cell: src[cell[0], cell[1], tile(row + shift), :] for cell in cells}
-
-        def one(row, carry, load=load, dst=dst):
-            before, x = ({cell: carry[j][i] for i, cell in enumerate(cells)} for j in range(2))
-            after = load(row + 1)
+        size = (rows - 2 - 2 * sweep) // PARTS
+
+        def block(i, carry, src=src, dst=dst, shift=shift, size=size, sweep=sweep):
+            first = sweep + 1 + i * size
+
+            def at(row):
+                return pl.ds(pl.multiple_of(row * SUB, SUB), size * SUB)
+
+            def tiles(t, c, move):
+                return src[t, c, at(first + shift + move), :].reshape(size, SUB, LANES)
+
+            sub = iota((size, SUB, LANES), 1)
+            x = [[tiles(t, c, 0) for c in range(2)] for t in range(steps)]
             for t in range(steps):
-                to_right = [roll(x[t, c], 1, 1) for c in range(2)]
-                to_left = [roll(x[t, c], LANES - 1, 1) for c in range(2)]
+                both = jnp.concatenate([x[t][c].reshape(size * SUB, LANES) for c in range(2)], axis=1)
+                high, low = halves(both)
+                beside = dot(high, near[...], NN) + dot(low, near[...], NN)
                 for c in range(2):
-                    total = jnp.where(lane == 0, to_right[1 - c], to_right[c])
-                    total = total + jnp.where(lane == LANES - 1, to_left[1 - c], to_left[c])
-                    total = total + (before[t, c] + after[t, c])
+                    total = beside[:, c * LANES : (c + 1) * LANES].reshape(size, SUB, LANES)
+                    total = total + (tiles(t, c, -1) + tiles(t, c, 1))
                     if t > 0:
-                        under = x[t - 1, c]
+                        under = x[t - 1][c]
                     else:
-                        under = jnp.where(sub == 0, 0.0, roll(x[steps - 1, c], 1, 0))
+                        under = jnp.where(sub == 0, 0.0, roll(x[steps - 1][c], 1, 1))
                     if t < steps - 1:
-                        over = x[t + 1, c]
+                        over = x[t + 1][c]
                     else:
-                        over = jnp.where(sub == SUB - 1, 0.0, roll(x[0, c], SUB - 1, 0))
-                    total = total + (under + over)
-                    value = a_ref[t, c, tile(row + offset), :] * total
+                        over = jnp.where(sub == SUB - 1, 0.0, roll(x[0][c], SUB - 1, 1))
+                    total = (total + (under + over)).reshape(size * SUB, LANES)
+                    value = a_ref[t, c, at(first + offset), :] * total
                     if t < f_ref.shape[0]:
-                        value = value + f_ref[t, c, tile(row), :]
-                    dst[t, c, tile(row), :] = value
-            return (
-                tuple(x[cell] for cell in cells),
-                tuple(after[cell] for cell in cells),
-            )
-
-        start = (tuple(load(sweep).values()), tuple(load(sweep + 1).values()))
-        lax.fori_loop(sweep + 1, rows - 1 - sweep, one, start, unroll=8)
+                        value = value + f_ref[t, c, at(first), :]
+                    dst[t, c, at(first), :] = value
+            return carry
+
+        lax.fori_loop(0, PARTS, block, 0, unroll=UNROLL)
         src = dst
 
 
@@ -503,7 +513,7 @@
     surface_ref, above_ref, below_ref, left_ref, right_ref, *rest,
 ):
     pieces, rest = rest[:lon_count], rest[lon_count:]
-    u_hbm, a_hbm, b_hbm, load_hbm, first, middle, u_out, a_out, b_out, load_out, f_scr, d_scr, sem = rest
+    u_hbm, a_hbm, b_hbm, load_hbm, first, middle, u_out, a_out, b_out, load_out, f_scr, d_scr, near, sem = rest
     rows = surface_ref.shape[0]
     steps = u_out.shape[0]
     a_of, b_of = [], []
@@ -545,7 +555,8 @@
     copies = [pltpu.make_async_copy(*pair, sem.at[i]) for i, pair in enumerate(kept)]
     for copy in copies[:-1]:
         copy.start()
-    run_sweeps(first, 0, a_out, f_scr, (middle, u_out))
+    lon_neighbours(near)
+    run_sweeps(first, 0, a_out, f_scr, (middle, u_out), near)
     copies[-1].start()
     put_density(
         mat_ref, contrast_ref, lambda k: layer_of(u_out, k, DEEP, rows), index_ref, d_scr, pieces
@@ -559,7 +570,7 @@
 ):
     parts, rest = rest[:lon_count], rest[lon_count:]
     pieces, rest = rest[:lon_count], rest[lon_count:]
-    field_out, middle, last, f_scr, pot, edge, d_scr = rest
+    field_out, middle, last, f_scr, pot, edge, d_scr, near = rest
     layers, rows, _ = field_out.shape
     steps = u_ref.shape[0]
     tall = rows + 2 * SHALLOW
@@ -592,7 +603,8 @@
         return carry
 
     lax.fori_loop(0, tall, force, 0, unroll=8)
-    run_sweeps(u_ref, DEEP - SHALLOW, a_ref, f_scr, (middle, last))
+    lon_neighbours(near)
+    run_sweeps(u_ref, DEEP - SHALLOW, a_ref, f_scr, (middle, last), near)
     for k in range(layers):
         field_out[k] = layer_of(last, k, SHALLOW, rows)
     put_density(mat_ref, contrast_ref, lambda k: field_out[k], index_ref, d_scr, pieces)
@@ -812,6 +824,7 @@
 
     deep = rows + 2 * DEEP
     flat = pltpu.VMEM((lon_count, share, rows, cols), jnp.float32)
+    near_shape = pltpu.VMEM((2 * LANES, 2 * LANES), HALF)
     out = call(
         functools.partial(first_sweeps_kernel, lon_count, total_lat),
         (f32(share, rows, cols),) * lon_count
@@ -820,7 +833,7 @@
         6.6,
         scratch=[pltpu.VMEM(worked(steps, deep), jnp.float32)] * 5
         + [pltpu.VMEM(worked(1, deep), jnp.float32)] * 2
-        + [flat, pltpu.SemaphoreType.DMA((4,))],
+        + [flat, near_shape, pltpu.SemaphoreType.DMA((4,))],
         smem=(0, 1, 2, 3),
         hbm=range(lon_count, lon_count + 4),
     )(index, shear, restoring, contrast, *own, above, below, left, right)
@@ -879,6 +892,7 @@
                     pltpu.VMEM((steps, tall * SUB, LANES), jnp.float32),
                     pltpu.VMEM((tall * SUB, LANES), jnp.float32),
                     flat,
+                    near_shape,
                 ],
                 smem=(0, 1),
             )(index, contrast, own[1], *state, *parts)

time: 156 us -> 152 us (0.974)
  Pallas kernels: 34.3 us -> 29.5 us
    pallas_call x14, Pallas kernels: 34.3 us -> 29.5 us  [run(): pl.pallas_call(kernel, out_shape=outs, in_specs=[place(i, smem, far) for...]
    ppermute x12, waiting for transfers between devices: 20.1 us -> 17.7 us  [exchange(): lax.ppermute(pieces[s], 'lon', [(i, (i + s) % count) for i in range(count)])]
    ppermute x4, waiting for transfers between devices: 2.01 us -> 4.35 us  [partner(): return lax.ppermute(x, 'lat', [(i, i ^ step) for i in range(lat_count)])]
  transfers between devices with their start and end apart: 20 -> 20, of which waited for: 16 -> 15; matrix products, arithmetic and copies ran while one was open for 0% -> 0% of each run, Pallas kernels for 7% -> 5%
where the time goes in v4:
time: 152 us; the launch traced here: 151 us
  blocking collectives  66.3 us (44%)
  waiting for transfers between devices  30.5 us (20%)
  Pallas kernels  29.5 us (19%)
  starting transfers between devices  22.5 us (15%)
    all_to_all x2, blocking collectives, on_device(): lax.all_to_all(synth.reshape(owners, rows + 2 * margin, LANES), BOTH, 0,...  34.1 us
    all_to_all x2, blocking collectives, on_device(): spectrum = lax.all_to_all(spectrum, BOTH, 0, 0, tiled=True)  32.2 us
    pallas_call x14, Pallas kernels, run(): pl.pallas_call(kernel, out_shape=outs, in_specs=[place(i, smem, far) for...  29.5 us
    ppermute x12, waiting for transfers between devices, exchange(): lax.ppermute(pieces[s], 'lon', [(i, (i + s) % count) for i in range(count)])  17.7 us
    ppermute x12, starting transfers between devices, exchange(): lax.ppermute(pieces[s], 'lon', [(i, (i + s) % count) for i in range(count)])  8.02 us
    ppermute x4, starting transfers between devices, partner(): return lax.ppermute(x, 'lat', [(i, i ^ step) for i in range(lat_count)])  6.85 us
    ppermute x1, waiting for transfers between devices, on_device(): lax.ppermute(last, 'lat', [(i, i + 1) for i in range(lat_count - 1)])  5.72 us
    ppermute x4, waiting for transfers between devices, partner(): return lax.ppermute(x, 'lat', [(i, i ^ step) for i in range(lat_count)])  4.35 us
  transfers between devices with their start and end apart: 20, of which 15 were waited for; matrix products, arithmetic and copies ran while one was open for 0% of the time, Pallas kernels for 5%

profile of v4, /device:TPU:1, one launch (start us, length us, event | category | flops | bytes accessed | tf_op | source)
XLA Modules:
  0.0 151.4 jit_solution(13761407620461285311)
XLA Ops:
  0.7 1.2 shard_map.96
  3.3 4.2 %collective-permute-start.4 = (f32[32,1024]{1,0:T(8,128)S(1)}, f32[32,1024]{1,0:T(8,128)S(1)}, u32[]{:S(2)}, u32[]{:S(2)}) collective-permute-start(f32[32,1024]{1,0:T(8,128)S(1)} %reshape.47), channel_id=1, source_target_pairs={{0,24},{4,28},{8,16},{12,20},{16,8},{20,12},{24,0},{28,4},{1,25},{... | collective-permute-start | bytes 393224 | tf_op jit(solution)/shard_map/ppermute | solution.py:786
  7.8 1.3 collective-permute-start.1
  9.1 4.0 %collective-permute-start = (f32[520,128]{1,0:T(8,128)S(1)}, f32[520,128]{1,0:T(8,128)S(1)}, u32[]{:S(2)}, u32[]{:S(2)}) collective-permute-start(f32[520,128]{1,0:T(8,128)S(1)} %bitcast.21), channel_id=1, source_target_pairs={{0,4},{4,8},{8,12},{12,16},{16,20},{20,24},{24,28},{1,5},{5,9},{9,... | collective-permute-start | bytes 798728 | tf_op jit(solution)/shard_map/ppermute | solution.py:778
  13.1 3.0 %shard_map.97 = (bf16[8,256,256]{2,1,0:T(8,128)(2,1)S(1)}, bf16[8,256,256]{2,1,0:T(8,128)(2,1)S(1)}) custom-call(s32[1]{0:T(128)} %bitcast.6.index_ref), custom_call_target="tpu_custom_call" | custom-call | flops 2900000000 | bytes 1 | tf_op jit(solution)/shard_map/pallas_call | solution.py:202
  16.3 1.9 %collective-permute-done.3 = f32[32,1024]{1,0:T(8,128)S(1)} collective-permute-done((f32[32,1024]{1,0:T(8,128)S(1)}, f32[32,1024]{1,0:T(8,128)S(1)}, u32[]{:S(2)}, u32[]{:S(2)}) %collective-permute-start.3) | collective-permute-done | bytes 131104 | tf_op jit(solution)/shard_map/ppermute | solution.py:786
  18.1 5.7 %collective-permute-done.above_ref = f32[520,128]{1,0:T(8,128)S(1)} collective-permute-done((f32[520,128]{1,0:T(8,128)S(1)}, f32[520,128]{1,0:T(8,128)S(1)}, u32[]{:S(2)}, u32[]{:S(2)}) %collective-permute-start) | collective-permute-done | bytes 266272 | tf_op jit(solution)/shard_map/ppermute | solution.py:778
  25.0 2.4 %collective-permute-start.5 = (f32[320,128]{1,0:T(8,128)S(1)}, f32[320,128]{1,0:T(8,128)S(1)}, u32[]{:S(2)}, u32[]{:S(2)}) collective-permute-start(f32[320,128]{1,0:T(8,128)S(1)} %get-tuple-element.65), channel_id=1, source_target_pairs={{0,1},{1,2},{2,3},{3,0},{4,5},{5,6},{6,7},{7,4},{8,9},{9,10},{10,1... | collective-permute-start | bytes 491528 | tf_op jit(solution)/shard_map/ppermute | solution.py:813
  27.4 2.3 %collective-permute-start.10 = (f32[128,1024]{1,0:T(8,128)S(1)}, f32[128,1024]{1,0:T(8,128)S(1)}, u32[]{:S(2)}, u32[]{:S(2)}) collective-permute-start(f32[128,1024]{1,0:T(8,128)S(1)} %constant_dynamic-update-slice_fusion.near_ref), channel_id=1, source_target_pairs={{0,4},{4,0},{8,12},{12,8},{16,20},{20,16},{24,28},{28,24},{1,5},{5... | collective-permute-start | bytes 1572872 | tf_op jit(solution)/shard_map/ppermute | solution.py:786
  30.5 1.9 %collective-permute-done.6.right_ref = f32[320,128]{1,0:T(8,128)S(1)} collective-permute-done((f32[320,128]{1,0:T(8,128)S(1)}, f32[320,128]{1,0:T(8,128)S(1)}, u32[]{:S(2)}, u32[]{:S(2)}) %collective-permute-start.6) | collective-permute-done | bytes 163872 | tf_op jit(solution)/shard_map/ppermute | solution.py:814
  32.4 4.4 %shard_map.99 = (f32[8,24,128]{2,1,0:T(8,128)S(1)}, f32[8,24,128]{2,1,0:T(8,128)S(1)}, f32[8,24,128]{2,1,0:T(8,128)S(1)}, f32[8,24,128]{2,1,0:T(8,128)S(1)}, f32...) custom-call(s32[2]{0:T(128)S(1)} %pad_add_fusion.index_ref, ...), custom_call_target="tpu_custom_call" | custom-call | flops 6600000000 | bytes 1 | tf_op jit(solution)/shard_map/pallas_call | solution.py:202
  38.8 2.5 %collective-permute-done.10.far_ref = f32[128,1024]{1,0:T(8,128)S(1)} collective-permute-done((f32[128,1024]{1,0:T(8,128)S(1)}, f32[128,1024]{1,0:T(8,128)S(1)}, u32[]{:S(2)}, u32[]{:S(2)}) %collective-permute-start.10) | collective-permute-done | bytes 524320 | tf_op jit(solution)/shard_map/ppermute | solution.py:786
  43.3 1.6 %shard_map.101 = f32[32,24,128]{2,1,0:T(8,128)S(1)} custom-call(s32[2]{0:T(128)S(1)} %pad_add_fusion.index_ref, f32[24,128]{1,0:T(8,128)S(1)} %broadcast_in_dim.10.weight_ref, bf16[512,512]{1,0:T(8,128)(2,1)S(1)} %get-tuple-element.71.high_ref, bf16[512,512]{1,0:T(8,128)(2,1)S(1)} %get-tuple-element.72.low_ref, f32[8,24,128]{2,1,0:T(8,128)S(1)} %get-tuple-element.83.rest_0_, ...), custom_call_target="tpu_custom_call" | custom-call | flops 2000000000 | bytes 1 | tf_op jit(solution)/shard_map/pallas_call | solution.py:202
  44.9 17.4 %all_to_all.20 = f32[32,24,128]{2,1,0:T(8,128)S(1)} all-to-all(f32[32,24,128]{2,1,0:T(8,128)S(1)} %shard_map.101), channel_id=1, replica_groups=mesh['lat'=8,'lon'=4] {'lat','lon'}, dimensions={0} | all-to-all | bytes 786432 | tf_op jit(solution)/shard_map/all_to_all | solution.py:859
  62.3 3.1 %shard_map.102 = f32[8,4,32,128]{3,2,1,0:T(8,128)S(1)} custom-call(bf16[8,256,256]{2,1,0:T(8,128)(2,1)S(1)} %get-tuple-element.73.high_ref, bf16[8,256,256]{2,1,0:T(8,128)(2,1)S(1)} %get-tuple-element.74.low_ref, f32[1024,256]{1,0:T(8,128)S(1)} %shard_map.100.green_ref, f32[8,4,24,128]{3,2,1,0:T(8,128)S(1)} %bitcast.15), custom_call_target="tpu_custom_call" | custom-call | flops 4000000000 | bytes 1 | tf_op jit(solution)/shard_map/pallas_call | solution.py:202
  65.5 18.5 %all_to_all.21.x_ref = f32[32,32,128]{2,1,0:T(8,128)S(1)} all-to-all(f32[32,32,128]{2,1,0:T(8,128)S(1)} %bitcast.12), channel_id=1, replica_groups=mesh['lat'=8,'lon'=4] {'lat','lon'}, dimensions={0} | all-to-all | bytes 1048576 | tf_op jit(solution)/shard_map/all_to_all | solution.py:872
  84.0 2.2 %shard_map.103 = (f32[288,128]{1,0:T(8,128)S(1)}, f32[288,128]{1,0:T(8,128)S(1)}, f32[288,128]{1,0:T(8,128)S(1)}, f32[288,128]{1,0:T(8,128)S(1)}) custom-call(s32[2]{0:T(128)S(1)} %pad_add_fusion.index_ref, bf16[512,512]{1,0:T(8,128)(2,1)S(1)} %get-tuple-element.71.high_ref, bf16[512,512]{1,0:T(8,128)(2,1)S(1)} %get-tuple-element.72.low_ref, ...), custom_call_target="tpu_custom_call" | custom-call | flops 2000000000 | bytes 1 | tf_op jit(solution)/shard_map/pallas_call | solution.py:202
  86.2 1.2 collective-permute-start.11
  88.2 1.9 %collective-permute-done.11.rest_1_ = f32[288,128]{1,0:T(8,128)S(1)} collective-permute-done((f32[288,128]{1,0:T(8,128)S(1)}, f32[288,128]{1,0:T(8,128)S(1)}, u32[]{:S(2)}, u32[]{:S(2)}) %collective-permute-start.11) | collective-permute-done | bytes 147488 | tf_op jit(solution)/shard_map/ppermute | solution.py:748
  90.1 4.8 %collective-permute-done.12.rest_2_ = f32[288,128]{1,0:T(8,128)S(1)} collective-permute-done((f32[288,128]{1,0:T(8,128)S(1)}, f32[288,128]{1,0:T(8,128)S(1)}, u32[]{:S(2)}, u32[]{:S(2)}) %collective-permute-start.12) | collective-permute-done | bytes 147488 | tf_op jit(solution)/shard_map/ppermute | solution.py:748
  95.5 4.1 %shard_map.104 = (f32[8,24,128]{2,1,0:T(8,128)S(1)}, f32[8,24,128]{2,1,0:T(8,128)S(1)}, f32[8,24,128]{2,1,0:T(8,128)S(1)}, f32[8,24,128]{2,1,0:T(8,128)S(1)}, f32[32,24,128]{2,1,0:T(8,128)}) custom-call(s32[2]{0:T(128)S(1)} %pad_add_fusion.index_ref, f32[4]{0:T(128)S(1)} %copy-done.4, s32[768,128]{1,0:T(8,128)S(1)} %bitcast.20, ...), custom_call_target="tpu_custom_call" | custom-call | flops 5400000000 | bytes 1 | tf_op jit(solution)/shard_map/pallas_call | solution.py:202
  101.2 2.6 %collective-permute-done.15.rest_2_ = f32[8,24,128]{2,1,0:T(8,128)S(1)} collective-permute-done((f32[8,24,128]{2,1,0:T(8,128)S(1)}, f32[8,24,128]{2,1,0:T(8,128)S(1)}, u32[]{:S(2)}, u32[]{:S(2)}) %collective-permute-start.15) | collective-permute-done | bytes 98336 | tf_op jit(solution)/shard_map/ppermute | solution.py:748
  103.8 1.5 %collective-permute-done.16.rest_3_ = f32[8,24,128]{2,1,0:T(8,128)S(1)} collective-permute-done((f32[8,24,128]{2,1,0:T(8,128)S(1)}, f32[8,24,128]{2,1,0:T(8,128)S(1)}, u32[]{:S(2)}, u32[]{:S(2)}) %collective-permute-start.16) | collective-permute-done | bytes 98336 | tf_op jit(solution)/shard_map/ppermute | solution.py:748
  105.4 1.6 %shard_map.105 = f32[32,24,128]{2,1,0:T(8,128)S(1)} custom-call(s32[2]{0:T(128)S(1)} %pad_add_fusion.index_ref, f32[24,128]{1,0:T(8,128)S(1)} %broadcast_in_dim.10.weight_ref, bf16[512,512]{1,0:T(8,128)(2,1)S(1)} %get-tuple-element.71.high_ref, bf16[512,512]{1,0:T(8,128)(2,1)S(1)} %get-tuple-element.72.low_ref, f32[8,24,128]{2,1,0:T(8,128)S(1)} %get-tuple-element.92.rest_0_, ...), custom_call_target="tpu_custom_call" | custom-call | flops 2000000000 | bytes 1 | tf_op jit(solution)/shard_map/pallas_call | solution.py:202
  107.0 14.8 %all_to_all.22 = f32[32,24,128]{2,1,0:T(8,128)S(1)} all-to-all(f32[32,24,128]{2,1,0:T(8,128)S(1)} %shard_map.105), channel_id=1, replica_groups=mesh['lat'=8,'lon'=4] {'lat','lon'}, dimensions={0} | all-to-all | bytes 786432 | tf_op jit(solution)/shard_map/all_to_all | solution.py:859
  121.8 3.1 %shard_map.106 = f32[8,4,24,128]{3,2,1,0:T(8,128)S(1)} custom-call(bf16[8,256,256]{2,1,0:T(8,128)(2,1)S(1)} %get-tuple-element.73.high_ref, bf16[8,256,256]{2,1,0:T(8,128)(2,1)S(1)} %get-tuple-element.74.low_ref, f32[1024,256]{1,0:T(8,128)S(1)} %shard_map.100.green_ref, f32[8,4,24,128]{3,2,1,0:T(8,128)S(1)} %bitcast.13), custom_call_target="tpu_custom_call" | custom-call | flops 4000000000 | bytes 1 | tf_op jit(solution)/shard_map/pallas_call | solution.py:202
  125.0 15.6 %all_to_all.23.x_ref = f32[32,24,128]{2,1,0:T(8,128)S(1)} all-to-all(f32[32,24,128]{2,1,0:T(8,128)S(1)} %bitcast.14), channel_id=1, replica_groups=mesh['lat'=8,'lon'=4] {'lat','lon'}, dimensions={0} | all-to-all | bytes 786432 | tf_op jit(solution)/shard_map/all_to_all | solution.py:872
  140.6 1.7 %shard_map.107 = (f32[192,128]{1,0:T(8,128)S(1)}, f32[192,128]{1,0:T(8,128)S(1)}, f32[192,128]{1,0:T(8,128)S(1)}, f32[192,128]{1,0:T(8,128)S(1)}) custom-call(s32[2]{0:T(128)S(1)} %pad_add_fusion.index_ref, bf16[512,512]{1,0:T(8,128)(2,1)S(1)} %get-tuple-element.71.high_ref, bf16[512,512]{1,0:T(8,128)(2,1)S(1)} %get-tuple-element.72.low_ref, ...), custom_call_target="tpu_custom_call" | custom-call | flops 2000000000 | bytes 1 | tf_op jit(solution)/shard_map/pallas_call | solution.py:202
  142.2 1.3 collective-permute-start.17
  143.5 1.3 collective-permute-start.18
  145.1 4.2 %collective-permute-done.18.rest_2_ = f32[192,128]{1,0:T(8,128)S(1)} collective-permute-done((f32[192,128]{1,0:T(8,128)S(1)}, f32[192,128]{1,0:T(8,128)S(1)}, u32[]{:S(2)}, u32[]{:S(2)}) %collective-permute-start.18) | collective-permute-done | bytes 98336 | tf_op jit(solution)/shard_map/ppermute | solution.py:748
  149.9 1.3 shard_map.108
  (51 shorter events, 11.8 us)
Async XLA Ops:
  0.6 1.3 copy-start.6
  0.6 1.3 copy-start.7
  0.7 1.3 copy-start.1
  0.7 1.3 copy-start
  2.0 1.0 copy-start.5
  3.3 13.0 %collective-permute-start.4 = (f32[32,1024]{1,0:T(8,128)S(1)}, f32[32,1024]{1,0:T(8,128)S(1)}, u32[]{:S(2)}, u32[]{:S(2)}) collective-permute-start(f32[32,1024]{1,0:T(8,128)S(1)} %reshape.47), channel_id=1, source_target_pairs={{0,24},{4,28},{8,16},{12,20},{16,8},{20,12},{24,0},{28,4},{1,25},{... | collective-permute-start | bytes 393224 | tf_op jit(solution)/shard_map/ppermute | solution.py:786
  7.5 10.7 %collective-permute-start.3 = (f32[32,1024]{1,0:T(8,128)S(1)}, f32[32,1024]{1,0:T(8,128)S(1)}, u32[]{:S(2)}, u32[]{:S(2)}) collective-permute-start(f32[32,1024]{1,0:T(8,128)S(1)} %reshape.47), channel_id=1, source_target_pairs={{0,16},{4,20},{8,24},{12,28},{16,0},{20,4},{24,8},{28,12},{1,17},{... | collective-permute-start | bytes 393224 | tf_op jit(solution)/shard_map/ppermute | solution.py:786
  7.5 10.7 %collective-permute-start.2 = (f32[32,1024]{1,0:T(8,128)S(1)}, f32[32,1024]{1,0:T(8,128)S(1)}, u32[]{:S(2)}, u32[]{:S(2)}) collective-permute-start(f32[32,1024]{1,0:T(8,128)S(1)} %reshape.47), channel_id=1, source_target_pairs={{0,8},{4,12},{8,0},{12,4},{16,24},{20,28},{24,16},{28,20},{1,9},{5... | collective-permute-start | bytes 393224 | tf_op jit(solution)/shard_map/ppermute | solution.py:786
  7.8 10.3 %collective-permute-start.1 = (f32[520,128]{1,0:T(8,128)S(1)}, f32[520,128]{1,0:T(8,128)S(1)}, u32[]{:S(2)}, u32[]{:S(2)}) collective-permute-start(f32[520,128]{1,0:T(8,128)S(1)} %bitcast.22), channel_id=1, source_target_pairs={{4,0},{8,4},{12,8},{16,12},{20,16},{24,20},{28,24},{5,1},{9,5},{13... | collective-permute-start | bytes 798728 | tf_op jit(solution)/shard_map/ppermute | solution.py:779
  9.1 14.7 %collective-permute-start = (f32[520,128]{1,0:T(8,128)S(1)}, f32[520,128]{1,0:T(8,128)S(1)}, u32[]{:S(2)}, u32[]{:S(2)}) collective-permute-start(f32[520,128]{1,0:T(8,128)S(1)} %bitcast.21), channel_id=1, source_target_pairs={{0,4},{4,8},{8,12},{12,16},{16,20},{20,24},{24,28},{1,5},{5,9},{9,... | collective-permute-start | bytes 798728 | tf_op jit(solution)/shard_map/ppermute | solution.py:778
  23.9 8.5 %copy-start.2 = (f32[4]{0:T(128)S(1)}, f32[4]{0:T(128)}, u32[]{:S(2)}) copy-start(f32[4]{0:T(128)} %shear_ref.1) | copy-start | bytes 52
  23.9 8.5 %copy-start.3 = (f32[4]{0:T(128)S(1)}, f32[4]{0:T(128)}, u32[]{:S(2)}) copy-start(f32[4]{0:T(128)} %restoring_ref.1) | copy-start | bytes 52
  23.9 8.5 %copy-start.4 = (f32[4]{0:T(128)S(1)}, f32[4]{0:T(128)}, u32[]{:S(2)}) copy-start(f32[4]{0:T(128)} %contrast_ref.3) | copy-start | bytes 52
  25.0 5.5 %collective-permute-start.5 = (f32[320,128]{1,0:T(8,128)S(1)}, f32[320,128]{1,0:T(8,128)S(1)}, u32[]{:S(2)}, u32[]{:S(2)}) collective-permute-start(f32[320,128]{1,0:T(8,128)S(1)} %get-tuple-element.65), channel_id=1, source_target_pairs={{0,1},{1,2},{2,3},{3,0},{4,5},{5,6},{6,7},{7,4},{8,9},{9,10},{10,1... | collective-permute-start | bytes 491528 | tf_op jit(solution)/shard_map/ppermute | solution.py:813
  27.3 5.0 %collective-permute-start.6 = (f32[320,128]{1,0:T(8,128)S(1)}, f32[320,128]{1,0:T(8,128)S(1)}, u32[]{:S(2)}, u32[]{:S(2)}) collective-permute-start(f32[320,128]{1,0:T(8,128)S(1)} %get-tuple-element.66), channel_id=1, source_target_pairs={{1,0},{2,1},{3,2},{0,3},{5,4},{6,5},{7,6},{4,7},{9,8},{10,9},{11,1... | collective-permute-start | bytes 491528 | tf_op jit(solution)/shard_map/ppermute | solution.py:814
  27.4 13.9 %collective-permute-start.10 = (f32[128,1024]{1,0:T(8,128)S(1)}, f32[128,1024]{1,0:T(8,128)S(1)}, u32[]{:S(2)}, u32[]{:S(2)}) collective-permute-start(f32[128,1024]{1,0:T(8,128)S(1)} %constant_dynamic-update-slice_fusion.near_ref), channel_id=1, source_target_pairs={{0,4},{4,0},{8,12},{12,8},{16,20},{20,16},{24,28},{28,24},{1,5},{5... | collective-permute-start | bytes 1572872 | tf_op jit(solution)/shard_map/ppermute | solution.py:786
  36.8 5.4 %collective-permute-start.7 = (f32[8,24,128]{2,1,0:T(8,128)S(1)}, f32[8,24,128]{2,1,0:T(8,128)S(1)}, u32[]{:S(2)}, u32[]{:S(2)}) collective-permute-start(f32[8,24,128]{2,1,0:T(8,128)S(1)} %get-tuple-element.76), channel_id=1, source_target_pairs={{0,1},{1,2},{2,3},{3,0},{4,5},{5,6},{6,7},{7,4},{8,9},{9,10},{10,1... | collective-permute-start | bytes 294920 | tf_op jit(solution)/shard_map/ppermute | solution.py:748
  37.5 4.8 %collective-permute-start.8 = (f32[8,24,128]{2,1,0:T(8,128)S(1)}, f32[8,24,128]{2,1,0:T(8,128)S(1)}, u32[]{:S(2)}, u32[]{:S(2)}) collective-permute-start(f32[8,24,128]{2,1,0:T(8,128)S(1)} %get-tuple-element.77), channel_id=1, source_target_pairs={{0,2},{1,3},{2,0},{3,1},{4,6},{5,7},{6,4},{7,5},{8,10},{9,11},{10,... | collective-permute-start | bytes 294920 | tf_op jit(solution)/shard_map/ppermute | solution.py:748
  38.1 5.1 %collective-permute-start.9 = (f32[8,24,128]{2,1,0:T(8,128)S(1)}, f32[8,24,128]{2,1,0:T(8,128)S(1)}, u32[]{:S(2)}, u32[]{:S(2)}) collective-permute-start(f32[8,24,128]{2,1,0:T(8,128)S(1)} %get-tuple-element.78), channel_id=1, source_target_pairs={{0,3},{1,0},{2,1},{3,2},{4,7},{5,4},{6,5},{7,6},{8,11},{9,8},{10,9... | collective-permute-start | bytes 294920 | tf_op jit(solution)/shard_map/ppermute | solution.py:748
  86.2 3.9 %collective-permute-start.11 = (f32[288,128]{1,0:T(8,128)S(1)}, f32[288,128]{1,0:T(8,128)S(1)}, u32[]{:S(2)}, u32[]{:S(2)}) collective-permute-start(f32[288,128]{1,0:T(8,128)S(1)} %get-tuple-element.88), channel_id=1, source_target_pairs={{0,1},{1,2},{2,3},{3,0},{4,5},{5,6},{6,7},{7,4},{8,9},{9,10},{10,1... | collective-permute-start | bytes 442376 | tf_op jit(solution)/shard_map/ppermute | solution.py:748
  87.4 7.5 %collective-permute-start.12 = (f32[288,128]{1,0:T(8,128)S(1)}, f32[288,128]{1,0:T(8,128)S(1)}, u32[]{:S(2)}, u32[]{:S(2)}) collective-permute-start(f32[288,128]{1,0:T(8,128)S(1)} %get-tuple-element.89), channel_id=1, source_target_pairs={{0,2},{1,3},{2,0},{3,1},{4,6},{5,7},{6,4},{7,5},{8,10},{9,11},{10,... | collective-permute-start | bytes 442376 | tf_op jit(solution)/shard_map/ppermute | solution.py:748
  88.2 7.3 %collective-permute-start.13 = (f32[288,128]{1,0:T(8,128)S(1)}, f32[288,128]{1,0:T(8,128)S(1)}, u32[]{:S(2)}, u32[]{:S(2)}) collective-permute-start(f32[288,128]{1,0:T(8,128)S(1)} %get-tuple-element.90), channel_id=1, source_target_pairs={{0,3},{1,0},{2,1},{3,2},{4,7},{5,4},{6,5},{7,6},{8,11},{9,8},{10,9... | collective-permute-start | bytes 442376 | tf_op jit(solution)/shard_map/ppermute | solution.py:748
  99.5 1.6 %collective-permute-start.14 = (f32[8,24,128]{2,1,0:T(8,128)S(1)}, f32[8,24,128]{2,1,0:T(8,128)S(1)}, u32[]{:S(2)}, u32[]{:S(2)}) collective-permute-start(f32[8,24,128]{2,1,0:T(8,128)S(1)} %get-tuple-element.93), channel_id=1, source_target_pairs={{0,1},{1,2},{2,3},{3,0},{4,5},{5,6},{6,7},{7,4},{8,9},{9,10},{10,1... | collective-permute-start | bytes 294920 | tf_op jit(solution)/shard_map/ppermute | solution.py:748
  99.5 4.3 %collective-permute-start.15 = (f32[8,24,128]{2,1,0:T(8,128)S(1)}, f32[8,24,128]{2,1,0:T(8,128)S(1)}, u32[]{:S(2)}, u32[]{:S(2)}) collective-permute-start(f32[8,24,128]{2,1,0:T(8,128)S(1)} %get-tuple-element.94), channel_id=1, source_target_pairs={{0,2},{1,3},{2,0},{3,1},{4,6},{5,7},{6,4},{7,5},{8,10},{9,11},{10,... | collective-permute-start | bytes 294920 | tf_op jit(solution)/shard_map/ppermute | solution.py:748
  100.2 5.2 %collective-permute-start.16 = (f32[8,24,128]{2,1,0:T(8,128)S(1)}, f32[8,24,128]{2,1,0:T(8,128)S(1)}, u32[]{:S(2)}, u32[]{:S(2)}) collective-permute-start(f32[8,24,128]{2,1,0:T(8,128)S(1)} %get-tuple-element.95), channel_id=1, source_target_pairs={{0,3},{1,0},{2,1},{3,2},{4,7},{5,4},{6,5},{7,6},{8,11},{9,8},{10,9... | collective-permute-start | bytes 294920 | tf_op jit(solution)/shard_map/ppermute | solution.py:748
  142.2 2.9 %collective-permute-start.17 = (f32[192,128]{1,0:T(8,128)S(1)}, f32[192,128]{1,0:T(8,128)S(1)}, u32[]{:S(2)}, u32[]{:S(2)}) collective-permute-start(f32[192,128]{1,0:T(8,128)S(1)} %get-tuple-element.97), channel_id=1, source_target_pairs={{0,1},{1,2},{2,3},{3,0},{4,5},{5,6},{6,7},{7,4},{8,9},{9,10},{10,1... | collective-permute-start | bytes 294920 | tf_op jit(solution)/shard_map/ppermute | solution.py:748
  143.5 5.8 %collective-permute-start.18 = (f32[192,128]{1,0:T(8,128)S(1)}, f32[192,128]{1,0:T(8,128)S(1)}, u32[]{:S(2)}, u32[]{:S(2)}) collective-permute-start(f32[192,128]{1,0:T(8,128)S(1)} %get-tuple-element.98), channel_id=1, source_target_pairs={{0,2},{1,3},{2,0},{3,1},{4,6},{5,7},{6,4},{7,5},{8,10},{9,11},{10,... | collective-permute-start | bytes 294920 | tf_op jit(solution)/shard_map/ppermute | solution.py:748
  144.8 5.2 %collective-permute-start.19 = (f32[192,128]{1,0:T(8,128)S(1)}, f32[192,128]{1,0:T(8,128)S(1)}, u32[]{:S(2)}, u32[]{:S(2)}) collective-permute-start(f32[192,128]{1,0:T(8,128)S(1)} %get-tuple-element.99), channel_id=1, source_target_pairs={{0,3},{1,0},{2,1},{3,2},{4,7},{5,4},{6,5},{7,6},{8,11},{9,8},{10,9... | collective-permute-start | bytes 294920 | tf_op jit(solution)/shard_map/ppermute | solution.py:748

commit v5 on v4

--- a/solution.py
+++ b/solution.py
@@ -289,7 +289,7 @@
     lax.fori_loop(0, total // shape[0], block, 0, unroll=2)
 
 
-def legendre_kernel(total_lat, share, index_ref, high_out, low_out, table, high_ref, low_ref, sem):
+def legendre_kernel(total_lat, share, index_ref, high_ref, low_ref, table):
     width = table.shape[0] * LANES
     base = index_ref[0] * share
     shape = (share, width)
@@ -341,7 +341,6 @@
         high, low = halves(every(table, m, share, LMAX))
         high_ref[m] = high
         low_ref[m] = low
-    copy_all(sem, (high_ref, high_out), (low_ref, low_out))
 
 
 def turn_kernel(size, index_ref, near_ref, far_ref, o_ref, ordered):
@@ -352,7 +351,8 @@
         first = i % (count // 2) * size
         at = pl.ds(pl.multiple_of((index_ref[0] ^ partner) * size, size), size)
         ordered[at, :] = block[first : first + size, :]
-    o_ref[...] = ordered[...].T
+    for c in range(o_ref.shape[0]):
+        o_ref[c] = ordered[c * LANES : (c + 1) * LANES, :].T
 
 
 def slab_kernel(u_ref, mat_ref, surface_ref, first_ref, last_ref):
@@ -513,7 +513,7 @@
     surface_ref, above_ref, below_ref, left_ref, right_ref, *rest,
 ):
     pieces, rest = rest[:lon_count], rest[lon_count:]
-    u_hbm, a_hbm, b_hbm, load_hbm, first, middle, u_out, a_out, b_out, load_out, f_scr, d_scr, near, sem = rest
+    u_out, a_out, b_out, load_out, first, middle, f_scr, d_scr, near = rest
     rows = surface_ref.shape[0]
     steps = u_out.shape[0]
     a_of, b_of = [], []
@@ -551,18 +551,11 @@
                     f_scr[0, c, at, :] = b * surface
 
     for_rows(rows, (u_ref, mat_ref, surface_ref), above_ref, below_ref, body)
-    kept = ((a_out, a_hbm), (b_out, b_hbm), (load_out, load_hbm), (u_out, u_hbm))
-    copies = [pltpu.make_async_copy(*pair, sem.at[i]) for i, pair in enumerate(kept)]
-    for copy in copies[:-1]:
-        copy.start()
     lon_neighbours(near)
     run_sweeps(first, 0, a_out, f_scr, (middle, u_out), near)
-    copies[-1].start()
     put_density(
         mat_ref, contrast_ref, lambda k: layer_of(u_out, k, DEEP, rows), index_ref, d_scr, pieces
     )
-    for copy in copies:
-        copy.wait()
 
 
 def second_sweeps_kernel(
@@ -631,12 +624,16 @@
     share, rows, cols = parts[0].shape
     chunk = LANES // share
     product = None
-    for s in range(lon_count):
-        source = lax.rem(index_ref[1] + (lon_count - s), lon_count)
-        at = pl.ds(pl.multiple_of(source * cols, cols), cols)
-        term = dot3(
-            halves(parts[s][...].reshape(share * rows, cols)), (high_ref[at, :], low_ref[at, :]), NN
-        )
+    for pair in zip(range(0, lon_count, 2), range(1, lon_count, 2)):
+        x = jnp.concatenate([parts[s][...].reshape(share * rows, cols) for s in pair], axis=1)
+        places = []
+        for s in pair:
+            source = lax.rem(index_ref[1] + (lon_count - s), lon_count)
+            places.append(pl.ds(pl.multiple_of(source * cols, cols), cols))
+        tables = [
+            jnp.concatenate([ref[at, :] for at in places], axis=0) for ref in (high_ref, low_ref)
+        ]
+        term = dot3(halves(x), tables, NN)
         product = term if product is None else product + term
     weight = weight_ref[...] * scale
     for g in range(product.shape[1] // LANES):
@@ -666,23 +663,16 @@
     for m in range(share):
         x = halves(every(turned, m, share, 2 * layers))
         put_every(coeffs, m, share, dot3(x, (high_ref[m], low_ref[m]), NT))
-    block = 4
+    block = 8
 
     def targets(i, carry):
         for c in range(degrees // LANES):
             sums = [jnp.zeros((size, LANES), jnp.float32) for _ in range(block)]
-            for k in range(0, layers, 8):
-                part = [
-                    green_ref[
-                        pl.ds(pl.multiple_of((i * block + t) * layers + k, 8), 8),
-                        c * LANES : (c + 1) * LANES,
-                    ]
-                    for t in range(block)
-                ]
-                for e in range(8):
-                    x = coeffs[c, (k + e) * size : (k + e + 1) * size, :]
-                    for t in range(block):
-                        sums[t] = sums[t] + part[t][e : e + 1] * x
+            for k in range(layers):
+                x = coeffs[c, k * size : (k + 1) * size, :]
+                for t in range(block):
+                    row = green_ref[c, pl.ds((i * block + t) * layers + k, 1), :]
+                    sums[t] = sums[t] + row * x
             for t in range(block):
                 pots[c, pl.ds(pl.multiple_of((i * block + t) * size, size), size), :] = sums[t]
         return carry
@@ -715,9 +705,11 @@
         [jnp.concatenate([group[k] for group in groups], axis=1) for k in range(share)], axis=0
     )
     terms = halves(terms)
-    for q in range(lon_count):
-        at = slice(q * cols, (q + 1) * cols)
-        columns[q] = dot3(terms, (high_ref[at, :], low_ref[at, :]), NT)
+    for q in range(0, lon_count, 2):
+        at = slice(q * cols, (q + 2) * cols)
+        both = dot3(terms, (high_ref[at, :], low_ref[at, :]), NT)
+        columns[q] = both[:, :cols]
+        columns[q + 1] = both[:, cols:]
     lane = iota((rows, LANES), 1)
     for s in range(lon_count):
         dest = lax.rem(index_ref[1] + s, lon_count)
@@ -793,14 +785,8 @@
         functools.partial(legendre_kernel, total_lat, orders),
         (jax.ShapeDtypeStruct(half_table, HALF),) * 2,
         2.9,
-        scratch=[
-            pltpu.VMEM((width // LANES, LMAX * orders, LANES), jnp.float32),
-            pltpu.VMEM(half_table, HALF),
-            pltpu.VMEM(half_table, HALF),
-            pltpu.SemaphoreType.DMA((2,)),
-        ],
+        scratch=[pltpu.VMEM((width // LANES, LMAX * orders, LANES), jnp.float32)],
         smem=(0,),
-        hbm=(0, 1),
     )(owner)
     above, below, others, table, legendre_table = lax.optimization_barrier(
         (above, below, others, table, legendre_table)
@@ -831,11 +817,9 @@
         + (f32(*worked(steps, deep)),) * 3
         + (f32(*worked(1, deep)),),
         6.6,
-        scratch=[pltpu.VMEM(worked(steps, deep), jnp.float32)] * 5
-        + [pltpu.VMEM(worked(1, deep), jnp.float32)] * 2
-        + [flat, near_shape, pltpu.SemaphoreType.DMA((4,))],
+        scratch=[pltpu.VMEM(worked(steps, deep), jnp.float32)] * 2
+        + [pltpu.VMEM(worked(1, deep), jnp.float32), flat, near_shape],
         smem=(0, 1, 2, 3),
-        hbm=range(lon_count, lon_count + 4),
     )(index, shear, restoring, contrast, *own, above, below, left, right)
     pieces, state = out[:lon_count], out[lon_count:]
     for iteration in range(ITERS):
@@ -844,7 +828,7 @@
         if iteration == 0:
             turned_green = call(
                 functools.partial(turn_kernel, green.shape[0]),
-                f32(layers * layers, LMAX),
+                f32(LMAX // LANES, layers * layers, LANES),
                 1.4,
                 scratch=[pltpu.VMEM((LMAX, layers * layers), jnp.float32)],
                 smem=(0,),
@@ -921,6 +905,7 @@
         and (2 * (layers // SUB) + 1) * DEEP <= LANES
         and (layers // lon_count) % (layers // SUB) == 0
         and lat_count > 2
+        and lon_count % 2 == 0
         and lat_count & (lat_count - 1) == 0
         and layers % lon_count == 0
         and LMAX % owners == 0

time: 152 us -> 150 us (0.987)
  Pallas kernels: 29.5 us -> 27.8 us
    pallas_call x14, Pallas kernels: 29.5 us -> 27.8 us  [run(): pl.pallas_call(kernel, out_shape=outs, in_specs=[place(i, smem, far) for...]
where the time goes in v5:
time: 150 us
  blocking collectives  66.3 us (44%)
  waiting for transfers between devices  30.7 us (20%)
  Pallas kernels  27.8 us (19%)
  starting transfers between devices  22.5 us (15%)
    all_to_all x2, blocking collectives, on_device(): lax.all_to_all(synth.reshape(owners, rows + 2 * margin, LANES), BOTH, 0,...  34.1 us
    all_to_all x2, blocking collectives, on_device(): spectrum = lax.all_to_all(spectrum, BOTH, 0, 0, tiled=True)  32.2 us
    pallas_call x14, Pallas kernels, run(): pl.pallas_call(kernel, out_shape=outs, in_specs=[place(i, smem, far) for...  27.8 us
    ppermute x12, waiting for transfers between devices, exchange(): lax.ppermute(pieces[s], 'lon', [(i, (i + s) % count) for i in range(count)])  17.6 us
    ppermute x12, starting transfers between devices, exchange(): lax.ppermute(pieces[s], 'lon', [(i, (i + s) % count) for i in range(count)])  8.03 us
    ppermute x4, starting transfers between devices, partner(): return lax.ppermute(x, 'lat', [(i, i ^ step) for i in range(lat_count)])  6.85 us
    ppermute x1, waiting for transfers between devices, on_device(): lax.ppermute(last, 'lat', [(i, i + 1) for i in range(lat_count - 1)])  5.72 us
    ppermute x4, waiting for transfers between devices, partner(): return lax.ppermute(x, 'lat', [(i, i ^ step) for i in range(lat_count)])  4.68 us
  transfers between devices with their start and end apart: 20, of which 15 were waited for; matrix products, arithmetic and copies ran while one was open for 0% of the time, Pallas kernels for 5%

profile of v5, /device:TPU:1, one launch (start us, length us, event | category | flops | bytes accessed | tf_op | source)
XLA Modules:
  0.0 149.9 jit_solution(2922727958956889109)
XLA Ops:
  0.7 1.2 shard_map.96
  3.3 4.2 %collective-permute-start.4 = (f32[32,1024]{1,0:T(8,128)S(1)}, f32[32,1024]{1,0:T(8,128)S(1)}, u32[]{:S(2)}, u32[]{:S(2)}) collective-permute-start(f32[32,1024]{1,0:T(8,128)S(1)} %reshape.47), channel_id=1, source_target_pairs={{0,24},{4,28},{8,16},{12,20},{16,8},{20,12},{24,0},{28,4},{1,25},{... | collective-permute-start | bytes 393224 | tf_op jit(solution)/shard_map/ppermute | solution.py:778
  7.8 1.3 collective-permute-start.1
  9.1 4.0 %collective-permute-start = (f32[520,128]{1,0:T(8,128)S(1)}, f32[520,128]{1,0:T(8,128)S(1)}, u32[]{:S(2)}, u32[]{:S(2)}) collective-permute-start(f32[520,128]{1,0:T(8,128)S(1)} %bitcast.21), channel_id=1, source_target_pairs={{0,4},{4,8},{8,12},{12,16},{16,20},{20,24},{24,28},{1,5},{5,9},{9,... | collective-permute-start | bytes 798728 | tf_op jit(solution)/shard_map/ppermute | solution.py:770
  13.1 2.8 %shard_map.97 = (bf16[8,256,256]{2,1,0:T(8,128)(2,1)S(1)}, bf16[8,256,256]{2,1,0:T(8,128)(2,1)S(1)}) custom-call(s32[1]{0:T(128)} %bitcast.6.index_ref), custom_call_target="tpu_custom_call" | custom-call | flops 2900000000 | bytes 1 | tf_op jit(solution)/shard_map/pallas_call | solution.py:202
  16.1 2.0 %collective-permute-done.3 = f32[32,1024]{1,0:T(8,128)S(1)} collective-permute-done((f32[32,1024]{1,0:T(8,128)S(1)}, f32[32,1024]{1,0:T(8,128)S(1)}, u32[]{:S(2)}, u32[]{:S(2)}) %collective-permute-start.3) | collective-permute-done | bytes 131104 | tf_op jit(solution)/shard_map/ppermute | solution.py:778
  18.1 5.7 %collective-permute-done.above_ref = f32[520,128]{1,0:T(8,128)S(1)} collective-permute-done((f32[520,128]{1,0:T(8,128)S(1)}, f32[520,128]{1,0:T(8,128)S(1)}, u32[]{:S(2)}, u32[]{:S(2)}) %collective-permute-start) | collective-permute-done | bytes 266272 | tf_op jit(solution)/shard_map/ppermute | solution.py:770
  25.0 2.4 %collective-permute-start.5 = (f32[320,128]{1,0:T(8,128)S(1)}, f32[320,128]{1,0:T(8,128)S(1)}, u32[]{:S(2)}, u32[]{:S(2)}) collective-permute-start(f32[320,128]{1,0:T(8,128)S(1)} %get-tuple-element.65), channel_id=1, source_target_pairs={{0,1},{1,2},{2,3},{3,0},{4,5},{5,6},{6,7},{7,4},{8,9},{9,10},{10,1... | collective-permute-start | bytes 491528 | tf_op jit(solution)/shard_map/ppermute | solution.py:799
  27.4 2.3 %collective-permute-start.10 = (f32[128,1024]{1,0:T(8,128)S(1)}, f32[128,1024]{1,0:T(8,128)S(1)}, u32[]{:S(2)}, u32[]{:S(2)}) collective-permute-start(f32[128,1024]{1,0:T(8,128)S(1)} %constant_dynamic-update-slice_fusion.near_ref), channel_id=1, source_target_pairs={{0,4},{4,0},{8,12},{12,8},{16,20},{20,16},{24,28},{28,24},{1,5},{5... | collective-permute-start | bytes 1572872 | tf_op jit(solution)/shard_map/ppermute | solution.py:778
  30.5 1.9 %collective-permute-done.6.right_ref = f32[320,128]{1,0:T(8,128)S(1)} collective-permute-done((f32[320,128]{1,0:T(8,128)S(1)}, f32[320,128]{1,0:T(8,128)S(1)}, u32[]{:S(2)}, u32[]{:S(2)}) %collective-permute-start.6) | collective-permute-done | bytes 163872 | tf_op jit(solution)/shard_map/ppermute | solution.py:800
  32.4 4.2 %shard_map.99 = (f32[8,24,128]{2,1,0:T(8,128)S(1)}, f32[8,24,128]{2,1,0:T(8,128)S(1)}, f32[8,24,128]{2,1,0:T(8,128)S(1)}, f32[8,24,128]{2,1,0:T(8,128)S(1)}, f32...) custom-call(s32[2]{0:T(128)S(1)} %pad_add_fusion.index_ref, ...), custom_call_target="tpu_custom_call" | custom-call | flops 6600000000 | bytes 1 | tf_op jit(solution)/shard_map/pallas_call | solution.py:202
  38.7 2.6 %collective-permute-done.10.far_ref = f32[128,1024]{1,0:T(8,128)S(1)} collective-permute-done((f32[128,1024]{1,0:T(8,128)S(1)}, f32[128,1024]{1,0:T(8,128)S(1)}, u32[]{:S(2)}, u32[]{:S(2)}) %collective-permute-start.10) | collective-permute-done | bytes 524320 | tf_op jit(solution)/shard_map/ppermute | solution.py:778
  43.1 1.3 shard_map.101
  44.5 17.4 %all_to_all.20 = f32[32,24,128]{2,1,0:T(8,128)S(1)} all-to-all(f32[32,24,128]{2,1,0:T(8,128)S(1)} %shard_map.101), channel_id=1, replica_groups=mesh['lat'=8,'lon'=4] {'lat','lon'}, dimensions={0} | all-to-all | bytes 786432 | tf_op jit(solution)/shard_map/all_to_all | solution.py:843
  61.9 3.1 %shard_map.102 = f32[8,4,32,128]{3,2,1,0:T(8,128)S(1)} custom-call(bf16[8,256,256]{2,1,0:T(8,128)(2,1)S(1)} %get-tuple-element.73.high_ref, bf16[8,256,256]{2,1,0:T(8,128)(2,1)S(1)} %get-tuple-element.74.low_ref, f32[2,1024,128]{2,1,0:T(8,128)S(1)} %shard_map.100.green_ref, f32[8,4,24,128]{3,2,1,0:T(8,128)S(1)} %bitcast.15), custom_call_target="tpu_custom_call" | custom-call | flops 4000000000 | bytes 1 | tf_op jit(solution)/shard_map/pallas_call | solution.py:202
  64.9 18.5 %all_to_all.21.x_ref = f32[32,32,128]{2,1,0:T(8,128)S(1)} all-to-all(f32[32,32,128]{2,1,0:T(8,128)S(1)} %bitcast.12), channel_id=1, replica_groups=mesh['lat'=8,'lon'=4] {'lat','lon'}, dimensions={0} | all-to-all | bytes 1048576 | tf_op jit(solution)/shard_map/all_to_all | solution.py:856
  83.4 1.9 %shard_map.103 = (f32[288,128]{1,0:T(8,128)S(1)}, f32[288,128]{1,0:T(8,128)S(1)}, f32[288,128]{1,0:T(8,128)S(1)}, f32[288,128]{1,0:T(8,128)S(1)}) custom-call(s32[2]{0:T(128)S(1)} %pad_add_fusion.index_ref, bf16[512,512]{1,0:T(8,128)(2,1)S(1)} %get-tuple-element.71.high_ref, bf16[512,512]{1,0:T(8,128)(2,1)S(1)} %get-tuple-element.72.low_ref, ...), custom_call_target="tpu_custom_call" | custom-call | flops 2000000000 | bytes 1 | tf_op jit(solution)/shard_map/pallas_call | solution.py:202
  85.3 1.2 collective-permute-start.11
  87.3 1.9 %collective-permute-done.11.rest_1_ = f32[288,128]{1,0:T(8,128)S(1)} collective-permute-done((f32[288,128]{1,0:T(8,128)S(1)}, f32[288,128]{1,0:T(8,128)S(1)}, u32[]{:S(2)}, u32[]{:S(2)}) %collective-permute-start.11) | collective-permute-done | bytes 147488 | tf_op jit(solution)/shard_map/ppermute | solution.py:740
  89.2 4.8 %collective-permute-done.12.rest_2_ = f32[288,128]{1,0:T(8,128)S(1)} collective-permute-done((f32[288,128]{1,0:T(8,128)S(1)}, f32[288,128]{1,0:T(8,128)S(1)}, u32[]{:S(2)}, u32[]{:S(2)}) %collective-permute-start.12) | collective-permute-done | bytes 147488 | tf_op jit(solution)/shard_map/ppermute | solution.py:740
  94.6 4.1 %shard_map.104 = (f32[8,24,128]{2,1,0:T(8,128)S(1)}, f32[8,24,128]{2,1,0:T(8,128)S(1)}, f32[8,24,128]{2,1,0:T(8,128)S(1)}, f32[8,24,128]{2,1,0:T(8,128)S(1)}, f32[32,24,128]{2,1,0:T(8,128)}) custom-call(s32[2]{0:T(128)S(1)} %pad_add_fusion.index_ref, f32[4]{0:T(128)S(1)} %copy-done.4, s32[768,128]{1,0:T(8,128)S(1)} %bitcast.20, ...), custom_call_target="tpu_custom_call" | custom-call | flops 5400000000 | bytes 1 | tf_op jit(solution)/shard_map/pallas_call | solution.py:202
  100.3 2.6 %collective-permute-done.15.rest_2_ = f32[8,24,128]{2,1,0:T(8,128)S(1)} collective-permute-done((f32[8,24,128]{2,1,0:T(8,128)S(1)}, f32[8,24,128]{2,1,0:T(8,128)S(1)}, u32[]{:S(2)}, u32[]{:S(2)}) %collective-permute-start.15) | collective-permute-done | bytes 98336 | tf_op jit(solution)/shard_map/ppermute | solution.py:740
  102.9 1.6 %collective-permute-done.16.rest_3_ = f32[8,24,128]{2,1,0:T(8,128)S(1)} collective-permute-done((f32[8,24,128]{2,1,0:T(8,128)S(1)}, f32[8,24,128]{2,1,0:T(8,128)S(1)}, u32[]{:S(2)}, u32[]{:S(2)}) %collective-permute-start.16) | collective-permute-done | bytes 98336 | tf_op jit(solution)/shard_map/ppermute | solution.py:740
  104.5 1.3 shard_map.105
  105.8 14.8 %all_to_all.22 = f32[32,24,128]{2,1,0:T(8,128)S(1)} all-to-all(f32[32,24,128]{2,1,0:T(8,128)S(1)} %shard_map.105), channel_id=1, replica_groups=mesh['lat'=8,'lon'=4] {'lat','lon'}, dimensions={0} | all-to-all | bytes 786432 | tf_op jit(solution)/shard_map/all_to_all | solution.py:843
  120.6 3.1 %shard_map.106 = f32[8,4,24,128]{3,2,1,0:T(8,128)S(1)} custom-call(bf16[8,256,256]{2,1,0:T(8,128)(2,1)S(1)} %get-tuple-element.73.high_ref, bf16[8,256,256]{2,1,0:T(8,128)(2,1)S(1)} %get-tuple-element.74.low_ref, f32[2,1024,128]{2,1,0:T(8,128)S(1)} %shard_map.100.green_ref, f32[8,4,24,128]{3,2,1,0:T(8,128)S(1)} %bitcast.13), custom_call_target="tpu_custom_call" | custom-call | flops 4000000000 | bytes 1 | tf_op jit(solution)/shard_map/pallas_call | solution.py:202
  123.7 15.6 %all_to_all.23.x_ref = f32[32,24,128]{2,1,0:T(8,128)S(1)} all-to-all(f32[32,24,128]{2,1,0:T(8,128)S(1)} %bitcast.14), channel_id=1, replica_groups=mesh['lat'=8,'lon'=4] {'lat','lon'}, dimensions={0} | all-to-all | bytes 786432 | tf_op jit(solution)/shard_map/all_to_all | solution.py:856
  139.3 1.4 shard_map.107
  140.7 1.3 collective-permute-start.17
  142.0 1.3 collective-permute-start.18
  143.6 4.2 %collective-permute-done.18.rest_2_ = f32[192,128]{1,0:T(8,128)S(1)} collective-permute-done((f32[192,128]{1,0:T(8,128)S(1)}, f32[192,128]{1,0:T(8,128)S(1)}, u32[]{:S(2)}, u32[]{:S(2)}) %collective-permute-start.18) | collective-permute-done | bytes 98336 | tf_op jit(solution)/shard_map/ppermute | solution.py:740
  148.4 1.3 shard_map.108
  (51 shorter events, 11.7 us)
Async XLA Ops:
  0.6 1.3 copy-start.6
  0.6 1.3 copy-start.7
  0.7 1.3 copy-start.1
  0.7 1.3 copy-start
  2.0 1.0 copy-start.5
  3.3 12.8 %collective-permute-start.4 = (f32[32,1024]{1,0:T(8,128)S(1)}, f32[32,1024]{1,0:T(8,128)S(1)}, u32[]{:S(2)}, u32[]{:S(2)}) collective-permute-start(f32[32,1024]{1,0:T(8,128)S(1)} %reshape.47), channel_id=1, source_target_pairs={{0,24},{4,28},{8,16},{12,20},{16,8},{20,12},{24,0},{28,4},{1,25},{... | collective-permute-start | bytes 393224 | tf_op jit(solution)/shard_map/ppermute | solution.py:778
  7.5 10.7 %collective-permute-start.3 = (f32[32,1024]{1,0:T(8,128)S(1)}, f32[32,1024]{1,0:T(8,128)S(1)}, u32[]{:S(2)}, u32[]{:S(2)}) collective-permute-start(f32[32,1024]{1,0:T(8,128)S(1)} %reshape.47), channel_id=1, source_target_pairs={{0,16},{4,20},{8,24},{12,28},{16,0},{20,4},{24,8},{28,12},{1,17},{... | collective-permute-start | bytes 393224 | tf_op jit(solution)/shard_map/ppermute | solution.py:778
  7.5 10.7 %collective-permute-start.2 = (f32[32,1024]{1,0:T(8,128)S(1)}, f32[32,1024]{1,0:T(8,128)S(1)}, u32[]{:S(2)}, u32[]{:S(2)}) collective-permute-start(f32[32,1024]{1,0:T(8,128)S(1)} %reshape.47), channel_id=1, source_target_pairs={{0,8},{4,12},{8,0},{12,4},{16,24},{20,28},{24,16},{28,20},{1,9},{5... | collective-permute-start | bytes 393224 | tf_op jit(solution)/shard_map/ppermute | solution.py:778
  7.8 10.3 %collective-permute-start.1 = (f32[520,128]{1,0:T(8,128)S(1)}, f32[520,128]{1,0:T(8,128)S(1)}, u32[]{:S(2)}, u32[]{:S(2)}) collective-permute-start(f32[520,128]{1,0:T(8,128)S(1)} %bitcast.22), channel_id=1, source_target_pairs={{4,0},{8,4},{12,8},{16,12},{20,16},{24,20},{28,24},{5,1},{9,5},{13... | collective-permute-start | bytes 798728 | tf_op jit(solution)/shard_map/ppermute | solution.py:771
  9.1 14.7 %collective-permute-start = (f32[520,128]{1,0:T(8,128)S(1)}, f32[520,128]{1,0:T(8,128)S(1)}, u32[]{:S(2)}, u32[]{:S(2)}) collective-permute-start(f32[520,128]{1,0:T(8,128)S(1)} %bitcast.21), channel_id=1, source_target_pairs={{0,4},{4,8},{8,12},{12,16},{16,20},{20,24},{24,28},{1,5},{5,9},{9,... | collective-permute-start | bytes 798728 | tf_op jit(solution)/shard_map/ppermute | solution.py:770
  23.9 8.5 %copy-start.2 = (f32[4]{0:T(128)S(1)}, f32[4]{0:T(128)}, u32[]{:S(2)}) copy-start(f32[4]{0:T(128)} %shear_ref.1) | copy-start | bytes 52
  23.9 8.5 %copy-start.3 = (f32[4]{0:T(128)S(1)}, f32[4]{0:T(128)}, u32[]{:S(2)}) copy-start(f32[4]{0:T(128)} %restoring_ref.1) | copy-start | bytes 52
  23.9 8.5 %copy-start.4 = (f32[4]{0:T(128)S(1)}, f32[4]{0:T(128)}, u32[]{:S(2)}) copy-start(f32[4]{0:T(128)} %contrast_ref.3) | copy-start | bytes 52
  25.0 5.5 %collective-permute-start.5 = (f32[320,128]{1,0:T(8,128)S(1)}, f32[320,128]{1,0:T(8,128)S(1)}, u32[]{:S(2)}, u32[]{:S(2)}) collective-permute-start(f32[320,128]{1,0:T(8,128)S(1)} %get-tuple-element.65), channel_id=1, source_target_pairs={{0,1},{1,2},{2,3},{3,0},{4,5},{5,6},{6,7},{7,4},{8,9},{9,10},{10,1... | collective-permute-start | bytes 491528 | tf_op jit(solution)/shard_map/ppermute | solution.py:799
  27.3 5.0 %collective-permute-start.6 = (f32[320,128]{1,0:T(8,128)S(1)}, f32[320,128]{1,0:T(8,128)S(1)}, u32[]{:S(2)}, u32[]{:S(2)}) collective-permute-start(f32[320,128]{1,0:T(8,128)S(1)} %get-tuple-element.66), channel_id=1, source_target_pairs={{1,0},{2,1},{3,2},{0,3},{5,4},{6,5},{7,6},{4,7},{9,8},{10,9},{11,1... | collective-permute-start | bytes 491528 | tf_op jit(solution)/shard_map/ppermute | solution.py:800
  27.4 13.9 %collective-permute-start.10 = (f32[128,1024]{1,0:T(8,128)S(1)}, f32[128,1024]{1,0:T(8,128)S(1)}, u32[]{:S(2)}, u32[]{:S(2)}) collective-permute-start(f32[128,1024]{1,0:T(8,128)S(1)} %constant_dynamic-update-slice_fusion.near_ref), channel_id=1, source_target_pairs={{0,4},{4,0},{8,12},{12,8},{16,20},{20,16},{24,28},{28,24},{1,5},{5... | collective-permute-start | bytes 1572872 | tf_op jit(solution)/shard_map/ppermute | solution.py:778
  36.6 5.6 %collective-permute-start.7 = (f32[8,24,128]{2,1,0:T(8,128)S(1)}, f32[8,24,128]{2,1,0:T(8,128)S(1)}, u32[]{:S(2)}, u32[]{:S(2)}) collective-permute-start(f32[8,24,128]{2,1,0:T(8,128)S(1)} %get-tuple-element.76), channel_id=1, source_target_pairs={{0,1},{1,2},{2,3},{3,0},{4,5},{5,6},{6,7},{7,4},{8,9},{9,10},{10,1... | collective-permute-start | bytes 294920 | tf_op jit(solution)/shard_map/ppermute | solution.py:740
  37.3 4.9 %collective-permute-start.8 = (f32[8,24,128]{2,1,0:T(8,128)S(1)}, f32[8,24,128]{2,1,0:T(8,128)S(1)}, u32[]{:S(2)}, u32[]{:S(2)}) collective-permute-start(f32[8,24,128]{2,1,0:T(8,128)S(1)} %get-tuple-element.77), channel_id=1, source_target_pairs={{0,2},{1,3},{2,0},{3,1},{4,6},{5,7},{6,4},{7,5},{8,10},{9,11},{10,... | collective-permute-start | bytes 294920 | tf_op jit(solution)/shard_map/ppermute | solution.py:740
  37.9 5.1 %collective-permute-start.9 = (f32[8,24,128]{2,1,0:T(8,128)S(1)}, f32[8,24,128]{2,1,0:T(8,128)S(1)}, u32[]{:S(2)}, u32[]{:S(2)}) collective-permute-start(f32[8,24,128]{2,1,0:T(8,128)S(1)} %get-tuple-element.78), channel_id=1, source_target_pairs={{0,3},{1,0},{2,1},{3,2},{4,7},{5,4},{6,5},{7,6},{8,11},{9,8},{10,9... | collective-permute-start | bytes 294920 | tf_op jit(solution)/shard_map/ppermute | solution.py:740
  85.3 3.9 %collective-permute-start.11 = (f32[288,128]{1,0:T(8,128)S(1)}, f32[288,128]{1,0:T(8,128)S(1)}, u32[]{:S(2)}, u32[]{:S(2)}) collective-permute-start(f32[288,128]{1,0:T(8,128)S(1)} %get-tuple-element.88), channel_id=1, source_target_pairs={{0,1},{1,2},{2,3},{3,0},{4,5},{5,6},{6,7},{7,4},{8,9},{9,10},{10,1... | collective-permute-start | bytes 442376 | tf_op jit(solution)/shard_map/ppermute | solution.py:740
  86.5 7.5 %collective-permute-start.12 = (f32[288,128]{1,0:T(8,128)S(1)}, f32[288,128]{1,0:T(8,128)S(1)}, u32[]{:S(2)}, u32[]{:S(2)}) collective-permute-start(f32[288,128]{1,0:T(8,128)S(1)} %get-tuple-element.89), channel_id=1, source_target_pairs={{0,2},{1,3},{2,0},{3,1},{4,6},{5,7},{6,4},{7,5},{8,10},{9,11},{10,... | collective-permute-start | bytes 442376 | tf_op jit(solution)/shard_map/ppermute | solution.py:740
  87.3 7.3 %collective-permute-start.13 = (f32[288,128]{1,0:T(8,128)S(1)}, f32[288,128]{1,0:T(8,128)S(1)}, u32[]{:S(2)}, u32[]{:S(2)}) collective-permute-start(f32[288,128]{1,0:T(8,128)S(1)} %get-tuple-element.90), channel_id=1, source_target_pairs={{0,3},{1,0},{2,1},{3,2},{4,7},{5,4},{6,5},{7,6},{8,11},{9,8},{10,9... | collective-permute-start | bytes 442376 | tf_op jit(solution)/shard_map/ppermute | solution.py:740
  98.6 1.6 %collective-permute-start.14 = (f32[8,24,128]{2,1,0:T(8,128)S(1)}, f32[8,24,128]{2,1,0:T(8,128)S(1)}, u32[]{:S(2)}, u32[]{:S(2)}) collective-permute-start(f32[8,24,128]{2,1,0:T(8,128)S(1)} %get-tuple-element.93), channel_id=1, source_target_pairs={{0,1},{1,2},{2,3},{3,0},{4,5},{5,6},{6,7},{7,4},{8,9},{9,10},{10,1... | collective-permute-start | bytes 294920 | tf_op jit(solution)/shard_map/ppermute | solution.py:740
  98.7 4.3 %collective-permute-start.15 = (f32[8,24,128]{2,1,0:T(8,128)S(1)}, f32[8,24,128]{2,1,0:T(8,128)S(1)}, u32[]{:S(2)}, u32[]{:S(2)}) collective-permute-start(f32[8,24,128]{2,1,0:T(8,128)S(1)} %get-tuple-element.94), channel_id=1, source_target_pairs={{0,2},{1,3},{2,0},{3,1},{4,6},{5,7},{6,4},{7,5},{8,10},{9,11},{10,... | collective-permute-start | bytes 294920 | tf_op jit(solution)/shard_map/ppermute | solution.py:740
  99.3 5.2 %collective-permute-start.16 = (f32[8,24,128]{2,1,0:T(8,128)S(1)}, f32[8,24,128]{2,1,0:T(8,128)S(1)}, u32[]{:S(2)}, u32[]{:S(2)}) collective-permute-start(f32[8,24,128]{2,1,0:T(8,128)S(1)} %get-tuple-element.95), channel_id=1, source_target_pairs={{0,3},{1,0},{2,1},{3,2},{4,7},{5,4},{6,5},{7,6},{8,11},{9,8},{10,9... | collective-permute-start | bytes 294920 | tf_op jit(solution)/shard_map/ppermute | solution.py:740
  140.7 2.9 %collective-permute-start.17 = (f32[192,128]{1,0:T(8,128)S(1)}, f32[192,128]{1,0:T(8,128)S(1)}, u32[]{:S(2)}, u32[]{:S(2)}) collective-permute-start(f32[192,128]{1,0:T(8,128)S(1)} %get-tuple-element.97), channel_id=1, source_target_pairs={{0,1},{1,2},{2,3},{3,0},{4,5},{5,6},{6,7},{7,4},{8,9},{9,10},{10,1... | collective-permute-start | bytes 294920 | tf_op jit(solution)/shard_map/ppermute | solution.py:740
  142.0 5.8 %collective-permute-start.18 = (f32[192,128]{1,0:T(8,128)S(1)}, f32[192,128]{1,0:T(8,128)S(1)}, u32[]{:S(2)}, u32[]{:S(2)}) collective-permute-start(f32[192,128]{1,0:T(8,128)S(1)} %get-tuple-element.98), channel_id=1, source_target_pairs={{0,2},{1,3},{2,0},{3,1},{4,6},{5,7},{6,4},{7,5},{8,10},{9,11},{10,... | collective-permute-start | bytes 294920 | tf_op jit(solution)/shard_map/ppermute | solution.py:740
  143.3 5.2 %collective-permute-start.19 = (f32[192,128]{1,0:T(8,128)S(1)}, f32[192,128]{1,0:T(8,128)S(1)}, u32[]{:S(2)}, u32[]{:S(2)}) collective-permute-start(f32[192,128]{1,0:T(8,128)S(1)} %get-tuple-element.99), channel_id=1, source_target_pairs={{0,3},{1,0},{2,1},{3,2},{4,7},{5,4},{6,5},{7,6},{8,11},{9,8},{10,9... | collective-permute-start | bytes 294920 | tf_op jit(solution)/shard_map/ppermute | solution.py:740

commit v6 on v5

--- a/solution.py
+++ b/solution.py
@@ -265,8 +265,9 @@
 def fourier_kernel(total, share, high_ref, low_ref):
     shape = (16, 2 * LMAX)
     column = iota(shape, 1)
-    order = column // (2 * share) * share + column % share
-    shift = (column // share) % 2 * (total - total // 4)
+    part = share // 2
+    order = column // share % 2 * (LMAX // 2) + column // (2 * share) * part + column % part
+    shift = column // part % 2 * (total - total // 4)
     first = iota(shape, 0) * order + shift
     quarter, half = total // 4, total // 2
 
@@ -291,9 +292,14 @@
 
 def legendre_kernel(total_lat, share, index_ref, high_ref, low_ref, table):
     width = table.shape[0] * LANES
-    base = index_ref[0] * share
+    part = share // 2
     shape = (share, width)
-    order = iota(shape, 0) + base
+
+    def orders(shape):
+        i = iota(shape, 0)
+        return i // part * (LMAX // 2) + index_ref[0] * part + i % part
+
+    order = orders(shape)
     order_f = order.astype(jnp.float32)
     row = iota(shape, 1)
     theta = (row.astype(jnp.float32) + 0.5) * (math.pi / total_lat)
@@ -303,14 +309,14 @@
     term = iota(terms, 1)
     term_f = jnp.maximum(term.astype(jnp.float32), 1.0)
     growth = 0.5 * jnp.log((2.0 * term_f + 1.0) / (2.0 * term_f))
-    used = (term >= 2) & (term <= iota(terms, 0) + base)
+    used = (term >= 2) & (term <= orders(terms))
     total = jnp.sum(jnp.where(used, growth, 0.0), axis=1, keepdims=True)
     log_diag = jnp.where(order >= 1, 0.5 * math.log(3.0) + total, 0.0)
     diagonal = jnp.exp(log_diag + order_f * jnp.log(sine))
     diagonal = jnp.where(row < total_lat, diagonal, 0.0)
     start_next = jnp.sqrt(2.0 * order_f + 3.0) * cosine * diagonal
     narrow = (share, LANES)
-    square = ((iota(narrow, 0) + base).astype(jnp.float32)) ** 2
+    square = orders(narrow).astype(jnp.float32) ** 2
 
     def wide(x):
         return jnp.concatenate([x] * (width // LANES), axis=1)
@@ -425,18 +431,18 @@
 ):
     rows = surface_ref.shape[0]
     steps = u_ref.shape[0] // rows // SUB
-    slot = iota((SUB, LANES), 1) // DEEP
+    lane = iota((SUB, LANES), 1)
+    chunk = 2 * DEEP
 
     def body(row, u, mat, load):
-        first = jnp.zeros((SUB, LANES), jnp.float32)
-        last = first
+        both = jnp.zeros((SUB, LANES), jnp.float32)
         fields = [u(t) for t in range(steps)] + [mat(t) for t in range(steps)]
-        fields.append(jnp.broadcast_to(load, (SUB, LANES)))
         for i, x in enumerate(fields):
-            first = jnp.where(slot == i, roll(x, i * DEEP, 1), first)
-            last = jnp.where(slot == i, roll(x, (i + 1) * DEEP, 1), last)
-        first_ref[tile(row), :] = first
-        last_ref[tile(row), :] = last
+            both = jnp.where(lane // chunk == i, roll(x, i * chunk + DEEP, 1), both)
+        load = jnp.broadcast_to(load, (SUB, LANES))
+        is_last = lane % chunk < DEEP
+        first_ref[tile(row), :] = jnp.where(is_last, load, both)
+        last_ref[tile(row), :] = jnp.where(is_last, both, roll(load, chunk, 1))
 
     for_rows(rows, (u_ref, mat_ref, surface_ref), above_ref, below_ref, body)
 
@@ -531,12 +537,13 @@
         global_row = index_ref[0] * rows - DEEP + row
         inside = ((global_row >= 0) & (global_row < total_lat)).astype(jnp.float32)
 
+        ends = jnp.where(lane % (2 * DEEP) < DEEP, left, right)
+
         def side(i):
-            after = roll(right, LANES - i * DEEP, 1)
-            before = roll(left, LANES - (i + 1) * DEEP, 1)
-            return jnp.where(lane < DEEP, after, jnp.where(lane >= LANES - DEEP, before, 0.0))
-
-        loads = (jnp.broadcast_to(load, (SUB, LANES)), side(2 * steps))
+            return roll(ends, LANES - (2 * i + 1) * DEEP, 1)
+
+        load_side = jnp.where(lane < DEEP, right, roll(left, LANES - 2 * DEEP, 1))
+        loads = (jnp.broadcast_to(load, (SUB, LANES)), load_side)
         for t in range(steps):
             fields = ((u(t), mat(t)), (side(t), side(steps + t)))
             for c in range(2):
@@ -563,7 +570,7 @@
 ):
     parts, rest = rest[:lon_count], rest[lon_count:]
     pieces, rest = rest[:lon_count], rest[lon_count:]
-    field_out, middle, last, f_scr, pot, edge, d_scr, near = rest
+    field_hbm, middle, last, f_scr, pot, edge, d_scr, near, field_out, sem = rest
     layers, rows, _ = field_out.shape
     steps = u_ref.shape[0]
     tall = rows + 2 * SHALLOW
@@ -585,9 +592,7 @@
         at, deep = tile(row), tile(row + DEEP - SHALLOW)
         ends = edge[at, :]
         for t in range(steps):
-            after = roll(ends, LANES - t * chunk, 1)
-            before = roll(ends, LANES - (t + 1) * chunk, 1)
-            potential = (pot[t, at, :], jnp.where(lane < DEEP, after, before))
+            potential = (pot[t, at, :], roll(ends, LANES - t * chunk - DEEP, 1))
             for c in range(2):
                 value = potential[c]
                 if t == 0:
@@ -600,7 +605,10 @@
     run_sweeps(u_ref, DEEP - SHALLOW, a_ref, f_scr, (middle, last), near)
     for k in range(layers):
         field_out[k] = layer_of(last, k, SHALLOW, rows)
+    copy = pltpu.make_async_copy(field_out, field_hbm, sem)
+    copy.start()
     put_density(mat_ref, contrast_ref, lambda k: field_out[k], index_ref, d_scr, pieces)
+    copy.wait()
 
 
 def swap_chunks(blocks, chunk):
@@ -654,6 +662,16 @@
     total_lat = lat_count * rows
     size = 2 * share
     layers = turned.shape[1] // size
+    part = share // 2
+    spots = [[m // part * share + c * part + m % part for c in range(2)] for m in range(share)]
+    skip = [m // part for m in range(share)]
+    used = [slice(first * LANES, degrees) for first in skip]
+
+    def put(ref, m, y):
+        first = ref.shape[0] - y.shape[1] // LANES
+        for i, r in enumerate(spots[m]):
+            put_every(ref.at[first:], r, size, y[i * layers : (i + 1) * layers, :])
+
     pad = jnp.zeros((width - total_lat, LANES), jnp.float32)
     for q in range(lon_count):
         x = x_ref[:, q].reshape(total_lat, LANES)
@@ -661,26 +679,30 @@
         for c in range(width // LANES):
             turned[c, q * LANES : (q + 1) * LANES, :] = x[c * LANES : (c + 1) * LANES].T
     for m in range(share):
-        x = halves(every(turned, m, share, 2 * layers))
-        put_every(coeffs, m, share, dot3(x, (high_ref[m], low_ref[m]), NT))
+        x = halves(jnp.concatenate([every(turned, r, size, layers) for r in spots[m]], axis=0))
+        y = dot3(x, [ref[m, used[m], :] for ref in (high_ref, low_ref)], NT)
+        put(coeffs, m, y)
     block = 8
 
     def targets(i, carry):
         for c in range(degrees // LANES):
-            sums = [jnp.zeros((size, LANES), jnp.float32) for _ in range(block)]
+            live = size if c > 0 else share
+            sums = [jnp.zeros((live, LANES), jnp.float32) for _ in range(block)]
             for k in range(layers):
-                x = coeffs[c, k * size : (k + 1) * size, :]
+                x = coeffs[c, k * size : k * size + live, :]
                 for t in range(block):
                     row = green_ref[c, pl.ds((i * block + t) * layers + k, 1), :]
                     sums[t] = sums[t] + row * x
             for t in range(block):
-                pots[c, pl.ds(pl.multiple_of((i * block + t) * size, size), size), :] = sums[t]
+                pots[c, pl.ds(pl.multiple_of((i * block + t) * size, size), live), :] = sums[t]
         return carry
 
     lax.fori_loop(0, layers // block, targets, 0)
     for m in range(share):
-        x = halves(every(pots, m, share, 2 * layers))
-        put_every(turned, m, share, dot3(x, (high_ref[m], low_ref[m]), NN))
+        x = [every(pots.at[skip[m] :], r, size, layers) for r in spots[m]]
+        x = halves(jnp.concatenate(x, axis=0))
+        y = dot3(x, [ref[m, used[m], :] for ref in (high_ref, low_ref)], NN)
+        put(turned, m, y)
     for q in range(lon_count):
         x = [turned[c, q * LANES : (q + 1) * LANES, :].T for c in range(width // LANES)]
         x = jnp.concatenate(x, axis=0)[:total_lat]
@@ -720,11 +742,9 @@
         before = lax.rem(dest + lon_count - 1, lon_count)
         packed = jnp.zeros((rows, LANES), jnp.float32)
         for k in range(share):
-            right = roll(columns[after, k * rows : (k + 1) * rows, :], k * chunk, 1)
-            left = roll(columns[before, k * rows : (k + 1) * rows, :], (k + 1) * chunk, 1)
-            packed = jnp.where(
-                lane // DEEP == 2 * k, right, jnp.where(lane // DEEP == 2 * k + 1, left, packed)
-            )
+            at = slice(k * rows, (k + 1) * rows)
+            ends = jnp.where(lane < LANES - DEEP, columns[after, at, :], columns[before, at, :])
+            packed = jnp.where(lane // chunk == k, roll(ends, k * chunk + DEEP, 1), packed)
         pieces[s][share * rows :] = packed
 
 
@@ -877,8 +897,11 @@
                     pltpu.VMEM((tall * SUB, LANES), jnp.float32),
                     flat,
                     near_shape,
+                    pltpu.VMEM((layers, rows, cols), jnp.float32),
+                    pltpu.SemaphoreType.DMA,
                 ],
                 smem=(0, 1),
+                hbm=(lon_count,),
             )(index, contrast, own[1], *state, *parts)
             pieces, field = out[:lon_count], out[lon_count]
     potential = call(
@@ -902,7 +925,7 @@
         and cols == LANES
         and rows % 8 == 0
         and layers % SUB == 0
-        and (2 * (layers // SUB) + 1) * DEEP <= LANES
+        and 2 * (layers // SUB) * 2 * DEEP <= LANES
         and (layers // lon_count) % (layers // SUB) == 0
         and lat_count > 2
         and lon_count % 2 == 0
@@ -911,7 +934,7 @@
         and LMAX % owners == 0
         and 2 * (LMAX // owners) * (layers // lon_count) == LANES
         and 2 * (LMAX // owners) == 2 * DEEP
-        and LMAX % LANES == 0
+        and LMAX == 2 * LANES
     )
 
 

time: 150 us -> 149 us (level)
  no operation moved by 1% of the time
where the time goes in v6:
time: 149 us
  blocking collectives  66.4 us (45%)
  waiting for transfers between devices  30.7 us (21%)
  Pallas kernels  26.8 us (18%)
  starting transfers between devices  22.6 us (15%)
    all_to_all x2, blocking collectives, on_device(): lax.all_to_all(synth.reshape(owners, rows + 2 * margin, LANES), BOTH, 0,...  34.1 us
    all_to_all x2, blocking collectives, on_device(): spectrum = lax.all_to_all(spectrum, BOTH, 0, 0, tiled=True)  32.3 us
    pallas_call x14, Pallas kernels, run(): pl.pallas_call(kernel, out_shape=outs, in_specs=[place(i, smem, far) for...  26.8 us
    ppermute x12, waiting for transfers between devices, exchange(): lax.ppermute(pieces[s], 'lon', [(i, (i + s) % count) for i in range(count)])  17.5 us
    ppermute x12, starting transfers between devices, exchange(): lax.ppermute(pieces[s], 'lon', [(i, (i + s) % count) for i in range(count)])  8.08 us
    ppermute x4, starting transfers between devices, partner(): return lax.ppermute(x, 'lat', [(i, i ^ step) for i in range(lat_count)])  6.85 us
    ppermute x1, waiting for transfers between devices, on_device(): lax.ppermute(last, 'lat', [(i, i + 1) for i in range(lat_count - 1)])  5.72 us
    ppermute x4, waiting for transfers between devices, partner(): return lax.ppermute(x, 'lat', [(i, i ^ step) for i in range(lat_count)])  4.77 us
  transfers between devices with their start and end apart: 20, of which 15 were waited for; matrix products, arithmetic and copies ran while one was open for 0% of the time, Pallas kernels for 5%

profile of v6, /device:TPU:1, one launch (start us, length us, event | category | flops | bytes accessed | tf_op | source)
XLA Modules:
  0.0 149.0 jit_solution(3455252287267773430)
XLA Ops:
  0.7 1.2 shard_map.96
  3.3 4.2 %collective-permute-start.4 = (f32[32,1024]{1,0:T(8,128)S(1)}, f32[32,1024]{1,0:T(8,128)S(1)}, u32[]{:S(2)}, u32[]{:S(2)}) collective-permute-start(f32[32,1024]{1,0:T(8,128)S(1)} %reshape.47), channel_id=1, source_target_pairs={{0,24},{4,28},{8,16},{12,20},{16,8},{20,12},{24,0},{28,4},{1,25},{... | collective-permute-start | bytes 393224 | tf_op jit(solution)/shard_map/ppermute | solution.py:798
  7.8 1.3 collective-permute-start.1
  9.1 4.0 %collective-permute-start = (f32[520,128]{1,0:T(8,128)S(1)}, f32[520,128]{1,0:T(8,128)S(1)}, u32[]{:S(2)}, u32[]{:S(2)}) collective-permute-start(f32[520,128]{1,0:T(8,128)S(1)} %bitcast.21), channel_id=1, source_target_pairs={{0,4},{4,8},{8,12},{12,16},{16,20},{20,24},{24,28},{1,5},{5,9},{9,... | collective-permute-start | bytes 798728 | tf_op jit(solution)/shard_map/ppermute | solution.py:790
  13.1 2.8 %shard_map.97 = (bf16[8,256,256]{2,1,0:T(8,128)(2,1)S(1)}, bf16[8,256,256]{2,1,0:T(8,128)(2,1)S(1)}) custom-call(s32[1]{0:T(128)} %bitcast.6.index_ref), custom_call_target="tpu_custom_call" | custom-call | flops 2900000000 | bytes 1 | tf_op jit(solution)/shard_map/pallas_call | solution.py:202
  16.1 2.0 %collective-permute-done.3 = f32[32,1024]{1,0:T(8,128)S(1)} collective-permute-done((f32[32,1024]{1,0:T(8,128)S(1)}, f32[32,1024]{1,0:T(8,128)S(1)}, u32[]{:S(2)}, u32[]{:S(2)}) %collective-permute-start.3) | collective-permute-done | bytes 131104 | tf_op jit(solution)/shard_map/ppermute | solution.py:798
  18.2 5.7 %collective-permute-done.above_ref = f32[520,128]{1,0:T(8,128)S(1)} collective-permute-done((f32[520,128]{1,0:T(8,128)S(1)}, f32[520,128]{1,0:T(8,128)S(1)}, u32[]{:S(2)}, u32[]{:S(2)}) %collective-permute-start) | collective-permute-done | bytes 266272 | tf_op jit(solution)/shard_map/ppermute | solution.py:790
  24.9 2.4 %collective-permute-start.5 = (f32[320,128]{1,0:T(8,128)S(1)}, f32[320,128]{1,0:T(8,128)S(1)}, u32[]{:S(2)}, u32[]{:S(2)}) collective-permute-start(f32[320,128]{1,0:T(8,128)S(1)} %get-tuple-element.65), channel_id=1, source_target_pairs={{0,1},{1,2},{2,3},{3,0},{4,5},{5,6},{6,7},{7,4},{8,9},{9,10},{10,1... | collective-permute-start | bytes 491528 | tf_op jit(solution)/shard_map/ppermute | solution.py:819
  27.3 2.3 %collective-permute-start.10 = (f32[128,1024]{1,0:T(8,128)S(1)}, f32[128,1024]{1,0:T(8,128)S(1)}, u32[]{:S(2)}, u32[]{:S(2)}) collective-permute-start(f32[128,1024]{1,0:T(8,128)S(1)} %constant_dynamic-update-slice_fusion.near_ref), channel_id=1, source_target_pairs={{0,4},{4,0},{8,12},{12,8},{16,20},{20,16},{24,28},{28,24},{1,5},{5... | collective-permute-start | bytes 1572872 | tf_op jit(solution)/shard_map/ppermute | solution.py:798
  30.5 1.9 %collective-permute-done.6.right_ref = f32[320,128]{1,0:T(8,128)S(1)} collective-permute-done((f32[320,128]{1,0:T(8,128)S(1)}, f32[320,128]{1,0:T(8,128)S(1)}, u32[]{:S(2)}, u32[]{:S(2)}) %collective-permute-start.6) | collective-permute-done | bytes 163872 | tf_op jit(solution)/shard_map/ppermute | solution.py:820
  32.3 4.1 %shard_map.99 = (f32[8,24,128]{2,1,0:T(8,128)S(1)}, f32[8,24,128]{2,1,0:T(8,128)S(1)}, f32[8,24,128]{2,1,0:T(8,128)S(1)}, f32[8,24,128]{2,1,0:T(8,128)S(1)}, f32...) custom-call(s32[2]{0:T(128)S(1)} %pad_add_fusion.index_ref, ...), custom_call_target="tpu_custom_call" | custom-call | flops 6600000000 | bytes 1 | tf_op jit(solution)/shard_map/pallas_call | solution.py:202
  38.5 2.7 %collective-permute-done.10.far_ref = f32[128,1024]{1,0:T(8,128)S(1)} collective-permute-done((f32[128,1024]{1,0:T(8,128)S(1)}, f32[128,1024]{1,0:T(8,128)S(1)}, u32[]{:S(2)}, u32[]{:S(2)}) %collective-permute-start.10) | collective-permute-done | bytes 524320 | tf_op jit(solution)/shard_map/ppermute | solution.py:798
  43.0 1.3 shard_map.101
  44.3 17.4 %all_to_all.20 = f32[32,24,128]{2,1,0:T(8,128)S(1)} all-to-all(f32[32,24,128]{2,1,0:T(8,128)S(1)} %shard_map.101), channel_id=1, replica_groups=mesh['lat'=8,'lon'=4] {'lat','lon'}, dimensions={0} | all-to-all | bytes 786432 | tf_op jit(solution)/shard_map/all_to_all | solution.py:863
  61.7 2.7 %shard_map.102 = f32[8,4,32,128]{3,2,1,0:T(8,128)S(1)} custom-call(bf16[8,256,256]{2,1,0:T(8,128)(2,1)S(1)} %get-tuple-element.73.high_ref, bf16[8,256,256]{2,1,0:T(8,128)(2,1)S(1)} %get-tuple-element.74.low_ref, f32[2,1024,128]{2,1,0:T(8,128)S(1)} %shard_map.100.green_ref, f32[8,4,24,128]{3,2,1,0:T(8,128)S(1)} %bitcast.15), custom_call_target="tpu_custom_call" | custom-call | flops 4000000000 | bytes 1 | tf_op jit(solution)/shard_map/pallas_call | solution.py:202
  64.4 18.5 %all_to_all.21.x_ref = f32[32,32,128]{2,1,0:T(8,128)S(1)} all-to-all(f32[32,32,128]{2,1,0:T(8,128)S(1)} %bitcast.12), channel_id=1, replica_groups=mesh['lat'=8,'lon'=4] {'lat','lon'}, dimensions={0} | all-to-all | bytes 1048576 | tf_op jit(solution)/shard_map/all_to_all | solution.py:876
  82.9 1.8 %shard_map.103 = (f32[288,128]{1,0:T(8,128)S(1)}, f32[288,128]{1,0:T(8,128)S(1)}, f32[288,128]{1,0:T(8,128)S(1)}, f32[288,128]{1,0:T(8,128)S(1)}) custom-call(s32[2]{0:T(128)S(1)} %pad_add_fusion.index_ref, bf16[512,512]{1,0:T(8,128)(2,1)S(1)} %get-tuple-element.71.high_ref, bf16[512,512]{1,0:T(8,128)(2,1)S(1)} %get-tuple-element.72.low_ref, ...), custom_call_target="tpu_custom_call" | custom-call | flops 2000000000 | bytes 1 | tf_op jit(solution)/shard_map/pallas_call | solution.py:202
  84.6 1.2 collective-permute-start.11
  86.7 1.9 %collective-permute-done.11.rest_1_ = f32[288,128]{1,0:T(8,128)S(1)} collective-permute-done((f32[288,128]{1,0:T(8,128)S(1)}, f32[288,128]{1,0:T(8,128)S(1)}, u32[]{:S(2)}, u32[]{:S(2)}) %collective-permute-start.11) | collective-permute-done | bytes 147488 | tf_op jit(solution)/shard_map/ppermute | solution.py:760
  88.6 4.8 %collective-permute-done.12.rest_2_ = f32[288,128]{1,0:T(8,128)S(1)} collective-permute-done((f32[288,128]{1,0:T(8,128)S(1)}, f32[288,128]{1,0:T(8,128)S(1)}, u32[]{:S(2)}, u32[]{:S(2)}) %collective-permute-start.12) | collective-permute-done | bytes 147488 | tf_op jit(solution)/shard_map/ppermute | solution.py:760
  93.9 4.1 %shard_map.104 = (f32[8,24,128]{2,1,0:T(8,128)S(1)}, f32[8,24,128]{2,1,0:T(8,128)S(1)}, f32[8,24,128]{2,1,0:T(8,128)S(1)}, f32[8,24,128]{2,1,0:T(8,128)S(1)}, f32[32,24,128]{2,1,0:T(8,128)}) custom-call(s32[2]{0:T(128)S(1)} %pad_add_fusion.index_ref, f32[4]{0:T(128)S(1)} %copy-done.4, s32[768,128]{1,0:T(8,128)S(1)} %bitcast.20, ...), custom_call_target="tpu_custom_call" | custom-call | flops 5400000000 | bytes 1 | tf_op jit(solution)/shard_map/pallas_call | solution.py:202
  99.7 2.6 %collective-permute-done.15.rest_2_ = f32[8,24,128]{2,1,0:T(8,128)S(1)} collective-permute-done((f32[8,24,128]{2,1,0:T(8,128)S(1)}, f32[8,24,128]{2,1,0:T(8,128)S(1)}, u32[]{:S(2)}, u32[]{:S(2)}) %collective-permute-start.15) | collective-permute-done | bytes 98336 | tf_op jit(solution)/shard_map/ppermute | solution.py:760
  102.4 1.5 %collective-permute-done.16.rest_3_ = f32[8,24,128]{2,1,0:T(8,128)S(1)} collective-permute-done((f32[8,24,128]{2,1,0:T(8,128)S(1)}, f32[8,24,128]{2,1,0:T(8,128)S(1)}, u32[]{:S(2)}, u32[]{:S(2)}) %collective-permute-start.16) | collective-permute-done | bytes 98336 | tf_op jit(solution)/shard_map/ppermute | solution.py:760
  103.9 1.3 shard_map.105
  105.3 14.9 %all_to_all.22 = f32[32,24,128]{2,1,0:T(8,128)S(1)} all-to-all(f32[32,24,128]{2,1,0:T(8,128)S(1)} %shard_map.105), channel_id=1, replica_groups=mesh['lat'=8,'lon'=4] {'lat','lon'}, dimensions={0} | all-to-all | bytes 786432 | tf_op jit(solution)/shard_map/all_to_all | solution.py:863
  120.2 2.7 %shard_map.106 = f32[8,4,24,128]{3,2,1,0:T(8,128)S(1)} custom-call(bf16[8,256,256]{2,1,0:T(8,128)(2,1)S(1)} %get-tuple-element.73.high_ref, bf16[8,256,256]{2,1,0:T(8,128)(2,1)S(1)} %get-tuple-element.74.low_ref, f32[2,1024,128]{2,1,0:T(8,128)S(1)} %shard_map.100.green_ref, f32[8,4,24,128]{3,2,1,0:T(8,128)S(1)} %bitcast.13), custom_call_target="tpu_custom_call" | custom-call | flops 4000000000 | bytes 1 | tf_op jit(solution)/shard_map/pallas_call | solution.py:202
  122.8 15.6 %all_to_all.23.x_ref = f32[32,24,128]{2,1,0:T(8,128)S(1)} all-to-all(f32[32,24,128]{2,1,0:T(8,128)S(1)} %bitcast.14), channel_id=1, replica_groups=mesh['lat'=8,'lon'=4] {'lat','lon'}, dimensions={0} | all-to-all | bytes 786432 | tf_op jit(solution)/shard_map/all_to_all | solution.py:876
  138.4 1.4 shard_map.107
  139.8 1.3 collective-permute-start.17
  141.1 1.3 collective-permute-start.18
  142.7 4.2 %collective-permute-done.18.rest_2_ = f32[192,128]{1,0:T(8,128)S(1)} collective-permute-done((f32[192,128]{1,0:T(8,128)S(1)}, f32[192,128]{1,0:T(8,128)S(1)}, u32[]{:S(2)}, u32[]{:S(2)}) %collective-permute-start.18) | collective-permute-done | bytes 98336 | tf_op jit(solution)/shard_map/ppermute | solution.py:760
  147.5 1.3 shard_map.108
  (51 shorter events, 11.6 us)
Async XLA Ops:
  0.6 1.3 copy-start.6
  0.6 1.3 copy-start.7
  0.7 1.3 copy-start.1
  0.7 1.3 copy-start
  2.0 1.0 copy-start.5
  3.3 12.9 %collective-permute-start.4 = (f32[32,1024]{1,0:T(8,128)S(1)}, f32[32,1024]{1,0:T(8,128)S(1)}, u32[]{:S(2)}, u32[]{:S(2)}) collective-permute-start(f32[32,1024]{1,0:T(8,128)S(1)} %reshape.47), channel_id=1, source_target_pairs={{0,24},{4,28},{8,16},{12,20},{16,8},{20,12},{24,0},{28,4},{1,25},{... | collective-permute-start | bytes 393224 | tf_op jit(solution)/shard_map/ppermute | solution.py:798
  7.5 10.7 %collective-permute-start.3 = (f32[32,1024]{1,0:T(8,128)S(1)}, f32[32,1024]{1,0:T(8,128)S(1)}, u32[]{:S(2)}, u32[]{:S(2)}) collective-permute-start(f32[32,1024]{1,0:T(8,128)S(1)} %reshape.47), channel_id=1, source_target_pairs={{0,16},{4,20},{8,24},{12,28},{16,0},{20,4},{24,8},{28,12},{1,17},{... | collective-permute-start | bytes 393224 | tf_op jit(solution)/shard_map/ppermute | solution.py:798
  7.5 10.7 %collective-permute-start.2 = (f32[32,1024]{1,0:T(8,128)S(1)}, f32[32,1024]{1,0:T(8,128)S(1)}, u32[]{:S(2)}, u32[]{:S(2)}) collective-permute-start(f32[32,1024]{1,0:T(8,128)S(1)} %reshape.47), channel_id=1, source_target_pairs={{0,8},{4,12},{8,0},{12,4},{16,24},{20,28},{24,16},{28,20},{1,9},{5... | collective-permute-start | bytes 393224 | tf_op jit(solution)/shard_map/ppermute | solution.py:798
  7.8 10.3 %collective-permute-start.1 = (f32[520,128]{1,0:T(8,128)S(1)}, f32[520,128]{1,0:T(8,128)S(1)}, u32[]{:S(2)}, u32[]{:S(2)}) collective-permute-start(f32[520,128]{1,0:T(8,128)S(1)} %bitcast.22), channel_id=1, source_target_pairs={{4,0},{8,4},{12,8},{16,12},{20,16},{24,20},{28,24},{5,1},{9,5},{13... | collective-permute-start | bytes 798728 | tf_op jit(solution)/shard_map/ppermute | solution.py:791
  9.1 14.7 %collective-permute-start = (f32[520,128]{1,0:T(8,128)S(1)}, f32[520,128]{1,0:T(8,128)S(1)}, u32[]{:S(2)}, u32[]{:S(2)}) collective-permute-start(f32[520,128]{1,0:T(8,128)S(1)} %bitcast.21), channel_id=1, source_target_pairs={{0,4},{4,8},{8,12},{12,16},{16,20},{20,24},{24,28},{1,5},{5,9},{9,... | collective-permute-start | bytes 798728 | tf_op jit(solution)/shard_map/ppermute | solution.py:790
  23.9 8.5 %copy-start.2 = (f32[4]{0:T(128)S(1)}, f32[4]{0:T(128)}, u32[]{:S(2)}) copy-start(f32[4]{0:T(128)} %shear_ref.1) | copy-start | bytes 52
  23.9 8.5 %copy-start.3 = (f32[4]{0:T(128)S(1)}, f32[4]{0:T(128)}, u32[]{:S(2)}) copy-start(f32[4]{0:T(128)} %restoring_ref.1) | copy-start | bytes 52
  23.9 8.5 %copy-start.4 = (f32[4]{0:T(128)S(1)}, f32[4]{0:T(128)}, u32[]{:S(2)}) copy-start(f32[4]{0:T(128)} %contrast_ref.3) | copy-start | bytes 52
  24.9 5.5 %collective-permute-start.5 = (f32[320,128]{1,0:T(8,128)S(1)}, f32[320,128]{1,0:T(8,128)S(1)}, u32[]{:S(2)}, u32[]{:S(2)}) collective-permute-start(f32[320,128]{1,0:T(8,128)S(1)} %get-tuple-element.65), channel_id=1, source_target_pairs={{0,1},{1,2},{2,3},{3,0},{4,5},{5,6},{6,7},{7,4},{8,9},{9,10},{10,1... | collective-permute-start | bytes 491528 | tf_op jit(solution)/shard_map/ppermute | solution.py:819
  27.3 5.0 %collective-permute-start.6 = (f32[320,128]{1,0:T(8,128)S(1)}, f32[320,128]{1,0:T(8,128)S(1)}, u32[]{:S(2)}, u32[]{:S(2)}) collective-permute-start(f32[320,128]{1,0:T(8,128)S(1)} %get-tuple-element.66), channel_id=1, source_target_pairs={{1,0},{2,1},{3,2},{0,3},{5,4},{6,5},{7,6},{4,7},{9,8},{10,9},{11,1... | collective-permute-start | bytes 491528 | tf_op jit(solution)/shard_map/ppermute | solution.py:820
  27.3 13.9 %collective-permute-start.10 = (f32[128,1024]{1,0:T(8,128)S(1)}, f32[128,1024]{1,0:T(8,128)S(1)}, u32[]{:S(2)}, u32[]{:S(2)}) collective-permute-start(f32[128,1024]{1,0:T(8,128)S(1)} %constant_dynamic-update-slice_fusion.near_ref), channel_id=1, source_target_pairs={{0,4},{4,0},{8,12},{12,8},{16,20},{20,16},{24,28},{28,24},{1,5},{5... | collective-permute-start | bytes 1572872 | tf_op jit(solution)/shard_map/ppermute | solution.py:798
  36.5 5.7 %collective-permute-start.7 = (f32[8,24,128]{2,1,0:T(8,128)S(1)}, f32[8,24,128]{2,1,0:T(8,128)S(1)}, u32[]{:S(2)}, u32[]{:S(2)}) collective-permute-start(f32[8,24,128]{2,1,0:T(8,128)S(1)} %get-tuple-element.76), channel_id=1, source_target_pairs={{0,1},{1,2},{2,3},{3,0},{4,5},{5,6},{6,7},{7,4},{8,9},{9,10},{10,1... | collective-permute-start | bytes 294920 | tf_op jit(solution)/shard_map/ppermute | solution.py:760
  37.2 5.0 %collective-permute-start.8 = (f32[8,24,128]{2,1,0:T(8,128)S(1)}, f32[8,24,128]{2,1,0:T(8,128)S(1)}, u32[]{:S(2)}, u32[]{:S(2)}) collective-permute-start(f32[8,24,128]{2,1,0:T(8,128)S(1)} %get-tuple-element.77), channel_id=1, source_target_pairs={{0,2},{1,3},{2,0},{3,1},{4,6},{5,7},{6,4},{7,5},{8,10},{9,11},{10,... | collective-permute-start | bytes 294920 | tf_op jit(solution)/shard_map/ppermute | solution.py:760
  37.8 5.1 %collective-permute-start.9 = (f32[8,24,128]{2,1,0:T(8,128)S(1)}, f32[8,24,128]{2,1,0:T(8,128)S(1)}, u32[]{:S(2)}, u32[]{:S(2)}) collective-permute-start(f32[8,24,128]{2,1,0:T(8,128)S(1)} %get-tuple-element.78), channel_id=1, source_target_pairs={{0,3},{1,0},{2,1},{3,2},{4,7},{5,4},{6,5},{7,6},{8,11},{9,8},{10,9... | collective-permute-start | bytes 294920 | tf_op jit(solution)/shard_map/ppermute | solution.py:760
  84.6 3.9 %collective-permute-start.11 = (f32[288,128]{1,0:T(8,128)S(1)}, f32[288,128]{1,0:T(8,128)S(1)}, u32[]{:S(2)}, u32[]{:S(2)}) collective-permute-start(f32[288,128]{1,0:T(8,128)S(1)} %get-tuple-element.88), channel_id=1, source_target_pairs={{0,1},{1,2},{2,3},{3,0},{4,5},{5,6},{6,7},{7,4},{8,9},{9,10},{10,1... | collective-permute-start | bytes 442376 | tf_op jit(solution)/shard_map/ppermute | solution.py:760
  85.9 7.5 %collective-permute-start.12 = (f32[288,128]{1,0:T(8,128)S(1)}, f32[288,128]{1,0:T(8,128)S(1)}, u32[]{:S(2)}, u32[]{:S(2)}) collective-permute-start(f32[288,128]{1,0:T(8,128)S(1)} %get-tuple-element.89), channel_id=1, source_target_pairs={{0,2},{1,3},{2,0},{3,1},{4,6},{5,7},{6,4},{7,5},{8,10},{9,11},{10,... | collective-permute-start | bytes 442376 | tf_op jit(solution)/shard_map/ppermute | solution.py:760
  86.7 7.3 %collective-permute-start.13 = (f32[288,128]{1,0:T(8,128)S(1)}, f32[288,128]{1,0:T(8,128)S(1)}, u32[]{:S(2)}, u32[]{:S(2)}) collective-permute-start(f32[288,128]{1,0:T(8,128)S(1)} %get-tuple-element.90), channel_id=1, source_target_pairs={{0,3},{1,0},{2,1},{3,2},{4,7},{5,4},{6,5},{7,6},{8,11},{9,8},{10,9... | collective-permute-start | bytes 442376 | tf_op jit(solution)/shard_map/ppermute | solution.py:760
  98.0 1.7 %collective-permute-start.14 = (f32[8,24,128]{2,1,0:T(8,128)S(1)}, f32[8,24,128]{2,1,0:T(8,128)S(1)}, u32[]{:S(2)}, u32[]{:S(2)}) collective-permute-start(f32[8,24,128]{2,1,0:T(8,128)S(1)} %get-tuple-element.93), channel_id=1, source_target_pairs={{0,1},{1,2},{2,3},{3,0},{4,5},{5,6},{6,7},{7,4},{8,9},{9,10},{10,1... | collective-permute-start | bytes 294920 | tf_op jit(solution)/shard_map/ppermute | solution.py:760
  98.1 4.3 %collective-permute-start.15 = (f32[8,24,128]{2,1,0:T(8,128)S(1)}, f32[8,24,128]{2,1,0:T(8,128)S(1)}, u32[]{:S(2)}, u32[]{:S(2)}) collective-permute-start(f32[8,24,128]{2,1,0:T(8,128)S(1)} %get-tuple-element.94), channel_id=1, source_target_pairs={{0,2},{1,3},{2,0},{3,1},{4,6},{5,7},{6,4},{7,5},{8,10},{9,11},{10,... | collective-permute-start | bytes 294920 | tf_op jit(solution)/shard_map/ppermute | solution.py:760
  98.8 5.1 %collective-permute-start.16 = (f32[8,24,128]{2,1,0:T(8,128)S(1)}, f32[8,24,128]{2,1,0:T(8,128)S(1)}, u32[]{:S(2)}, u32[]{:S(2)}) collective-permute-start(f32[8,24,128]{2,1,0:T(8,128)S(1)} %get-tuple-element.95), channel_id=1, source_target_pairs={{0,3},{1,0},{2,1},{3,2},{4,7},{5,4},{6,5},{7,6},{8,11},{9,8},{10,9... | collective-permute-start | bytes 294920 | tf_op jit(solution)/shard_map/ppermute | solution.py:760
  139.8 2.9 %collective-permute-start.17 = (f32[192,128]{1,0:T(8,128)S(1)}, f32[192,128]{1,0:T(8,128)S(1)}, u32[]{:S(2)}, u32[]{:S(2)}) collective-permute-start(f32[192,128]{1,0:T(8,128)S(1)} %get-tuple-element.97), channel_id=1, source_target_pairs={{0,1},{1,2},{2,3},{3,0},{4,5},{5,6},{6,7},{7,4},{8,9},{9,10},{10,1... | collective-permute-start | bytes 294920 | tf_op jit(solution)/shard_map/ppermute | solution.py:760
  141.1 5.8 %collective-permute-start.18 = (f32[192,128]{1,0:T(8,128)S(1)}, f32[192,128]{1,0:T(8,128)S(1)}, u32[]{:S(2)}, u32[]{:S(2)}) collective-permute-start(f32[192,128]{1,0:T(8,128)S(1)} %get-tuple-element.98), channel_id=1, source_target_pairs={{0,2},{1,3},{2,0},{3,1},{4,6},{5,7},{6,4},{7,5},{8,10},{9,11},{10,... | collective-permute-start | bytes 294920 | tf_op jit(solution)/shard_map/ppermute | solution.py:760
  142.4 5.2 %collective-permute-start.19 = (f32[192,128]{1,0:T(8,128)S(1)}, f32[192,128]{1,0:T(8,128)S(1)}, u32[]{:S(2)}, u32[]{:S(2)}) collective-permute-start(f32[192,128]{1,0:T(8,128)S(1)} %get-tuple-element.99), channel_id=1, source_target_pairs={{0,3},{1,0},{2,1},{3,2},{4,7},{5,4},{6,5},{7,6},{8,11},{9,8},{10,9... | collective-permute-start | bytes 294920 | tf_op jit(solution)/shard_map/ppermute | solution.py:760

commit v7 on v6

--- a/solution.py
+++ b/solution.py
@@ -427,7 +427,7 @@
 
 
 def pack_kernel(
-    u_ref, mat_ref, surface_ref, above_ref, below_ref, first_ref, last_ref
+    u_ref, mat_ref, surface_ref, above_ref, below_ref, first_ref, last_ref, ends, loads
 ):
     rows = surface_ref.shape[0]
     steps = u_ref.shape[0] // rows // SUB
@@ -439,12 +439,29 @@
         fields = [u(t) for t in range(steps)] + [mat(t) for t in range(steps)]
         for i, x in enumerate(fields):
             both = jnp.where(lane // chunk == i, roll(x, i * chunk + DEEP, 1), both)
-        load = jnp.broadcast_to(load, (SUB, LANES))
-        is_last = lane % chunk < DEEP
-        first_ref[tile(row), :] = jnp.where(is_last, load, both)
-        last_ref[tile(row), :] = jnp.where(is_last, both, roll(load, chunk, 1))
+        ends[tile(row), :] = both
+        loads[tile(row), :] = jnp.broadcast_to(load, (SUB, LANES))
 
     for_rows(rows, (u_ref, mat_ref, surface_ref), above_ref, below_ref, body)
+    is_last = lane % chunk < DEEP
+    half = ends.shape[0] // 2
+    for j in range(0, half, SUB):
+        low, high = ends[j : j + SUB, :], ends[half + j : half + j + SUB, :]
+        first_ref[j : j + SUB, :] = jnp.where(is_last, roll(high, LANES - DEEP, 1), low)
+        last_ref[j : j + SUB, :] = jnp.where(is_last, low, roll(high, DEEP, 1))
+    sub = iota((SUB, LANES), 0)
+    first = jnp.zeros((SUB, LANES), jnp.float32)
+    last = first
+    tall = loads.shape[0] // SUB
+    for i in range(SUB):
+        x = first
+        for r in range(i, tall, SUB):
+            x = jnp.where(sub == r // SUB, loads[r * SUB : (r + 1) * SUB, :], x)
+        chosen = lane // chunk == i
+        first = jnp.where(chosen, roll(x, i * chunk, 1), first)
+        last = jnp.where(chosen, roll(x, i * chunk + DEEP, 1), last)
+    first_ref[half:, :] = first
+    last_ref[half:, :] = last
 
 
 def lon_neighbours(near):
@@ -531,9 +548,15 @@
     lane = iota((SUB, LANES), 1)
     sub = iota((SUB, LANES), 0)
 
+    half = rows // 2 + DEEP
+
     def body(row, u, mat, load):
         at = tile(row)
-        left, right = left_ref[at, :], right_ref[at, :]
+        upper = row >= half
+        ends_at = tile(row - jnp.where(upper, half, 0))
+        left, right = left_ref[ends_at, :], right_ref[ends_at, :]
+        left = jnp.where(upper, roll(left, LANES - DEEP, 1), left)
+        right = jnp.where(upper, roll(right, DEEP, 1), right)
         global_row = index_ref[0] * rows - DEEP + row
         inside = ((global_row >= 0) & (global_row < total_lat)).astype(jnp.float32)
 
@@ -542,7 +565,13 @@
         def side(i):
             return roll(ends, LANES - (2 * i + 1) * DEEP, 1)
 
-        load_side = jnp.where(lane < DEEP, right, roll(left, LANES - 2 * DEEP, 1))
+        load_at = pl.ds(half * SUB + row // SUB, 1)
+        place = row % SUB * 2 * DEEP
+        after = jnp.broadcast_to(right_ref[load_at, :], (SUB, LANES))
+        after = pltpu.roll(after, (LANES - place) % LANES, 1)
+        before = jnp.broadcast_to(left_ref[load_at, :], (SUB, LANES))
+        before = pltpu.roll(before, (2 * LANES - DEEP - place) % LANES, 1)
+        load_side = jnp.where(lane < DEEP, after, before)
         loads = (jnp.broadcast_to(load, (SUB, LANES)), load_side)
         for t in range(steps):
             fields = ((u(t), mat(t)), (side(t), side(steps + t)))
@@ -756,10 +785,10 @@
 
 def exchange(pieces):
     count = len(pieces)
-    return [pieces[0]] + [
-        lax.ppermute(pieces[s], "lon", [(i, (i + s) % count) for i in range(count)])
-        for s in range(1, count)
-    ]
+    got = {0: pieces[0]}
+    for s in (2, 1, 3) if count == 4 else range(1, count):
+        got[s] = lax.ppermute(pieces[s], "lon", [(i, (i + s) % count) for i in range(count)])
+    return [got[s] for s in range(count)]
 
 
 def on_device(displacement, materials, ice_mask, ice_height, shear, restoring, contrast, green):
@@ -813,7 +842,10 @@
     )
     near = jnp.concatenate([near, *others], axis=0)
     far = partner(near, 1)
-    first, last = call(pack_kernel, (f32((rows + 2 * DEEP) * SUB, cols),) * 2, 1.5)(
+    deep = rows + 2 * DEEP
+    edge_tiles = f32((deep // 2 + 1) * SUB, cols)
+    whole = pltpu.VMEM((deep * SUB, cols), jnp.float32)
+    first, last = call(pack_kernel, (edge_tiles,) * 2, 1.5, scratch=[whole, whole])(
         *own, above, below
     )
     left = lax.ppermute(last, "lon", [(i, (i + 1) % lon_count) for i in range(lon_count)])
@@ -828,7 +860,6 @@
     def worked(t, height):
         return (t, 2, height * SUB, LANES)
 
-    deep = rows + 2 * DEEP
     flat = pltpu.VMEM((lon_count, share, rows, cols), jnp.float32)
     near_shape = pltpu.VMEM((2 * LANES, 2 * LANES), HALF)
     out = call(
@@ -924,6 +955,7 @@
         ITERS == 2
         and cols == LANES
         and rows % 8 == 0
+        and rows + 2 * DEEP <= SUB * SUB
         and layers % SUB == 0
         and 2 * (layers // SUB) * 2 * DEEP <= LANES
         and (layers // lon_count) % (layers // SUB) == 0

time: 149 us -> 149 us (level)
    ppermute x4, waiting for transfers between devices: 4.77 us -> 6.42 us  [partner(): return lax.ppermute(x, 'lat', [(i, i ^ step) for i in range(lat_count)])]
  transfers between devices with their start and end apart: 20 -> 20, of which waited for: 15 -> 13; matrix products, arithmetic and copies ran while one was open for 0% -> 0% of each run, Pallas kernels for 5% -> 6%
where the time goes in v7:
time: 149 us; the launch traced here: 148 us
  blocking collectives  66.3 us (44%)
  waiting for transfers between devices  30.5 us (20%)
  Pallas kernels  27.3 us (18%)
  starting transfers between devices  21.7 us (15%)
    all_to_all x2, blocking collectives, on_device(): lax.all_to_all(synth.reshape(owners, rows + 2 * margin, LANES), BOTH, 0,...  34.1 us
    all_to_all x2, blocking collectives, on_device(): spectrum = lax.all_to_all(spectrum, BOTH, 0, 0, tiled=True)  32.1 us
    pallas_call x14, Pallas kernels, run(): pl.pallas_call(kernel, out_shape=outs, in_specs=[place(i, smem, far) for...  27.3 us
    ppermute x12, waiting for transfers between devices, exchange(): lax.ppermute(pieces[s], 'lon', [(i, (i + s) % count) for i in range(count)])  16.8 us
    ppermute x12, starting transfers between devices, exchange(): lax.ppermute(pieces[s], 'lon', [(i, (i + s) % count) for i in range(count)])  7.26 us
    ppermute x4, starting transfers between devices, partner(): return lax.ppermute(x, 'lat', [(i, i ^ step) for i in range(lat_count)])  6.85 us
    ppermute x4, waiting for transfers between devices, partner(): return lax.ppermute(x, 'lat', [(i, i ^ step) for i in range(lat_count)])  6.42 us
    ppermute x1, waiting for transfers between devices, on_device(): lax.ppermute(last, 'lat', [(i, i + 1) for i in range(lat_count - 1)])  5.72 us
  transfers between devices with their start and end apart: 20, of which 13 were waited for; matrix products, arithmetic and copies ran while one was open for 0% of the time, Pallas kernels for 6%

profile of v7, /device:TPU:1, one launch (start us, length us, event | category | flops | bytes accessed | tf_op | source)
XLA Modules:
  0.0 148.3 jit_solution(7400550798603239682)
XLA Ops:
  0.7 1.2 shard_map.96
  3.3 4.2 %collective-permute-start.4 = (f32[32,1024]{1,0:T(8,128)S(1)}, f32[32,1024]{1,0:T(8,128)S(1)}, u32[]{:S(2)}, u32[]{:S(2)}) collective-permute-start(f32[32,1024]{1,0:T(8,128)S(1)} %reshape.47), channel_id=1, source_target_pairs={{0,24},{4,28},{8,16},{12,20},{16,8},{20,12},{24,0},{28,4},{1,25},{... | collective-permute-start | bytes 393224 | tf_op jit(solution)/shard_map/ppermute | solution.py:827
  7.8 1.3 collective-permute-start.1
  9.1 4.0 %collective-permute-start = (f32[520,128]{1,0:T(8,128)S(1)}, f32[520,128]{1,0:T(8,128)S(1)}, u32[]{:S(2)}, u32[]{:S(2)}) collective-permute-start(f32[520,128]{1,0:T(8,128)S(1)} %bitcast.21), channel_id=1, source_target_pairs={{0,4},{4,8},{8,12},{12,16},{16,20},{20,24},{24,28},{1,5},{5,9},{9,... | collective-permute-start | bytes 798728 | tf_op jit(solution)/shard_map/ppermute | solution.py:819
  13.1 2.8 %shard_map.97 = (bf16[8,256,256]{2,1,0:T(8,128)(2,1)S(1)}, bf16[8,256,256]{2,1,0:T(8,128)(2,1)S(1)}) custom-call(s32[1]{0:T(128)} %bitcast.6.index_ref), custom_call_target="tpu_custom_call" | custom-call | flops 2900000000 | bytes 1 | tf_op jit(solution)/shard_map/pallas_call | solution.py:202
  16.1 2.0 %collective-permute-done.3 = f32[32,1024]{1,0:T(8,128)S(1)} collective-permute-done((f32[32,1024]{1,0:T(8,128)S(1)}, f32[32,1024]{1,0:T(8,128)S(1)}, u32[]{:S(2)}, u32[]{:S(2)}) %collective-permute-start.3) | collective-permute-done | bytes 131104 | tf_op jit(solution)/shard_map/ppermute | solution.py:827
  18.2 5.7 %collective-permute-done.above_ref = f32[520,128]{1,0:T(8,128)S(1)} collective-permute-done((f32[520,128]{1,0:T(8,128)S(1)}, f32[520,128]{1,0:T(8,128)S(1)}, u32[]{:S(2)}, u32[]{:S(2)}) %collective-permute-start) | collective-permute-done | bytes 266272 | tf_op jit(solution)/shard_map/ppermute | solution.py:819
  23.9 1.3 shard_map.98
  25.2 2.3 %collective-permute-start.5 = (f32[168,128]{1,0:T(8,128)S(1)}, f32[168,128]{1,0:T(8,128)S(1)}, u32[]{:S(2)}, u32[]{:S(2)}) collective-permute-start(f32[168,128]{1,0:T(8,128)S(1)} %get-tuple-element.65), channel_id=1, source_target_pairs={{0,1},{1,2},{2,3},{3,0},{4,5},{5,6},{6,7},{7,4},{8,9},{9,10},{10,1... | collective-permute-start | bytes 258056 | tf_op jit(solution)/shard_map/ppermute | solution.py:851
  27.6 2.3 %collective-permute-start.10 = (f32[128,1024]{1,0:T(8,128)S(1)}, f32[128,1024]{1,0:T(8,128)S(1)}, u32[]{:S(2)}, u32[]{:S(2)}) collective-permute-start(f32[128,1024]{1,0:T(8,128)S(1)} %constant_dynamic-update-slice_fusion.near_ref), channel_id=1, source_target_pairs={{0,4},{4,0},{8,12},{12,8},{16,20},{20,16},{24,28},{28,24},{1,5},{5... | collective-permute-start | bytes 1572872 | tf_op jit(solution)/shard_map/ppermute | solution.py:827
  29.8 1.6 %collective-permute-done.6.right_ref = f32[168,128]{1,0:T(8,128)S(1)} collective-permute-done((f32[168,128]{1,0:T(8,128)S(1)}, f32[168,128]{1,0:T(8,128)S(1)}, u32[]{:S(2)}, u32[]{:S(2)}) %collective-permute-start.6) | collective-permute-done | bytes 86048 | tf_op jit(solution)/shard_map/ppermute | solution.py:852
  31.4 4.4 %shard_map.99 = (f32[8,24,128]{2,1,0:T(8,128)S(1)}, f32[8,24,128]{2,1,0:T(8,128)S(1)}, f32[8,24,128]{2,1,0:T(8,128)S(1)}, f32[8,24,128]{2,1,0:T(8,128)S(1)}, f32...) custom-call(s32[2]{0:T(128)S(1)} %pad_add_fusion.index_ref, ...), custom_call_target="tpu_custom_call" | custom-call | flops 6600000000 | bytes 1 | tf_op jit(solution)/shard_map/pallas_call | solution.py:202
  37.1 4.4 %collective-permute-done.10.far_ref = f32[128,1024]{1,0:T(8,128)S(1)} collective-permute-done((f32[128,1024]{1,0:T(8,128)S(1)}, f32[128,1024]{1,0:T(8,128)S(1)}, u32[]{:S(2)}, u32[]{:S(2)}) %collective-permute-start.10) | collective-permute-done | bytes 524320 | tf_op jit(solution)/shard_map/ppermute | solution.py:827
  42.5 1.3 shard_map.101
  43.9 17.2 %all_to_all.20 = f32[32,24,128]{2,1,0:T(8,128)S(1)} all-to-all(f32[32,24,128]{2,1,0:T(8,128)S(1)} %shard_map.101), channel_id=1, replica_groups=mesh['lat'=8,'lon'=4] {'lat','lon'}, dimensions={0} | all-to-all | bytes 786432 | tf_op jit(solution)/shard_map/all_to_all | solution.py:894
  61.1 2.7 %shard_map.102 = f32[8,4,32,128]{3,2,1,0:T(8,128)S(1)} custom-call(bf16[8,256,256]{2,1,0:T(8,128)(2,1)S(1)} %get-tuple-element.73.high_ref, bf16[8,256,256]{2,1,0:T(8,128)(2,1)S(1)} %get-tuple-element.74.low_ref, f32[2,1024,128]{2,1,0:T(8,128)S(1)} %shard_map.100.green_ref, f32[8,4,24,128]{3,2,1,0:T(8,128)S(1)} %bitcast.15), custom_call_target="tpu_custom_call" | custom-call | flops 4000000000 | bytes 1 | tf_op jit(solution)/shard_map/pallas_call | solution.py:202
  63.8 18.5 %all_to_all.21.x_ref = f32[32,32,128]{2,1,0:T(8,128)S(1)} all-to-all(f32[32,32,128]{2,1,0:T(8,128)S(1)} %bitcast.12), channel_id=1, replica_groups=mesh['lat'=8,'lon'=4] {'lat','lon'}, dimensions={0} | all-to-all | bytes 1048576 | tf_op jit(solution)/shard_map/all_to_all | solution.py:907
  82.3 1.8 %shard_map.103 = (f32[288,128]{1,0:T(8,128)S(1)}, f32[288,128]{1,0:T(8,128)S(1)}, f32[288,128]{1,0:T(8,128)S(1)}, f32[288,128]{1,0:T(8,128)S(1)}) custom-call(s32[2]{0:T(128)S(1)} %pad_add_fusion.index_ref, bf16[512,512]{1,0:T(8,128)(2,1)S(1)} %get-tuple-element.71.high_ref, bf16[512,512]{1,0:T(8,128)(2,1)S(1)} %get-tuple-element.72.low_ref, ...), custom_call_target="tpu_custom_call" | custom-call | flops 2000000000 | bytes 1 | tf_op jit(solution)/shard_map/pallas_call | solution.py:202
  86.1 1.9 %collective-permute-done.11.rest_1_ = f32[288,128]{1,0:T(8,128)S(1)} collective-permute-done((f32[288,128]{1,0:T(8,128)S(1)}, f32[288,128]{1,0:T(8,128)S(1)}, u32[]{:S(2)}, u32[]{:S(2)}) %collective-permute-start.11) | collective-permute-done | bytes 147488 | tf_op jit(solution)/shard_map/ppermute | solution.py:790
  88.0 4.8 %collective-permute-done.12.rest_2_ = f32[288,128]{1,0:T(8,128)S(1)} collective-permute-done((f32[288,128]{1,0:T(8,128)S(1)}, f32[288,128]{1,0:T(8,128)S(1)}, u32[]{:S(2)}, u32[]{:S(2)}) %collective-permute-start.12) | collective-permute-done | bytes 147488 | tf_op jit(solution)/shard_map/ppermute | solution.py:790
  93.3 4.0 %shard_map.104 = (f32[8,24,128]{2,1,0:T(8,128)S(1)}, f32[8,24,128]{2,1,0:T(8,128)S(1)}, f32[8,24,128]{2,1,0:T(8,128)S(1)}, f32[8,24,128]{2,1,0:T(8,128)S(1)}, f32[32,24,128]{2,1,0:T(8,128)}) custom-call(s32[2]{0:T(128)S(1)} %pad_add_fusion.index_ref, f32[4]{0:T(128)S(1)} %copy-done.4, s32[768,128]{1,0:T(8,128)S(1)} %bitcast.20, ...), custom_call_target="tpu_custom_call" | custom-call | flops 5400000000 | bytes 1 | tf_op jit(solution)/shard_map/pallas_call | solution.py:202
  99.1 2.6 %collective-permute-done.15.rest_2_ = f32[8,24,128]{2,1,0:T(8,128)S(1)} collective-permute-done((f32[8,24,128]{2,1,0:T(8,128)S(1)}, f32[8,24,128]{2,1,0:T(8,128)S(1)}, u32[]{:S(2)}, u32[]{:S(2)}) %collective-permute-start.15) | collective-permute-done | bytes 98336 | tf_op jit(solution)/shard_map/ppermute | solution.py:790
  101.7 1.5 %collective-permute-done.16.rest_3_ = f32[8,24,128]{2,1,0:T(8,128)S(1)} collective-permute-done((f32[8,24,128]{2,1,0:T(8,128)S(1)}, f32[8,24,128]{2,1,0:T(8,128)S(1)}, u32[]{:S(2)}, u32[]{:S(2)}) %collective-permute-start.16) | collective-permute-done | bytes 98336 | tf_op jit(solution)/shard_map/ppermute | solution.py:790
  103.2 1.3 shard_map.105
  104.6 14.9 %all_to_all.22 = f32[32,24,128]{2,1,0:T(8,128)S(1)} all-to-all(f32[32,24,128]{2,1,0:T(8,128)S(1)} %shard_map.105), channel_id=1, replica_groups=mesh['lat'=8,'lon'=4] {'lat','lon'}, dimensions={0} | all-to-all | bytes 786432 | tf_op jit(solution)/shard_map/all_to_all | solution.py:894
  119.5 2.7 %shard_map.106 = f32[8,4,24,128]{3,2,1,0:T(8,128)S(1)} custom-call(bf16[8,256,256]{2,1,0:T(8,128)(2,1)S(1)} %get-tuple-element.73.high_ref, bf16[8,256,256]{2,1,0:T(8,128)(2,1)S(1)} %get-tuple-element.74.low_ref, f32[2,1024,128]{2,1,0:T(8,128)S(1)} %shard_map.100.green_ref, f32[8,4,24,128]{3,2,1,0:T(8,128)S(1)} %bitcast.13), custom_call_target="tpu_custom_call" | custom-call | flops 4000000000 | bytes 1 | tf_op jit(solution)/shard_map/pallas_call | solution.py:202
  122.1 15.6 %all_to_all.23.x_ref = f32[32,24,128]{2,1,0:T(8,128)S(1)} all-to-all(f32[32,24,128]{2,1,0:T(8,128)S(1)} %bitcast.14), channel_id=1, replica_groups=mesh['lat'=8,'lon'=4] {'lat','lon'}, dimensions={0} | all-to-all | bytes 786432 | tf_op jit(solution)/shard_map/all_to_all | solution.py:907
  137.8 1.4 shard_map.107
  139.2 1.3 collective-permute-start.17
  140.4 1.2 collective-permute-start.18
  142.1 4.2 %collective-permute-done.18.rest_2_ = f32[192,128]{1,0:T(8,128)S(1)} collective-permute-done((f32[192,128]{1,0:T(8,128)S(1)}, f32[192,128]{1,0:T(8,128)S(1)}, u32[]{:S(2)}, u32[]{:S(2)}) %collective-permute-start.18) | collective-permute-done | bytes 98336 | tf_op jit(solution)/shard_map/ppermute | solution.py:790
  146.9 1.3 shard_map.108
  (51 shorter events, 9.4 us)
Async XLA Ops:
  0.6 1.3 copy-start.6
  0.6 1.3 copy-start.7
  0.7 1.3 copy-start.1
  0.7 1.3 copy-start
  2.0 1.0 copy-start.5
  3.3 12.9 %collective-permute-start.4 = (f32[32,1024]{1,0:T(8,128)S(1)}, f32[32,1024]{1,0:T(8,128)S(1)}, u32[]{:S(2)}, u32[]{:S(2)}) collective-permute-start(f32[32,1024]{1,0:T(8,128)S(1)} %reshape.47), channel_id=1, source_target_pairs={{0,24},{4,28},{8,16},{12,20},{16,8},{20,12},{24,0},{28,4},{1,25},{... | collective-permute-start | bytes 393224 | tf_op jit(solution)/shard_map/ppermute | solution.py:827
  7.5 10.7 %collective-permute-start.3 = (f32[32,1024]{1,0:T(8,128)S(1)}, f32[32,1024]{1,0:T(8,128)S(1)}, u32[]{:S(2)}, u32[]{:S(2)}) collective-permute-start(f32[32,1024]{1,0:T(8,128)S(1)} %reshape.47), channel_id=1, source_target_pairs={{0,16},{4,20},{8,24},{12,28},{16,0},{20,4},{24,8},{28,12},{1,17},{... | collective-permute-start | bytes 393224 | tf_op jit(solution)/shard_map/ppermute | solution.py:827
  7.5 10.7 %collective-permute-start.2 = (f32[32,1024]{1,0:T(8,128)S(1)}, f32[32,1024]{1,0:T(8,128)S(1)}, u32[]{:S(2)}, u32[]{:S(2)}) collective-permute-start(f32[32,1024]{1,0:T(8,128)S(1)} %reshape.47), channel_id=1, source_target_pairs={{0,8},{4,12},{8,0},{12,4},{16,24},{20,28},{24,16},{28,20},{1,9},{5... | collective-permute-start | bytes 393224 | tf_op jit(solution)/shard_map/ppermute | solution.py:827
  7.8 10.3 %collective-permute-start.1 = (f32[520,128]{1,0:T(8,128)S(1)}, f32[520,128]{1,0:T(8,128)S(1)}, u32[]{:S(2)}, u32[]{:S(2)}) collective-permute-start(f32[520,128]{1,0:T(8,128)S(1)} %bitcast.22), channel_id=1, source_target_pairs={{4,0},{8,4},{12,8},{16,12},{20,16},{24,20},{28,24},{5,1},{9,5},{13... | collective-permute-start | bytes 798728 | tf_op jit(solution)/shard_map/ppermute | solution.py:820
  9.1 14.7 %collective-permute-start = (f32[520,128]{1,0:T(8,128)S(1)}, f32[520,128]{1,0:T(8,128)S(1)}, u32[]{:S(2)}, u32[]{:S(2)}) collective-permute-start(f32[520,128]{1,0:T(8,128)S(1)} %bitcast.21), channel_id=1, source_target_pairs={{0,4},{4,8},{8,12},{12,16},{16,20},{20,24},{24,28},{1,5},{5,9},{9,... | collective-permute-start | bytes 798728 | tf_op jit(solution)/shard_map/ppermute | solution.py:819
  23.9 7.6 %copy-start.2 = (f32[4]{0:T(128)S(1)}, f32[4]{0:T(128)}, u32[]{:S(2)}) copy-start(f32[4]{0:T(128)} %shear_ref.1) | copy-start | bytes 52
  23.9 7.6 %copy-start.3 = (f32[4]{0:T(128)S(1)}, f32[4]{0:T(128)}, u32[]{:S(2)}) copy-start(f32[4]{0:T(128)} %restoring_ref.1) | copy-start | bytes 52
  23.9 7.6 %copy-start.4 = (f32[4]{0:T(128)S(1)}, f32[4]{0:T(128)}, u32[]{:S(2)}) copy-start(f32[4]{0:T(128)} %contrast_ref.3) | copy-start | bytes 52
  25.2 4.7 %collective-permute-start.5 = (f32[168,128]{1,0:T(8,128)S(1)}, f32[168,128]{1,0:T(8,128)S(1)}, u32[]{:S(2)}, u32[]{:S(2)}) collective-permute-start(f32[168,128]{1,0:T(8,128)S(1)} %get-tuple-element.65), channel_id=1, source_target_pairs={{0,1},{1,2},{2,3},{3,0},{4,5},{5,6},{6,7},{7,4},{8,9},{9,10},{10,1... | collective-permute-start | bytes 258056 | tf_op jit(solution)/shard_map/ppermute | solution.py:851
  27.5 3.9 %collective-permute-start.6 = (f32[168,128]{1,0:T(8,128)S(1)}, f32[168,128]{1,0:T(8,128)S(1)}, u32[]{:S(2)}, u32[]{:S(2)}) collective-permute-start(f32[168,128]{1,0:T(8,128)S(1)} %get-tuple-element.66), channel_id=1, source_target_pairs={{1,0},{2,1},{3,2},{0,3},{5,4},{6,5},{7,6},{4,7},{9,8},{10,9},{11,1... | collective-permute-start | bytes 258056 | tf_op jit(solution)/shard_map/ppermute | solution.py:852
  27.6 13.9 %collective-permute-start.10 = (f32[128,1024]{1,0:T(8,128)S(1)}, f32[128,1024]{1,0:T(8,128)S(1)}, u32[]{:S(2)}, u32[]{:S(2)}) collective-permute-start(f32[128,1024]{1,0:T(8,128)S(1)} %constant_dynamic-update-slice_fusion.near_ref), channel_id=1, source_target_pairs={{0,4},{4,0},{8,12},{12,8},{16,20},{20,16},{24,28},{28,24},{1,5},{5... | collective-permute-start | bytes 1572872 | tf_op jit(solution)/shard_map/ppermute | solution.py:827
  35.9 6.6 %collective-permute-start.7 = (f32[8,24,128]{2,1,0:T(8,128)S(1)}, f32[8,24,128]{2,1,0:T(8,128)S(1)}, u32[]{:S(2)}, u32[]{:S(2)}) collective-permute-start(f32[8,24,128]{2,1,0:T(8,128)S(1)} %get-tuple-element.76), channel_id=1, source_target_pairs={{0,1},{1,2},{2,3},{3,0},{4,5},{5,6},{6,7},{7,4},{8,9},{9,10},{10,1... | collective-permute-start | bytes 294920 | tf_op jit(solution)/shard_map/ppermute | solution.py:790
  36.4 6.1 %collective-permute-start.8 = (f32[8,24,128]{2,1,0:T(8,128)S(1)}, f32[8,24,128]{2,1,0:T(8,128)S(1)}, u32[]{:S(2)}, u32[]{:S(2)}) collective-permute-start(f32[8,24,128]{2,1,0:T(8,128)S(1)} %get-tuple-element.77), channel_id=1, source_target_pairs={{0,2},{1,3},{2,0},{3,1},{4,6},{5,7},{6,4},{7,5},{8,10},{9,11},{10,... | collective-permute-start | bytes 294920 | tf_op jit(solution)/shard_map/ppermute | solution.py:790
  36.7 5.8 %collective-permute-start.9 = (f32[8,24,128]{2,1,0:T(8,128)S(1)}, f32[8,24,128]{2,1,0:T(8,128)S(1)}, u32[]{:S(2)}, u32[]{:S(2)}) collective-permute-start(f32[8,24,128]{2,1,0:T(8,128)S(1)} %get-tuple-element.78), channel_id=1, source_target_pairs={{0,3},{1,0},{2,1},{3,2},{4,7},{5,4},{6,5},{7,6},{8,11},{9,8},{10,9... | collective-permute-start | bytes 294920 | tf_op jit(solution)/shard_map/ppermute | solution.py:790
  84.1 3.9 %collective-permute-start.11 = (f32[288,128]{1,0:T(8,128)S(1)}, f32[288,128]{1,0:T(8,128)S(1)}, u32[]{:S(2)}, u32[]{:S(2)}) collective-permute-start(f32[288,128]{1,0:T(8,128)S(1)} %get-tuple-element.88), channel_id=1, source_target_pairs={{0,1},{1,2},{2,3},{3,0},{4,5},{5,6},{6,7},{7,4},{8,9},{9,10},{10,1... | collective-permute-start | bytes 442376 | tf_op jit(solution)/shard_map/ppermute | solution.py:790
  85.3 7.5 %collective-permute-start.12 = (f32[288,128]{1,0:T(8,128)S(1)}, f32[288,128]{1,0:T(8,128)S(1)}, u32[]{:S(2)}, u32[]{:S(2)}) collective-permute-start(f32[288,128]{1,0:T(8,128)S(1)} %get-tuple-element.89), channel_id=1, source_target_pairs={{0,2},{1,3},{2,0},{3,1},{4,6},{5,7},{6,4},{7,5},{8,10},{9,11},{10,... | collective-permute-start | bytes 442376 | tf_op jit(solution)/shard_map/ppermute | solution.py:790
  86.1 7.3 %collective-permute-start.13 = (f32[288,128]{1,0:T(8,128)S(1)}, f32[288,128]{1,0:T(8,128)S(1)}, u32[]{:S(2)}, u32[]{:S(2)}) collective-permute-start(f32[288,128]{1,0:T(8,128)S(1)} %get-tuple-element.90), channel_id=1, source_target_pairs={{0,3},{1,0},{2,1},{3,2},{4,7},{5,4},{6,5},{7,6},{8,11},{9,8},{10,9... | collective-permute-start | bytes 442376 | tf_op jit(solution)/shard_map/ppermute | solution.py:790
  97.4 1.7 %collective-permute-start.14 = (f32[8,24,128]{2,1,0:T(8,128)S(1)}, f32[8,24,128]{2,1,0:T(8,128)S(1)}, u32[]{:S(2)}, u32[]{:S(2)}) collective-permute-start(f32[8,24,128]{2,1,0:T(8,128)S(1)} %get-tuple-element.93), channel_id=1, source_target_pairs={{0,1},{1,2},{2,3},{3,0},{4,5},{5,6},{6,7},{7,4},{8,9},{9,10},{10,1... | collective-permute-start | bytes 294920 | tf_op jit(solution)/shard_map/ppermute | solution.py:790
  97.4 4.3 %collective-permute-start.15 = (f32[8,24,128]{2,1,0:T(8,128)S(1)}, f32[8,24,128]{2,1,0:T(8,128)S(1)}, u32[]{:S(2)}, u32[]{:S(2)}) collective-permute-start(f32[8,24,128]{2,1,0:T(8,128)S(1)} %get-tuple-element.94), channel_id=1, source_target_pairs={{0,2},{1,3},{2,0},{3,1},{4,6},{5,7},{6,4},{7,5},{8,10},{9,11},{10,... | collective-permute-start | bytes 294920 | tf_op jit(solution)/shard_map/ppermute | solution.py:790
  98.2 5.1 %collective-permute-start.16 = (f32[8,24,128]{2,1,0:T(8,128)S(1)}, f32[8,24,128]{2,1,0:T(8,128)S(1)}, u32[]{:S(2)}, u32[]{:S(2)}) collective-permute-start(f32[8,24,128]{2,1,0:T(8,128)S(1)} %get-tuple-element.95), channel_id=1, source_target_pairs={{0,3},{1,0},{2,1},{3,2},{4,7},{5,4},{6,5},{7,6},{8,11},{9,8},{10,9... | collective-permute-start | bytes 294920 | tf_op jit(solution)/shard_map/ppermute | solution.py:790
  139.2 2.9 %collective-permute-start.17 = (f32[192,128]{1,0:T(8,128)S(1)}, f32[192,128]{1,0:T(8,128)S(1)}, u32[]{:S(2)}, u32[]{:S(2)}) collective-permute-start(f32[192,128]{1,0:T(8,128)S(1)} %get-tuple-element.97), channel_id=1, source_target_pairs={{0,1},{1,2},{2,3},{3,0},{4,5},{5,6},{6,7},{7,4},{8,9},{9,10},{10,1... | collective-permute-start | bytes 294920 | tf_op jit(solution)/shard_map/ppermute | solution.py:790
  140.4 5.8 %collective-permute-start.18 = (f32[192,128]{1,0:T(8,128)S(1)}, f32[192,128]{1,0:T(8,128)S(1)}, u32[]{:S(2)}, u32[]{:S(2)}) collective-permute-start(f32[192,128]{1,0:T(8,128)S(1)} %get-tuple-element.98), channel_id=1, source_target_pairs={{0,2},{1,3},{2,0},{3,1},{4,6},{5,7},{6,4},{7,5},{8,10},{9,11},{10,... | collective-permute-start | bytes 294920 | tf_op jit(solution)/shard_map/ppermute | solution.py:790
  141.7 5.2 %collective-permute-start.19 = (f32[192,128]{1,0:T(8,128)S(1)}, f32[192,128]{1,0:T(8,128)S(1)}, u32[]{:S(2)}, u32[]{:S(2)}) collective-permute-start(f32[192,128]{1,0:T(8,128)S(1)} %get-tuple-element.99), channel_id=1, source_target_pairs={{0,3},{1,0},{2,1},{3,2},{4,7},{5,4},{6,5},{7,6},{8,11},{9,8},{10,9... | collective-permute-start | bytes 294920 | tf_op jit(solution)/shard_map/ppermute | solution.py:790

commit v8 on v7

--- a/solution.py
+++ b/solution.py
@@ -422,7 +422,7 @@
         return carry
 
     margin(above, 0)
-    lax.fori_loop(0, rows, inner, 0, unroll=8)
+    lax.fori_loop(0, rows, inner, 0, unroll=True)
     margin(below, rows + DEEP)
 
 
@@ -599,7 +599,7 @@
 ):
     parts, rest = rest[:lon_count], rest[lon_count:]
     pieces, rest = rest[:lon_count], rest[lon_count:]
-    field_hbm, middle, last, f_scr, pot, edge, d_scr, near, field_out, sem = rest
+    field_out, middle, last, f_scr, pot, edge, d_scr, near = rest
     layers, rows, _ = field_out.shape
     steps = u_ref.shape[0]
     tall = rows + 2 * SHALLOW
@@ -629,15 +629,12 @@
                 f_scr[t, c, at, :] = b_ref[t, c, deep, :] * value
         return carry
 
-    lax.fori_loop(0, tall, force, 0, unroll=8)
+    lax.fori_loop(0, tall, force, 0, unroll=True)
     lon_neighbours(near)
     run_sweeps(u_ref, DEEP - SHALLOW, a_ref, f_scr, (middle, last), near)
     for k in range(layers):
         field_out[k] = layer_of(last, k, SHALLOW, rows)
-    copy = pltpu.make_async_copy(field_out, field_hbm, sem)
-    copy.start()
     put_density(mat_ref, contrast_ref, lambda k: field_out[k], index_ref, d_scr, pieces)
-    copy.wait()
 
 
 def swap_chunks(blocks, chunk):
@@ -928,11 +925,8 @@
                     pltpu.VMEM((tall * SUB, LANES), jnp.float32),
                     flat,
                     near_shape,
-                    pltpu.VMEM((layers, rows, cols), jnp.float32),
-                    pltpu.SemaphoreType.DMA,
                 ],
                 smem=(0, 1),
-                hbm=(lon_count,),
             )(index, contrast, own[1], *state, *parts)
             pieces, field = out[:lon_count], out[lon_count]
     potential = call(

time: 149 us -> 148 us (level)
  transfers between devices with their start and end apart: 20 -> 20, of which waited for: 13 -> 13; matrix products, arithmetic and copies ran while one was open for 0% -> 0% of each run, Pallas kernels for 6% -> 5%
where the time goes in v8:
time: 148 us; the launch traced here: 147 us
  blocking collectives  66.2 us (45%)
  waiting for transfers between devices  31 us (21%)
  Pallas kernels  26 us (18%)
  starting transfers between devices  21.7 us (15%)
    all_to_all x2, blocking collectives, on_device(): lax.all_to_all(synth.reshape(owners, rows + 2 * margin, LANES), BOTH, 0,...  34.1 us
    all_to_all x2, blocking collectives, on_device(): spectrum = lax.all_to_all(spectrum, BOTH, 0, 0, tiled=True)  32.1 us
    pallas_call x14, Pallas kernels, run(): pl.pallas_call(kernel, out_shape=outs, in_specs=[place(i, smem, far) for...  26 us
    ppermute x12, waiting for transfers between devices, exchange(): lax.ppermute(pieces[s], 'lon', [(i, (i + s) % count) for i in range(count)])  16.8 us
    ppermute x12, starting transfers between devices, exchange(): lax.ppermute(pieces[s], 'lon', [(i, (i + s) % count) for i in range(count)])  7.21 us
    ppermute x4, waiting for transfers between devices, partner(): return lax.ppermute(x, 'lat', [(i, i ^ step) for i in range(lat_count)])  6.94 us
    ppermute x4, starting transfers between devices, partner(): return lax.ppermute(x, 'lat', [(i, i ^ step) for i in range(lat_count)])  6.85 us
    ppermute x1, waiting for transfers between devices, on_device(): lax.ppermute(last, 'lat', [(i, i + 1) for i in range(lat_count - 1)])  5.72 us
  transfers between devices with their start and end apart: 20, of which 13 were waited for; matrix products, arithmetic and copies ran while one was open for 0% of the time, Pallas kernels for 5%

profile of v8, /device:TPU:1, one launch (start us, length us, event | category | flops | bytes accessed | tf_op | source)
XLA Modules:
  0.0 147.4 jit_solution(5667734854857157526)
XLA Ops:
  0.7 1.2 shard_map.96
  3.3 4.2 %collective-permute-start.4 = (f32[32,1024]{1,0:T(8,128)S(1)}, f32[32,1024]{1,0:T(8,128)S(1)}, u32[]{:S(2)}, u32[]{:S(2)}) collective-permute-start(f32[32,1024]{1,0:T(8,128)S(1)} %reshape.47), channel_id=1, source_target_pairs={{0,24},{4,28},{8,16},{12,20},{16,8},{20,12},{24,0},{28,4},{1,25},{... | collective-permute-start | bytes 393224 | tf_op jit(solution)/shard_map/ppermute | solution.py:824
  7.8 1.3 collective-permute-start.1
  9.1 4.0 %collective-permute-start = (f32[520,128]{1,0:T(8,128)S(1)}, f32[520,128]{1,0:T(8,128)S(1)}, u32[]{:S(2)}, u32[]{:S(2)}) collective-permute-start(f32[520,128]{1,0:T(8,128)S(1)} %bitcast.21), channel_id=1, source_target_pairs={{0,4},{4,8},{8,12},{12,16},{16,20},{20,24},{24,28},{1,5},{5,9},{9,... | collective-permute-start | bytes 798728 | tf_op jit(solution)/shard_map/ppermute | solution.py:816
  13.1 2.8 %shard_map.97 = (bf16[8,256,256]{2,1,0:T(8,128)(2,1)S(1)}, bf16[8,256,256]{2,1,0:T(8,128)(2,1)S(1)}) custom-call(s32[1]{0:T(128)} %bitcast.6.index_ref), custom_call_target="tpu_custom_call" | custom-call | flops 2900000000 | bytes 1 | tf_op jit(solution)/shard_map/pallas_call | solution.py:202
  16.1 2.0 %collective-permute-done.3 = f32[32,1024]{1,0:T(8,128)S(1)} collective-permute-done((f32[32,1024]{1,0:T(8,128)S(1)}, f32[32,1024]{1,0:T(8,128)S(1)}, u32[]{:S(2)}, u32[]{:S(2)}) %collective-permute-start.3) | collective-permute-done | bytes 131104 | tf_op jit(solution)/shard_map/ppermute | solution.py:824
  18.2 5.7 %collective-permute-done.above_ref = f32[520,128]{1,0:T(8,128)S(1)} collective-permute-done((f32[520,128]{1,0:T(8,128)S(1)}, f32[520,128]{1,0:T(8,128)S(1)}, u32[]{:S(2)}, u32[]{:S(2)}) %collective-permute-start) | collective-permute-done | bytes 266272 | tf_op jit(solution)/shard_map/ppermute | solution.py:816
  24.7 2.3 %collective-permute-start.5 = (f32[168,128]{1,0:T(8,128)S(1)}, f32[168,128]{1,0:T(8,128)S(1)}, u32[]{:S(2)}, u32[]{:S(2)}) collective-permute-start(f32[168,128]{1,0:T(8,128)S(1)} %get-tuple-element.65), channel_id=1, source_target_pairs={{0,1},{1,2},{2,3},{3,0},{4,5},{5,6},{6,7},{7,4},{8,9},{9,10},{10,1... | collective-permute-start | bytes 258056 | tf_op jit(solution)/shard_map/ppermute | solution.py:848
  27.1 2.3 %collective-permute-start.10 = (f32[128,1024]{1,0:T(8,128)S(1)}, f32[128,1024]{1,0:T(8,128)S(1)}, u32[]{:S(2)}, u32[]{:S(2)}) collective-permute-start(f32[128,1024]{1,0:T(8,128)S(1)} %constant_dynamic-update-slice_fusion.near_ref), channel_id=1, source_target_pairs={{0,4},{4,0},{8,12},{12,8},{16,20},{20,16},{24,28},{28,24},{1,5},{5... | collective-permute-start | bytes 1572872 | tf_op jit(solution)/shard_map/ppermute | solution.py:824
  29.4 1.6 %collective-permute-done.6.right_ref = f32[168,128]{1,0:T(8,128)S(1)} collective-permute-done((f32[168,128]{1,0:T(8,128)S(1)}, f32[168,128]{1,0:T(8,128)S(1)}, u32[]{:S(2)}, u32[]{:S(2)}) %collective-permute-start.6) | collective-permute-done | bytes 86048 | tf_op jit(solution)/shard_map/ppermute | solution.py:849
  31.0 3.9 %shard_map.99 = (f32[8,24,128]{2,1,0:T(8,128)S(1)}, f32[8,24,128]{2,1,0:T(8,128)S(1)}, f32[8,24,128]{2,1,0:T(8,128)S(1)}, f32[8,24,128]{2,1,0:T(8,128)S(1)}, f32...) custom-call(s32[2]{0:T(128)S(1)} %pad_add_fusion.index_ref, ...), custom_call_target="tpu_custom_call" | custom-call | flops 6600000000 | bytes 1 | tf_op jit(solution)/shard_map/pallas_call | solution.py:202
  36.1 4.9 %collective-permute-done.10.far_ref = f32[128,1024]{1,0:T(8,128)S(1)} collective-permute-done((f32[128,1024]{1,0:T(8,128)S(1)}, f32[128,1024]{1,0:T(8,128)S(1)}, u32[]{:S(2)}, u32[]{:S(2)}) %collective-permute-start.10) | collective-permute-done | bytes 524320 | tf_op jit(solution)/shard_map/ppermute | solution.py:824
  42.1 1.3 shard_map.101
  43.5 17.2 %all_to_all.20 = f32[32,24,128]{2,1,0:T(8,128)S(1)} all-to-all(f32[32,24,128]{2,1,0:T(8,128)S(1)} %shard_map.101), channel_id=1, replica_groups=mesh['lat'=8,'lon'=4] {'lat','lon'}, dimensions={0} | all-to-all | bytes 786432 | tf_op jit(solution)/shard_map/all_to_all | solution.py:891
  60.7 2.7 %shard_map.102 = f32[8,4,32,128]{3,2,1,0:T(8,128)S(1)} custom-call(bf16[8,256,256]{2,1,0:T(8,128)(2,1)S(1)} %get-tuple-element.73.high_ref, bf16[8,256,256]{2,1,0:T(8,128)(2,1)S(1)} %get-tuple-element.74.low_ref, f32[2,1024,128]{2,1,0:T(8,128)S(1)} %shard_map.100.green_ref, f32[8,4,24,128]{3,2,1,0:T(8,128)S(1)} %bitcast.15), custom_call_target="tpu_custom_call" | custom-call | flops 4000000000 | bytes 1 | tf_op jit(solution)/shard_map/pallas_call | solution.py:202
  63.4 18.5 %all_to_all.21.x_ref = f32[32,32,128]{2,1,0:T(8,128)S(1)} all-to-all(f32[32,32,128]{2,1,0:T(8,128)S(1)} %bitcast.12), channel_id=1, replica_groups=mesh['lat'=8,'lon'=4] {'lat','lon'}, dimensions={0} | all-to-all | bytes 1048576 | tf_op jit(solution)/shard_map/all_to_all | solution.py:904
  81.8 1.8 %shard_map.103 = (f32[288,128]{1,0:T(8,128)S(1)}, f32[288,128]{1,0:T(8,128)S(1)}, f32[288,128]{1,0:T(8,128)S(1)}, f32[288,128]{1,0:T(8,128)S(1)}) custom-call(s32[2]{0:T(128)S(1)} %pad_add_fusion.index_ref, bf16[512,512]{1,0:T(8,128)(2,1)S(1)} %get-tuple-element.71.high_ref, bf16[512,512]{1,0:T(8,128)(2,1)S(1)} %get-tuple-element.72.low_ref, ...), custom_call_target="tpu_custom_call" | custom-call | flops 2000000000 | bytes 1 | tf_op jit(solution)/shard_map/pallas_call | solution.py:202
  83.6 1.2 collective-permute-start.11
  85.6 1.9 %collective-permute-done.11.rest_1_ = f32[288,128]{1,0:T(8,128)S(1)} collective-permute-done((f32[288,128]{1,0:T(8,128)S(1)}, f32[288,128]{1,0:T(8,128)S(1)}, u32[]{:S(2)}, u32[]{:S(2)}) %collective-permute-start.11) | collective-permute-done | bytes 147488 | tf_op jit(solution)/shard_map/ppermute | solution.py:787
  87.5 4.8 %collective-permute-done.12.rest_2_ = f32[288,128]{1,0:T(8,128)S(1)} collective-permute-done((f32[288,128]{1,0:T(8,128)S(1)}, f32[288,128]{1,0:T(8,128)S(1)}, u32[]{:S(2)}, u32[]{:S(2)}) %collective-permute-start.12) | collective-permute-done | bytes 147488 | tf_op jit(solution)/shard_map/ppermute | solution.py:787
  92.9 3.7 %shard_map.104 = (f32[8,24,128]{2,1,0:T(8,128)S(1)}, f32[8,24,128]{2,1,0:T(8,128)S(1)}, f32[8,24,128]{2,1,0:T(8,128)S(1)}, f32[8,24,128]{2,1,0:T(8,128)S(1)}, f32[32,24,128]{2,1,0:T(8,128)}) custom-call(s32[2]{0:T(128)S(1)} %pad_add_fusion.index_ref, f32[4]{0:T(128)S(1)} %copy-done.4, s32[768,128]{1,0:T(8,128)S(1)} %bitcast.20, ...), custom_call_target="tpu_custom_call" | custom-call | flops 5400000000 | bytes 1 | tf_op jit(solution)/shard_map/pallas_call | solution.py:202
  98.2 2.7 %collective-permute-done.15.rest_2_ = f32[8,24,128]{2,1,0:T(8,128)S(1)} collective-permute-done((f32[8,24,128]{2,1,0:T(8,128)S(1)}, f32[8,24,128]{2,1,0:T(8,128)S(1)}, u32[]{:S(2)}, u32[]{:S(2)}) %collective-permute-start.15) | collective-permute-done | bytes 98336 | tf_op jit(solution)/shard_map/ppermute | solution.py:787
  100.9 1.5 %collective-permute-done.16.rest_3_ = f32[8,24,128]{2,1,0:T(8,128)S(1)} collective-permute-done((f32[8,24,128]{2,1,0:T(8,128)S(1)}, f32[8,24,128]{2,1,0:T(8,128)S(1)}, u32[]{:S(2)}, u32[]{:S(2)}) %collective-permute-start.16) | collective-permute-done | bytes 98336 | tf_op jit(solution)/shard_map/ppermute | solution.py:787
  102.4 1.3 shard_map.105
  103.7 14.8 %all_to_all.22 = f32[32,24,128]{2,1,0:T(8,128)S(1)} all-to-all(f32[32,24,128]{2,1,0:T(8,128)S(1)} %shard_map.105), channel_id=1, replica_groups=mesh['lat'=8,'lon'=4] {'lat','lon'}, dimensions={0} | all-to-all | bytes 786432 | tf_op jit(solution)/shard_map/all_to_all | solution.py:891
  118.6 2.7 %shard_map.106 = f32[8,4,24,128]{3,2,1,0:T(8,128)S(1)} custom-call(bf16[8,256,256]{2,1,0:T(8,128)(2,1)S(1)} %get-tuple-element.73.high_ref, bf16[8,256,256]{2,1,0:T(8,128)(2,1)S(1)} %get-tuple-element.74.low_ref, f32[2,1024,128]{2,1,0:T(8,128)S(1)} %shard_map.100.green_ref, f32[8,4,24,128]{3,2,1,0:T(8,128)S(1)} %bitcast.13), custom_call_target="tpu_custom_call" | custom-call | flops 4000000000 | bytes 1 | tf_op jit(solution)/shard_map/pallas_call | solution.py:202
  121.2 15.6 %all_to_all.23.x_ref = f32[32,24,128]{2,1,0:T(8,128)S(1)} all-to-all(f32[32,24,128]{2,1,0:T(8,128)S(1)} %bitcast.14), channel_id=1, replica_groups=mesh['lat'=8,'lon'=4] {'lat','lon'}, dimensions={0} | all-to-all | bytes 786432 | tf_op jit(solution)/shard_map/all_to_all | solution.py:904
  136.9 1.4 shard_map.107
  138.3 1.3 collective-permute-start.17
  139.5 1.3 collective-permute-start.18
  141.2 4.2 %collective-permute-done.18.rest_2_ = f32[192,128]{1,0:T(8,128)S(1)} collective-permute-done((f32[192,128]{1,0:T(8,128)S(1)}, f32[192,128]{1,0:T(8,128)S(1)}, u32[]{:S(2)}, u32[]{:S(2)}) %collective-permute-start.18) | collective-permute-done | bytes 98336 | tf_op jit(solution)/shard_map/ppermute | solution.py:787
  145.9 1.3 shard_map.108
  (51 shorter events, 9.0 us)
Async XLA Ops:
  0.6 1.3 copy-start.6
  0.6 1.3 copy-start.7
  0.7 1.3 copy-start.1
  0.7 1.3 copy-start
  2.0 1.0 copy-start.5
  3.3 12.9 %collective-permute-start.4 = (f32[32,1024]{1,0:T(8,128)S(1)}, f32[32,1024]{1,0:T(8,128)S(1)}, u32[]{:S(2)}, u32[]{:S(2)}) collective-permute-start(f32[32,1024]{1,0:T(8,128)S(1)} %reshape.47), channel_id=1, source_target_pairs={{0,24},{4,28},{8,16},{12,20},{16,8},{20,12},{24,0},{28,4},{1,25},{... | collective-permute-start | bytes 393224 | tf_op jit(solution)/shard_map/ppermute | solution.py:824
  7.5 10.7 %collective-permute-start.3 = (f32[32,1024]{1,0:T(8,128)S(1)}, f32[32,1024]{1,0:T(8,128)S(1)}, u32[]{:S(2)}, u32[]{:S(2)}) collective-permute-start(f32[32,1024]{1,0:T(8,128)S(1)} %reshape.47), channel_id=1, source_target_pairs={{0,16},{4,20},{8,24},{12,28},{16,0},{20,4},{24,8},{28,12},{1,17},{... | collective-permute-start | bytes 393224 | tf_op jit(solution)/shard_map/ppermute | solution.py:824
  7.5 10.7 %collective-permute-start.2 = (f32[32,1024]{1,0:T(8,128)S(1)}, f32[32,1024]{1,0:T(8,128)S(1)}, u32[]{:S(2)}, u32[]{:S(2)}) collective-permute-start(f32[32,1024]{1,0:T(8,128)S(1)} %reshape.47), channel_id=1, source_target_pairs={{0,8},{4,12},{8,0},{12,4},{16,24},{20,28},{24,16},{28,20},{1,9},{5... | collective-permute-start | bytes 393224 | tf_op jit(solution)/shard_map/ppermute | solution.py:824
  7.8 10.3 %collective-permute-start.1 = (f32[520,128]{1,0:T(8,128)S(1)}, f32[520,128]{1,0:T(8,128)S(1)}, u32[]{:S(2)}, u32[]{:S(2)}) collective-permute-start(f32[520,128]{1,0:T(8,128)S(1)} %bitcast.22), channel_id=1, source_target_pairs={{4,0},{8,4},{12,8},{16,12},{20,16},{24,20},{28,24},{5,1},{9,5},{13... | collective-permute-start | bytes 798728 | tf_op jit(solution)/shard_map/ppermute | solution.py:817
  9.1 14.7 %collective-permute-start = (f32[520,128]{1,0:T(8,128)S(1)}, f32[520,128]{1,0:T(8,128)S(1)}, u32[]{:S(2)}, u32[]{:S(2)}) collective-permute-start(f32[520,128]{1,0:T(8,128)S(1)} %bitcast.21), channel_id=1, source_target_pairs={{0,4},{4,8},{8,12},{12,16},{16,20},{20,24},{24,28},{1,5},{5,9},{9,... | collective-permute-start | bytes 798728 | tf_op jit(solution)/shard_map/ppermute | solution.py:816
  23.9 7.1 %copy-start.2 = (f32[4]{0:T(128)S(1)}, f32[4]{0:T(128)}, u32[]{:S(2)}) copy-start(f32[4]{0:T(128)} %shear_ref.1) | copy-start | bytes 52
  23.9 7.1 %copy-start.3 = (f32[4]{0:T(128)S(1)}, f32[4]{0:T(128)}, u32[]{:S(2)}) copy-start(f32[4]{0:T(128)} %restoring_ref.1) | copy-start | bytes 52
  23.9 7.1 %copy-start.4 = (f32[4]{0:T(128)S(1)}, f32[4]{0:T(128)}, u32[]{:S(2)}) copy-start(f32[4]{0:T(128)} %contrast_ref.3) | copy-start | bytes 52
  24.7 4.7 %collective-permute-start.5 = (f32[168,128]{1,0:T(8,128)S(1)}, f32[168,128]{1,0:T(8,128)S(1)}, u32[]{:S(2)}, u32[]{:S(2)}) collective-permute-start(f32[168,128]{1,0:T(8,128)S(1)} %get-tuple-element.65), channel_id=1, source_target_pairs={{0,1},{1,2},{2,3},{3,0},{4,5},{5,6},{6,7},{7,4},{8,9},{9,10},{10,1... | collective-permute-start | bytes 258056 | tf_op jit(solution)/shard_map/ppermute | solution.py:848
  27.1 3.9 %collective-permute-start.6 = (f32[168,128]{1,0:T(8,128)S(1)}, f32[168,128]{1,0:T(8,128)S(1)}, u32[]{:S(2)}, u32[]{:S(2)}) collective-permute-start(f32[168,128]{1,0:T(8,128)S(1)} %get-tuple-element.66), channel_id=1, source_target_pairs={{1,0},{2,1},{3,2},{0,3},{5,4},{6,5},{7,6},{4,7},{9,8},{10,9},{11,1... | collective-permute-start | bytes 258056 | tf_op jit(solution)/shard_map/ppermute | solution.py:849
  27.1 13.9 %collective-permute-start.10 = (f32[128,1024]{1,0:T(8,128)S(1)}, f32[128,1024]{1,0:T(8,128)S(1)}, u32[]{:S(2)}, u32[]{:S(2)}) collective-permute-start(f32[128,1024]{1,0:T(8,128)S(1)} %constant_dynamic-update-slice_fusion.near_ref), channel_id=1, source_target_pairs={{0,4},{4,0},{8,12},{12,8},{16,20},{20,16},{24,28},{28,24},{1,5},{5... | collective-permute-start | bytes 1572872 | tf_op jit(solution)/shard_map/ppermute | solution.py:824
  34.9 7.1 %collective-permute-start.7 = (f32[8,24,128]{2,1,0:T(8,128)S(1)}, f32[8,24,128]{2,1,0:T(8,128)S(1)}, u32[]{:S(2)}, u32[]{:S(2)}) collective-permute-start(f32[8,24,128]{2,1,0:T(8,128)S(1)} %get-tuple-element.76), channel_id=1, source_target_pairs={{0,1},{1,2},{2,3},{3,0},{4,5},{5,6},{6,7},{7,4},{8,9},{9,10},{10,1... | collective-permute-start | bytes 294920 | tf_op jit(solution)/shard_map/ppermute | solution.py:787
  35.4 6.6 %collective-permute-start.8 = (f32[8,24,128]{2,1,0:T(8,128)S(1)}, f32[8,24,128]{2,1,0:T(8,128)S(1)}, u32[]{:S(2)}, u32[]{:S(2)}) collective-permute-start(f32[8,24,128]{2,1,0:T(8,128)S(1)} %get-tuple-element.77), channel_id=1, source_target_pairs={{0,2},{1,3},{2,0},{3,1},{4,6},{5,7},{6,4},{7,5},{8,10},{9,11},{10,... | collective-permute-start | bytes 294920 | tf_op jit(solution)/shard_map/ppermute | solution.py:787
  35.7 6.3 %collective-permute-start.9 = (f32[8,24,128]{2,1,0:T(8,128)S(1)}, f32[8,24,128]{2,1,0:T(8,128)S(1)}, u32[]{:S(2)}, u32[]{:S(2)}) collective-permute-start(f32[8,24,128]{2,1,0:T(8,128)S(1)} %get-tuple-element.78), channel_id=1, source_target_pairs={{0,3},{1,0},{2,1},{3,2},{4,7},{5,4},{6,5},{7,6},{8,11},{9,8},{10,9... | collective-permute-start | bytes 294920 | tf_op jit(solution)/shard_map/ppermute | solution.py:787
  83.6 3.9 %collective-permute-start.11 = (f32[288,128]{1,0:T(8,128)S(1)}, f32[288,128]{1,0:T(8,128)S(1)}, u32[]{:S(2)}, u32[]{:S(2)}) collective-permute-start(f32[288,128]{1,0:T(8,128)S(1)} %get-tuple-element.88), channel_id=1, source_target_pairs={{0,1},{1,2},{2,3},{3,0},{4,5},{5,6},{6,7},{7,4},{8,9},{9,10},{10,1... | collective-permute-start | bytes 442376 | tf_op jit(solution)/shard_map/ppermute | solution.py:787
  84.8 7.5 %collective-permute-start.12 = (f32[288,128]{1,0:T(8,128)S(1)}, f32[288,128]{1,0:T(8,128)S(1)}, u32[]{:S(2)}, u32[]{:S(2)}) collective-permute-start(f32[288,128]{1,0:T(8,128)S(1)} %get-tuple-element.89), channel_id=1, source_target_pairs={{0,2},{1,3},{2,0},{3,1},{4,6},{5,7},{6,4},{7,5},{8,10},{9,11},{10,... | collective-permute-start | bytes 442376 | tf_op jit(solution)/shard_map/ppermute | solution.py:787
  85.6 7.3 %collective-permute-start.13 = (f32[288,128]{1,0:T(8,128)S(1)}, f32[288,128]{1,0:T(8,128)S(1)}, u32[]{:S(2)}, u32[]{:S(2)}) collective-permute-start(f32[288,128]{1,0:T(8,128)S(1)} %get-tuple-element.90), channel_id=1, source_target_pairs={{0,3},{1,0},{2,1},{3,2},{4,7},{5,4},{6,5},{7,6},{8,11},{9,8},{10,9... | collective-permute-start | bytes 442376 | tf_op jit(solution)/shard_map/ppermute | solution.py:787
  96.6 1.6 %collective-permute-start.14 = (f32[8,24,128]{2,1,0:T(8,128)S(1)}, f32[8,24,128]{2,1,0:T(8,128)S(1)}, u32[]{:S(2)}, u32[]{:S(2)}) collective-permute-start(f32[8,24,128]{2,1,0:T(8,128)S(1)} %get-tuple-element.93), channel_id=1, source_target_pairs={{0,1},{1,2},{2,3},{3,0},{4,5},{5,6},{6,7},{7,4},{8,9},{9,10},{10,1... | collective-permute-start | bytes 294920 | tf_op jit(solution)/shard_map/ppermute | solution.py:787
  96.6 4.3 %collective-permute-start.15 = (f32[8,24,128]{2,1,0:T(8,128)S(1)}, f32[8,24,128]{2,1,0:T(8,128)S(1)}, u32[]{:S(2)}, u32[]{:S(2)}) collective-permute-start(f32[8,24,128]{2,1,0:T(8,128)S(1)} %get-tuple-element.94), channel_id=1, source_target_pairs={{0,2},{1,3},{2,0},{3,1},{4,6},{5,7},{6,4},{7,5},{8,10},{9,11},{10,... | collective-permute-start | bytes 294920 | tf_op jit(solution)/shard_map/ppermute | solution.py:787
  97.2 5.2 %collective-permute-start.16 = (f32[8,24,128]{2,1,0:T(8,128)S(1)}, f32[8,24,128]{2,1,0:T(8,128)S(1)}, u32[]{:S(2)}, u32[]{:S(2)}) collective-permute-start(f32[8,24,128]{2,1,0:T(8,128)S(1)} %get-tuple-element.95), channel_id=1, source_target_pairs={{0,3},{1,0},{2,1},{3,2},{4,7},{5,4},{6,5},{7,6},{8,11},{9,8},{10,9... | collective-permute-start | bytes 294920 | tf_op jit(solution)/shard_map/ppermute | solution.py:787
  138.3 2.9 %collective-permute-start.17 = (f32[192,128]{1,0:T(8,128)S(1)}, f32[192,128]{1,0:T(8,128)S(1)}, u32[]{:S(2)}, u32[]{:S(2)}) collective-permute-start(f32[192,128]{1,0:T(8,128)S(1)} %get-tuple-element.97), channel_id=1, source_target_pairs={{0,1},{1,2},{2,3},{3,0},{4,5},{5,6},{6,7},{7,4},{8,9},{9,10},{10,1... | collective-permute-start | bytes 294920 | tf_op jit(solution)/shard_map/ppermute | solution.py:787
  139.5 5.8 %collective-permute-start.18 = (f32[192,128]{1,0:T(8,128)S(1)}, f32[192,128]{1,0:T(8,128)S(1)}, u32[]{:S(2)}, u32[]{:S(2)}) collective-permute-start(f32[192,128]{1,0:T(8,128)S(1)} %get-tuple-element.98), channel_id=1, source_target_pairs={{0,2},{1,3},{2,0},{3,1},{4,6},{5,7},{6,4},{7,5},{8,10},{9,11},{10,... | collective-permute-start | bytes 294920 | tf_op jit(solution)/shard_map/ppermute | solution.py:787
  140.8 5.2 %collective-permute-start.19 = (f32[192,128]{1,0:T(8,128)S(1)}, f32[192,128]{1,0:T(8,128)S(1)}, u32[]{:S(2)}, u32[]{:S(2)}) collective-permute-start(f32[192,128]{1,0:T(8,128)S(1)} %get-tuple-element.99), channel_id=1, source_target_pairs={{0,3},{1,0},{2,1},{3,2},{4,7},{5,4},{6,5},{7,6},{8,11},{9,8},{10,9... | collective-permute-start | bytes 294920 | tf_op jit(solution)/shard_map/ppermute | solution.py:787

commit v9 on v8

--- a/solution.py
+++ b/solution.py
@@ -371,7 +371,7 @@
 
 
 SUB = 8
-PARTS = 2
+PARTS = 1
 UNROLL = True
 
 
@@ -682,6 +682,12 @@
             o_ref[g * share + i] = blocks[i]
 
 
+def forward_and_turn_kernel(lon_count, scale, size, *refs):
+    *inputs, near_ref, far_ref, o_ref, green_ref, ordered = refs
+    turn_kernel(size, inputs[0], near_ref, far_ref, green_ref, ordered)
+    forward_kernel(lon_count, scale, *inputs, o_ref)
+
+
 def spectral_kernel(margin, high_ref, low_ref, green_ref, x_ref, o_ref, turned, coeffs, pots):
     share, degrees, width = high_ref.shape
     lat_count, lon_count, rows, _ = x_ref.shape
@@ -723,7 +729,7 @@
                 pots[c, pl.ds(pl.multiple_of((i * block + t) * size, size), live), :] = sums[t]
         return carry
 
-    lax.fori_loop(0, layers // block, targets, 0)
+    lax.fori_loop(0, layers // block, targets, 0, unroll=True)
     for m in range(share):
         x = [every(pots.at[skip[m] :], r, size, layers) for r in spots[m]]
         x = halves(jnp.concatenate(x, axis=0))
@@ -873,21 +879,25 @@
     for iteration in range(ITERS):
         margin = SHALLOW if iteration < ITERS - 1 else 0
         parts = exchange(pieces)
+        scale = 2.0 * math.pi / total_lon
         if iteration == 0:
-            turned_green = call(
-                functools.partial(turn_kernel, green.shape[0]),
-                f32(LMAX // LANES, layers * layers, LANES),
-                1.4,
+            spectrum, turned_green = call(
+                functools.partial(forward_and_turn_kernel, lon_count, scale, green.shape[0]),
+                (
+                    f32(owners, rows, LANES),
+                    f32(LMAX // LANES, layers * layers, LANES),
+                ),
+                3.0,
                 scratch=[pltpu.VMEM((LMAX, layers * layers), jnp.float32)],
                 smem=(0,),
-            )(index, near, far)
-            parts, turned_green = lax.optimization_barrier((parts, turned_green))
-        spectrum = call(
-            functools.partial(forward_kernel, lon_count, 2.0 * math.pi / total_lon),
-            f32(owners, rows, LANES),
-            2.0,
-            smem=(0,),
-        )(index, weight, *table, *parts)
+            )(index, weight, *table, *parts, near, far)
+        else:
+            spectrum = call(
+                functools.partial(forward_kernel, lon_count, scale),
+                f32(owners, rows, LANES),
+                2.0,
+                smem=(0,),
+            )(index, weight, *table, *parts)
         spectrum = lax.all_to_all(spectrum, BOTH, 0, 0, tiled=True)
         square = pltpu.VMEM((width // LANES, lon_count * LANES, LANES), jnp.float32)
         coeff_shape = pltpu.VMEM((LMAX // LANES, lon_count * LANES, LANES), jnp.float32)

time: 148 us -> 146 us (0.986)
  local copies, waits for them, and re-layouts: 1.37 us -> 3.31 us
  Pallas kernels: 26 us -> 24.1 us
  waiting for transfers between devices: 31 us -> 29.4 us
    ppermute x4, waiting for transfers between devices: 6.94 us -> 0.14 us  [partner(): return lax.ppermute(x, 'lat', [(i, i ^ step) for i in range(lat_count)])]
    ppermute x12, waiting for transfers between devices: 16.8 us -> 21.9 us  [exchange(): lax.ppermute(pieces[s], 'lon', [(i, (i + s) % count) for i in range(count)])]
    unnamed x19 -> x27, local copies, waits for them, and re-layouts: 1.05 us -> 3 us
    pallas_call x14 -> x13, Pallas kernels: 26 us -> 24.1 us  [run(): pl.pallas_call(kernel, out_shape=outs, in_specs=[place(i, smem, far) for...]
  transfers between devices with their start and end apart: 20 -> 20, of which waited for: 13 -> 15; matrix products, arithmetic and copies ran while one was open for 0% -> 0% of each run, Pallas kernels for 5% -> 4%
where the time goes in v9:
time: 146 us
  blocking collectives  66.2 us (45%)
  waiting for transfers between devices  29.4 us (20%)
  Pallas kernels  24.1 us (17%)
  starting transfers between devices  21.7 us (15%)
  local copies, waits for them, and re-layouts  3.31 us (2%)
    all_to_all x2, blocking collectives, on_device(): lax.all_to_all(synth.reshape(owners, rows + 2 * margin, LANES), BOTH, 0,...  34.1 us
    all_to_all x2, blocking collectives, on_device(): spectrum = lax.all_to_all(spectrum, BOTH, 0, 0, tiled=True)  32.1 us
    pallas_call x13, Pallas kernels, run(): pl.pallas_call(kernel, out_shape=outs, in_specs=[place(i, smem, far) for...  24.1 us
    ppermute x12, waiting for transfers between devices, exchange(): lax.ppermute(pieces[s], 'lon', [(i, (i + s) % count) for i in range(count)])  21.9 us
    ppermute x12, starting transfers between devices, exchange(): lax.ppermute(pieces[s], 'lon', [(i, (i + s) % count) for i in range(count)])  7.23 us
    ppermute x4, starting transfers between devices, partner(): return lax.ppermute(x, 'lat', [(i, i ^ step) for i in range(lat_count)])  6.85 us
    ppermute x1, waiting for transfers between devices, on_device(): lax.ppermute(last, 'lat', [(i, i + 1) for i in range(lat_count - 1)])  5.72 us
    ppermute x1, starting transfers between devices, on_device(): lax.ppermute(last, 'lat', [(i, i + 1) for i in range(lat_count - 1)])  4 us
  transfers between devices with their start and end apart: 20, of which 15 were waited for; matrix products, arithmetic and copies ran while one was open for 0% of the time, Pallas kernels for 4%

profile of v9, /device:TPU:1, one launch (start us, length us, event | category | flops | bytes accessed | tf_op | source)
XLA Modules:
  0.0 145.8 jit_solution(7883239353057017930)
XLA Ops:
  0.7 1.2 shard_map.96
  3.3 4.2 %collective-permute-start.4 = (f32[32,1024]{1,0:T(8,128)S(1)}, f32[32,1024]{1,0:T(8,128)S(1)}, u32[]{:S(2)}, u32[]{:S(2)}) collective-permute-start(f32[32,1024]{1,0:T(8,128)S(1)} %reshape.47), channel_id=1, source_target_pairs={{0,24},{4,28},{8,16},{12,20},{16,8},{20,12},{24,0},{28,4},{1,25},{... | collective-permute-start | bytes 393224 | tf_op jit(solution)/shard_map/ppermute | solution.py:830
  7.8 1.3 collective-permute-start.1
  9.1 4.0 %collective-permute-start = (f32[520,128]{1,0:T(8,128)S(1)}, f32[520,128]{1,0:T(8,128)S(1)}, u32[]{:S(2)}, u32[]{:S(2)}) collective-permute-start(f32[520,128]{1,0:T(8,128)S(1)} %bitcast.21), channel_id=1, source_target_pairs={{0,4},{4,8},{8,12},{12,16},{16,20},{20,24},{24,28},{1,5},{5,9},{9,... | collective-permute-start | bytes 798728 | tf_op jit(solution)/shard_map/ppermute | solution.py:822
  13.1 2.8 %shard_map.97 = (bf16[8,256,256]{2,1,0:T(8,128)(2,1)S(1)}, bf16[8,256,256]{2,1,0:T(8,128)(2,1)S(1)}) custom-call(s32[1]{0:T(128)} %bitcast.6.index_ref), custom_call_target="tpu_custom_call" | custom-call | flops 2900000000 | bytes 1 | tf_op jit(solution)/shard_map/pallas_call | solution.py:202
  18.2 5.7 %collective-permute-done.above_ref = f32[520,128]{1,0:T(8,128)S(1)} collective-permute-done((f32[520,128]{1,0:T(8,128)S(1)}, f32[520,128]{1,0:T(8,128)S(1)}, u32[]{:S(2)}, u32[]{:S(2)}) %collective-permute-start) | collective-permute-done | bytes 266272 | tf_op jit(solution)/shard_map/ppermute | solution.py:822
  24.7 2.3 %collective-permute-start.5 = (f32[168,128]{1,0:T(8,128)S(1)}, f32[168,128]{1,0:T(8,128)S(1)}, u32[]{:S(2)}, u32[]{:S(2)}) collective-permute-start(f32[168,128]{1,0:T(8,128)S(1)} %get-tuple-element.62), channel_id=1, source_target_pairs={{0,1},{1,2},{2,3},{3,0},{4,5},{5,6},{6,7},{7,4},{8,9},{9,10},{10,1... | collective-permute-start | bytes 258056 | tf_op jit(solution)/shard_map/ppermute | solution.py:854
  27.1 2.3 %collective-permute-start.10 = (f32[128,1024]{1,0:T(8,128)S(1)}, f32[128,1024]{1,0:T(8,128)S(1)}, u32[]{:S(2)}, u32[]{:S(2)}) collective-permute-start(f32[128,1024]{1,0:T(8,128)S(1)} %constant_dynamic-update-slice_fusion.refs_8_), channel_id=1, source_target_pairs={{0,4},{4,0},{8,12},{12,8},{16,20},{20,16},{24,28},{28,24},{1,5},{5... | collective-permute-start | bytes 1572872 | tf_op jit(solution)/shard_map/ppermute | solution.py:830
  29.4 1.6 %collective-permute-done.6.right_ref = f32[168,128]{1,0:T(8,128)S(1)} collective-permute-done((f32[168,128]{1,0:T(8,128)S(1)}, f32[168,128]{1,0:T(8,128)S(1)}, u32[]{:S(2)}, u32[]{:S(2)}) %collective-permute-start.6) | collective-permute-done | bytes 86048 | tf_op jit(solution)/shard_map/ppermute | solution.py:855
  31.0 3.7 %shard_map.99 = (f32[8,24,128]{2,1,0:T(8,128)S(1)}, f32[8,24,128]{2,1,0:T(8,128)S(1)}, f32[8,24,128]{2,1,0:T(8,128)S(1)}, f32[8,24,128]{2,1,0:T(8,128)S(1)}, f32...) custom-call(s32[2]{0:T(128)S(1)} %pad_add_fusion.index_ref.refs_0_, ...), custom_call_target="tpu_custom_call" | custom-call | flops 6600000000 | bytes 1 | tf_op jit(solution)/shard_map/pallas_call | solution.py:202
  36.8 2.7 %collective-permute-done.8.refs_6_ = f32[8,24,128]{2,1,0:T(8,128)S(1)} collective-permute-done((f32[8,24,128]{2,1,0:T(8,128)S(1)}, f32[8,24,128]{2,1,0:T(8,128)S(1)}, u32[]{:S(2)}, u32[]{:S(2)}) %collective-permute-start.8) | collective-permute-done | bytes 98336 | tf_op jit(solution)/shard_map/ppermute | solution.py:793
  39.6 1.5 %collective-permute-done.9.refs_7_ = f32[8,24,128]{2,1,0:T(8,128)S(1)} collective-permute-done((f32[8,24,128]{2,1,0:T(8,128)S(1)}, f32[8,24,128]{2,1,0:T(8,128)S(1)}, u32[]{:S(2)}, u32[]{:S(2)}) %collective-permute-start.9) | collective-permute-done | bytes 98336 | tf_op jit(solution)/shard_map/ppermute | solution.py:793
  41.1 1.4 shard_map.100
  42.5 17.2 %all_to_all.20 = f32[32,24,128]{2,1,0:T(8,128)S(1)} all-to-all(f32[32,24,128]{2,1,0:T(8,128)S(1)} %get-tuple-element.80), channel_id=1, replica_groups=mesh['lat'=8,'lon'=4] {'lat','lon'}, dimensions={0} | all-to-all | bytes 786432 | tf_op jit(solution)/shard_map/all_to_all | solution.py:901
  59.8 2.5 %shard_map.101 = f32[8,4,32,128]{3,2,1,0:T(8,128)S(1)} custom-call(bf16[8,256,256]{2,1,0:T(8,128)(2,1)S(1)} %copy-done.6, bf16[8,256,256]{2,1,0:T(8,128)(2,1)S(1)} %copy-done.8, f32[2,1024,128]{2,1,0:T(8,128)S(1)} %get-tuple-element.79.green_ref, f32[8,4,24,128]{3,2,1,0:T(8,128)S(1)} %bitcast.15), custom_call_target="tpu_custom_call" | custom-call | flops 4000000000 | bytes 1 | tf_op jit(solution)/shard_map/pallas_call | solution.py:202
  62.3 18.5 %all_to_all.21.x_ref = f32[32,32,128]{2,1,0:T(8,128)S(1)} all-to-all(f32[32,32,128]{2,1,0:T(8,128)S(1)} %bitcast.12), channel_id=1, replica_groups=mesh['lat'=8,'lon'=4] {'lat','lon'}, dimensions={0} | all-to-all | bytes 1048576 | tf_op jit(solution)/shard_map/all_to_all | solution.py:914
  80.8 1.8 %shard_map.102 = (f32[288,128]{1,0:T(8,128)S(1)}, f32[288,128]{1,0:T(8,128)S(1)}, f32[288,128]{1,0:T(8,128)S(1)}, f32[288,128]{1,0:T(8,128)S(1)}) custom-call(s32[2]{0:T(128)S(1)} %pad_add_fusion.index_ref.refs_0_, bf16[512,512]{1,0:T(8,128)(2,1)S(1)} %get-tuple-element.68.refs_2_.high_ref, bf16[512,512]{1,0:T(8,128)(2,1)S(1)} %get-tuple-element.69.refs_3_.low_ref, ...), custom_call_target="tpu_custom_call" | custom-call | flops 2000000000 | bytes 1 | tf_op jit(solution)/shard_map/pallas_call | solution.py:202
  82.5 1.2 collective-permute-start.11
  84.6 1.9 %collective-permute-done.11.rest_1_ = f32[288,128]{1,0:T(8,128)S(1)} collective-permute-done((f32[288,128]{1,0:T(8,128)S(1)}, f32[288,128]{1,0:T(8,128)S(1)}, u32[]{:S(2)}, u32[]{:S(2)}) %collective-permute-start.11) | collective-permute-done | bytes 147488 | tf_op jit(solution)/shard_map/ppermute | solution.py:793
  86.4 4.8 %collective-permute-done.12.rest_2_ = f32[288,128]{1,0:T(8,128)S(1)} collective-permute-done((f32[288,128]{1,0:T(8,128)S(1)}, f32[288,128]{1,0:T(8,128)S(1)}, u32[]{:S(2)}, u32[]{:S(2)}) %collective-permute-start.12) | collective-permute-done | bytes 147488 | tf_op jit(solution)/shard_map/ppermute | solution.py:793
  91.8 3.3 %shard_map.103 = (f32[8,24,128]{2,1,0:T(8,128)S(1)}, f32[8,24,128]{2,1,0:T(8,128)S(1)}, f32[8,24,128]{2,1,0:T(8,128)S(1)}, f32[8,24,128]{2,1,0:T(8,128)S(1)}, f32[32,24,128]{2,1,0:T(8,128)}) custom-call(s32[2]{0:T(128)S(1)} %pad_add_fusion.index_ref.refs_0_, f32[4]{0:T(128)S(1)} %copy-done.4, s32[768,128]{1,0:T(8,128)S(1)} %bitcast.20, ...), custom_call_target="tpu_custom_call" | custom-call | flops 5400000000 | bytes 1 | tf_op jit(solution)/shard_map/pallas_call | solution.py:202
  96.8 2.7 %collective-permute-done.15.rest_2_ = f32[8,24,128]{2,1,0:T(8,128)S(1)} collective-permute-done((f32[8,24,128]{2,1,0:T(8,128)S(1)}, f32[8,24,128]{2,1,0:T(8,128)S(1)}, u32[]{:S(2)}, u32[]{:S(2)}) %collective-permute-start.15) | collective-permute-done | bytes 98336 | tf_op jit(solution)/shard_map/ppermute | solution.py:793
  99.4 1.5 %collective-permute-done.16.rest_3_ = f32[8,24,128]{2,1,0:T(8,128)S(1)} collective-permute-done((f32[8,24,128]{2,1,0:T(8,128)S(1)}, f32[8,24,128]{2,1,0:T(8,128)S(1)}, u32[]{:S(2)}, u32[]{:S(2)}) %collective-permute-start.16) | collective-permute-done | bytes 98336 | tf_op jit(solution)/shard_map/ppermute | solution.py:793
  101.0 1.3 shard_map.104
  102.3 14.8 %all_to_all.22 = f32[32,24,128]{2,1,0:T(8,128)S(1)} all-to-all(f32[32,24,128]{2,1,0:T(8,128)S(1)} %shard_map.104), channel_id=1, replica_groups=mesh['lat'=8,'lon'=4] {'lat','lon'}, dimensions={0} | all-to-all | bytes 786432 | tf_op jit(solution)/shard_map/all_to_all | solution.py:901
  117.1 2.5 %shard_map.105 = f32[8,4,24,128]{3,2,1,0:T(8,128)S(1)} custom-call(bf16[8,256,256]{2,1,0:T(8,128)(2,1)S(1)} %copy-done.6, bf16[8,256,256]{2,1,0:T(8,128)(2,1)S(1)} %copy-done.8, f32[2,1024,128]{2,1,0:T(8,128)S(1)} %get-tuple-element.79.green_ref, f32[8,4,24,128]{3,2,1,0:T(8,128)S(1)} %bitcast.13), custom_call_target="tpu_custom_call" | custom-call | flops 4000000000 | bytes 1 | tf_op jit(solution)/shard_map/pallas_call | solution.py:202
  119.6 15.6 %all_to_all.23.x_ref = f32[32,24,128]{2,1,0:T(8,128)S(1)} all-to-all(f32[32,24,128]{2,1,0:T(8,128)S(1)} %bitcast.14), channel_id=1, replica_groups=mesh['lat'=8,'lon'=4] {'lat','lon'}, dimensions={0} | all-to-all | bytes 786432 | tf_op jit(solution)/shard_map/all_to_all | solution.py:914
  135.2 1.4 shard_map.106
  136.6 1.3 collective-permute-start.17
  137.9 1.3 collective-permute-start.18
  139.5 4.2 %collective-permute-done.18.rest_2_ = f32[192,128]{1,0:T(8,128)S(1)} collective-permute-done((f32[192,128]{1,0:T(8,128)S(1)}, f32[192,128]{1,0:T(8,128)S(1)}, u32[]{:S(2)}, u32[]{:S(2)}) %collective-permute-start.18) | collective-permute-done | bytes 98336 | tf_op jit(solution)/shard_map/ppermute | solution.py:793
  144.3 1.3 shard_map.107
  (58 shorter events, 11.0 us)
Async XLA Ops:
  0.6 1.3 copy-start.10
  0.6 1.3 copy-start.11
  0.7 1.3 copy-start.1
  0.7 1.3 copy-start
  2.0 1.0 copy-start.9
  3.3 14.7 %collective-permute-start.4 = (f32[32,1024]{1,0:T(8,128)S(1)}, f32[32,1024]{1,0:T(8,128)S(1)}, u32[]{:S(2)}, u32[]{:S(2)}) collective-permute-start(f32[32,1024]{1,0:T(8,128)S(1)} %reshape.47), channel_id=1, source_target_pairs={{0,24},{4,28},{8,16},{12,20},{16,8},{20,12},{24,0},{28,4},{1,25},{... | collective-permute-start | bytes 393224 | tf_op jit(solution)/shard_map/ppermute | solution.py:830
  7.5 10.7 %collective-permute-start.3 = (f32[32,1024]{1,0:T(8,128)S(1)}, f32[32,1024]{1,0:T(8,128)S(1)}, u32[]{:S(2)}, u32[]{:S(2)}) collective-permute-start(f32[32,1024]{1,0:T(8,128)S(1)} %reshape.47), channel_id=1, source_target_pairs={{0,16},{4,20},{8,24},{12,28},{16,0},{20,4},{24,8},{28,12},{1,17},{... | collective-permute-start | bytes 393224 | tf_op jit(solution)/shard_map/ppermute | solution.py:830
  7.5 10.7 %collective-permute-start.2 = (f32[32,1024]{1,0:T(8,128)S(1)}, f32[32,1024]{1,0:T(8,128)S(1)}, u32[]{:S(2)}, u32[]{:S(2)}) collective-permute-start(f32[32,1024]{1,0:T(8,128)S(1)} %reshape.47), channel_id=1, source_target_pairs={{0,8},{4,12},{8,0},{12,4},{16,24},{20,28},{24,16},{28,20},{1,9},{5... | collective-permute-start | bytes 393224 | tf_op jit(solution)/shard_map/ppermute | solution.py:830
  7.8 10.3 %collective-permute-start.1 = (f32[520,128]{1,0:T(8,128)S(1)}, f32[520,128]{1,0:T(8,128)S(1)}, u32[]{:S(2)}, u32[]{:S(2)}) collective-permute-start(f32[520,128]{1,0:T(8,128)S(1)} %bitcast.22), channel_id=1, source_target_pairs={{4,0},{8,4},{12,8},{16,12},{20,16},{24,20},{28,24},{5,1},{9,5},{13... | collective-permute-start | bytes 798728 | tf_op jit(solution)/shard_map/ppermute | solution.py:823
  9.1 14.7 %collective-permute-start = (f32[520,128]{1,0:T(8,128)S(1)}, f32[520,128]{1,0:T(8,128)S(1)}, u32[]{:S(2)}, u32[]{:S(2)}) collective-permute-start(f32[520,128]{1,0:T(8,128)S(1)} %bitcast.21), channel_id=1, source_target_pairs={{0,4},{4,8},{8,12},{12,16},{16,20},{20,24},{24,28},{1,5},{5,9},{9,... | collective-permute-start | bytes 798728 | tf_op jit(solution)/shard_map/ppermute | solution.py:822
  16.0 1.0 copy-start.5
  16.9 1.0 copy-start.7
  23.9 7.1 %copy-start.2 = (f32[4]{0:T(128)S(1)}, f32[4]{0:T(128)}, u32[]{:S(2)}) copy-start(f32[4]{0:T(128)} %shear_ref.1) | copy-start | bytes 52
  23.9 7.1 %copy-start.3 = (f32[4]{0:T(128)S(1)}, f32[4]{0:T(128)}, u32[]{:S(2)}) copy-start(f32[4]{0:T(128)} %restoring_ref.1) | copy-start | bytes 52
  23.9 7.1 %copy-start.4 = (f32[4]{0:T(128)S(1)}, f32[4]{0:T(128)}, u32[]{:S(2)}) copy-start(f32[4]{0:T(128)} %contrast_ref.3) | copy-start | bytes 52
  24.7 4.7 %collective-permute-start.5 = (f32[168,128]{1,0:T(8,128)S(1)}, f32[168,128]{1,0:T(8,128)S(1)}, u32[]{:S(2)}, u32[]{:S(2)}) collective-permute-start(f32[168,128]{1,0:T(8,128)S(1)} %get-tuple-element.62), channel_id=1, source_target_pairs={{0,1},{1,2},{2,3},{3,0},{4,5},{5,6},{6,7},{7,4},{8,9},{9,10},{10,1... | collective-permute-start | bytes 258056 | tf_op jit(solution)/shard_map/ppermute | solution.py:854
  27.1 3.9 %collective-permute-start.6 = (f32[168,128]{1,0:T(8,128)S(1)}, f32[168,128]{1,0:T(8,128)S(1)}, u32[]{:S(2)}, u32[]{:S(2)}) collective-permute-start(f32[168,128]{1,0:T(8,128)S(1)} %get-tuple-element.63), channel_id=1, source_target_pairs={{1,0},{2,1},{3,2},{0,3},{5,4},{6,5},{7,6},{4,7},{9,8},{10,9},{11,1... | collective-permute-start | bytes 258056 | tf_op jit(solution)/shard_map/ppermute | solution.py:855
  27.1 13.9 %collective-permute-start.10 = (f32[128,1024]{1,0:T(8,128)S(1)}, f32[128,1024]{1,0:T(8,128)S(1)}, u32[]{:S(2)}, u32[]{:S(2)}) collective-permute-start(f32[128,1024]{1,0:T(8,128)S(1)} %constant_dynamic-update-slice_fusion.refs_8_), channel_id=1, source_target_pairs={{0,4},{4,0},{8,12},{12,8},{16,20},{20,16},{24,28},{28,24},{1,5},{5... | collective-permute-start | bytes 1572872 | tf_op jit(solution)/shard_map/ppermute | solution.py:830
  34.7 2.2 %collective-permute-start.7 = (f32[8,24,128]{2,1,0:T(8,128)S(1)}, f32[8,24,128]{2,1,0:T(8,128)S(1)}, u32[]{:S(2)}, u32[]{:S(2)}) collective-permute-start(f32[8,24,128]{2,1,0:T(8,128)S(1)} %get-tuple-element.73), channel_id=1, source_target_pairs={{0,1},{1,2},{2,3},{3,0},{4,5},{5,6},{6,7},{7,4},{8,9},{9,10},{10,1... | collective-permute-start | bytes 294920 | tf_op jit(solution)/shard_map/ppermute | solution.py:793
  35.2 4.4 %collective-permute-start.8 = (f32[8,24,128]{2,1,0:T(8,128)S(1)}, f32[8,24,128]{2,1,0:T(8,128)S(1)}, u32[]{:S(2)}, u32[]{:S(2)}) collective-permute-start(f32[8,24,128]{2,1,0:T(8,128)S(1)} %get-tuple-element.74), channel_id=1, source_target_pairs={{0,2},{1,3},{2,0},{3,1},{4,6},{5,7},{6,4},{7,5},{8,10},{9,11},{10,... | collective-permute-start | bytes 294920 | tf_op jit(solution)/shard_map/ppermute | solution.py:793
  35.5 5.6 %collective-permute-start.9 = (f32[8,24,128]{2,1,0:T(8,128)S(1)}, f32[8,24,128]{2,1,0:T(8,128)S(1)}, u32[]{:S(2)}, u32[]{:S(2)}) collective-permute-start(f32[8,24,128]{2,1,0:T(8,128)S(1)} %get-tuple-element.75), channel_id=1, source_target_pairs={{0,3},{1,0},{2,1},{3,2},{4,7},{5,4},{6,5},{7,6},{8,11},{9,8},{10,9... | collective-permute-start | bytes 294920 | tf_op jit(solution)/shard_map/ppermute | solution.py:793
  41.1 18.6 %copy-start.6 = (bf16[8,256,256]{2,1,0:T(8,128)(2,1)S(1)}, bf16[8,256,256]{2,1,0:T(8,128)(2,1)}, u32[]{:S(2)}) copy-start(bf16[8,256,256]{2,1,0:T(8,128)(2,1)} %copy-done.5) | copy-start | bytes 3145732
  41.1 18.6 %copy-start.8 = (bf16[8,256,256]{2,1,0:T(8,128)(2,1)S(1)}, bf16[8,256,256]{2,1,0:T(8,128)(2,1)}, u32[]{:S(2)}) copy-start(bf16[8,256,256]{2,1,0:T(8,128)(2,1)} %copy-done.7) | copy-start | bytes 3145732
  82.5 3.9 %collective-permute-start.11 = (f32[288,128]{1,0:T(8,128)S(1)}, f32[288,128]{1,0:T(8,128)S(1)}, u32[]{:S(2)}, u32[]{:S(2)}) collective-permute-start(f32[288,128]{1,0:T(8,128)S(1)} %get-tuple-element.82), channel_id=1, source_target_pairs={{0,1},{1,2},{2,3},{3,0},{4,5},{5,6},{6,7},{7,4},{8,9},{9,10},{10,1... | collective-permute-start | bytes 442376 | tf_op jit(solution)/shard_map/ppermute | solution.py:793
  83.7 7.5 %collective-permute-start.12 = (f32[288,128]{1,0:T(8,128)S(1)}, f32[288,128]{1,0:T(8,128)S(1)}, u32[]{:S(2)}, u32[]{:S(2)}) collective-permute-start(f32[288,128]{1,0:T(8,128)S(1)} %get-tuple-element.83), channel_id=1, source_target_pairs={{0,2},{1,3},{2,0},{3,1},{4,6},{5,7},{6,4},{7,5},{8,10},{9,11},{10,... | collective-permute-start | bytes 442376 | tf_op jit(solution)/shard_map/ppermute | solution.py:793
  84.5 7.3 %collective-permute-start.13 = (f32[288,128]{1,0:T(8,128)S(1)}, f32[288,128]{1,0:T(8,128)S(1)}, u32[]{:S(2)}, u32[]{:S(2)}) collective-permute-start(f32[288,128]{1,0:T(8,128)S(1)} %get-tuple-element.84), channel_id=1, source_target_pairs={{0,3},{1,0},{2,1},{3,2},{4,7},{5,4},{6,5},{7,6},{8,11},{9,8},{10,9... | collective-permute-start | bytes 442376 | tf_op jit(solution)/shard_map/ppermute | solution.py:793
  95.1 1.6 %collective-permute-start.14 = (f32[8,24,128]{2,1,0:T(8,128)S(1)}, f32[8,24,128]{2,1,0:T(8,128)S(1)}, u32[]{:S(2)}, u32[]{:S(2)}) collective-permute-start(f32[8,24,128]{2,1,0:T(8,128)S(1)} %get-tuple-element.87), channel_id=1, source_target_pairs={{0,1},{1,2},{2,3},{3,0},{4,5},{5,6},{6,7},{7,4},{8,9},{9,10},{10,1... | collective-permute-start | bytes 294920 | tf_op jit(solution)/shard_map/ppermute | solution.py:793
  95.1 4.3 %collective-permute-start.15 = (f32[8,24,128]{2,1,0:T(8,128)S(1)}, f32[8,24,128]{2,1,0:T(8,128)S(1)}, u32[]{:S(2)}, u32[]{:S(2)}) collective-permute-start(f32[8,24,128]{2,1,0:T(8,128)S(1)} %get-tuple-element.88), channel_id=1, source_target_pairs={{0,2},{1,3},{2,0},{3,1},{4,6},{5,7},{6,4},{7,5},{8,10},{9,11},{10,... | collective-permute-start | bytes 294920 | tf_op jit(solution)/shard_map/ppermute | solution.py:793
  95.8 5.2 %collective-permute-start.16 = (f32[8,24,128]{2,1,0:T(8,128)S(1)}, f32[8,24,128]{2,1,0:T(8,128)S(1)}, u32[]{:S(2)}, u32[]{:S(2)}) collective-permute-start(f32[8,24,128]{2,1,0:T(8,128)S(1)} %get-tuple-element.89), channel_id=1, source_target_pairs={{0,3},{1,0},{2,1},{3,2},{4,7},{5,4},{6,5},{7,6},{8,11},{9,8},{10,9... | collective-permute-start | bytes 294920 | tf_op jit(solution)/shard_map/ppermute | solution.py:793
  136.6 2.9 %collective-permute-start.17 = (f32[192,128]{1,0:T(8,128)S(1)}, f32[192,128]{1,0:T(8,128)S(1)}, u32[]{:S(2)}, u32[]{:S(2)}) collective-permute-start(f32[192,128]{1,0:T(8,128)S(1)} %get-tuple-element.91), channel_id=1, source_target_pairs={{0,1},{1,2},{2,3},{3,0},{4,5},{5,6},{6,7},{7,4},{8,9},{9,10},{10,1... | collective-permute-start | bytes 294920 | tf_op jit(solution)/shard_map/ppermute | solution.py:793
  137.9 5.8 %collective-permute-start.18 = (f32[192,128]{1,0:T(8,128)S(1)}, f32[192,128]{1,0:T(8,128)S(1)}, u32[]{:S(2)}, u32[]{:S(2)}) collective-permute-start(f32[192,128]{1,0:T(8,128)S(1)} %get-tuple-element.92), channel_id=1, source_target_pairs={{0,2},{1,3},{2,0},{3,1},{4,6},{5,7},{6,4},{7,5},{8,10},{9,11},{10,... | collective-permute-start | bytes 294920 | tf_op jit(solution)/shard_map/ppermute | solution.py:793
  139.2 5.2 %collective-permute-start.19 = (f32[192,128]{1,0:T(8,128)S(1)}, f32[192,128]{1,0:T(8,128)S(1)}, u32[]{:S(2)}, u32[]{:S(2)}) collective-permute-start(f32[192,128]{1,0:T(8,128)S(1)} %get-tuple-element.93), channel_id=1, source_target_pairs={{0,3},{1,0},{2,1},{3,2},{4,7},{5,4},{6,5},{7,6},{8,11},{9,8},{10,9... | collective-permute-start | bytes 294920 | tf_op jit(solution)/shard_map/ppermute | solution.py:793

commit v10 on v9

--- a/solution.py
+++ b/solution.py
@@ -657,18 +657,13 @@
     parts, (o_ref,) = rest[:lon_count], rest[lon_count:]
     share, rows, cols = parts[0].shape
     chunk = LANES // share
-    product = None
-    for pair in zip(range(0, lon_count, 2), range(1, lon_count, 2)):
-        x = jnp.concatenate([parts[s][...].reshape(share * rows, cols) for s in pair], axis=1)
-        places = []
-        for s in pair:
-            source = lax.rem(index_ref[1] + (lon_count - s), lon_count)
-            places.append(pl.ds(pl.multiple_of(source * cols, cols), cols))
-        tables = [
-            jnp.concatenate([ref[at, :] for at in places], axis=0) for ref in (high_ref, low_ref)
-        ]
-        term = dot3(halves(x), tables, NN)
-        product = term if product is None else product + term
+    x = jnp.concatenate([part[...].reshape(share * rows, cols) for part in parts], axis=1)
+    places = []
+    for s in range(lon_count):
+        source = lax.rem(index_ref[1] + (lon_count - s), lon_count)
+        places.append(pl.ds(pl.multiple_of(source * cols, cols), cols))
+    tables = [jnp.concatenate([ref[at, :] for at in places], axis=0) for ref in (high_ref, low_ref)]
+    product = dot3(halves(x), tables, NN)
     weight = weight_ref[...] * scale
     for g in range(product.shape[1] // LANES):
         blocks = swap_chunks(
@@ -759,11 +754,9 @@
         [jnp.concatenate([group[k] for group in groups], axis=1) for k in range(share)], axis=0
     )
     terms = halves(terms)
-    for q in range(0, lon_count, 2):
-        at = slice(q * cols, (q + 2) * cols)
-        both = dot3(terms, (high_ref[at, :], low_ref[at, :]), NT)
-        columns[q] = both[:, :cols]
-        columns[q + 1] = both[:, cols:]
+    whole = dot3(terms, (high_ref[...], low_ref[...]), NT)
+    for q in range(lon_count):
+        columns[q] = whole[:, q * cols : (q + 1) * cols]
     lane = iota((rows, LANES), 1)
     for s in range(lon_count):
         dest = lax.rem(index_ref[1] + s, lon_count)

time: 146 us -> 146 us (level)
  no operation moved by 1% of the time
where the time goes in v10:
time: 146 us
  blocking collectives  66.2 us (45%)
  waiting for transfers between devices  29.4 us (20%)
  Pallas kernels  24.1 us (17%)
  starting transfers between devices  21.7 us (15%)
  local copies, waits for them, and re-layouts  3.31 us (2%)
    all_to_all x2, blocking collectives, on_device(): lax.all_to_all(synth.reshape(owners, rows + 2 * margin, LANES), BOTH, 0,...  34.1 us
    all_to_all x2, blocking collectives, on_device(): spectrum = lax.all_to_all(spectrum, BOTH, 0, 0, tiled=True)  32.1 us
    pallas_call x13, Pallas kernels, run(): pl.pallas_call(kernel, out_shape=outs, in_specs=[place(i, smem, far) for...  24.1 us
    ppermute x12, waiting for transfers between devices, exchange(): lax.ppermute(pieces[s], 'lon', [(i, (i + s) % count) for i in range(count)])  21.9 us
    ppermute x12, starting transfers between devices, exchange(): lax.ppermute(pieces[s], 'lon', [(i, (i + s) % count) for i in range(count)])  7.23 us
    ppermute x4, starting transfers between devices, partner(): return lax.ppermute(x, 'lat', [(i, i ^ step) for i in range(lat_count)])  6.85 us
    ppermute x1, waiting for transfers between devices, on_device(): lax.ppermute(last, 'lat', [(i, i + 1) for i in range(lat_count - 1)])  5.72 us
    ppermute x1, starting transfers between devices, on_device(): lax.ppermute(last, 'lat', [(i, i + 1) for i in range(lat_count - 1)])  4 us
  transfers between devices with their start and end apart: 20, of which 15 were waited for; matrix products, arithmetic and copies ran while one was open for 0% of the time, Pallas kernels for 4%

profile of v10, /device:TPU:1, one launch (start us, length us, event | category | flops | bytes accessed | tf_op | source)
XLA Modules:
  0.0 145.8 jit_solution(10478190293160014531)
XLA Ops:
  0.7 1.2 shard_map.96
  3.3 4.2 %collective-permute-start.4 = (f32[32,1024]{1,0:T(8,128)S(1)}, f32[32,1024]{1,0:T(8,128)S(1)}, u32[]{:S(2)}, u32[]{:S(2)}) collective-permute-start(f32[32,1024]{1,0:T(8,128)S(1)} %reshape.47), channel_id=1, source_target_pairs={{0,24},{4,28},{8,16},{12,20},{16,8},{20,12},{24,0},{28,4},{1,25},{... | collective-permute-start | bytes 393224 | tf_op jit(solution)/shard_map/ppermute | solution.py:823
  7.8 1.3 collective-permute-start.1
  9.1 4.0 %collective-permute-start = (f32[520,128]{1,0:T(8,128)S(1)}, f32[520,128]{1,0:T(8,128)S(1)}, u32[]{:S(2)}, u32[]{:S(2)}) collective-permute-start(f32[520,128]{1,0:T(8,128)S(1)} %bitcast.21), channel_id=1, source_target_pairs={{0,4},{4,8},{8,12},{12,16},{16,20},{20,24},{24,28},{1,5},{5,9},{9,... | collective-permute-start | bytes 798728 | tf_op jit(solution)/shard_map/ppermute | solution.py:815
  13.1 2.8 %shard_map.97 = (bf16[8,256,256]{2,1,0:T(8,128)(2,1)S(1)}, bf16[8,256,256]{2,1,0:T(8,128)(2,1)S(1)}) custom-call(s32[1]{0:T(128)} %bitcast.6.index_ref), custom_call_target="tpu_custom_call" | custom-call | flops 2900000000 | bytes 1 | tf_op jit(solution)/shard_map/pallas_call | solution.py:202
  18.2 5.7 %collective-permute-done.above_ref = f32[520,128]{1,0:T(8,128)S(1)} collective-permute-done((f32[520,128]{1,0:T(8,128)S(1)}, f32[520,128]{1,0:T(8,128)S(1)}, u32[]{:S(2)}, u32[]{:S(2)}) %collective-permute-start) | collective-permute-done | bytes 266272 | tf_op jit(solution)/shard_map/ppermute | solution.py:815
  24.7 2.3 %collective-permute-start.5 = (f32[168,128]{1,0:T(8,128)S(1)}, f32[168,128]{1,0:T(8,128)S(1)}, u32[]{:S(2)}, u32[]{:S(2)}) collective-permute-start(f32[168,128]{1,0:T(8,128)S(1)} %get-tuple-element.62), channel_id=1, source_target_pairs={{0,1},{1,2},{2,3},{3,0},{4,5},{5,6},{6,7},{7,4},{8,9},{9,10},{10,1... | collective-permute-start | bytes 258056 | tf_op jit(solution)/shard_map/ppermute | solution.py:847
  27.1 2.3 %collective-permute-start.10 = (f32[128,1024]{1,0:T(8,128)S(1)}, f32[128,1024]{1,0:T(8,128)S(1)}, u32[]{:S(2)}, u32[]{:S(2)}) collective-permute-start(f32[128,1024]{1,0:T(8,128)S(1)} %constant_dynamic-update-slice_fusion.refs_8_), channel_id=1, source_target_pairs={{0,4},{4,0},{8,12},{12,8},{16,20},{20,16},{24,28},{28,24},{1,5},{5... | collective-permute-start | bytes 1572872 | tf_op jit(solution)/shard_map/ppermute | solution.py:823
  29.4 1.6 %collective-permute-done.6.right_ref = f32[168,128]{1,0:T(8,128)S(1)} collective-permute-done((f32[168,128]{1,0:T(8,128)S(1)}, f32[168,128]{1,0:T(8,128)S(1)}, u32[]{:S(2)}, u32[]{:S(2)}) %collective-permute-start.6) | collective-permute-done | bytes 86048 | tf_op jit(solution)/shard_map/ppermute | solution.py:848
  31.0 3.7 %shard_map.99 = (f32[8,24,128]{2,1,0:T(8,128)S(1)}, f32[8,24,128]{2,1,0:T(8,128)S(1)}, f32[8,24,128]{2,1,0:T(8,128)S(1)}, f32[8,24,128]{2,1,0:T(8,128)S(1)}, f32...) custom-call(s32[2]{0:T(128)S(1)} %pad_add_fusion.index_ref.refs_0_, ...), custom_call_target="tpu_custom_call" | custom-call | flops 6600000000 | bytes 1 | tf_op jit(solution)/shard_map/pallas_call | solution.py:202
  36.8 2.7 %collective-permute-done.8.refs_6_ = f32[8,24,128]{2,1,0:T(8,128)S(1)} collective-permute-done((f32[8,24,128]{2,1,0:T(8,128)S(1)}, f32[8,24,128]{2,1,0:T(8,128)S(1)}, u32[]{:S(2)}, u32[]{:S(2)}) %collective-permute-start.8) | collective-permute-done | bytes 98336 | tf_op jit(solution)/shard_map/ppermute | solution.py:786
  39.6 1.5 %collective-permute-done.9.refs_7_ = f32[8,24,128]{2,1,0:T(8,128)S(1)} collective-permute-done((f32[8,24,128]{2,1,0:T(8,128)S(1)}, f32[8,24,128]{2,1,0:T(8,128)S(1)}, u32[]{:S(2)}, u32[]{:S(2)}) %collective-permute-start.9) | collective-permute-done | bytes 98336 | tf_op jit(solution)/shard_map/ppermute | solution.py:786
  41.1 1.4 shard_map.100
  42.5 17.2 %all_to_all.20 = f32[32,24,128]{2,1,0:T(8,128)S(1)} all-to-all(f32[32,24,128]{2,1,0:T(8,128)S(1)} %get-tuple-element.80), channel_id=1, replica_groups=mesh['lat'=8,'lon'=4] {'lat','lon'}, dimensions={0} | all-to-all | bytes 786432 | tf_op jit(solution)/shard_map/all_to_all | solution.py:894
  59.8 2.5 %shard_map.101 = f32[8,4,32,128]{3,2,1,0:T(8,128)S(1)} custom-call(bf16[8,256,256]{2,1,0:T(8,128)(2,1)S(1)} %copy-done.6, bf16[8,256,256]{2,1,0:T(8,128)(2,1)S(1)} %copy-done.8, f32[2,1024,128]{2,1,0:T(8,128)S(1)} %get-tuple-element.79.green_ref, f32[8,4,24,128]{3,2,1,0:T(8,128)S(1)} %bitcast.15), custom_call_target="tpu_custom_call" | custom-call | flops 4000000000 | bytes 1 | tf_op jit(solution)/shard_map/pallas_call | solution.py:202
  62.3 18.5 %all_to_all.21.x_ref = f32[32,32,128]{2,1,0:T(8,128)S(1)} all-to-all(f32[32,32,128]{2,1,0:T(8,128)S(1)} %bitcast.12), channel_id=1, replica_groups=mesh['lat'=8,'lon'=4] {'lat','lon'}, dimensions={0} | all-to-all | bytes 1048576 | tf_op jit(solution)/shard_map/all_to_all | solution.py:907
  80.8 1.8 %shard_map.102 = (f32[288,128]{1,0:T(8,128)S(1)}, f32[288,128]{1,0:T(8,128)S(1)}, f32[288,128]{1,0:T(8,128)S(1)}, f32[288,128]{1,0:T(8,128)S(1)}) custom-call(s32[2]{0:T(128)S(1)} %pad_add_fusion.index_ref.refs_0_, bf16[512,512]{1,0:T(8,128)(2,1)S(1)} %get-tuple-element.68.refs_2_.high_ref, bf16[512,512]{1,0:T(8,128)(2,1)S(1)} %get-tuple-element.69.refs_3_.low_ref, ...), custom_call_target="tpu_custom_call" | custom-call | flops 2000000000 | bytes 1 | tf_op jit(solution)/shard_map/pallas_call | solution.py:202
  82.5 1.2 collective-permute-start.11
  84.6 1.9 %collective-permute-done.11.rest_1_ = f32[288,128]{1,0:T(8,128)S(1)} collective-permute-done((f32[288,128]{1,0:T(8,128)S(1)}, f32[288,128]{1,0:T(8,128)S(1)}, u32[]{:S(2)}, u32[]{:S(2)}) %collective-permute-start.11) | collective-permute-done | bytes 147488 | tf_op jit(solution)/shard_map/ppermute | solution.py:786
  86.5 4.8 %collective-permute-done.12.rest_2_ = f32[288,128]{1,0:T(8,128)S(1)} collective-permute-done((f32[288,128]{1,0:T(8,128)S(1)}, f32[288,128]{1,0:T(8,128)S(1)}, u32[]{:S(2)}, u32[]{:S(2)}) %collective-permute-start.12) | collective-permute-done | bytes 147488 | tf_op jit(solution)/shard_map/ppermute | solution.py:786
  91.8 3.3 %shard_map.103 = (f32[8,24,128]{2,1,0:T(8,128)S(1)}, f32[8,24,128]{2,1,0:T(8,128)S(1)}, f32[8,24,128]{2,1,0:T(8,128)S(1)}, f32[8,24,128]{2,1,0:T(8,128)S(1)}, f32[32,24,128]{2,1,0:T(8,128)}) custom-call(s32[2]{0:T(128)S(1)} %pad_add_fusion.index_ref.refs_0_, f32[4]{0:T(128)S(1)} %copy-done.4, s32[768,128]{1,0:T(8,128)S(1)} %bitcast.20, ...), custom_call_target="tpu_custom_call" | custom-call | flops 5400000000 | bytes 1 | tf_op jit(solution)/shard_map/pallas_call | solution.py:202
  96.8 2.7 %collective-permute-done.15.rest_2_ = f32[8,24,128]{2,1,0:T(8,128)S(1)} collective-permute-done((f32[8,24,128]{2,1,0:T(8,128)S(1)}, f32[8,24,128]{2,1,0:T(8,128)S(1)}, u32[]{:S(2)}, u32[]{:S(2)}) %collective-permute-start.15) | collective-permute-done | bytes 98336 | tf_op jit(solution)/shard_map/ppermute | solution.py:786
  99.4 1.5 %collective-permute-done.16.rest_3_ = f32[8,24,128]{2,1,0:T(8,128)S(1)} collective-permute-done((f32[8,24,128]{2,1,0:T(8,128)S(1)}, f32[8,24,128]{2,1,0:T(8,128)S(1)}, u32[]{:S(2)}, u32[]{:S(2)}) %collective-permute-start.16) | collective-permute-done | bytes 98336 | tf_op jit(solution)/shard_map/ppermute | solution.py:786
  101.0 1.3 shard_map.104
  102.3 14.8 %all_to_all.22 = f32[32,24,128]{2,1,0:T(8,128)S(1)} all-to-all(f32[32,24,128]{2,1,0:T(8,128)S(1)} %shard_map.104), channel_id=1, replica_groups=mesh['lat'=8,'lon'=4] {'lat','lon'}, dimensions={0} | all-to-all | bytes 786432 | tf_op jit(solution)/shard_map/all_to_all | solution.py:894
  117.1 2.5 %shard_map.105 = f32[8,4,24,128]{3,2,1,0:T(8,128)S(1)} custom-call(bf16[8,256,256]{2,1,0:T(8,128)(2,1)S(1)} %copy-done.6, bf16[8,256,256]{2,1,0:T(8,128)(2,1)S(1)} %copy-done.8, f32[2,1024,128]{2,1,0:T(8,128)S(1)} %get-tuple-element.79.green_ref, f32[8,4,24,128]{3,2,1,0:T(8,128)S(1)} %bitcast.13), custom_call_target="tpu_custom_call" | custom-call | flops 4000000000 | bytes 1 | tf_op jit(solution)/shard_map/pallas_call | solution.py:202
  119.6 15.6 %all_to_all.23.x_ref = f32[32,24,128]{2,1,0:T(8,128)S(1)} all-to-all(f32[32,24,128]{2,1,0:T(8,128)S(1)} %bitcast.14), channel_id=1, replica_groups=mesh['lat'=8,'lon'=4] {'lat','lon'}, dimensions={0} | all-to-all | bytes 786432 | tf_op jit(solution)/shard_map/all_to_all | solution.py:907
  135.3 1.4 shard_map.106
  136.7 1.3 collective-permute-start.17
  137.9 1.3 collective-permute-start.18
  139.6 4.2 %collective-permute-done.18.rest_2_ = f32[192,128]{1,0:T(8,128)S(1)} collective-permute-done((f32[192,128]{1,0:T(8,128)S(1)}, f32[192,128]{1,0:T(8,128)S(1)}, u32[]{:S(2)}, u32[]{:S(2)}) %collective-permute-start.18) | collective-permute-done | bytes 98336 | tf_op jit(solution)/shard_map/ppermute | solution.py:786
  144.3 1.3 shard_map.107
  (58 shorter events, 11.0 us)
Async XLA Ops:
  0.6 1.3 copy-start.10
  0.6 1.3 copy-start.11
  0.7 1.3 copy-start.1
  0.7 1.3 copy-start
  2.0 1.0 copy-start.9
  3.3 14.7 %collective-permute-start.4 = (f32[32,1024]{1,0:T(8,128)S(1)}, f32[32,1024]{1,0:T(8,128)S(1)}, u32[]{:S(2)}, u32[]{:S(2)}) collective-permute-start(f32[32,1024]{1,0:T(8,128)S(1)} %reshape.47), channel_id=1, source_target_pairs={{0,24},{4,28},{8,16},{12,20},{16,8},{20,12},{24,0},{28,4},{1,25},{... | collective-permute-start | bytes 393224 | tf_op jit(solution)/shard_map/ppermute | solution.py:823
  7.5 10.7 %collective-permute-start.3 = (f32[32,1024]{1,0:T(8,128)S(1)}, f32[32,1024]{1,0:T(8,128)S(1)}, u32[]{:S(2)}, u32[]{:S(2)}) collective-permute-start(f32[32,1024]{1,0:T(8,128)S(1)} %reshape.47), channel_id=1, source_target_pairs={{0,16},{4,20},{8,24},{12,28},{16,0},{20,4},{24,8},{28,12},{1,17},{... | collective-permute-start | bytes 393224 | tf_op jit(solution)/shard_map/ppermute | solution.py:823
  7.5 10.7 %collective-permute-start.2 = (f32[32,1024]{1,0:T(8,128)S(1)}, f32[32,1024]{1,0:T(8,128)S(1)}, u32[]{:S(2)}, u32[]{:S(2)}) collective-permute-start(f32[32,1024]{1,0:T(8,128)S(1)} %reshape.47), channel_id=1, source_target_pairs={{0,8},{4,12},{8,0},{12,4},{16,24},{20,28},{24,16},{28,20},{1,9},{5... | collective-permute-start | bytes 393224 | tf_op jit(solution)/shard_map/ppermute | solution.py:823
  7.8 10.3 %collective-permute-start.1 = (f32[520,128]{1,0:T(8,128)S(1)}, f32[520,128]{1,0:T(8,128)S(1)}, u32[]{:S(2)}, u32[]{:S(2)}) collective-permute-start(f32[520,128]{1,0:T(8,128)S(1)} %bitcast.22), channel_id=1, source_target_pairs={{4,0},{8,4},{12,8},{16,12},{20,16},{24,20},{28,24},{5,1},{9,5},{13... | collective-permute-start | bytes 798728 | tf_op jit(solution)/shard_map/ppermute | solution.py:816
  9.1 14.7 %collective-permute-start = (f32[520,128]{1,0:T(8,128)S(1)}, f32[520,128]{1,0:T(8,128)S(1)}, u32[]{:S(2)}, u32[]{:S(2)}) collective-permute-start(f32[520,128]{1,0:T(8,128)S(1)} %bitcast.21), channel_id=1, source_target_pairs={{0,4},{4,8},{8,12},{12,16},{16,20},{20,24},{24,28},{1,5},{5,9},{9,... | collective-permute-start | bytes 798728 | tf_op jit(solution)/shard_map/ppermute | solution.py:815
  16.0 1.0 copy-start.5
  16.9 1.0 copy-start.7
  23.9 7.1 %copy-start.2 = (f32[4]{0:T(128)S(1)}, f32[4]{0:T(128)}, u32[]{:S(2)}) copy-start(f32[4]{0:T(128)} %shear_ref.1) | copy-start | bytes 52
  23.9 7.1 %copy-start.3 = (f32[4]{0:T(128)S(1)}, f32[4]{0:T(128)}, u32[]{:S(2)}) copy-start(f32[4]{0:T(128)} %restoring_ref.1) | copy-start | bytes 52
  23.9 7.1 %copy-start.4 = (f32[4]{0:T(128)S(1)}, f32[4]{0:T(128)}, u32[]{:S(2)}) copy-start(f32[4]{0:T(128)} %contrast_ref.3) | copy-start | bytes 52
  24.7 4.7 %collective-permute-start.5 = (f32[168,128]{1,0:T(8,128)S(1)}, f32[168,128]{1,0:T(8,128)S(1)}, u32[]{:S(2)}, u32[]{:S(2)}) collective-permute-start(f32[168,128]{1,0:T(8,128)S(1)} %get-tuple-element.62), channel_id=1, source_target_pairs={{0,1},{1,2},{2,3},{3,0},{4,5},{5,6},{6,7},{7,4},{8,9},{9,10},{10,1... | collective-permute-start | bytes 258056 | tf_op jit(solution)/shard_map/ppermute | solution.py:847
  27.1 3.9 %collective-permute-start.6 = (f32[168,128]{1,0:T(8,128)S(1)}, f32[168,128]{1,0:T(8,128)S(1)}, u32[]{:S(2)}, u32[]{:S(2)}) collective-permute-start(f32[168,128]{1,0:T(8,128)S(1)} %get-tuple-element.63), channel_id=1, source_target_pairs={{1,0},{2,1},{3,2},{0,3},{5,4},{6,5},{7,6},{4,7},{9,8},{10,9},{11,1... | collective-permute-start | bytes 258056 | tf_op jit(solution)/shard_map/ppermute | solution.py:848
  27.1 13.9 %collective-permute-start.10 = (f32[128,1024]{1,0:T(8,128)S(1)}, f32[128,1024]{1,0:T(8,128)S(1)}, u32[]{:S(2)}, u32[]{:S(2)}) collective-permute-start(f32[128,1024]{1,0:T(8,128)S(1)} %constant_dynamic-update-slice_fusion.refs_8_), channel_id=1, source_target_pairs={{0,4},{4,0},{8,12},{12,8},{16,20},{20,16},{24,28},{28,24},{1,5},{5... | collective-permute-start | bytes 1572872 | tf_op jit(solution)/shard_map/ppermute | solution.py:823
  34.7 2.2 %collective-permute-start.7 = (f32[8,24,128]{2,1,0:T(8,128)S(1)}, f32[8,24,128]{2,1,0:T(8,128)S(1)}, u32[]{:S(2)}, u32[]{:S(2)}) collective-permute-start(f32[8,24,128]{2,1,0:T(8,128)S(1)} %get-tuple-element.73), channel_id=1, source_target_pairs={{0,1},{1,2},{2,3},{3,0},{4,5},{5,6},{6,7},{7,4},{8,9},{9,10},{10,1... | collective-permute-start | bytes 294920 | tf_op jit(solution)/shard_map/ppermute | solution.py:786
  35.2 4.4 %collective-permute-start.8 = (f32[8,24,128]{2,1,0:T(8,128)S(1)}, f32[8,24,128]{2,1,0:T(8,128)S(1)}, u32[]{:S(2)}, u32[]{:S(2)}) collective-permute-start(f32[8,24,128]{2,1,0:T(8,128)S(1)} %get-tuple-element.74), channel_id=1, source_target_pairs={{0,2},{1,3},{2,0},{3,1},{4,6},{5,7},{6,4},{7,5},{8,10},{9,11},{10,... | collective-permute-start | bytes 294920 | tf_op jit(solution)/shard_map/ppermute | solution.py:786
  35.5 5.6 %collective-permute-start.9 = (f32[8,24,128]{2,1,0:T(8,128)S(1)}, f32[8,24,128]{2,1,0:T(8,128)S(1)}, u32[]{:S(2)}, u32[]{:S(2)}) collective-permute-start(f32[8,24,128]{2,1,0:T(8,128)S(1)} %get-tuple-element.75), channel_id=1, source_target_pairs={{0,3},{1,0},{2,1},{3,2},{4,7},{5,4},{6,5},{7,6},{8,11},{9,8},{10,9... | collective-permute-start | bytes 294920 | tf_op jit(solution)/shard_map/ppermute | solution.py:786
  41.1 18.7 %copy-start.6 = (bf16[8,256,256]{2,1,0:T(8,128)(2,1)S(1)}, bf16[8,256,256]{2,1,0:T(8,128)(2,1)}, u32[]{:S(2)}) copy-start(bf16[8,256,256]{2,1,0:T(8,128)(2,1)} %copy-done.5) | copy-start | bytes 3145732
  41.1 18.7 %copy-start.8 = (bf16[8,256,256]{2,1,0:T(8,128)(2,1)S(1)}, bf16[8,256,256]{2,1,0:T(8,128)(2,1)}, u32[]{:S(2)}) copy-start(bf16[8,256,256]{2,1,0:T(8,128)(2,1)} %copy-done.7) | copy-start | bytes 3145732
  82.5 3.9 %collective-permute-start.11 = (f32[288,128]{1,0:T(8,128)S(1)}, f32[288,128]{1,0:T(8,128)S(1)}, u32[]{:S(2)}, u32[]{:S(2)}) collective-permute-start(f32[288,128]{1,0:T(8,128)S(1)} %get-tuple-element.82), channel_id=1, source_target_pairs={{0,1},{1,2},{2,3},{3,0},{4,5},{5,6},{6,7},{7,4},{8,9},{9,10},{10,1... | collective-permute-start | bytes 442376 | tf_op jit(solution)/shard_map/ppermute | solution.py:786
  83.8 7.5 %collective-permute-start.12 = (f32[288,128]{1,0:T(8,128)S(1)}, f32[288,128]{1,0:T(8,128)S(1)}, u32[]{:S(2)}, u32[]{:S(2)}) collective-permute-start(f32[288,128]{1,0:T(8,128)S(1)} %get-tuple-element.83), channel_id=1, source_target_pairs={{0,2},{1,3},{2,0},{3,1},{4,6},{5,7},{6,4},{7,5},{8,10},{9,11},{10,... | collective-permute-start | bytes 442376 | tf_op jit(solution)/shard_map/ppermute | solution.py:786
  84.6 7.3 %collective-permute-start.13 = (f32[288,128]{1,0:T(8,128)S(1)}, f32[288,128]{1,0:T(8,128)S(1)}, u32[]{:S(2)}, u32[]{:S(2)}) collective-permute-start(f32[288,128]{1,0:T(8,128)S(1)} %get-tuple-element.84), channel_id=1, source_target_pairs={{0,3},{1,0},{2,1},{3,2},{4,7},{5,4},{6,5},{7,6},{8,11},{9,8},{10,9... | collective-permute-start | bytes 442376 | tf_op jit(solution)/shard_map/ppermute | solution.py:786
  95.1 1.6 %collective-permute-start.14 = (f32[8,24,128]{2,1,0:T(8,128)S(1)}, f32[8,24,128]{2,1,0:T(8,128)S(1)}, u32[]{:S(2)}, u32[]{:S(2)}) collective-permute-start(f32[8,24,128]{2,1,0:T(8,128)S(1)} %get-tuple-element.87), channel_id=1, source_target_pairs={{0,1},{1,2},{2,3},{3,0},{4,5},{5,6},{6,7},{7,4},{8,9},{9,10},{10,1... | collective-permute-start | bytes 294920 | tf_op jit(solution)/shard_map/ppermute | solution.py:786
  95.1 4.3 %collective-permute-start.15 = (f32[8,24,128]{2,1,0:T(8,128)S(1)}, f32[8,24,128]{2,1,0:T(8,128)S(1)}, u32[]{:S(2)}, u32[]{:S(2)}) collective-permute-start(f32[8,24,128]{2,1,0:T(8,128)S(1)} %get-tuple-element.88), channel_id=1, source_target_pairs={{0,2},{1,3},{2,0},{3,1},{4,6},{5,7},{6,4},{7,5},{8,10},{9,11},{10,... | collective-permute-start | bytes 294920 | tf_op jit(solution)/shard_map/ppermute | solution.py:786
  95.8 5.2 %collective-permute-start.16 = (f32[8,24,128]{2,1,0:T(8,128)S(1)}, f32[8,24,128]{2,1,0:T(8,128)S(1)}, u32[]{:S(2)}, u32[]{:S(2)}) collective-permute-start(f32[8,24,128]{2,1,0:T(8,128)S(1)} %get-tuple-element.89), channel_id=1, source_target_pairs={{0,3},{1,0},{2,1},{3,2},{4,7},{5,4},{6,5},{7,6},{8,11},{9,8},{10,9... | collective-permute-start | bytes 294920 | tf_op jit(solution)/shard_map/ppermute | solution.py:786
  136.7 2.9 %collective-permute-start.17 = (f32[192,128]{1,0:T(8,128)S(1)}, f32[192,128]{1,0:T(8,128)S(1)}, u32[]{:S(2)}, u32[]{:S(2)}) collective-permute-start(f32[192,128]{1,0:T(8,128)S(1)} %get-tuple-element.91), channel_id=1, source_target_pairs={{0,1},{1,2},{2,3},{3,0},{4,5},{5,6},{6,7},{7,4},{8,9},{9,10},{10,1... | collective-permute-start | bytes 294920 | tf_op jit(solution)/shard_map/ppermute | solution.py:786
  137.9 5.8 %collective-permute-start.18 = (f32[192,128]{1,0:T(8,128)S(1)}, f32[192,128]{1,0:T(8,128)S(1)}, u32[]{:S(2)}, u32[]{:S(2)}) collective-permute-start(f32[192,128]{1,0:T(8,128)S(1)} %get-tuple-element.92), channel_id=1, source_target_pairs={{0,2},{1,3},{2,0},{3,1},{4,6},{5,7},{6,4},{7,5},{8,10},{9,11},{10,... | collective-permute-start | bytes 294920 | tf_op jit(solution)/shard_map/ppermute | solution.py:786
  139.2 5.2 %collective-permute-start.19 = (f32[192,128]{1,0:T(8,128)S(1)}, f32[192,128]{1,0:T(8,128)S(1)}, u32[]{:S(2)}, u32[]{:S(2)}) collective-permute-start(f32[192,128]{1,0:T(8,128)S(1)} %get-tuple-element.93), channel_id=1, source_target_pairs={{0,3},{1,0},{2,1},{3,2},{4,7},{5,4},{6,5},{7,6},{8,11},{9,8},{10,9... | collective-permute-start | bytes 294920 | tf_op jit(solution)/shard_map/ppermute | solution.py:786
